TPU v7x, 32 devices: a whole 2x2x4 slice. The times are simulated.
32 devices in a mesh: seg: 16 (over z, y, core), blk: 2 (over x).
Axes of the slice: x: 2, y: 2, z: 4, core: 2. Of those that a mesh axis runs over, the one named last changes fastest.
Arguments:
- state: bfloat16 [16, 4, 128, 2048], P('seg', 'blk'), may hold values from -6 to 6
- left_env: bfloat16 [16, 14, 4, 128, 128], P('seg', None, 'blk'), may hold values from -5 to 5
- right_env: bfloat16 [16, 14, 4, 128, 128], P('seg', None, 'blk'), may hold values from -3 to 3
- site_ops: bfloat16 [16, 14, 16, 16], P('seg'), may hold values from -4 to 4
- sector_map: int32 [16, 14, 4], P('seg'), may hold values from 0 to 3, as said below
- ranks: int32 [16, 4], P('seg', 'blk'), may hold values from 1 to 128
Outputs:
- new_state: bfloat16 [16, 4, 128, 2048], P('seg', 'blk')
- from_left: float32 [16, 14, 4, 128, 128], P('seg', None, 'blk')
- from_right: float32 [16, 14, 4, 128, 128], P('seg', None, 'blk')
Inputs may be any that keep to these rules, and one draw needn't show every extreme that they name: `sector_map`: channel 0 carries every block into itself; the other channels' source blocks are arbitrary.
All inputs are finite; a program needn't handle non-finite values.
Results may differ from a plain program's by a relative error of at most 0.012.
Values may be sent and summed in bfloat16 or wider, within the bound.
No kernel may reach another device: no remote copies, remote signals or barrier semaphores. Data moves between devices by JAX's collectives and lax.ppermute only.
A program may use at most 192 MiB of HBM per device.

v0:
```python
import functools
import math

import jax
import jax.numpy as jnp
from jax import lax
from jax.experimental import pallas as pl
from jax.experimental.pallas import tpu as pltpu
from jax.sharding import PartitionSpec as P

STEP_SIZE = 0.25
EPSILON = 1e-06
LANES = 128
ROWS = 16
CHUNK = 32
F32 = jnp.float32
BF16 = jnp.bfloat16
VMEM = pl.BlockSpec(memory_space=pltpu.VMEM)
HBM = pl.BlockSpec(memory_space=pltpu.HBM)
SMEM = pl.BlockSpec(memory_space=pltpu.SMEM)
COST = pl.CostEstimate(flops=1024, bytes_accessed=1024, transcendentals=0)
PARAMS = pltpu.CompilerParams(vmem_limit_bytes=32 * 1024 * 1024)


def dot(left, right):
    return lax.dot_general(
        left, right, (((1,), (0,)), ((), ())), preferred_element_type=F32
    )


def make_kron(ops_ref, kron_ref, spread_ref):
    chan, phys, _ = ops_ref.shape
    wide = phys * ROWS
    columns = lax.broadcasted_iota(jnp.int32, (phys, wide), 1)
    spread = (columns // ROWS == lax.broadcasted_iota(jnp.int32, (phys, wide), 0)).astype(F32)
    spread_ref[...] = dot(ops_ref[...].reshape(chan * phys, phys), spread.astype(BF16))
    same = lax.broadcasted_iota(jnp.int32, (ROWS, wide), 1) % ROWS == lax.broadcasted_iota(
        jnp.int32, (ROWS, wide), 0
    )

    def one(k, carry):
        rows = spread_ref[pl.ds(pl.multiple_of(k * phys, phys), phys), :]
        for p in range(phys):
            full = jnp.broadcast_to(rows[p : p + 1], (ROWS, wide))
            kron_ref[k, p * ROWS : (p + 1) * ROWS, :] = jnp.where(same, full, 0.0).astype(BF16)
        return carry

    lax.fori_loop(0, chan, one, 0)


def list_pairs(rel_ref, low, high, chan_list, src_list, live_list, dest_list, only=None):
    chan, dests = rel_ref.shape
    place = jnp.int32(0)
    for b in range(dests) if only is None else only:
        for k in range(chan):
            source = rel_ref[k, b]
            chan_list[place] = k
            src_list[place] = source - low
            live_list[place] = 1
            dest_list[place] = b
            place = place + jnp.where((source >= low) & (source < high), 1, 0)
        chan_list[place] = 0
        src_list[place] = 0
        live_list[place] = 0
        dest_list[place] = b
        place = place + lax.rem(place, 2)
    return place // 2


def add_pairs(steps, lists, kron_ref, x_ref, left_ref, right_t_ref, acc_ref, mixed_ref, part_ref):
    chan_list, src_list, live_list, dest_list = lists
    rows = x_ref.shape[1]
    phys = x_ref.shape[2] // LANES

    def mix(s):
        for i in range(2):
            source = src_list[2 * s + i]
            kron = kron_ref[chan_list[2 * s + i]]
            for g in range(rows // (2 * ROWS)):
                halves = []
                for j in range(2):
                    r0 = (2 * g + j) * ROWS
                    halves.append(
                        jnp.concatenate(
                            [
                                x_ref[source, r0 : r0 + ROWS, q * LANES : (q + 1) * LANES]
                                for q in range(phys)
                            ],
                            axis=0,
                        )
                    )
                out = dot(kron, jnp.concatenate(halves, axis=1)).astype(BF16)
                for j in range(2):
                    r0 = (2 * g + j) * ROWS
                    for p in range(phys):
                        mixed_ref[i, r0 : r0 + ROWS, p * LANES : (p + 1) * LANES] = out[
                            p * ROWS : (p + 1) * ROWS, j * LANES : (j + 1) * LANES
                        ]

    def step(s, follow):
        dest = dest_list[2 * s]
        weights = []
        for i in range(2):
            k = chan_list[2 * s + i]
            part = dot(left_ref[k, dest], mixed_ref[i]).astype(BF16)
            for p in range(phys):
                part_ref[p * rows : (p + 1) * rows, i * LANES : (i + 1) * LANES] = part[
                    :, p * LANES : (p + 1) * LANES
                ]
            right = right_t_ref[k, dest]
            if i == 1:
                right = jnp.where(live_list[2 * s + 1] > 0, right, jnp.zeros_like(right))
            weights.append(right)
        if follow:
            mix(s + 1)
        image = dot(part_ref[...], jnp.concatenate(weights, axis=0))
        for p in range(phys):
            acc_ref[dest, :, p * LANES : (p + 1) * LANES] += image[p * rows : (p + 1) * rows]

    def middle(s, carry):
        step(s, True)
        return carry

    @pl.when(steps > 0)
    def _():
        mix(0)
        lax.fori_loop(0, steps - 1, middle, 0)
        step(steps - 1, False)


def fold(values):
    total = values[:, :LANES]
    for p in range(1, values.shape[1] // LANES):
        total = total + values[:, p * LANES : (p + 1) * LANES]
    return total


def row_loop(blocks, rows, body, count, first=0):
    zeros = tuple(jnp.zeros((CHUNK, LANES), F32) for _ in range(count))
    per = rows // CHUNK

    def step(n, carry):
        start = pl.multiple_of(lax.rem(n, per) * CHUNK, CHUNK)
        return body(first + n // per, pl.ds(start, CHUNK), start, carry)

    return lax.fori_loop(0, blocks * per, step, zeros)


def kept_rows(rank, start):
    row = start + lax.broadcasted_iota(jnp.int32, (CHUNK, LANES), 0)
    return (row < rank).astype(F32)


def put_sums(out_ref, values, first=0):
    for n, value in enumerate(values):
        out_ref[first + n : first + n + 1, :] = jnp.full((1, LANES), 1.0, F32) * jnp.sum(value)


def common_shift(mine_ref, theirs_ref):
    num = mine_ref[0:1, :] + theirs_ref[0:1, :]
    den = mine_ref[1:2, :] + theirs_ref[1:2, :]
    return jnp.where(den > 0, num / jnp.where(den > 0, den, 1.0), 0.0)


def cut(b, x_ref, out_ref):
    out_ref[0] = x_ref[b]


def first_local(
    rel_ref, ops_ref, x_ref, left_ref, right_ref,
    kron_ref, right_t_ref, image_ref, sums_ref,
    mixed_ref, part_ref, chan_list, src_list, live_list, dest_list, spread_ref, fetched_ref, sem,
):
    lists = (chan_list, src_list, live_list, dest_list)
    fetch = pltpu.make_async_copy(right_ref, fetched_ref, sem)
    fetch.start()
    make_kron(ops_ref, kron_ref, spread_ref)
    chan, dests = left_ref.shape[:2]
    fetch.wait()

    def turn(n, carry):
        for k in range(2):
            for b in range(dests):
                right_t_ref[2 * n + k, b] = fetched_ref[2 * n + k, b].T
        return carry

    lax.fori_loop(0, chan // 2, turn, 0)
    image_ref[...] = jnp.zeros_like(image_ref)
    steps = list_pairs(rel_ref, 0, dests, *lists)
    add_pairs(steps, lists, kron_ref, x_ref, left_ref, right_t_ref, image_ref, mixed_ref, part_ref)

    def sums(b, r, start, carry):
        x = x_ref[b, r, :].astype(F32)
        return carry[0] + fold(x * image_ref[b, r, :]), carry[1] + fold(x * x)

    totals = row_loop(dests, x_ref.shape[1], sums, 2)
    sums_ref[...] = jnp.zeros_like(sums_ref)
    put_sums(sums_ref, totals)


def local_sources(
    rel_ref, kron_ref, x_ref, left_ref, right_t_ref,
    acc_ref,
    mixed_ref, part_ref, *lists,
):
    acc_ref[...] = jnp.zeros_like(acc_ref)
    steps = list_pairs(rel_ref, 0, left_ref.shape[1], *lists)
    add_pairs(steps, lists, kron_ref, x_ref, left_ref, right_t_ref, acc_ref, mixed_ref, part_ref)


def first_remote(
    rel_ref, kron_ref, other_ref, left_ref, right_t_ref, before_ref, local_sums_ref,
    acc_ref, sums_ref,
    mixed_ref, part_ref, *lists,
):
    dests = left_ref.shape[1]
    sums_ref[...] = local_sums_ref[...]
    steps = list_pairs(rel_ref, dests, dests + 1, *lists)
    add_pairs(steps, lists, kron_ref, other_ref, left_ref, right_t_ref, acc_ref, mixed_ref, part_ref)


def first_finish(
    dest, rel_ref, kron_ref, other_ref, left_ref, right_t_ref, before_ref, x_ref, mine_ref,
    theirs_ref, *refs,
):
    dests = left_ref.shape[1]
    last = dest == dests - 1
    if last:
        earlier_ref, acc_ref, guess_ref, all_ref = refs[:4]
        all_ref[0:dest] = earlier_ref[...]
    else:
        acc_ref, guess_ref = refs[:2]
    mixed_ref, part_ref = refs[-6:-4]
    lists = refs[-4:]
    steps = list_pairs(rel_ref, dests + 1, 2 * dests, *lists, only=(dest,))
    add_pairs(steps, lists, kron_ref, other_ref, left_ref, right_t_ref, acc_ref, mixed_ref, part_ref)
    shift = common_shift(mine_ref, theirs_ref)
    keep_state = jnp.tile(1.0 + STEP_SIZE * shift, (1, x_ref.shape[2] // LANES))

    def update(b, r, start, carry):
        x = x_ref[b, r, :].astype(F32)
        guess = (keep_state * x - STEP_SIZE * acc_ref[b, r, :]).astype(BF16)
        guess_ref[0, r, :] = guess
        if last:
            all_ref[b, r, :] = guess
        return carry

    row_loop(1, x_ref.shape[1], update, 0, first=dest)


def second_remote(
    rel_ref, rank_ref, kron_ref, other_ref, left_ref, right_t_ref, before_ref, x_ref, image_ref,
    guess_ref,
    acc_ref, sums_ref,
    mixed_ref, part_ref, *lists,
):
    dests, rows, _ = x_ref.shape
    steps = list_pairs(rel_ref, dests, dests + 1, *lists)
    add_pairs(steps, lists, kron_ref, other_ref, left_ref, right_t_ref, acc_ref, mixed_ref, part_ref)

    def sums(b, r, start, carry):
        x = x_ref[b, r, :].astype(F32)
        guess = guess_ref[b, r, :].astype(F32)
        image = image_ref[b, r, :]
        keep = kept_rows(rank_ref[b], start)
        xx, xg, gg = fold(x * x), fold(x * guess), fold(guess * guess)
        new = (fold(x * image), xx, fold(guess * image), xg, gg, keep * gg, keep * xx, keep * xg)
        return tuple(total + value for total, value in zip(carry, new))

    put_sums(sums_ref, row_loop(dests, rows, sums, 8))


def second_finish(
    rel_ref, rank_ref, kron_ref, other_ref, left_ref, right_t_ref, before_ref, x_ref, guess_ref,
    mine_ref, theirs_ref, early_ref,
    kept_ref, sums_ref,
    mixed_ref, part_ref, *lists,
):
    dests, rows, width = x_ref.shape
    steps = list_pairs(rel_ref, dests + 1, 2 * dests, *lists)
    add_pairs(steps, lists, kron_ref, other_ref, left_ref, right_t_ref, kept_ref, mixed_ref, part_ref)
    shift = common_shift(mine_ref, theirs_ref)
    keep_guess = jnp.tile(1.0 + STEP_SIZE * shift, (1, width // LANES))

    def sums(b, r, start, carry):
        x = x_ref[b, r, :].astype(F32)
        guess = guess_ref[b, r, :].astype(F32)
        kept = keep_guess * guess - STEP_SIZE * kept_ref[b, r, :]
        kept_ref[b, r, :] = kept
        keep = kept_rows(rank_ref[b], start)
        kg, kx = fold(kept * guess), fold(kept * x)
        new = (kg, kx, keep * kg, keep * kx, keep * fold(kept * kept))
        return tuple(total + value for total, value in zip(carry, new))

    totals = row_loop(dests, rows, sums, 5)
    sums_ref[0:8, :] = early_ref[...]
    put_sums(sums_ref, totals, first=8)
    sums_ref[13:16, :] = jnp.zeros((3, LANES), F32)


def normalize(
    cells, rank_ref, kept_ref, guess_ref, x_ref, mine_ref, theirs_ref, my_sums_ref, their_sums_ref,
    state_ref, turned_ref,
):
    both = my_sums_ref[...] + their_sums_ref[...]
    xv, xx, gv, xg, gg, gg_kept, xx_kept, xg_kept, kg, kx, kg_kept, kx_kept, kk_kept = (
        both[n : n + 1] for n in range(13)
    )
    shift = common_shift(mine_ref, theirs_ref)
    delta = STEP_SIZE * (xv / xx - shift)
    scale = (1.0 + STEP_SIZE * shift) / STEP_SIZE
    gw, xw = scale * gg - kg / STEP_SIZE, scale * xg - kx / STEP_SIZE
    num = gw + delta * (xw + gv + delta * xv)
    den = gg + delta * (2.0 * xg + delta * xx)
    beta = STEP_SIZE * (num / den - shift)
    of_guess, of_state = beta + delta, beta * delta
    norm = (
        kk_kept
        + of_guess * (2.0 * kg_kept + of_guess * gg_kept)
        + of_state * (2.0 * kx_kept + of_state * xx_kept + 2.0 * of_guess * xg_kept)
    )
    gain = jnp.sqrt(cells / (jnp.maximum(norm, 0.0) + EPSILON))
    blocks, rows, width = kept_ref.shape
    group = 8 * LANES
    per = width // group
    row = lax.broadcasted_iota(jnp.int32, (rows, LANES), 0)

    def one(n, carry):
        b = n // per
        factor = jnp.where(row < rank_ref[b], gain, 0.0)
        for p in range(8):
            cols = pl.ds(pl.multiple_of(lax.rem(n, per) * group + p * LANES, LANES), LANES)
            kept = (
                kept_ref[b, :, cols]
                + of_guess * guess_ref[b, :, cols].astype(F32)
                + of_state * x_ref[b, :, cols].astype(F32)
            )
            state = (kept * factor).astype(BF16)
            state_ref[b, :, cols] = state
            turned_ref[b, :, cols] = state.T
        return carry

    lax.fori_loop(0, blocks * per, one, 0)


def environments(first, count, scale, env_ref, inner_ref, outer_ref, out_ref, mid_ref):
    dests, rows, width = outer_ref.shape
    phys = width // LANES
    pairs = mid_ref.shape[0] // dests

    def step(n, carry):
        for j in range(pairs):
            k = first + 2 * (n * pairs + j)
            for b in range(dests):
                env = jnp.concatenate([env_ref[k, b], env_ref[k + 1, b]], axis=0)
                mid = dot(env, inner_ref[b]).astype(BF16)
                for p in range(phys):
                    for i in range(2):
                        mid_ref[
                            j * dests + b, p * rows : (p + 1) * rows, i * LANES : (i + 1) * LANES
                        ] = mid[i * rows : (i + 1) * rows, p * LANES : (p + 1) * LANES]
        for j in range(pairs):
            place = 2 * (n * pairs + j)
            for b in range(dests):
                out = (dot(outer_ref[b], mid_ref[j * dests + b]) * scale).astype(BF16)
                out_ref[place, b] = out[:, :LANES]
                out_ref[place + 1, b] = out[:, LANES:]
        return carry

    lax.fori_loop(0, count // (2 * pairs), step, 0)


def normalize_and_left(
    first, count, scale, cells,
    rank_ref, kept_ref, guess_ref, x_ref, mine_ref, theirs_ref, my_sums_ref, their_sums_ref, env_ref,
    new_ref, state_ref, turned_ref, out_ref,
    mid_ref, sem,
):
    normalize(
        cells, rank_ref, kept_ref, guess_ref, x_ref, mine_ref, theirs_ref, my_sums_ref,
        their_sums_ref, state_ref, turned_ref,
    )
    copy = pltpu.make_async_copy(state_ref, new_ref, sem)
    copy.start()
    environments(first, count, scale, env_ref, state_ref, turned_ref, out_ref, mid_ref)
    copy.wait()


def widen(places, *refs):
    pieces, (outs, wides, sems) = refs[: len(places)], (refs[-5:-3], refs[-3:-1], refs[-1])
    copies = []
    for piece, (side, begin) in zip(pieces, places):
        for n in range(0, piece.shape[0], 2):
            span = pl.ds(begin + n, 2)
            wides[side][begin + n : begin + n + 2] = piece[n : n + 2].astype(F32)
            copy = pltpu.make_async_copy(
                wides[side].at[span], outs[side].at[span], sems.at[len(copies)]
            )
            copy.start()
            copies.append(copy)
    for copy in copies:
        copy.wait()


def shards(state, left_env, right_env, site_ops, sector_map, ranks):
    dests, rows, width = state.shape[1:]
    chan, phys = site_ops.shape[1:3]
    groups = lax.axis_size("blk")
    total_blocks = groups * dests
    first_block = lax.axis_index("blk") * dests
    x, left, right, ops = state[0], left_env[0], right_env[0], site_ops[0]
    local_map = lax.dynamic_slice_in_dim(sector_map[0], first_block, dests, 1)
    rel = lax.rem(local_map - first_block + total_blocks, total_blocks)

    swap = [(g, groups - 1 - g) for g in range(groups)]

    def trade(value):
        return lax.ppermute(value, "blk", swap)

    def shape(dims, kind):
        return jax.ShapeDtypeStruct(dims, kind)

    wave = (dests, rows, width)
    wave_f32 = shape(wave, F32)
    wave_b16 = shape(wave, BF16)
    sums_kind = shape((8, LANES), F32)
    lists = [pltpu.SMEM((chan * dests + 2 * dests + 1,), jnp.int32)] * 4
    pair_scratch = [
        pltpu.VMEM((2, rows, width), BF16), pltpu.VMEM((phys * rows, 2 * LANES), BF16)
    ] + lists

    def call(body, specs, outs, scratch, *args, aliases={}):
        return pl.pallas_call(
            body,
            in_specs=specs,
            out_specs=jax.tree.map(lambda _: VMEM, outs),
            out_shape=outs,
            scratch_shapes=scratch,
            compiler_params=PARAMS,
            cost_estimate=COST,
            input_output_aliases=aliases,
        )(*args)

    block = shape((1, rows, width), BF16)
    own = [
        call(functools.partial(cut, b), [VMEM], block, [], x) for b in range(dests)
    ]
    other = [trade(value) for value in own]
    kron, right_t, image, mine = call(
        first_local, [SMEM] + [VMEM] * 3 + [HBM],
        (shape((chan, phys * ROWS, phys * ROWS), BF16), shape(right.shape, BF16), wave_f32, sums_kind),
        pair_scratch
        + [
            pltpu.VMEM((chan * phys, phys * ROWS), F32),
            pltpu.VMEM(right.shape, BF16),
            pltpu.SemaphoreType.DMA,
        ],
        rel, ops, x, left, right,
    )
    image, mine = call(
        first_remote, [SMEM] + [VMEM] * 6, (wave_f32, sums_kind), pair_scratch,
        rel, kron, other[0], left, right_t, image, mine, aliases={5: 0},
    )
    theirs = trade(mine)
    image, first_guess = call(
        functools.partial(first_finish, 0), [SMEM] + [VMEM] * 8,
        (wave_f32, block), pair_scratch,
        rel, kron, other[1], left, right_t, image, x, mine, theirs, aliases={5: 0},
    )
    image, last_guess, guess = call(
        functools.partial(first_finish, 1), [SMEM] + [VMEM] * 9,
        (wave_f32, block, wave_b16), pair_scratch,
        rel, kron, other[1], left, right_t, image, x, mine, theirs, first_guess, aliases={5: 0},
    )
    other = [trade(first_guess), trade(last_guess)]
    acc = call(
        local_sources, [SMEM] + [VMEM] * 4, wave_f32, pair_scratch,
        rel, kron, guess, left, right_t,
    )
    acc, early_sums = call(
        second_remote, [SMEM] * 2 + [VMEM] * 8, (wave_f32, sums_kind), pair_scratch,
        rel, ranks[0], kron, other[0], left, right_t, acc, x, image, guess, aliases={6: 0},
    )
    kept, my_sums = call(
        second_finish, [SMEM] * 2 + [VMEM] * 10, (wave_f32, shape((16, LANES), F32)), pair_scratch,
        rel, ranks[0], kron, other[1], left, right_t, acc, x, guess, mine, theirs, early_sums,
        aliases={6: 0},
    )
    their_sums = trade(my_sums)

    env_scale = 1.0 / math.sqrt(phys * rows)
    cells = float(total_blocks * rows * width)
    early, later = 8, 8

    def mid(count):
        pairs = next(n for n in (2, 3, 1) if count % (2 * n) == 0)
        return [pltpu.VMEM((pairs * dests, width, 2 * LANES), BF16)]

    def sent(value, steps):
        count = lax.axis_size("seg")
        begin, end = max(0, -steps), min(count, count - steps)
        return lax.ppermute(value, "seg", [(s, s + steps) for s in range(begin, end)])

    def env_kind(count):
        return shape((count,) + left.shape[1:], BF16)

    def env_call(begin, count, env, inner, outer):
        return call(
            functools.partial(environments, begin, count, env_scale),
            [VMEM] * 3, env_kind(count), mid(count), env, inner, outer,
        )

    new_state, state_kept, turned, piece = pl.pallas_call(
        functools.partial(normalize_and_left, 0, early, env_scale, cells),
        in_specs=[SMEM] + [VMEM] * 8,
        out_specs=(HBM, VMEM, VMEM, VMEM),
        out_shape=(wave_b16, wave_b16, wave_b16, env_kind(early)),
        scratch_shapes=mid(early) + [pltpu.SemaphoreType.DMA],
        compiler_params=PARAMS,
        cost_estimate=COST,
    )(ranks[0], kept, guess, x, mine, theirs, my_sums, their_sums, left)
    pieces = [
        sent(piece, 1),
        sent(env_call(0, later, right, turned, state_kept), -1),
        sent(env_call(early, chan - early, left, state_kept, turned), 1),
        sent(env_call(later, chan - later, right, turned, state_kept), -1),
    ]
    env_f32 = shape(left.shape, F32)

    def widened(places, values, filled):
        count = len(values)
        return pl.pallas_call(
            functools.partial(widen, places),
            in_specs=[VMEM] * count + [HBM] * len(filled),
            out_specs=(HBM, HBM),
            out_shape=(env_f32, env_f32),
            input_output_aliases={count + n: n for n in range(len(filled))},
            scratch_shapes=[pltpu.VMEM(left.shape, F32)] * 2 + [pltpu.SemaphoreType.DMA((chan,))],
            compiler_params=PARAMS,
            cost_estimate=COST,
        )(*values, *filled)

    filled = widened(((0, 0),), pieces[:1], ())
    filled = widened(((1, 0),), pieces[1:2], filled)
    received_left, received_right = widened(((0, early), (1, later)), pieces[2:], filled)
    return (new_state[None], received_left[None], received_right[None])


def solution(mesh):
    placed = (
        P("seg", "blk", None, None),
        P("seg", None, "blk", None, None),
        P("seg", None, "blk", None, None),
        P("seg", None, None, None),
        P("seg", None, None),
        P("seg", "blk"),
    )
    return jax.shard_map(
        shards,
        mesh=mesh,
        in_specs=placed,
        out_specs=(
            P("seg", "blk", None, None),
            P("seg", None, "blk", None, None),
            P("seg", None, "blk", None, None),
        ),
        check_vma=False,
    )
```

profile of v0, /device:TPU:1, one launch (start us, length us, event | category | flops | bytes accessed | tf_op | source)
XLA Modules:
  0.0 101.8 jit_solution(1328901686046449437)
XLA Ops:
  0.6 0.0 copy-start
  0.6 0.0 copy-start.1
  0.7 1.3 %copy-done.1 = bf16[1,2,128,2048]{3,2,1,0:T(8,128)(2,1)S(1)} copy-done((bf16[1,2,128,2048]{3,2,1,0:T(8,128)(2,1)S(1)}, bf16[1,2,128,2048]{3,2,1,0:T(8,128)(2,1)}, u32[]{:S(2)}) %copy-start.1) | copy-done | bytes 1048600
  1.9 0.0 copy-start.6
  1.9 0.0 copy-start.2
  2.0 0.0 copy-start.3
  2.0 0.0 copy-start.4
  2.0 0.8 shard_map.87
  2.8 2.0 %collective-permute-start.1 = (bf16[1,128,2048]{2,1,0:T(8,128)(2,1)}, bf16[1,128,2048]{2,1,0:T(8,128)(2,1)}, u32[]{:S(2)}, u32[]{:S(2)}) collective-permute-start(bf16[1,128,2048]{2,1,0:T(8,128)(2,1)} %shard_map.87), channel_id=1, source_target_pairs={{0,1},{1,0},{2,3},{3,2},{4,5},{5,4},{6,7},{7,6},{8,9},{9,8},{10,11... | collective-permute-start | bytes 1572872 | tf_op jit(solution)/shard_map/ppermute | solution.py:418
  4.8 0.8 shard_map.86
  5.7 0.0 collective-permute-start
  5.7 0.0 copy-done.6
  5.7 0.1 copy.18
  5.8 0.0 copy-done
  5.8 0.0 copy-done.2
  5.8 0.0 copy-done.3
  5.8 0.0 copy-done.4
  5.8 11.8 %shard_map.85 = (bf16[14,256,256]{2,1,0:T(8,128)(2,1)S(1)}, bf16[14,2,128,128]{3,2,1,0:T(8,128)(2,1)S(1)}, f32[2,128,2048]{2,1,0:T(8,128)S(1)}, f32[8,128]{1,0:T(8,128)S(1)}) custom-call(s32[14,2]{1,0:T(8,128)S(1)} %negate_select_fusion.rel_ref, bf16[14,16,16]{2,1,0:T(8,128)(2,1)S(1)} %bitcast.30, bf16[2,128,2048]{2,1,0:T(8,128)(2,1)S(1)} %bitcast.21, ...), custom_call_target="tpu_custom_call" | custom-call | flops 1024 | bytes 1024 | tf_op jit(solution)/shard_map/pallas_call | solution.py:433
  17.6 0.0 collective-permute-done.1.other_ref
  17.6 6.3 %shard_map.88 = (f32[2,128,2048]{2,1,0:T(8,128)S(1)}, f32[8,128]{1,0:T(8,128)S(1)}) custom-call(s32[14,2]{1,0:T(8,128)S(1)} %negate_select_fusion.rel_ref, bf16[14,256,256]{2,1,0:T(8,128)(2,1)S(1)} %get-tuple-element.28.kron_ref, bf16[1,128,2048]{2,1,0:T(8,128)(2,1)} %collective-permute-done.1.other_ref, ...), custom_call_target="tpu_custom_call", output_to_operand_aliasing={{0}: (5, {})} | custom-call | flops 1024 | bytes 1024 | tf_op jit(solution)/shard_map/pallas_call | solution.py:433
  23.9 0.6 collective-permute-start.2
  24.4 3.5 %collective-permute-done.other_ref = bf16[1,128,2048]{2,1,0:T(8,128)(2,1)S(1)} collective-permute-done((bf16[1,128,2048]{2,1,0:T(8,128)(2,1)}, bf16[1,128,2048]{2,1,0:T(8,128)(2,1)S(1)}, u32[]{:S(2)}, u32[]{:S(2)}) %collective-permute-start) | collective-permute-done | bytes 524320 | tf_op jit(solution)/shard_map/ppermute | solution.py:418
  27.9 0.1 collective-permute-done.2.theirs_ref
  28.0 2.2 %shard_map.89 = (f32[2,128,2048]{2,1,0:T(8,128)S(1)}, bf16[1,128,2048]{2,1,0:T(8,128)(2,1)S(1)}) custom-call(s32[14,2]{1,0:T(8,128)S(1)} %negate_select_fusion.rel_ref, bf16[14,256,256]{2,1,0:T(8,128)(2,1)S(1)} %get-tuple-element.28.kron_ref, bf16[1,128,2048]{2,1,0:T(8,128)(2,1)S(1)} %collective-permute-done.other_ref, ...), custom_call_target="tpu_custom_call", output_to_operand_aliasing={{0}: (5, {})} | custom-call | flops 1024 | bytes 1024 | tf_op jit(solution)/shard_map/pallas_call | solution.py:433
  30.2 1.2 %collective-permute-start.4 = (bf16[1,128,2048]{2,1,0:T(8,128)(2,1)S(1)}, bf16[1,128,2048]{2,1,0:T(8,128)(2,1)S(1)}, u32[]{:S(2)}, u32[]{:S(2)}) collective-permute-start(bf16[1,128,2048]{2,1,0:T(8,128)(2,1)S(1)} %get-tuple-element.35.refs_0_), channel_id=1, source_target_pairs={{0,1},{1,0},{2,3},{3,2},{4,5},{5,4},{6,7},{7,6},{8,9},{9,8},{10,11... | collective-permute-start | bytes 1572872 | tf_op jit(solution)/shard_map/ppermute | solution.py:418
  31.4 2.2 %shard_map.90 = (f32[2,128,2048]{2,1,0:T(8,128)S(1)}, bf16[1,128,2048]{2,1,0:T(8,128)(2,1)S(1)}, bf16[2,128,2048]{2,1,0:T(8,128)(2,1)S(1)}) custom-call(s32[14,2]{1,0:T(8,128)S(1)} %negate_select_fusion.rel_ref, bf16[14,256,256]{2,1,0:T(8,128)(2,1)S(1)} %get-tuple-element.28.kron_ref, ...), custom_call_target="tpu_custom_call", output_to_operand_aliasing={{0}: (5, {})} | custom-call | flops 1024 | bytes 1024 | tf_op jit(solution)/shard_map/pallas_call | solution.py:433
  33.5 1.4 %collective-permute-start.3 = (bf16[1,128,2048]{2,1,0:T(8,128)(2,1)S(1)}, bf16[1,128,2048]{2,1,0:T(8,128)(2,1)S(1)}, u32[]{:S(2)}, u32[]{:S(2)}) collective-permute-start(bf16[1,128,2048]{2,1,0:T(8,128)(2,1)S(1)} %get-tuple-element.36), channel_id=1, source_target_pairs={{0,1},{1,0},{2,3},{3,2},{4,5},{5,4},{6,7},{7,6},{8,9},{9,8},{10,11... | collective-permute-start | bytes 1572872 | tf_op jit(solution)/shard_map/ppermute | solution.py:418
  34.9 0.0 copy-start.5
  34.9 9.8 %shard_map.91.before_ref = f32[2,128,2048]{2,1,0:T(8,128)S(1)} custom-call(s32[14,2]{1,0:T(8,128)S(1)} %negate_select_fusion.rel_ref, bf16[14,256,256]{2,1,0:T(8,128)(2,1)S(1)} %get-tuple-element.28.kron_ref, bf16[2,128,2048]{2,1,0:T(8,128)(2,1)S(1)} %get-tuple-element.37.x_ref.guess_ref, bf16[14,2,128,128]{3,2,1,0:T(8,128)(2,1)S(1)} %bitcast.14, ...), custom_call_target="tpu_custom_call" | custom-call | flops 1024 | bytes 1024 | tf_op jit(solution)/shard_map/pallas_call | solution.py:433
  44.7 0.0 collective-permute-done.4.other_ref
  44.7 0.0 copy-done.5
  44.7 7.6 %shard_map.92 = (f32[2,128,2048]{2,1,0:T(8,128)S(1)}, f32[8,128]{1,0:T(8,128)S(1)}) custom-call(s32[14,2]{1,0:T(8,128)S(1)} %negate_select_fusion.rel_ref, s32[2]{0:T(128)S(1)} %bitcast.31, bf16[14,256,256]{2,1,0:T(8,128)(2,1)S(1)} %get-tuple-element.28.kron_ref, ...), custom_call_target="tpu_custom_call", output_to_operand_aliasing={{0}: (6, {})} | custom-call | flops 1024 | bytes 1024 | tf_op jit(solution)/shard_map/pallas_call | solution.py:433
  52.4 0.3 collective-permute-done.3.other_ref
  52.7 4.0 %shard_map.93 = (f32[2,128,2048]{2,1,0:T(8,128)S(1)}, f32[16,128]{1,0:T(8,128)S(1)}) custom-call(s32[14,2]{1,0:T(8,128)S(1)} %negate_select_fusion.rel_ref, s32[2]{0:T(128)S(1)} %bitcast.32, bf16[14,256,256]{2,1,0:T(8,128)(2,1)S(1)} %get-tuple-element.28.kron_ref, ...), custom_call_target="tpu_custom_call", output_to_operand_aliasing={{0}: (6, {})} | custom-call | flops 1024 | bytes 1024 | tf_op jit(solution)/shard_map/pallas_call | solution.py:433
  56.7 1.9 %collective-permute-start.5 = (f32[16,128]{1,0:T(8,128)S(1)}, f32[16,128]{1,0:T(8,128)S(1)}, u32[]{:S(2)}, u32[]{:S(2)}) collective-permute-start(f32[16,128]{1,0:T(8,128)S(1)} %get-tuple-element.42.my_sums_ref), channel_id=1, source_target_pairs={{0,1},{1,0},{2,3},{3,2},{4,5},{5,4},{6,7},{7,6},{8,9},{9,8},{10,11... | collective-permute-start | bytes 24584 | tf_op jit(solution)/shard_map/ppermute | solution.py:418
  58.6 1.0 %collective-permute-done.5.their_sums_ref = f32[16,128]{1,0:T(8,128)S(1)} collective-permute-done((f32[16,128]{1,0:T(8,128)S(1)}, f32[16,128]{1,0:T(8,128)S(1)}, u32[]{:S(2)}, u32[]{:S(2)}) %collective-permute-start.5) | collective-permute-done | bytes 8224 | tf_op jit(solution)/shard_map/ppermute | solution.py:418
  59.6 5.3 %shard_map.94 = (bf16[2,128,2048]{2,1,0:T(8,128)(2,1)}, bf16[2,128,2048]{2,1,0:T(8,128)(2,1)S(1)}, bf16[2,128,2048]{2,1,0:T(8,128)(2,1)S(1)}, bf16[8,2,128,128]{3,2,1,0:T(8,128)(2,1)S(1)}) custom-call(s32[2]{0:T(128)S(1)} %bitcast.33, f32[2,128,2048]{2,1,0:T(8,128)S(1)} %get-tuple-element.41.kept_ref, ...), custom_call_target="tpu_custom_call" | custom-call | flops 1024 | bytes 1024 | tf_op jit(solution)/shard_map/pallas_call | solution.py:513
  64.9 11.8 %collective-permute-start.9 = (bf16[8,2,128,128]{3,2,1,0:T(8,128)(2,1)S(1)}, bf16[8,2,128,128]{3,2,1,0:T(8,128)(2,1)S(1)}, u32[]{:S(2)}, u32[]{:S(2)}) collective-permute-start(bf16[8,2,128,128]{3,2,1,0:T(8,128)(2,1)S(1)} %get-tuple-element.46), channel_id=1, source_target_pairs={{0,2},{2,4},{4,6},{6,8},{8,10},{10,12},{12,14},{14,16},{16,18},{18... | collective-permute-start | bytes 1572872 | tf_op jit(solution)/shard_map/ppermute | solution.py:502
  76.7 3.7 %shard_map.97 = bf16[8,2,128,128]{3,2,1,0:T(8,128)(2,1)S(1)} custom-call(bf16[14,2,128,128]{3,2,1,0:T(8,128)(2,1)S(1)} %bitcast.28, bf16[2,128,2048]{2,1,0:T(8,128)(2,1)S(1)} %get-tuple-element.45.outer_ref.inner_ref, bf16[2,128,2048]{2,1,0:T(8,128)(2,1)S(1)} %get-tuple-element.44.inner_ref.outer_ref), custom_call_target="tpu_custom_call" | custom-call | flops 1024 | bytes 1024 | tf_op jit(solution)/shard_map/pallas_call | solution.py:433
  80.4 1.9 %collective-permute-start.8 = (bf16[8,2,128,128]{3,2,1,0:T(8,128)(2,1)S(1)}, bf16[8,2,128,128]{3,2,1,0:T(8,128)(2,1)S(1)}, u32[]{:S(2)}, u32[]{:S(2)}) collective-permute-start(bf16[8,2,128,128]{3,2,1,0:T(8,128)(2,1)S(1)} %shard_map.97), channel_id=1, source_target_pairs={{2,0},{4,2},{6,4},{8,6},{10,8},{12,10},{14,12},{16,14},{18,16},{20... | collective-permute-start | bytes 1572872 | tf_op jit(solution)/shard_map/ppermute | solution.py:502
  82.3 2.6 %shard_map.95 = bf16[6,2,128,128]{3,2,1,0:T(8,128)(2,1)S(1)} custom-call(bf16[14,2,128,128]{3,2,1,0:T(8,128)(2,1)S(1)} %bitcast.18, bf16[2,128,2048]{2,1,0:T(8,128)(2,1)S(1)} %get-tuple-element.44.inner_ref.outer_ref, bf16[2,128,2048]{2,1,0:T(8,128)(2,1)S(1)} %get-tuple-element.45.outer_ref.inner_ref), custom_call_target="tpu_custom_call" | custom-call | flops 1024 | bytes 1024 | tf_op jit(solution)/shard_map/pallas_call | solution.py:433
  84.9 3.6 %collective-permute-start.6 = (bf16[6,2,128,128]{3,2,1,0:T(8,128)(2,1)S(1)}, bf16[6,2,128,128]{3,2,1,0:T(8,128)(2,1)S(1)}, u32[]{:S(2)}, u32[]{:S(2)}) collective-permute-start(bf16[6,2,128,128]{3,2,1,0:T(8,128)(2,1)S(1)} %shard_map.95), channel_id=1, source_target_pairs={{0,2},{2,4},{4,6},{6,8},{8,10},{10,12},{12,14},{14,16},{16,18},{18... | collective-permute-start | bytes 1179656 | tf_op jit(solution)/shard_map/ppermute | solution.py:502
  88.6 2.7 %shard_map.96 = bf16[6,2,128,128]{3,2,1,0:T(8,128)(2,1)S(1)} custom-call(bf16[14,2,128,128]{3,2,1,0:T(8,128)(2,1)S(1)} %bitcast.29, bf16[2,128,2048]{2,1,0:T(8,128)(2,1)S(1)} %get-tuple-element.45.outer_ref.inner_ref, bf16[2,128,2048]{2,1,0:T(8,128)(2,1)S(1)} %get-tuple-element.44.inner_ref.outer_ref), custom_call_target="tpu_custom_call" | custom-call | flops 1024 | bytes 1024 | tf_op jit(solution)/shard_map/pallas_call | solution.py:433
  91.3 1.9 %collective-permute-start.7 = (bf16[6,2,128,128]{3,2,1,0:T(8,128)(2,1)S(1)}, bf16[6,2,128,128]{3,2,1,0:T(8,128)(2,1)S(1)}, u32[]{:S(2)}, u32[]{:S(2)}) collective-permute-start(bf16[6,2,128,128]{3,2,1,0:T(8,128)(2,1)S(1)} %shard_map.96), channel_id=1, source_target_pairs={{2,0},{4,2},{6,4},{8,6},{10,8},{12,10},{14,12},{16,14},{18,16},{20... | collective-permute-start | bytes 1179656 | tf_op jit(solution)/shard_map/ppermute | solution.py:502
  93.2 0.0 collective-permute-done.9.refs_0_
  93.2 1.1 %shard_map.98 = (f32[14,2,128,128]{3,2,1,0:T(8,128)}, f32[14,2,128,128]{3,2,1,0:T(8,128)}) custom-call(bf16[8,2,128,128]{3,2,1,0:T(8,128)(2,1)S(1)} %collective-permute-done.9.refs_0_), custom_call_target="tpu_custom_call" | custom-call | flops 1024 | bytes 1024 | tf_op jit(solution)/shard_map/pallas_call | solution.py:532
  94.3 0.0 collective-permute-done.8.refs_0_
  94.3 1.1 %shard_map.99 = (f32[14,2,128,128]{3,2,1,0:T(8,128)}, f32[14,2,128,128]{3,2,1,0:T(8,128)}) custom-call(bf16[8,2,128,128]{3,2,1,0:T(8,128)(2,1)S(1)} %collective-permute-done.8.refs_0_, f32[14,2,128,128]{3,2,1,0:T(8,128)} %get-tuple-element.47.refs_1_, f32[14,2,128,128]{3,2,1,0:T(8,128)} %get-tuple-element.48.refs_2_), custom_call_target="tpu_custom_call", output_to_operand_aliasing={{0}: (1, {}), {1}: (2, {})} | custom-call | flops 1024 | bytes 1024 | tf_op jit(solution)/shard_map/pallas_call | solution.py:532
  95.5 0.0 collective-permute-done.6.refs_0_
  95.5 4.9 %collective-permute-done.7.refs_1_ = bf16[6,2,128,128]{3,2,1,0:T(8,128)(2,1)S(1)} collective-permute-done((bf16[6,2,128,128]{3,2,1,0:T(8,128)(2,1)S(1)}, bf16[6,2,128,128]{3,2,1,0:T(8,128)(2,1)S(1)}, u32[]{:S(2)}, u32[]{:S(2)}) %collective-permute-start.7) | collective-permute-done | bytes 393248 | tf_op jit(solution)/shard_map/ppermute | solution.py:502
  100.4 1.3 %shard_map.100 = (f32[14,2,128,128]{3,2,1,0:T(8,128)}, f32[14,2,128,128]{3,2,1,0:T(8,128)}) custom-call(bf16[6,2,128,128]{3,2,1,0:T(8,128)(2,1)S(1)} %collective-permute-done.6.refs_0_, bf16[6,2,128,128]{3,2,1,0:T(8,128)(2,1)S(1)} %collective-permute-done.7.refs_1_, ...), custom_call_target="tpu_custom_call", output_to_operand_aliasing={{0}: (2, {}), {1}: (3, {})} | custom-call | flops 1024 | bytes 1024 | tf_op jit(solution)/shard_map/pallas_call | solution.py:532
  (2 shorter events, 0.0 us)
Async XLA Ops:
  0.6 5.2 %copy-start = (bf16[1,14,2,128,128]{4,3,2,1,0:T(8,128)(2,1)S(1)}, bf16[1,14,2,128,128]{4,3,2,1,0:T(8,128)(2,1)}, u32[]{:S(2)}) copy-start(bf16[1,14,2,128,128]{4,3,2,1,0:T(8,128)(2,1)} %param.7) | copy-start | bytes 2752516
  0.6 1.3 %copy-start.1 = (bf16[1,2,128,2048]{3,2,1,0:T(8,128)(2,1)S(1)}, bf16[1,2,128,2048]{3,2,1,0:T(8,128)(2,1)}, u32[]{:S(2)}) copy-start(bf16[1,2,128,2048]{3,2,1,0:T(8,128)(2,1)} %param.6) | copy-start | bytes 3145732
  1.9 3.7 %copy-start.6 = (s32[1,14,4]{1,2,0:T(4,128)S(1)}, s32[1,14,4]{1,2,0:T(4,128)}, u32[]{:S(2)}) copy-start(s32[1,14,4]{1,2,0:T(4,128)} %param.10) | copy-start | bytes 676
  1.9 3.8 %copy-start.2 = (bf16[1,2,128,2048]{3,2,1,0:T(8,128)(2,1)S(1)}, bf16[1,2,128,2048]{3,2,1,0:T(8,128)(2,1)}, u32[]{:S(2)}) copy-start(bf16[1,2,128,2048]{3,2,1,0:T(8,128)(2,1)} %param.6) | copy-start | bytes 3145732
  2.0 3.8 %copy-start.3 = (bf16[1,14,2,128,128]{4,3,2,1,0:T(8,128)(2,1)S(1)}, bf16[1,14,2,128,128]{4,3,2,1,0:T(8,128)(2,1)}, u32[]{:S(2)}) copy-start(bf16[1,14,2,128,128]{4,3,2,1,0:T(8,128)(2,1)} %param.8) | copy-start | bytes 2752516
  2.0 3.8 %copy-start.4 = (bf16[1,14,16,16]{3,2,1,0:T(8,128)(2,1)S(1)}, bf16[1,14,16,16]{3,2,1,0:T(8,128)(2,1)}, u32[]{:S(2)}) copy-start(bf16[1,14,16,16]{3,2,1,0:T(8,128)(2,1)} %param.9) | copy-start | bytes 21508
  2.8 14.8 %collective-permute-start.1 = (bf16[1,128,2048]{2,1,0:T(8,128)(2,1)}, bf16[1,128,2048]{2,1,0:T(8,128)(2,1)}, u32[]{:S(2)}, u32[]{:S(2)}) collective-permute-start(bf16[1,128,2048]{2,1,0:T(8,128)(2,1)} %shard_map.87), channel_id=1, source_target_pairs={{0,1},{1,0},{2,3},{3,2},{4,5},{5,4},{6,7},{7,6},{8,9},{9,8},{10,11... | collective-permute-start | bytes 1572872 | tf_op jit(solution)/shard_map/ppermute | solution.py:418
  5.7 22.3 %collective-permute-start = (bf16[1,128,2048]{2,1,0:T(8,128)(2,1)}, bf16[1,128,2048]{2,1,0:T(8,128)(2,1)S(1)}, u32[]{:S(2)}, u32[]{:S(2)}) collective-permute-start(bf16[1,128,2048]{2,1,0:T(8,128)(2,1)} %shard_map.86), channel_id=1, source_target_pairs={{0,1},{1,0},{2,3},{3,2},{4,5},{5,4},{6,7},{7,6},{8,9},{9,8},{10,11... | collective-permute-start | bytes 1572872 | tf_op jit(solution)/shard_map/ppermute | solution.py:418
  23.9 4.1 %collective-permute-start.2 = (f32[8,128]{1,0:T(8,128)S(1)}, f32[8,128]{1,0:T(8,128)S(1)}, u32[]{:S(2)}, u32[]{:S(2)}) collective-permute-start(f32[8,128]{1,0:T(8,128)S(1)} %get-tuple-element.33.mine_ref), channel_id=1, source_target_pairs={{0,1},{1,0},{2,3},{3,2},{4,5},{5,4},{6,7},{7,6},{8,9},{9,8},{10,11... | collective-permute-start | bytes 12296 | tf_op jit(solution)/shard_map/ppermute | solution.py:418
  30.2 14.6 %collective-permute-start.4 = (bf16[1,128,2048]{2,1,0:T(8,128)(2,1)S(1)}, bf16[1,128,2048]{2,1,0:T(8,128)(2,1)S(1)}, u32[]{:S(2)}, u32[]{:S(2)}) collective-permute-start(bf16[1,128,2048]{2,1,0:T(8,128)(2,1)S(1)} %get-tuple-element.35.refs_0_), channel_id=1, source_target_pairs={{0,1},{1,0},{2,3},{3,2},{4,5},{5,4},{6,7},{7,6},{8,9},{9,8},{10,11... | collective-permute-start | bytes 1572872 | tf_op jit(solution)/shard_map/ppermute | solution.py:418
  33.5 19.1 %collective-permute-start.3 = (bf16[1,128,2048]{2,1,0:T(8,128)(2,1)S(1)}, bf16[1,128,2048]{2,1,0:T(8,128)(2,1)S(1)}, u32[]{:S(2)}, u32[]{:S(2)}) collective-permute-start(bf16[1,128,2048]{2,1,0:T(8,128)(2,1)S(1)} %get-tuple-element.36), channel_id=1, source_target_pairs={{0,1},{1,0},{2,3},{3,2},{4,5},{5,4},{6,7},{7,6},{8,9},{9,8},{10,11... | collective-permute-start | bytes 1572872 | tf_op jit(solution)/shard_map/ppermute | solution.py:418
  34.9 9.8 %copy-start.5 = (s32[1,2]{1,0:T(1,128)S(1)}, s32[1,2]{1,0:T(1,128)}, u32[]{:S(2)}) copy-start(s32[1,2]{1,0:T(1,128)} %param.11) | copy-start | bytes 28
  56.7 2.9 %collective-permute-start.5 = (f32[16,128]{1,0:T(8,128)S(1)}, f32[16,128]{1,0:T(8,128)S(1)}, u32[]{:S(2)}, u32[]{:S(2)}) collective-permute-start(f32[16,128]{1,0:T(8,128)S(1)} %get-tuple-element.42.my_sums_ref), channel_id=1, source_target_pairs={{0,1},{1,0},{2,3},{3,2},{4,5},{5,4},{6,7},{7,6},{8,9},{9,8},{10,11... | collective-permute-start | bytes 24584 | tf_op jit(solution)/shard_map/ppermute | solution.py:418
  64.9 28.3 %collective-permute-start.9 = (bf16[8,2,128,128]{3,2,1,0:T(8,128)(2,1)S(1)}, bf16[8,2,128,128]{3,2,1,0:T(8,128)(2,1)S(1)}, u32[]{:S(2)}, u32[]{:S(2)}) collective-permute-start(bf16[8,2,128,128]{3,2,1,0:T(8,128)(2,1)S(1)} %get-tuple-element.46), channel_id=1, source_target_pairs={{0,2},{2,4},{4,6},{6,8},{8,10},{10,12},{12,14},{14,16},{16,18},{18... | collective-permute-start | bytes 1572872 | tf_op jit(solution)/shard_map/ppermute | solution.py:502
  80.4 13.9 %collective-permute-start.8 = (bf16[8,2,128,128]{3,2,1,0:T(8,128)(2,1)S(1)}, bf16[8,2,128,128]{3,2,1,0:T(8,128)(2,1)S(1)}, u32[]{:S(2)}, u32[]{:S(2)}) collective-permute-start(bf16[8,2,128,128]{3,2,1,0:T(8,128)(2,1)S(1)} %shard_map.97), channel_id=1, source_target_pairs={{2,0},{4,2},{6,4},{8,6},{10,8},{12,10},{14,12},{16,14},{18,16},{20... | collective-permute-start | bytes 1572872 | tf_op jit(solution)/shard_map/ppermute | solution.py:502
  84.9 10.5 %collective-permute-start.6 = (bf16[6,2,128,128]{3,2,1,0:T(8,128)(2,1)S(1)}, bf16[6,2,128,128]{3,2,1,0:T(8,128)(2,1)S(1)}, u32[]{:S(2)}, u32[]{:S(2)}) collective-permute-start(bf16[6,2,128,128]{3,2,1,0:T(8,128)(2,1)S(1)} %shard_map.95), channel_id=1, source_target_pairs={{0,2},{2,4},{4,6},{6,8},{8,10},{10,12},{12,14},{14,16},{16,18},{18... | collective-permute-start | bytes 1179656 | tf_op jit(solution)/shard_map/ppermute | solution.py:502
  91.3 9.1 %collective-permute-start.7 = (bf16[6,2,128,128]{3,2,1,0:T(8,128)(2,1)S(1)}, bf16[6,2,128,128]{3,2,1,0:T(8,128)(2,1)S(1)}, u32[]{:S(2)}, u32[]{:S(2)}) collective-permute-start(bf16[6,2,128,128]{3,2,1,0:T(8,128)(2,1)S(1)} %shard_map.96), channel_id=1, source_target_pairs={{2,0},{4,2},{6,4},{8,6},{10,8},{12,10},{14,12},{16,14},{18,16},{20... | collective-permute-start | bytes 1179656 | tf_op jit(solution)/shard_map/ppermute | solution.py:502
where the time goes:
time: 102 us
  Pallas kernels  63.2 us (62%)
  starting transfers between devices  26.3 us (26%)
  waiting for transfers between devices  9.85 us (10%)
  local copies, waits for them, and re-layouts  1.42 us (1%)
    pallas_call x12, Pallas kernels, call(): pl.pallas_call(body, in_specs=specs, out_specs=jax.tree.map(lambda _: VME...  54.4 us
    ppermute x4, starting transfers between devices, sent(): lax.ppermute(value, 'seg', [(s, s + steps) for s in range(begin, end)])  19.3 us
    ppermute x6, starting transfers between devices, trade(): return lax.ppermute(value, 'blk', swap)  7.06 us
    pallas_call x1, Pallas kernels, shards(): pl.pallas_call(functools.partial(normalize_and_left, 0, early, env_scale,...  5.29 us
    ppermute x6, waiting for transfers between devices, trade(): return lax.ppermute(value, 'blk', swap)  4.93 us
    ppermute x4, waiting for transfers between devices, sent(): lax.ppermute(value, 'seg', [(s, s + steps) for s in range(begin, end)])  4.92 us
    pallas_call x3, Pallas kernels, widened(): pl.pallas_call(functools.partial(widen, places), in_specs=[VMEM] * count...  3.49 us
  transfers between devices with their start and end apart: 10, of which 5 were waited for; matrix products, arithmetic and copies ran while one was open for 0% of the time, Pallas kernels for 49%

commit v1 on v0

--- a/solution.py
+++ b/solution.py
@@ -11,7 +11,7 @@
 STEP_SIZE = 0.25
 EPSILON = 1e-06
 LANES = 128
-ROWS = 16
+GROUP = 8
 CHUNK = 32
 F32 = jnp.float32
 BF16 = jnp.bfloat16
@@ -30,19 +30,21 @@
 
 def make_kron(ops_ref, kron_ref, spread_ref):
     chan, phys, _ = ops_ref.shape
-    wide = phys * ROWS
+    wide = phys * GROUP
     columns = lax.broadcasted_iota(jnp.int32, (phys, wide), 1)
-    spread = (columns // ROWS == lax.broadcasted_iota(jnp.int32, (phys, wide), 0)).astype(F32)
+    spread = (columns // GROUP == lax.broadcasted_iota(jnp.int32, (phys, wide), 0)).astype(F32)
     spread_ref[...] = dot(ops_ref[...].reshape(chan * phys, phys), spread.astype(BF16))
-    same = lax.broadcasted_iota(jnp.int32, (ROWS, wide), 1) % ROWS == lax.broadcasted_iota(
-        jnp.int32, (ROWS, wide), 0
+    same = lax.broadcasted_iota(jnp.int32, (GROUP, wide), 1) % GROUP == lax.broadcasted_iota(
+        jnp.int32, (GROUP, wide), 0
     )
 
     def one(k, carry):
         rows = spread_ref[pl.ds(pl.multiple_of(k * phys, phys), phys), :]
-        for p in range(phys):
-            full = jnp.broadcast_to(rows[p : p + 1], (ROWS, wide))
-            kron_ref[k, p * ROWS : (p + 1) * ROWS, :] = jnp.where(same, full, 0.0).astype(BF16)
+        full = [
+            jnp.where(same, jnp.broadcast_to(rows[p : p + 1], (GROUP, wide)), 0.0)
+            for p in range(phys)
+        ]
+        kron_ref[k] = jnp.concatenate(full, axis=0).astype(BF16)
         return carry
 
     lax.fori_loop(0, chan, one, 0)
@@ -52,80 +54,78 @@
     chan, dests = rel_ref.shape
     place = jnp.int32(0)
     for b in range(dests) if only is None else only:
-        for k in range(chan):
-            source = rel_ref[k, b]
-            chan_list[place] = k
+        for source in range(low, high):
+            for k in range(chan):
+                chan_list[place] = k
+                src_list[place] = source - low
+                live_list[place] = 1
+                dest_list[place] = b
+                place = place + jnp.where(rel_ref[k, b] == source, 1, 0)
+            chan_list[place] = 0
             src_list[place] = source - low
-            live_list[place] = 1
+            live_list[place] = 0
             dest_list[place] = b
-            place = place + jnp.where((source >= low) & (source < high), 1, 0)
-        chan_list[place] = 0
-        src_list[place] = 0
-        live_list[place] = 0
-        dest_list[place] = b
-        place = place + lax.rem(place, 2)
+            place = place + lax.rem(place, 2)
     return place // 2
 
 
-def add_pairs(steps, lists, kron_ref, x_ref, left_ref, right_t_ref, acc_ref, mixed_ref, part_ref):
+def add_pairs(steps, lists, kron_ref, x_ref, left_ref, right_t_ref, acc_ref, turned_ref, mixed_ref):
     chan_list, src_list, live_list, dest_list = lists
     rows = x_ref.shape[1]
     phys = x_ref.shape[2] // LANES
-
-    def mix(s):
+    groups = rows // GROUP
+
+    def lanes(n):
+        return slice(n * LANES, (n + 1) * LANES)
+
+    def act_right(s):
+        source, dest = src_list[2 * s], dest_list[2 * s]
+        tall = jnp.concatenate([x_ref[source, :, lanes(q)] for q in range(phys)], axis=0)
+        second = right_t_ref[chan_list[2 * s + 1], dest]
+        second = jnp.where(live_list[2 * s + 1] > 0, second, jnp.zeros_like(second))
+        out = dot(tall, jnp.concatenate([right_t_ref[chan_list[2 * s], dest], second], axis=1))
         for i in range(2):
-            source = src_list[2 * s + i]
+            for g in range(groups):
+                turned_ref[i, g] = jnp.concatenate(
+                    [
+                        out[q * rows + g * GROUP : q * rows + (g + 1) * GROUP, lanes(i)]
+                        for q in range(phys)
+                    ],
+                    axis=0,
+                ).astype(BF16)
+
+    def act_site(s):
+        for i in range(2):
             kron = kron_ref[chan_list[2 * s + i]]
-            for g in range(rows // (2 * ROWS)):
-                halves = []
-                for j in range(2):
-                    r0 = (2 * g + j) * ROWS
-                    halves.append(
-                        jnp.concatenate(
-                            [
-                                x_ref[source, r0 : r0 + ROWS, q * LANES : (q + 1) * LANES]
-                                for q in range(phys)
-                            ],
-                            axis=0,
-                        )
-                    )
-                out = dot(kron, jnp.concatenate(halves, axis=1)).astype(BF16)
-                for j in range(2):
-                    r0 = (2 * g + j) * ROWS
-                    for p in range(phys):
-                        mixed_ref[i, r0 : r0 + ROWS, p * LANES : (p + 1) * LANES] = out[
-                            p * ROWS : (p + 1) * ROWS, j * LANES : (j + 1) * LANES
-                        ]
-
-    def step(s, follow):
+            for h in range(groups // 2):
+                both = jnp.concatenate([turned_ref[i, 2 * h], turned_ref[i, 2 * h + 1]], axis=1)
+                out = dot(kron, both)
+                r0 = i * rows + 2 * h * GROUP
+                for p in range(phys):
+                    row = slice(p * GROUP, (p + 1) * GROUP)
+                    mixed_ref[r0 : r0 + 2 * GROUP, lanes(p)] = jnp.concatenate(
+                        [out[row, lanes(0)], out[row, lanes(1)]], axis=0
+                    ).astype(BF16)
+
+    def act_left(s):
         dest = dest_list[2 * s]
-        weights = []
-        for i in range(2):
-            k = chan_list[2 * s + i]
-            part = dot(left_ref[k, dest], mixed_ref[i]).astype(BF16)
-            for p in range(phys):
-                part_ref[p * rows : (p + 1) * rows, i * LANES : (i + 1) * LANES] = part[
-                    :, p * LANES : (p + 1) * LANES
-                ]
-            right = right_t_ref[k, dest]
-            if i == 1:
-                right = jnp.where(live_list[2 * s + 1] > 0, right, jnp.zeros_like(right))
-            weights.append(right)
-        if follow:
-            mix(s + 1)
-        image = dot(part_ref[...], jnp.concatenate(weights, axis=0))
-        for p in range(phys):
-            acc_ref[dest, :, p * LANES : (p + 1) * LANES] += image[p * rows : (p + 1) * rows]
+        left = jnp.concatenate(
+            [left_ref[chan_list[2 * s], dest], left_ref[chan_list[2 * s + 1], dest]], axis=1
+        )
+        acc_ref[dest] += dot(left, mixed_ref[...])
 
     def middle(s, carry):
-        step(s, True)
+        act_site(s)
+        act_right(s + 1)
+        act_left(s)
         return carry
 
     @pl.when(steps > 0)
     def _():
-        mix(0)
+        act_right(0)
         lax.fori_loop(0, steps - 1, middle, 0)
-        step(steps - 1, False)
+        act_site(steps - 1)
+        act_left(steps - 1)
 
 
 def fold(values):
@@ -162,32 +162,28 @@
     return jnp.where(den > 0, num / jnp.where(den > 0, den, 1.0), 0.0)
 
 
-def cut(b, x_ref, out_ref):
-    out_ref[0] = x_ref[b]
+def cut(x_ref, *out_refs):
+    for b, out_ref in enumerate(out_refs):
+        out_ref[0] = x_ref[b]
 
 
 def first_local(
-    rel_ref, ops_ref, x_ref, left_ref, right_ref,
-    kron_ref, right_t_ref, image_ref, sums_ref,
-    mixed_ref, part_ref, chan_list, src_list, live_list, dest_list, spread_ref, fetched_ref, sem,
-):
-    lists = (chan_list, src_list, live_list, dest_list)
-    fetch = pltpu.make_async_copy(right_ref, fetched_ref, sem)
-    fetch.start()
-    make_kron(ops_ref, kron_ref, spread_ref)
+    rel_ref, kron_ref, x_ref, left_ref, right_ref,
+    right_t_ref, image_ref, sums_ref,
+    turned_ref, mixed_ref, *lists,
+):
     chan, dests = left_ref.shape[:2]
-    fetch.wait()
 
     def turn(n, carry):
         for k in range(2):
             for b in range(dests):
-                right_t_ref[2 * n + k, b] = fetched_ref[2 * n + k, b].T
+                right_t_ref[2 * n + k, b] = right_ref[2 * n + k, b].T
         return carry
 
     lax.fori_loop(0, chan // 2, turn, 0)
     image_ref[...] = jnp.zeros_like(image_ref)
     steps = list_pairs(rel_ref, 0, dests, *lists)
-    add_pairs(steps, lists, kron_ref, x_ref, left_ref, right_t_ref, image_ref, mixed_ref, part_ref)
+    add_pairs(steps, lists, kron_ref, x_ref, left_ref, right_t_ref, image_ref, turned_ref, mixed_ref)
 
     def sums(b, r, start, carry):
         x = x_ref[b, r, :].astype(F32)
@@ -201,22 +197,22 @@
 def local_sources(
     rel_ref, kron_ref, x_ref, left_ref, right_t_ref,
     acc_ref,
-    mixed_ref, part_ref, *lists,
+    turned_ref, mixed_ref, *lists,
 ):
     acc_ref[...] = jnp.zeros_like(acc_ref)
     steps = list_pairs(rel_ref, 0, left_ref.shape[1], *lists)
-    add_pairs(steps, lists, kron_ref, x_ref, left_ref, right_t_ref, acc_ref, mixed_ref, part_ref)
+    add_pairs(steps, lists, kron_ref, x_ref, left_ref, right_t_ref, acc_ref, turned_ref, mixed_ref)
 
 
 def first_remote(
     rel_ref, kron_ref, other_ref, left_ref, right_t_ref, before_ref, local_sums_ref,
     acc_ref, sums_ref,
-    mixed_ref, part_ref, *lists,
+    turned_ref, mixed_ref, *lists,
 ):
     dests = left_ref.shape[1]
     sums_ref[...] = local_sums_ref[...]
     steps = list_pairs(rel_ref, dests, dests + 1, *lists)
-    add_pairs(steps, lists, kron_ref, other_ref, left_ref, right_t_ref, acc_ref, mixed_ref, part_ref)
+    add_pairs(steps, lists, kron_ref, other_ref, left_ref, right_t_ref, acc_ref, turned_ref, mixed_ref)
 
 
 def first_finish(
@@ -230,10 +226,10 @@
         all_ref[0:dest] = earlier_ref[...]
     else:
         acc_ref, guess_ref = refs[:2]
-    mixed_ref, part_ref = refs[-6:-4]
+    turned_ref, mixed_ref = refs[-6:-4]
     lists = refs[-4:]
     steps = list_pairs(rel_ref, dests + 1, 2 * dests, *lists, only=(dest,))
-    add_pairs(steps, lists, kron_ref, other_ref, left_ref, right_t_ref, acc_ref, mixed_ref, part_ref)
+    add_pairs(steps, lists, kron_ref, other_ref, left_ref, right_t_ref, acc_ref, turned_ref, mixed_ref)
     shift = common_shift(mine_ref, theirs_ref)
     keep_state = jnp.tile(1.0 + STEP_SIZE * shift, (1, x_ref.shape[2] // LANES))
 
@@ -252,11 +248,11 @@
     rel_ref, rank_ref, kron_ref, other_ref, left_ref, right_t_ref, before_ref, x_ref, image_ref,
     guess_ref,
     acc_ref, sums_ref,
-    mixed_ref, part_ref, *lists,
+    turned_ref, mixed_ref, *lists,
 ):
     dests, rows, _ = x_ref.shape
     steps = list_pairs(rel_ref, dests, dests + 1, *lists)
-    add_pairs(steps, lists, kron_ref, other_ref, left_ref, right_t_ref, acc_ref, mixed_ref, part_ref)
+    add_pairs(steps, lists, kron_ref, other_ref, left_ref, right_t_ref, acc_ref, turned_ref, mixed_ref)
 
     def sums(b, r, start, carry):
         x = x_ref[b, r, :].astype(F32)
@@ -274,11 +270,11 @@
     rel_ref, rank_ref, kron_ref, other_ref, left_ref, right_t_ref, before_ref, x_ref, guess_ref,
     mine_ref, theirs_ref, early_ref,
     kept_ref, sums_ref,
-    mixed_ref, part_ref, *lists,
+    turned_ref, mixed_ref, *lists,
 ):
     dests, rows, width = x_ref.shape
     steps = list_pairs(rel_ref, dests + 1, 2 * dests, *lists)
-    add_pairs(steps, lists, kron_ref, other_ref, left_ref, right_t_ref, kept_ref, mixed_ref, part_ref)
+    add_pairs(steps, lists, kron_ref, other_ref, left_ref, right_t_ref, kept_ref, turned_ref, mixed_ref)
     shift = common_shift(mine_ref, theirs_ref)
     keep_guess = jnp.tile(1.0 + STEP_SIZE * shift, (1, width // LANES))
 
@@ -424,9 +420,10 @@
     wave_f32 = shape(wave, F32)
     wave_b16 = shape(wave, BF16)
     sums_kind = shape((8, LANES), F32)
-    lists = [pltpu.SMEM((chan * dests + 2 * dests + 1,), jnp.int32)] * 4
+    lists = [pltpu.SMEM((chan * dests + 2 * dests * dests + 1,), jnp.int32)] * 4
     pair_scratch = [
-        pltpu.VMEM((2, rows, width), BF16), pltpu.VMEM((phys * rows, 2 * LANES), BF16)
+        pltpu.VMEM((2, rows // GROUP, phys * GROUP, LANES), BF16),
+        pltpu.VMEM((2 * rows, width), BF16),
     ] + lists
 
     def call(body, specs, outs, scratch, *args, aliases={}):
@@ -442,20 +439,16 @@
         )(*args)
 
     block = shape((1, rows, width), BF16)
-    own = [
-        call(functools.partial(cut, b), [VMEM], block, [], x) for b in range(dests)
-    ]
+    own = call(cut, [VMEM], (block,) * dests, [], x)
     other = [trade(value) for value in own]
-    kron, right_t, image, mine = call(
-        first_local, [SMEM] + [VMEM] * 3 + [HBM],
-        (shape((chan, phys * ROWS, phys * ROWS), BF16), shape(right.shape, BF16), wave_f32, sums_kind),
-        pair_scratch
-        + [
-            pltpu.VMEM((chan * phys, phys * ROWS), F32),
-            pltpu.VMEM(right.shape, BF16),
-            pltpu.SemaphoreType.DMA,
-        ],
-        rel, ops, x, left, right,
+    kron = call(
+        make_kron, [VMEM], shape((chan, phys * GROUP, phys * GROUP), BF16),
+        [pltpu.VMEM((chan * phys, phys * GROUP), F32)], ops,
+    )
+    right_t, image, mine = call(
+        first_local, [SMEM] + [VMEM] * 4,
+        (shape(right.shape, BF16), wave_f32, sums_kind), pair_scratch,
+        rel, kron, x, left, right,
     )
     image, mine = call(
         first_remote, [SMEM] + [VMEM] * 6, (wave_f32, sums_kind), pair_scratch,

time: 102 us -> 101 us (level)
  Pallas kernels: 63.2 us -> 57.1 us
  waiting for transfers between devices: 9.85 us -> 15.8 us
  starting transfers between devices: 26.3 us -> 20.7 us
  local copies, waits for them, and re-layouts: 1.42 us -> 4.63 us
    ppermute x4, starting transfers between devices: 19.3 us -> 12.7 us  [sent(): lax.ppermute(value, 'seg', [(s, s + steps) for s in range(begin, end)])]
    pallas_call x12, Pallas kernels: 54.4 us -> 48.3 us  [call(): pl.pallas_call(body, in_specs=specs, out_specs=jax.tree.map(lambda _: VME...]
    ppermute x6, waiting for transfers between devices: 4.93 us -> 10.9 us  [trade(): return lax.ppermute(value, 'blk', swap)]
    unnamed x14 -> x16, local copies, waits for them, and re-layouts: 1.32 us -> 4.54 us
  transfers between devices with their start and end apart: 10 -> 10, of which waited for: 5 -> 6; matrix products, arithmetic and copies ran while one was open for 0% -> 1% of each run, Pallas kernels for 49% -> 42%
where the time goes in v1:
time: 101 us; the launch traced here: 100 us
  Pallas kernels  57.1 us (57%)
  starting transfers between devices  20.7 us (20%)
  waiting for transfers between devices  15.8 us (16%)
  local copies, waits for them, and re-layouts  4.63 us (5%)
  between operations  1.02 us (1%)
    pallas_call x12, Pallas kernels, call(): pl.pallas_call(body, in_specs=specs, out_specs=jax.tree.map(lambda _: VME...  48.3 us
    ppermute x4, starting transfers between devices, sent(): lax.ppermute(value, 'seg', [(s, s + steps) for s in range(begin, end)])  12.7 us
    ppermute x6, waiting for transfers between devices, trade(): return lax.ppermute(value, 'blk', swap)  10.9 us
    ppermute x6, starting transfers between devices, trade(): return lax.ppermute(value, 'blk', swap)  8.04 us
    pallas_call x1, Pallas kernels, shards(): pl.pallas_call(functools.partial(normalize_and_left, 0, early, env_scale,...  5.29 us
    ppermute x4, waiting for transfers between devices, sent(): lax.ppermute(value, 'seg', [(s, s + steps) for s in range(begin, end)])  4.92 us
    unnamed x16, local copies, waits for them, and re-layouts  4.54 us
    pallas_call x3, Pallas kernels, widened(): pl.pallas_call(functools.partial(widen, places), in_specs=[VMEM] * count...  3.49 us
  transfers between devices with their start and end apart: 10, of which 6 were waited for; matrix products, arithmetic and copies ran while one was open for 1% of the time, Pallas kernels for 42%

profile of v1, /device:TPU:1, one launch (start us, length us, event | category | flops | bytes accessed | tf_op | source)
XLA Modules:
  0.0 100.0 jit_solution(18391577350937709725)
XLA Ops:
  0.6 0.0 copy-start
  0.6 0.0 copy-start.1
  0.7 1.3 %copy-done.1 = bf16[1,2,128,2048]{3,2,1,0:T(8,128)(2,1)S(1)} copy-done((bf16[1,2,128,2048]{3,2,1,0:T(8,128)(2,1)S(1)}, bf16[1,2,128,2048]{3,2,1,0:T(8,128)(2,1)}, u32[]{:S(2)}) %copy-start.1) | copy-done | bytes 1048600
  1.9 0.1 shard_map.86
  2.0 2.1 %collective-permute-start.1 = (bf16[1,128,2048]{2,1,0:T(8,128)(2,1)S(1)}, bf16[1,128,2048]{2,1,0:T(8,128)(2,1)S(1)}, u32[]{:S(2)}, u32[]{:S(2)}) collective-permute-start(bf16[1,128,2048]{2,1,0:T(8,128)(2,1)S(1)} %get-tuple-element.31), channel_id=1, source_target_pairs={{0,1},{1,0},{2,3},{3,2},{4,5},{5,4},{6,7},{7,6},{8,9},{9,8},{10,11... | collective-permute-start | bytes 1572872 | tf_op jit(solution)/shard_map/ppermute | solution.py:414
  4.1 0.1 collective-permute-start
  4.2 0.0 copy-start.6
  4.2 0.8 copy-done.6
  5.0 0.3 shard_map.85.kron_ref
  5.3 0.7 add_bitcast_fusion
  6.0 0.1 copy.18
  6.1 0.0 copy-done
  6.1 0.0 copy-start.2
  6.1 1.2 %copy-done.2 = bf16[1,2,128,2048]{3,2,1,0:T(8,128)(2,1)S(1)} copy-done((bf16[1,2,128,2048]{3,2,1,0:T(8,128)(2,1)S(1)}, bf16[1,2,128,2048]{3,2,1,0:T(8,128)(2,1)}, u32[]{:S(2)}) %copy-start.2) | copy-done | bytes 1048600
  7.3 0.0 copy-start.4
  7.3 1.2 %copy-done.4 = bf16[1,14,2,128,128]{4,3,2,1,0:T(8,128)(2,1)S(1)} copy-done((bf16[1,14,2,128,128]{4,3,2,1,0:T(8,128)(2,1)S(1)}, bf16[1,14,2,128,128]{4,3,2,1,0:T(8,128)(2,1)}, u32[]{:S(2)}) %copy-start.4) | copy-done | bytes 917528
  8.5 9.2 %shard_map.87 = (bf16[14,2,128,128]{3,2,1,0:T(8,128)(2,1)S(1)}, f32[2,128,2048]{2,1,0:T(8,128)S(1)}, f32[8,128]{1,0:T(8,128)S(1)}) custom-call(s32[14,2]{1,0:T(8,128)S(1)} %negate_select_fusion.rel_ref, bf16[14,128,128]{2,1,0:T(8,128)(2,1)S(1)} %shard_map.85.kron_ref, bf16[2,128,2048]{2,1,0:T(8,128)(2,1)S(1)} %bitcast.20, ...), custom_call_target="tpu_custom_call" | custom-call | flops 1024 | bytes 1024 | tf_op jit(solution)/shard_map/pallas_call | solution.py:430
  17.7 0.0 collective-permute-done.1.other_ref
  17.7 0.0 copy-start.3
  17.7 4.4 %shard_map.88 = (f32[2,128,2048]{2,1,0:T(8,128)S(1)}, f32[8,128]{1,0:T(8,128)S(1)}) custom-call(s32[14,2]{1,0:T(8,128)S(1)} %negate_select_fusion.rel_ref, bf16[14,128,128]{2,1,0:T(8,128)(2,1)S(1)} %shard_map.85.kron_ref, bf16[1,128,2048]{2,1,0:T(8,128)(2,1)S(1)} %collective-permute-done.1.other_ref, ...), custom_call_target="tpu_custom_call", output_to_operand_aliasing={{0}: (5, {})} | custom-call | flops 1024 | bytes 1024 | tf_op jit(solution)/shard_map/pallas_call | solution.py:430
  22.2 0.6 collective-permute-start.2
  22.8 4.2 %collective-permute-done.other_ref = bf16[1,128,2048]{2,1,0:T(8,128)(2,1)S(1)} collective-permute-done((bf16[1,128,2048]{2,1,0:T(8,128)(2,1)S(1)}, bf16[1,128,2048]{2,1,0:T(8,128)(2,1)S(1)}, u32[]{:S(2)}, u32[]{:S(2)}) %collective-permute-start) | collective-permute-done | bytes 524320 | tf_op jit(solution)/shard_map/ppermute | solution.py:414
  27.0 0.1 collective-permute-done.2.theirs_ref
  27.1 0.0 copy-done.3
  27.1 2.9 %shard_map.89 = (f32[2,128,2048]{2,1,0:T(8,128)S(1)}, bf16[1,128,2048]{2,1,0:T(8,128)(2,1)S(1)}) custom-call(s32[14,2]{1,0:T(8,128)S(1)} %negate_select_fusion.rel_ref, bf16[14,128,128]{2,1,0:T(8,128)(2,1)S(1)} %shard_map.85.kron_ref, bf16[1,128,2048]{2,1,0:T(8,128)(2,1)S(1)} %collective-permute-done.other_ref, ...), custom_call_target="tpu_custom_call", output_to_operand_aliasing={{0}: (5, {})} | custom-call | flops 1024 | bytes 1024 | tf_op jit(solution)/shard_map/pallas_call | solution.py:430
  30.0 2.0 %collective-permute-start.4 = (bf16[1,128,2048]{2,1,0:T(8,128)(2,1)S(1)}, bf16[1,128,2048]{2,1,0:T(8,128)(2,1)S(1)}, u32[]{:S(2)}, u32[]{:S(2)}) collective-permute-start(bf16[1,128,2048]{2,1,0:T(8,128)(2,1)S(1)} %get-tuple-element.37.refs_0_), channel_id=1, source_target_pairs={{0,1},{1,0},{2,3},{3,2},{4,5},{5,4},{6,7},{7,6},{8,9},{9,8},{10,11... | collective-permute-start | bytes 1572872 | tf_op jit(solution)/shard_map/ppermute | solution.py:414
  32.1 2.9 %shard_map.90 = (f32[2,128,2048]{2,1,0:T(8,128)S(1)}, bf16[1,128,2048]{2,1,0:T(8,128)(2,1)S(1)}, bf16[2,128,2048]{2,1,0:T(8,128)(2,1)S(1)}) custom-call(s32[14,2]{1,0:T(8,128)S(1)} %negate_select_fusion.rel_ref, bf16[14,128,128]{2,1,0:T(8,128)(2,1)S(1)} %shard_map.85.kron_ref, ...), custom_call_target="tpu_custom_call", output_to_operand_aliasing={{0}: (5, {})} | custom-call | flops 1024 | bytes 1024 | tf_op jit(solution)/shard_map/pallas_call | solution.py:430
  35.0 0.1 collective-permute-start.3
  35.0 0.0 copy-start.7
  35.1 8.0 %shard_map.91.before_ref = f32[2,128,2048]{2,1,0:T(8,128)S(1)} custom-call(s32[14,2]{1,0:T(8,128)S(1)} %negate_select_fusion.rel_ref, bf16[14,128,128]{2,1,0:T(8,128)(2,1)S(1)} %shard_map.85.kron_ref, bf16[2,128,2048]{2,1,0:T(8,128)(2,1)S(1)} %get-tuple-element.39.x_ref.guess_ref, bf16[14,2,128,128]{3,2,1,0:T(8,128)(2,1)S(1)} %bitcast.14, ...), custom_call_target="tpu_custom_call" | custom-call | flops 1024 | bytes 1024 | tf_op jit(solution)/shard_map/pallas_call | solution.py:430
  43.1 0.4 collective-permute-done.4.other_ref
  43.5 0.0 copy-done.7
  43.5 6.1 %shard_map.92 = (f32[2,128,2048]{2,1,0:T(8,128)S(1)}, f32[8,128]{1,0:T(8,128)S(1)}) custom-call(s32[14,2]{1,0:T(8,128)S(1)} %negate_select_fusion.rel_ref, s32[2]{0:T(128)S(1)} %bitcast.30, bf16[14,128,128]{2,1,0:T(8,128)(2,1)S(1)} %shard_map.85.kron_ref, ...), custom_call_target="tpu_custom_call", output_to_operand_aliasing={{0}: (6, {})} | custom-call | flops 1024 | bytes 1024 | tf_op jit(solution)/shard_map/pallas_call | solution.py:430
  49.6 5.1 %collective-permute-done.3.other_ref = bf16[1,128,2048]{2,1,0:T(8,128)(2,1)S(1)} collective-permute-done((bf16[1,128,2048]{2,1,0:T(8,128)(2,1)S(1)}, bf16[1,128,2048]{2,1,0:T(8,128)(2,1)S(1)}, u32[]{:S(2)}, u32[]{:S(2)}) %collective-permute-start.3) | collective-permute-done | bytes 524320 | tf_op jit(solution)/shard_map/ppermute | solution.py:414
  54.7 5.5 %shard_map.93 = (f32[2,128,2048]{2,1,0:T(8,128)S(1)}, f32[16,128]{1,0:T(8,128)S(1)}) custom-call(s32[14,2]{1,0:T(8,128)S(1)} %negate_select_fusion.rel_ref, s32[2]{0:T(128)S(1)} %bitcast.31, bf16[14,128,128]{2,1,0:T(8,128)(2,1)S(1)} %shard_map.85.kron_ref, ...), custom_call_target="tpu_custom_call", output_to_operand_aliasing={{0}: (6, {})} | custom-call | flops 1024 | bytes 1024 | tf_op jit(solution)/shard_map/pallas_call | solution.py:430
  60.2 3.1 %collective-permute-start.5 = (f32[16,128]{1,0:T(8,128)S(1)}, f32[16,128]{1,0:T(8,128)S(1)}, u32[]{:S(2)}, u32[]{:S(2)}) collective-permute-start(f32[16,128]{1,0:T(8,128)S(1)} %get-tuple-element.44.my_sums_ref), channel_id=1, source_target_pairs={{0,1},{1,0},{2,3},{3,2},{4,5},{5,4},{6,7},{7,6},{8,9},{9,8},{10,11... | collective-permute-start | bytes 24584 | tf_op jit(solution)/shard_map/ppermute | solution.py:414
  63.4 1.0 %collective-permute-done.5.their_sums_ref = f32[16,128]{1,0:T(8,128)S(1)} collective-permute-done((f32[16,128]{1,0:T(8,128)S(1)}, f32[16,128]{1,0:T(8,128)S(1)}, u32[]{:S(2)}, u32[]{:S(2)}) %collective-permute-start.5) | collective-permute-done | bytes 8224 | tf_op jit(solution)/shard_map/ppermute | solution.py:414
  64.4 0.0 copy-start.5
  64.4 5.3 %shard_map.94 = (bf16[2,128,2048]{2,1,0:T(8,128)(2,1)}, bf16[2,128,2048]{2,1,0:T(8,128)(2,1)S(1)}, bf16[2,128,2048]{2,1,0:T(8,128)(2,1)S(1)}, bf16[8,2,128,128]{3,2,1,0:T(8,128)(2,1)S(1)}) custom-call(s32[2]{0:T(128)S(1)} %bitcast.32, f32[2,128,2048]{2,1,0:T(8,128)S(1)} %get-tuple-element.43.kept_ref, ...), custom_call_target="tpu_custom_call" | custom-call | flops 1024 | bytes 1024 | tf_op jit(solution)/shard_map/pallas_call | solution.py:506
  69.7 5.2 %collective-permute-start.9 = (bf16[8,2,128,128]{3,2,1,0:T(8,128)(2,1)S(1)}, bf16[8,2,128,128]{3,2,1,0:T(8,128)(2,1)S(1)}, u32[]{:S(2)}, u32[]{:S(2)}) collective-permute-start(bf16[8,2,128,128]{3,2,1,0:T(8,128)(2,1)S(1)} %get-tuple-element.48), channel_id=1, source_target_pairs={{0,2},{2,4},{4,6},{6,8},{8,10},{10,12},{12,14},{14,16},{16,18},{18... | collective-permute-start | bytes 1572872 | tf_op jit(solution)/shard_map/ppermute | solution.py:495
  74.9 0.0 copy-done.5
  74.9 3.7 %shard_map.97 = bf16[8,2,128,128]{3,2,1,0:T(8,128)(2,1)S(1)} custom-call(bf16[14,2,128,128]{3,2,1,0:T(8,128)(2,1)S(1)} %bitcast.27, bf16[2,128,2048]{2,1,0:T(8,128)(2,1)S(1)} %get-tuple-element.47.outer_ref.inner_ref, bf16[2,128,2048]{2,1,0:T(8,128)(2,1)S(1)} %get-tuple-element.46.inner_ref.outer_ref), custom_call_target="tpu_custom_call" | custom-call | flops 1024 | bytes 1024 | tf_op jit(solution)/shard_map/pallas_call | solution.py:430
  78.6 1.9 %collective-permute-start.8 = (bf16[8,2,128,128]{3,2,1,0:T(8,128)(2,1)S(1)}, bf16[8,2,128,128]{3,2,1,0:T(8,128)(2,1)S(1)}, u32[]{:S(2)}, u32[]{:S(2)}) collective-permute-start(bf16[8,2,128,128]{3,2,1,0:T(8,128)(2,1)S(1)} %shard_map.97), channel_id=1, source_target_pairs={{2,0},{4,2},{6,4},{8,6},{10,8},{12,10},{14,12},{16,14},{18,16},{20... | collective-permute-start | bytes 1572872 | tf_op jit(solution)/shard_map/ppermute | solution.py:495
  80.5 2.6 %shard_map.95 = bf16[6,2,128,128]{3,2,1,0:T(8,128)(2,1)S(1)} custom-call(bf16[14,2,128,128]{3,2,1,0:T(8,128)(2,1)S(1)} %bitcast.18, bf16[2,128,2048]{2,1,0:T(8,128)(2,1)S(1)} %get-tuple-element.46.inner_ref.outer_ref, bf16[2,128,2048]{2,1,0:T(8,128)(2,1)S(1)} %get-tuple-element.47.outer_ref.inner_ref), custom_call_target="tpu_custom_call" | custom-call | flops 1024 | bytes 1024 | tf_op jit(solution)/shard_map/pallas_call | solution.py:430
  83.1 3.6 %collective-permute-start.6 = (bf16[6,2,128,128]{3,2,1,0:T(8,128)(2,1)S(1)}, bf16[6,2,128,128]{3,2,1,0:T(8,128)(2,1)S(1)}, u32[]{:S(2)}, u32[]{:S(2)}) collective-permute-start(bf16[6,2,128,128]{3,2,1,0:T(8,128)(2,1)S(1)} %shard_map.95), channel_id=1, source_target_pairs={{0,2},{2,4},{4,6},{6,8},{8,10},{10,12},{12,14},{14,16},{16,18},{18... | collective-permute-start | bytes 1179656 | tf_op jit(solution)/shard_map/ppermute | solution.py:495
  86.8 2.7 %shard_map.96 = bf16[6,2,128,128]{3,2,1,0:T(8,128)(2,1)S(1)} custom-call(bf16[14,2,128,128]{3,2,1,0:T(8,128)(2,1)S(1)} %bitcast.28, bf16[2,128,2048]{2,1,0:T(8,128)(2,1)S(1)} %get-tuple-element.47.outer_ref.inner_ref, bf16[2,128,2048]{2,1,0:T(8,128)(2,1)S(1)} %get-tuple-element.46.inner_ref.outer_ref), custom_call_target="tpu_custom_call" | custom-call | flops 1024 | bytes 1024 | tf_op jit(solution)/shard_map/pallas_call | solution.py:430
  89.5 1.9 %collective-permute-start.7 = (bf16[6,2,128,128]{3,2,1,0:T(8,128)(2,1)S(1)}, bf16[6,2,128,128]{3,2,1,0:T(8,128)(2,1)S(1)}, u32[]{:S(2)}, u32[]{:S(2)}) collective-permute-start(bf16[6,2,128,128]{3,2,1,0:T(8,128)(2,1)S(1)} %shard_map.96), channel_id=1, source_target_pairs={{2,0},{4,2},{6,4},{8,6},{10,8},{12,10},{14,12},{16,14},{18,16},{20... | collective-permute-start | bytes 1179656 | tf_op jit(solution)/shard_map/ppermute | solution.py:495
  91.4 0.0 collective-permute-done.9.refs_0_
  91.4 1.1 %shard_map.98 = (f32[14,2,128,128]{3,2,1,0:T(8,128)}, f32[14,2,128,128]{3,2,1,0:T(8,128)}) custom-call(bf16[8,2,128,128]{3,2,1,0:T(8,128)(2,1)S(1)} %collective-permute-done.9.refs_0_), custom_call_target="tpu_custom_call" | custom-call | flops 1024 | bytes 1024 | tf_op jit(solution)/shard_map/pallas_call | solution.py:525
  92.5 0.0 collective-permute-done.8.refs_0_
  92.5 1.1 %shard_map.99 = (f32[14,2,128,128]{3,2,1,0:T(8,128)}, f32[14,2,128,128]{3,2,1,0:T(8,128)}) custom-call(bf16[8,2,128,128]{3,2,1,0:T(8,128)(2,1)S(1)} %collective-permute-done.8.refs_0_, f32[14,2,128,128]{3,2,1,0:T(8,128)} %get-tuple-element.49.refs_1_, f32[14,2,128,128]{3,2,1,0:T(8,128)} %get-tuple-element.50.refs_2_), custom_call_target="tpu_custom_call", output_to_operand_aliasing={{0}: (1, {}), {1}: (2, {})} | custom-call | flops 1024 | bytes 1024 | tf_op jit(solution)/shard_map/pallas_call | solution.py:525
  93.6 0.0 collective-permute-done.6.refs_0_
  93.6 4.9 %collective-permute-done.7.refs_1_ = bf16[6,2,128,128]{3,2,1,0:T(8,128)(2,1)S(1)} collective-permute-done((bf16[6,2,128,128]{3,2,1,0:T(8,128)(2,1)S(1)}, bf16[6,2,128,128]{3,2,1,0:T(8,128)(2,1)S(1)}, u32[]{:S(2)}, u32[]{:S(2)}) %collective-permute-start.7) | collective-permute-done | bytes 393248 | tf_op jit(solution)/shard_map/ppermute | solution.py:495
  98.6 1.3 %shard_map.100 = (f32[14,2,128,128]{3,2,1,0:T(8,128)}, f32[14,2,128,128]{3,2,1,0:T(8,128)}) custom-call(bf16[6,2,128,128]{3,2,1,0:T(8,128)(2,1)S(1)} %collective-permute-done.6.refs_0_, bf16[6,2,128,128]{3,2,1,0:T(8,128)(2,1)S(1)} %collective-permute-done.7.refs_1_, ...), custom_call_target="tpu_custom_call", output_to_operand_aliasing={{0}: (2, {}), {1}: (3, {})} | custom-call | flops 1024 | bytes 1024 | tf_op jit(solution)/shard_map/pallas_call | solution.py:525
  (1 shorter events, 0.0 us)
Async XLA Ops:
  0.6 5.5 %copy-start = (bf16[1,14,2,128,128]{4,3,2,1,0:T(8,128)(2,1)S(1)}, bf16[1,14,2,128,128]{4,3,2,1,0:T(8,128)(2,1)}, u32[]{:S(2)}) copy-start(bf16[1,14,2,128,128]{4,3,2,1,0:T(8,128)(2,1)} %param.7) | copy-start | bytes 2752516
  0.6 1.3 %copy-start.1 = (bf16[1,2,128,2048]{3,2,1,0:T(8,128)(2,1)S(1)}, bf16[1,2,128,2048]{3,2,1,0:T(8,128)(2,1)}, u32[]{:S(2)}) copy-start(bf16[1,2,128,2048]{3,2,1,0:T(8,128)(2,1)} %param.6) | copy-start | bytes 3145732
  2.0 15.7 %collective-permute-start.1 = (bf16[1,128,2048]{2,1,0:T(8,128)(2,1)S(1)}, bf16[1,128,2048]{2,1,0:T(8,128)(2,1)S(1)}, u32[]{:S(2)}, u32[]{:S(2)}) collective-permute-start(bf16[1,128,2048]{2,1,0:T(8,128)(2,1)S(1)} %get-tuple-element.31), channel_id=1, source_target_pairs={{0,1},{1,0},{2,3},{3,2},{4,5},{5,4},{6,7},{7,6},{8,9},{9,8},{10,11... | collective-permute-start | bytes 1572872 | tf_op jit(solution)/shard_map/ppermute | solution.py:414
  4.1 22.9 %collective-permute-start = (bf16[1,128,2048]{2,1,0:T(8,128)(2,1)S(1)}, bf16[1,128,2048]{2,1,0:T(8,128)(2,1)S(1)}, u32[]{:S(2)}, u32[]{:S(2)}) collective-permute-start(bf16[1,128,2048]{2,1,0:T(8,128)(2,1)S(1)} %get-tuple-element.29), channel_id=1, source_target_pairs={{0,1},{1,0},{2,3},{3,2},{4,5},{5,4},{6,7},{7,6},{8,9},{9,8},{10,11... | collective-permute-start | bytes 1572872 | tf_op jit(solution)/shard_map/ppermute | solution.py:414
  4.2 0.8 copy-start.6
  6.1 1.2 %copy-start.2 = (bf16[1,2,128,2048]{3,2,1,0:T(8,128)(2,1)S(1)}, bf16[1,2,128,2048]{3,2,1,0:T(8,128)(2,1)}, u32[]{:S(2)}) copy-start(bf16[1,2,128,2048]{3,2,1,0:T(8,128)(2,1)} %param.6) | copy-start | bytes 3145732
  7.3 1.2 %copy-start.4 = (bf16[1,14,2,128,128]{4,3,2,1,0:T(8,128)(2,1)S(1)}, bf16[1,14,2,128,128]{4,3,2,1,0:T(8,128)(2,1)}, u32[]{:S(2)}) copy-start(bf16[1,14,2,128,128]{4,3,2,1,0:T(8,128)(2,1)} %param.8) | copy-start | bytes 2752516
  17.7 9.4 %copy-start.3 = (bf16[1,2,128,2048]{3,2,1,0:T(8,128)(2,1)S(1)}, bf16[1,2,128,2048]{3,2,1,0:T(8,128)(2,1)}, u32[]{:S(2)}) copy-start(bf16[1,2,128,2048]{3,2,1,0:T(8,128)(2,1)} %param.6) | copy-start | bytes 3145732
  22.2 4.9 %collective-permute-start.2 = (f32[8,128]{1,0:T(8,128)S(1)}, f32[8,128]{1,0:T(8,128)S(1)}, u32[]{:S(2)}, u32[]{:S(2)}) collective-permute-start(f32[8,128]{1,0:T(8,128)S(1)} %get-tuple-element.35.mine_ref), channel_id=1, source_target_pairs={{0,1},{1,0},{2,3},{3,2},{4,5},{5,4},{6,7},{7,6},{8,9},{9,8},{10,11... | collective-permute-start | bytes 12296 | tf_op jit(solution)/shard_map/ppermute | solution.py:414
  30.0 13.5 %collective-permute-start.4 = (bf16[1,128,2048]{2,1,0:T(8,128)(2,1)S(1)}, bf16[1,128,2048]{2,1,0:T(8,128)(2,1)S(1)}, u32[]{:S(2)}, u32[]{:S(2)}) collective-permute-start(bf16[1,128,2048]{2,1,0:T(8,128)(2,1)S(1)} %get-tuple-element.37.refs_0_), channel_id=1, source_target_pairs={{0,1},{1,0},{2,3},{3,2},{4,5},{5,4},{6,7},{7,6},{8,9},{9,8},{10,11... | collective-permute-start | bytes 1572872 | tf_op jit(solution)/shard_map/ppermute | solution.py:414
  35.0 19.7 %collective-permute-start.3 = (bf16[1,128,2048]{2,1,0:T(8,128)(2,1)S(1)}, bf16[1,128,2048]{2,1,0:T(8,128)(2,1)S(1)}, u32[]{:S(2)}, u32[]{:S(2)}) collective-permute-start(bf16[1,128,2048]{2,1,0:T(8,128)(2,1)S(1)} %get-tuple-element.38), channel_id=1, source_target_pairs={{0,1},{1,0},{2,3},{3,2},{4,5},{5,4},{6,7},{7,6},{8,9},{9,8},{10,11... | collective-permute-start | bytes 1572872 | tf_op jit(solution)/shard_map/ppermute | solution.py:414
  35.0 8.4 %copy-start.7 = (s32[1,2]{1,0:T(1,128)S(1)}, s32[1,2]{1,0:T(1,128)}, u32[]{:S(2)}) copy-start(s32[1,2]{1,0:T(1,128)} %param.11) | copy-start | bytes 28
  60.2 4.2 %collective-permute-start.5 = (f32[16,128]{1,0:T(8,128)S(1)}, f32[16,128]{1,0:T(8,128)S(1)}, u32[]{:S(2)}, u32[]{:S(2)}) collective-permute-start(f32[16,128]{1,0:T(8,128)S(1)} %get-tuple-element.44.my_sums_ref), channel_id=1, source_target_pairs={{0,1},{1,0},{2,3},{3,2},{4,5},{5,4},{6,7},{7,6},{8,9},{9,8},{10,11... | collective-permute-start | bytes 24584 | tf_op jit(solution)/shard_map/ppermute | solution.py:414
  64.4 10.5 %copy-start.5 = (bf16[1,14,2,128,128]{4,3,2,1,0:T(8,128)(2,1)S(1)}, bf16[1,14,2,128,128]{4,3,2,1,0:T(8,128)(2,1)}, u32[]{:S(2)}) copy-start(bf16[1,14,2,128,128]{4,3,2,1,0:T(8,128)(2,1)} %param.8) | copy-start | bytes 2752516
  69.7 21.7 %collective-permute-start.9 = (bf16[8,2,128,128]{3,2,1,0:T(8,128)(2,1)S(1)}, bf16[8,2,128,128]{3,2,1,0:T(8,128)(2,1)S(1)}, u32[]{:S(2)}, u32[]{:S(2)}) collective-permute-start(bf16[8,2,128,128]{3,2,1,0:T(8,128)(2,1)S(1)} %get-tuple-element.48), channel_id=1, source_target_pairs={{0,2},{2,4},{4,6},{6,8},{8,10},{10,12},{12,14},{14,16},{16,18},{18... | collective-permute-start | bytes 1572872 | tf_op jit(solution)/shard_map/ppermute | solution.py:495
  78.6 13.9 %collective-permute-start.8 = (bf16[8,2,128,128]{3,2,1,0:T(8,128)(2,1)S(1)}, bf16[8,2,128,128]{3,2,1,0:T(8,128)(2,1)S(1)}, u32[]{:S(2)}, u32[]{:S(2)}) collective-permute-start(bf16[8,2,128,128]{3,2,1,0:T(8,128)(2,1)S(1)} %shard_map.97), channel_id=1, source_target_pairs={{2,0},{4,2},{6,4},{8,6},{10,8},{12,10},{14,12},{16,14},{18,16},{20... | collective-permute-start | bytes 1572872 | tf_op jit(solution)/shard_map/ppermute | solution.py:495
  83.1 10.5 %collective-permute-start.6 = (bf16[6,2,128,128]{3,2,1,0:T(8,128)(2,1)S(1)}, bf16[6,2,128,128]{3,2,1,0:T(8,128)(2,1)S(1)}, u32[]{:S(2)}, u32[]{:S(2)}) collective-permute-start(bf16[6,2,128,128]{3,2,1,0:T(8,128)(2,1)S(1)} %shard_map.95), channel_id=1, source_target_pairs={{0,2},{2,4},{4,6},{6,8},{8,10},{10,12},{12,14},{14,16},{16,18},{18... | collective-permute-start | bytes 1179656 | tf_op jit(solution)/shard_map/ppermute | solution.py:495
  89.5 9.1 %collective-permute-start.7 = (bf16[6,2,128,128]{3,2,1,0:T(8,128)(2,1)S(1)}, bf16[6,2,128,128]{3,2,1,0:T(8,128)(2,1)S(1)}, u32[]{:S(2)}, u32[]{:S(2)}) collective-permute-start(bf16[6,2,128,128]{3,2,1,0:T(8,128)(2,1)S(1)} %shard_map.96), channel_id=1, source_target_pairs={{2,0},{4,2},{6,4},{8,6},{10,8},{12,10},{14,12},{16,14},{18,16},{20... | collective-permute-start | bytes 1179656 | tf_op jit(solution)/shard_map/ppermute | solution.py:495

commit v2 on v1

--- a/solution.py
+++ b/solution.py
@@ -26,6 +26,12 @@
     return lax.dot_general(
         left, right, (((1,), (0,)), ((), ())), preferred_element_type=F32
     )
+
+
+def pieces_of(blocks, rows):
+    last = rows - rows // 4
+    whole = [(b, 0, rows) for b in range(blocks - 1)]
+    return whole + [(blocks - 1, 0, last), (blocks - 1, last, rows)]
 
 
 def make_kron(ops_ref, kron_ref, spread_ref):
@@ -69,7 +75,9 @@
     return place // 2
 
 
-def add_pairs(steps, lists, kron_ref, x_ref, left_ref, right_t_ref, acc_ref, turned_ref, mixed_ref):
+def add_pairs(
+    steps, lists, kron_ref, x_ref, left_ref, right_t_ref, acc_ref, turned_ref, mixed_ref, start=0
+):
     chan_list, src_list, live_list, dest_list = lists
     rows = x_ref.shape[1]
     phys = x_ref.shape[2] // LANES
@@ -110,9 +118,9 @@
     def act_left(s):
         dest = dest_list[2 * s]
         left = jnp.concatenate(
-            [left_ref[chan_list[2 * s], dest], left_ref[chan_list[2 * s + 1], dest]], axis=1
+            [left_ref[chan_list[2 * s + i], dest][:, start : start + rows] for i in range(2)], axis=1
         )
-        acc_ref[dest] += dot(left, mixed_ref[...])
+        acc_ref[dest] += dot(left, mixed_ref[0 : 2 * rows, :])
 
     def middle(s, carry):
         act_site(s)
@@ -163,8 +171,8 @@
 
 
 def cut(x_ref, *out_refs):
-    for b, out_ref in enumerate(out_refs):
-        out_ref[0] = x_ref[b]
+    for (b, begin, end), out_ref in zip(pieces_of(*x_ref.shape[:2]), out_refs):
+        out_ref[0] = x_ref[b, begin:end]
 
 
 def first_local(
@@ -215,6 +223,16 @@
     add_pairs(steps, lists, kron_ref, other_ref, left_ref, right_t_ref, acc_ref, turned_ref, mixed_ref)
 
 
+def more_remote(
+    rel_ref, kron_ref, other_ref, left_ref, right_t_ref, before_ref,
+    acc_ref,
+    turned_ref, mixed_ref, *lists,
+):
+    dests = left_ref.shape[1]
+    steps = list_pairs(rel_ref, dests + 1, 2 * dests, *lists)
+    add_pairs(steps, lists, kron_ref, other_ref, left_ref, right_t_ref, acc_ref, turned_ref, mixed_ref)
+
+
 def first_finish(
     dest, rel_ref, kron_ref, other_ref, left_ref, right_t_ref, before_ref, x_ref, mine_ref,
     theirs_ref, *refs,
@@ -222,26 +240,34 @@
     dests = left_ref.shape[1]
     last = dest == dests - 1
     if last:
-        earlier_ref, acc_ref, guess_ref, all_ref = refs[:4]
+        earlier_ref, acc_ref, head_ref, tail_ref, all_ref = refs[:5]
         all_ref[0:dest] = earlier_ref[...]
     else:
         acc_ref, guess_ref = refs[:2]
     turned_ref, mixed_ref = refs[-6:-4]
     lists = refs[-4:]
+    rows = x_ref.shape[1]
+    begin = rows - other_ref.shape[1]
     steps = list_pairs(rel_ref, dests + 1, 2 * dests, *lists, only=(dest,))
-    add_pairs(steps, lists, kron_ref, other_ref, left_ref, right_t_ref, acc_ref, turned_ref, mixed_ref)
+    add_pairs(
+        steps, lists, kron_ref, other_ref, left_ref, right_t_ref, acc_ref, turned_ref, mixed_ref, begin
+    )
     shift = common_shift(mine_ref, theirs_ref)
     keep_state = jnp.tile(1.0 + STEP_SIZE * shift, (1, x_ref.shape[2] // LANES))
 
     def update(b, r, start, carry):
         x = x_ref[b, r, :].astype(F32)
         guess = (keep_state * x - STEP_SIZE * acc_ref[b, r, :]).astype(BF16)
-        guess_ref[0, r, :] = guess
         if last:
             all_ref[b, r, :] = guess
+        else:
+            guess_ref[0, r, :] = guess
         return carry
 
-    row_loop(1, x_ref.shape[1], update, 0, first=dest)
+    row_loop(1, rows, update, 0, first=dest)
+    if last:
+        head_ref[0] = all_ref[dest, 0:begin]
+        tail_ref[0] = all_ref[dest, begin:rows]
 
 
 def second_remote(
@@ -274,7 +300,10 @@
 ):
     dests, rows, width = x_ref.shape
     steps = list_pairs(rel_ref, dests + 1, 2 * dests, *lists)
-    add_pairs(steps, lists, kron_ref, other_ref, left_ref, right_t_ref, kept_ref, turned_ref, mixed_ref)
+    add_pairs(
+        steps, lists, kron_ref, other_ref, left_ref, right_t_ref, kept_ref, turned_ref, mixed_ref,
+        rows - other_ref.shape[1],
+    )
     shift = common_shift(mine_ref, theirs_ref)
     keep_guess = jnp.tile(1.0 + STEP_SIZE * shift, (1, width // LANES))
 
@@ -438,8 +467,9 @@
             input_output_aliases=aliases,
         )(*args)
 
-    block = shape((1, rows, width), BF16)
-    own = call(cut, [VMEM], (block,) * dests, [], x)
+    places = pieces_of(dests, rows)
+    kinds = tuple(shape((1, end - begin, width), BF16) for _, begin, end in places)
+    own = call(cut, [VMEM], kinds, [], x)
     other = [trade(value) for value in own]
     kron = call(
         make_kron, [VMEM], shape((chan, phys * GROUP, phys * GROUP), BF16),
@@ -455,17 +485,21 @@
         rel, kron, other[0], left, right_t, image, mine, aliases={5: 0},
     )
     theirs = trade(mine)
+    image = call(
+        more_remote, [SMEM] + [VMEM] * 5, wave_f32, pair_scratch,
+        rel, kron, other[1], left, right_t, image, aliases={5: 0},
+    )
     image, first_guess = call(
         functools.partial(first_finish, 0), [SMEM] + [VMEM] * 8,
-        (wave_f32, block), pair_scratch,
-        rel, kron, other[1], left, right_t, image, x, mine, theirs, aliases={5: 0},
-    )
-    image, last_guess, guess = call(
+        (wave_f32, kinds[0]), pair_scratch,
+        rel, kron, other[2], left, right_t, image, x, mine, theirs, aliases={5: 0},
+    )
+    image, head, tail, guess = call(
         functools.partial(first_finish, 1), [SMEM] + [VMEM] * 9,
-        (wave_f32, block, wave_b16), pair_scratch,
-        rel, kron, other[1], left, right_t, image, x, mine, theirs, first_guess, aliases={5: 0},
-    )
-    other = [trade(first_guess), trade(last_guess)]
+        (wave_f32, kinds[1], kinds[2], wave_b16), pair_scratch,
+        rel, kron, other[2], left, right_t, image, x, mine, theirs, first_guess, aliases={5: 0},
+    )
+    other = [trade(first_guess), trade(head), trade(tail)]
     acc = call(
         local_sources, [SMEM] + [VMEM] * 4, wave_f32, pair_scratch,
         rel, kron, guess, left, right_t,
@@ -474,9 +508,13 @@
         second_remote, [SMEM] * 2 + [VMEM] * 8, (wave_f32, sums_kind), pair_scratch,
         rel, ranks[0], kron, other[0], left, right_t, acc, x, image, guess, aliases={6: 0},
     )
+    acc = call(
+        more_remote, [SMEM] + [VMEM] * 5, wave_f32, pair_scratch,
+        rel, kron, other[1], left, right_t, acc, aliases={5: 0},
+    )
     kept, my_sums = call(
         second_finish, [SMEM] * 2 + [VMEM] * 10, (wave_f32, shape((16, LANES), F32)), pair_scratch,
-        rel, ranks[0], kron, other[1], left, right_t, acc, x, guess, mine, theirs, early_sums,
+        rel, ranks[0], kron, other[2], left, right_t, acc, x, guess, mine, theirs, early_sums,
         aliases={6: 0},
     )
     their_sums = trade(my_sums)

time: 101 us -> 103 us (1.020)
  starting transfers between devices: 20.7 us -> 29.9 us
  waiting for transfers between devices: 15.8 us -> 7.7 us
  Pallas kernels: 57.1 us -> 58.7 us
    ppermute x6 -> x8, waiting for transfers between devices: 10.9 us -> 2.78 us  [trade(): return lax.ppermute(value, 'blk', swap)]
    ppermute x6 -> x8, starting transfers between devices: 8.04 us -> 14.2 us  [trade(): return lax.ppermute(value, 'blk', swap)]
    ppermute x4, starting transfers between devices: 12.7 us -> 15.6 us  [sent(): lax.ppermute(value, 'seg', [(s, s + steps) for s in range(begin, end)])]
    pallas_call x12 -> x14, Pallas kernels: 48.3 us -> 49.9 us  [call(): pl.pallas_call(body, in_specs=specs, out_specs=jax.tree.map(lambda _: VME...]
  transfers between devices with their start and end apart: 10 -> 12, of which waited for: 6 -> 5; matrix products, arithmetic and copies ran while one was open for 1% -> 1% of each run, Pallas kernels for 42% -> 46%
where the time goes in v2:
time: 103 us
  Pallas kernels  58.7 us (57%)
  starting transfers between devices  29.9 us (29%)
  waiting for transfers between devices  7.7 us (7%)
  local copies, waits for them, and re-layouts  4.63 us (4%)
  between operations  1.06 us (1%)
    pallas_call x14, Pallas kernels, call(): pl.pallas_call(body, in_specs=specs, out_specs=jax.tree.map(lambda _: VME...  49.9 us
    ppermute x4, starting transfers between devices, sent(): lax.ppermute(value, 'seg', [(s, s + steps) for s in range(begin, end)])  15.6 us
    ppermute x8, starting transfers between devices, trade(): return lax.ppermute(value, 'blk', swap)  14.2 us
    pallas_call x1, Pallas kernels, shards(): pl.pallas_call(functools.partial(normalize_and_left, 0, early, env_scale,...  5.29 us
    ppermute x4, waiting for transfers between devices, sent(): lax.ppermute(value, 'seg', [(s, s + steps) for s in range(begin, end)])  4.92 us
    unnamed x16, local copies, waits for them, and re-layouts  4.54 us
    pallas_call x3, Pallas kernels, widened(): pl.pallas_call(functools.partial(widen, places), in_specs=[VMEM] * count...  3.49 us
    ppermute x8, waiting for transfers between devices, trade(): return lax.ppermute(value, 'blk', swap)  2.78 us
  transfers between devices with their start and end apart: 12, of which 5 were waited for; matrix products, arithmetic and copies ran while one was open for 1% of the time, Pallas kernels for 46%

profile of v2, /device:TPU:1, one launch (start us, length us, event | category | flops | bytes accessed | tf_op | source)
XLA Modules:
  0.0 102.7 jit_solution(17777066500439873120)
XLA Ops:
  0.6 0.0 copy-start
  0.6 0.0 copy-start.1
  0.7 1.3 %copy-done.1 = bf16[1,2,128,2048]{3,2,1,0:T(8,128)(2,1)S(1)} copy-done((bf16[1,2,128,2048]{3,2,1,0:T(8,128)(2,1)S(1)}, bf16[1,2,128,2048]{3,2,1,0:T(8,128)(2,1)}, u32[]{:S(2)}) %copy-start.1) | copy-done | bytes 1048600
  1.9 0.1 shard_map.86
  2.0 2.1 %collective-permute-start.2 = (bf16[1,128,2048]{2,1,0:T(8,128)(2,1)S(1)}, bf16[1,128,2048]{2,1,0:T(8,128)(2,1)S(1)}, u32[]{:S(2)}, u32[]{:S(2)}) collective-permute-start(bf16[1,128,2048]{2,1,0:T(8,128)(2,1)S(1)} %get-tuple-element.34), channel_id=1, source_target_pairs={{0,1},{1,0},{2,3},{3,2},{4,5},{5,4},{6,7},{7,6},{8,9},{9,8},{10,11... | collective-permute-start | bytes 1572872 | tf_op jit(solution)/shard_map/ppermute | solution.py:443
  4.1 0.1 collective-permute-start.1
  4.2 1.4 %collective-permute-start = (bf16[1,32,2048]{2,1,0:T(8,128)(2,1)S(1)}, bf16[1,32,2048]{2,1,0:T(8,128)(2,1)S(1)}, u32[]{:S(2)}, u32[]{:S(2)}) collective-permute-start(bf16[1,32,2048]{2,1,0:T(8,128)(2,1)S(1)} %get-tuple-element.31), channel_id=1, source_target_pairs={{0,1},{1,0},{2,3},{3,2},{4,5},{5,4},{6,7},{7,6},{8,9},{9,8},{10,11... | collective-permute-start | bytes 393224 | tf_op jit(solution)/shard_map/ppermute | solution.py:443
  5.6 0.0 copy-start.6
  5.6 0.8 copy-done.6
  6.4 0.3 shard_map.85.kron_ref
  6.7 0.7 add_bitcast_fusion
  7.4 0.1 copy.20
  7.5 0.0 copy-done
  7.5 0.0 copy-start.2
  7.5 1.2 %copy-done.2 = bf16[1,2,128,2048]{3,2,1,0:T(8,128)(2,1)S(1)} copy-done((bf16[1,2,128,2048]{3,2,1,0:T(8,128)(2,1)S(1)}, bf16[1,2,128,2048]{3,2,1,0:T(8,128)(2,1)}, u32[]{:S(2)}) %copy-start.2) | copy-done | bytes 1048600
  8.7 0.0 copy-start.4
  8.7 1.2 %copy-done.4 = bf16[1,14,2,128,128]{4,3,2,1,0:T(8,128)(2,1)S(1)} copy-done((bf16[1,14,2,128,128]{4,3,2,1,0:T(8,128)(2,1)S(1)}, bf16[1,14,2,128,128]{4,3,2,1,0:T(8,128)(2,1)}, u32[]{:S(2)}) %copy-start.4) | copy-done | bytes 917528
  9.9 9.2 %shard_map.87 = (bf16[14,2,128,128]{3,2,1,0:T(8,128)(2,1)S(1)}, f32[2,128,2048]{2,1,0:T(8,128)S(1)}, f32[8,128]{1,0:T(8,128)S(1)}) custom-call(s32[14,2]{1,0:T(8,128)S(1)} %negate_select_fusion.rel_ref, bf16[14,128,128]{2,1,0:T(8,128)(2,1)S(1)} %shard_map.85.kron_ref, bf16[2,128,2048]{2,1,0:T(8,128)(2,1)S(1)} %bitcast.22, ...), custom_call_target="tpu_custom_call" | custom-call | flops 1024 | bytes 1024 | tf_op jit(solution)/shard_map/pallas_call | solution.py:459
  19.1 0.0 collective-permute-done.2.other_ref
  19.1 5.3 %shard_map.88 = (f32[2,128,2048]{2,1,0:T(8,128)S(1)}, f32[8,128]{1,0:T(8,128)S(1)}) custom-call(s32[14,2]{1,0:T(8,128)S(1)} %negate_select_fusion.rel_ref, bf16[14,128,128]{2,1,0:T(8,128)(2,1)S(1)} %shard_map.85.kron_ref, bf16[1,128,2048]{2,1,0:T(8,128)(2,1)S(1)} %collective-permute-done.2.other_ref, ...), custom_call_target="tpu_custom_call", output_to_operand_aliasing={{0}: (5, {})} | custom-call | flops 1024 | bytes 1024 | tf_op jit(solution)/shard_map/pallas_call | solution.py:459
  24.4 0.1 collective-permute-start.3
  24.4 0.0 collective-permute-done.1.other_ref
  24.5 0.0 copy-start.3
  24.5 2.5 %shard_map.89.before_ref = f32[2,128,2048]{2,1,0:T(8,128)S(1)} custom-call(s32[14,2]{1,0:T(8,128)S(1)} %negate_select_fusion.rel_ref, bf16[14,128,128]{2,1,0:T(8,128)(2,1)S(1)} %shard_map.85.kron_ref, bf16[1,96,2048]{2,1,0:T(8,128)(2,1)S(1)} %collective-permute-done.1.other_ref, ...), custom_call_target="tpu_custom_call", output_to_operand_aliasing={{}: (5, {})} | custom-call | flops 1024 | bytes 1024 | tf_op jit(solution)/shard_map/pallas_call | solution.py:459
  27.0 0.0 collective-permute-done.other_ref
  27.0 0.3 collective-permute-done.3.theirs_ref
  27.3 0.0 copy-done.3
  27.3 1.6 %shard_map.90 = (f32[2,128,2048]{2,1,0:T(8,128)S(1)}, bf16[1,128,2048]{2,1,0:T(8,128)(2,1)S(1)}) custom-call(s32[14,2]{1,0:T(8,128)S(1)} %negate_select_fusion.rel_ref, bf16[14,128,128]{2,1,0:T(8,128)(2,1)S(1)} %shard_map.85.kron_ref, bf16[1,32,2048]{2,1,0:T(8,128)(2,1)S(1)} %collective-permute-done.other_ref, ...), custom_call_target="tpu_custom_call", output_to_operand_aliasing={{0}: (5, {})} | custom-call | flops 1024 | bytes 1024 | tf_op jit(solution)/shard_map/pallas_call | solution.py:459
  28.9 4.4 %collective-permute-start.6 = (bf16[1,128,2048]{2,1,0:T(8,128)(2,1)S(1)}, bf16[1,128,2048]{2,1,0:T(8,128)(2,1)S(1)}, u32[]{:S(2)}, u32[]{:S(2)}) collective-permute-start(bf16[1,128,2048]{2,1,0:T(8,128)(2,1)S(1)} %get-tuple-element.40.refs_0_), channel_id=1, source_target_pairs={{0,1},{1,0},{2,3},{3,2},{4,5},{5,4},{6,7},{7,6},{8,9},{9,8},{10,11... | collective-permute-start | bytes 1572872 | tf_op jit(solution)/shard_map/ppermute | solution.py:443
  33.3 1.7 %shard_map.91 = (f32[2,128,2048]{2,1,0:T(8,128)S(1)}, bf16[1,96,2048]{2,1,0:T(8,128)(2,1)S(1)}, bf16[1,32,2048]{2,1,0:T(8,128)(2,1)S(1)}, bf16[2,128,2048]{2,1,0:T(8,128)(2,1)S(1)}) custom-call(s32[14,2]{1,0:T(8,128)S(1)} %negate_select_fusion.rel_ref, bf16[14,128,128]{2,1,0:T(8,128)(2,1)S(1)} %shard_map.85.kron_ref, ...), custom_call_target="tpu_custom_call", output_to_operand_aliasing={{0}: (5, {})} | custom-call | flops 1024 | bytes 1024 | tf_op jit(solution)/shard_map/pallas_call | solution.py:459
  35.0 0.6 collective-permute-start.5
  35.6 0.9 collective-permute-start.4
  36.5 0.0 copy-start.7
  36.5 8.0 %shard_map.92.before_ref = f32[2,128,2048]{2,1,0:T(8,128)S(1)} custom-call(s32[14,2]{1,0:T(8,128)S(1)} %negate_select_fusion.rel_ref, bf16[14,128,128]{2,1,0:T(8,128)(2,1)S(1)} %shard_map.85.kron_ref, bf16[2,128,2048]{2,1,0:T(8,128)(2,1)S(1)} %get-tuple-element.43.x_ref.guess_ref, bf16[14,2,128,128]{3,2,1,0:T(8,128)(2,1)S(1)} %bitcast.15, ...), custom_call_target="tpu_custom_call" | custom-call | flops 1024 | bytes 1024 | tf_op jit(solution)/shard_map/pallas_call | solution.py:459
  44.5 0.0 collective-permute-done.6.other_ref
  44.5 0.0 copy-done.7
  44.5 6.9 %shard_map.93 = (f32[2,128,2048]{2,1,0:T(8,128)S(1)}, f32[8,128]{1,0:T(8,128)S(1)}) custom-call(s32[14,2]{1,0:T(8,128)S(1)} %negate_select_fusion.rel_ref, s32[2]{0:T(128)S(1)} %bitcast.32, bf16[14,128,128]{2,1,0:T(8,128)(2,1)S(1)} %shard_map.85.kron_ref, ...), custom_call_target="tpu_custom_call", output_to_operand_aliasing={{0}: (6, {})} | custom-call | flops 1024 | bytes 1024 | tf_op jit(solution)/shard_map/pallas_call | solution.py:459
  51.5 1.1 %collective-permute-done.5.other_ref = bf16[1,96,2048]{2,1,0:T(8,128)(2,1)S(1)} collective-permute-done((bf16[1,96,2048]{2,1,0:T(8,128)(2,1)S(1)}, bf16[1,96,2048]{2,1,0:T(8,128)(2,1)S(1)}, u32[]{:S(2)}, u32[]{:S(2)}) %collective-permute-start.5) | collective-permute-done | bytes 393248 | tf_op jit(solution)/shard_map/ppermute | solution.py:443
  52.6 2.5 %shard_map.94.before_ref = f32[2,128,2048]{2,1,0:T(8,128)S(1)} custom-call(s32[14,2]{1,0:T(8,128)S(1)} %negate_select_fusion.rel_ref, bf16[14,128,128]{2,1,0:T(8,128)(2,1)S(1)} %shard_map.85.kron_ref, bf16[1,96,2048]{2,1,0:T(8,128)(2,1)S(1)} %collective-permute-done.5.other_ref, ...), custom_call_target="tpu_custom_call", output_to_operand_aliasing={{}: (5, {})} | custom-call | flops 1024 | bytes 1024 | tf_op jit(solution)/shard_map/pallas_call | solution.py:459
  55.0 0.3 collective-permute-done.4.other_ref
  55.4 3.0 %shard_map.95 = (f32[2,128,2048]{2,1,0:T(8,128)S(1)}, f32[16,128]{1,0:T(8,128)S(1)}) custom-call(s32[14,2]{1,0:T(8,128)S(1)} %negate_select_fusion.rel_ref, s32[2]{0:T(128)S(1)} %bitcast.33, bf16[14,128,128]{2,1,0:T(8,128)(2,1)S(1)} %shard_map.85.kron_ref, ...), custom_call_target="tpu_custom_call", output_to_operand_aliasing={{0}: (6, {})} | custom-call | flops 1024 | bytes 1024 | tf_op jit(solution)/shard_map/pallas_call | solution.py:459
  58.4 4.7 %collective-permute-start.7 = (f32[16,128]{1,0:T(8,128)S(1)}, f32[16,128]{1,0:T(8,128)S(1)}, u32[]{:S(2)}, u32[]{:S(2)}) collective-permute-start(f32[16,128]{1,0:T(8,128)S(1)} %get-tuple-element.48.my_sums_ref), channel_id=1, source_target_pairs={{0,1},{1,0},{2,3},{3,2},{4,5},{5,4},{6,7},{7,6},{8,9},{9,8},{10,11... | collective-permute-start | bytes 24584 | tf_op jit(solution)/shard_map/ppermute | solution.py:443
  63.0 1.0 %collective-permute-done.7.their_sums_ref = f32[16,128]{1,0:T(8,128)S(1)} collective-permute-done((f32[16,128]{1,0:T(8,128)S(1)}, f32[16,128]{1,0:T(8,128)S(1)}, u32[]{:S(2)}, u32[]{:S(2)}) %collective-permute-start.7) | collective-permute-done | bytes 8224 | tf_op jit(solution)/shard_map/ppermute | solution.py:443
  64.1 0.0 copy-start.5
  64.1 5.3 %shard_map.96 = (bf16[2,128,2048]{2,1,0:T(8,128)(2,1)}, bf16[2,128,2048]{2,1,0:T(8,128)(2,1)S(1)}, bf16[2,128,2048]{2,1,0:T(8,128)(2,1)S(1)}, bf16[8,2,128,128]{3,2,1,0:T(8,128)(2,1)S(1)}) custom-call(s32[2]{0:T(128)S(1)} %bitcast.34, f32[2,128,2048]{2,1,0:T(8,128)S(1)} %get-tuple-element.47.kept_ref, ...), custom_call_target="tpu_custom_call" | custom-call | flops 1024 | bytes 1024 | tf_op jit(solution)/shard_map/pallas_call | solution.py:544
  69.4 8.2 %collective-permute-start.11 = (bf16[8,2,128,128]{3,2,1,0:T(8,128)(2,1)S(1)}, bf16[8,2,128,128]{3,2,1,0:T(8,128)(2,1)S(1)}, u32[]{:S(2)}, u32[]{:S(2)}) collective-permute-start(bf16[8,2,128,128]{3,2,1,0:T(8,128)(2,1)S(1)} %get-tuple-element.52), channel_id=1, source_target_pairs={{0,2},{2,4},{4,6},{6,8},{8,10},{10,12},{12,14},{14,16},{16,18},{18... | collective-permute-start | bytes 1572872 | tf_op jit(solution)/shard_map/ppermute | solution.py:533
  77.6 0.0 copy-done.5
  77.6 3.7 %shard_map.99 = bf16[8,2,128,128]{3,2,1,0:T(8,128)(2,1)S(1)} custom-call(bf16[14,2,128,128]{3,2,1,0:T(8,128)(2,1)S(1)} %bitcast.29, bf16[2,128,2048]{2,1,0:T(8,128)(2,1)S(1)} %get-tuple-element.51.outer_ref.inner_ref, bf16[2,128,2048]{2,1,0:T(8,128)(2,1)S(1)} %get-tuple-element.50.inner_ref.outer_ref), custom_call_target="tpu_custom_call" | custom-call | flops 1024 | bytes 1024 | tf_op jit(solution)/shard_map/pallas_call | solution.py:459
  81.3 1.9 %collective-permute-start.10 = (bf16[8,2,128,128]{3,2,1,0:T(8,128)(2,1)S(1)}, bf16[8,2,128,128]{3,2,1,0:T(8,128)(2,1)S(1)}, u32[]{:S(2)}, u32[]{:S(2)}) collective-permute-start(bf16[8,2,128,128]{3,2,1,0:T(8,128)(2,1)S(1)} %shard_map.99), channel_id=1, source_target_pairs={{2,0},{4,2},{6,4},{8,6},{10,8},{12,10},{14,12},{16,14},{18,16},{20... | collective-permute-start | bytes 1572872 | tf_op jit(solution)/shard_map/ppermute | solution.py:533
  83.2 2.6 %shard_map.97 = bf16[6,2,128,128]{3,2,1,0:T(8,128)(2,1)S(1)} custom-call(bf16[14,2,128,128]{3,2,1,0:T(8,128)(2,1)S(1)} %bitcast.20, bf16[2,128,2048]{2,1,0:T(8,128)(2,1)S(1)} %get-tuple-element.50.inner_ref.outer_ref, bf16[2,128,2048]{2,1,0:T(8,128)(2,1)S(1)} %get-tuple-element.51.outer_ref.inner_ref), custom_call_target="tpu_custom_call" | custom-call | flops 1024 | bytes 1024 | tf_op jit(solution)/shard_map/pallas_call | solution.py:459
  85.8 3.6 %collective-permute-start.8 = (bf16[6,2,128,128]{3,2,1,0:T(8,128)(2,1)S(1)}, bf16[6,2,128,128]{3,2,1,0:T(8,128)(2,1)S(1)}, u32[]{:S(2)}, u32[]{:S(2)}) collective-permute-start(bf16[6,2,128,128]{3,2,1,0:T(8,128)(2,1)S(1)} %shard_map.97), channel_id=1, source_target_pairs={{0,2},{2,4},{4,6},{6,8},{8,10},{10,12},{12,14},{14,16},{16,18},{18... | collective-permute-start | bytes 1179656 | tf_op jit(solution)/shard_map/ppermute | solution.py:533
  89.4 2.7 %shard_map.98 = bf16[6,2,128,128]{3,2,1,0:T(8,128)(2,1)S(1)} custom-call(bf16[14,2,128,128]{3,2,1,0:T(8,128)(2,1)S(1)} %bitcast.30, bf16[2,128,2048]{2,1,0:T(8,128)(2,1)S(1)} %get-tuple-element.51.outer_ref.inner_ref, bf16[2,128,2048]{2,1,0:T(8,128)(2,1)S(1)} %get-tuple-element.50.inner_ref.outer_ref), custom_call_target="tpu_custom_call" | custom-call | flops 1024 | bytes 1024 | tf_op jit(solution)/shard_map/pallas_call | solution.py:459
  92.1 1.9 %collective-permute-start.9 = (bf16[6,2,128,128]{3,2,1,0:T(8,128)(2,1)S(1)}, bf16[6,2,128,128]{3,2,1,0:T(8,128)(2,1)S(1)}, u32[]{:S(2)}, u32[]{:S(2)}) collective-permute-start(bf16[6,2,128,128]{3,2,1,0:T(8,128)(2,1)S(1)} %shard_map.98), channel_id=1, source_target_pairs={{2,0},{4,2},{6,4},{8,6},{10,8},{12,10},{14,12},{16,14},{18,16},{20... | collective-permute-start | bytes 1179656 | tf_op jit(solution)/shard_map/ppermute | solution.py:533
  94.1 0.0 collective-permute-done.11.refs_0_
  94.1 1.1 %shard_map.100 = (f32[14,2,128,128]{3,2,1,0:T(8,128)}, f32[14,2,128,128]{3,2,1,0:T(8,128)}) custom-call(bf16[8,2,128,128]{3,2,1,0:T(8,128)(2,1)S(1)} %collective-permute-done.11.refs_0_), custom_call_target="tpu_custom_call" | custom-call | flops 1024 | bytes 1024 | tf_op jit(solution)/shard_map/pallas_call | solution.py:563
  95.2 0.0 collective-permute-done.10.refs_0_
  95.2 1.1 %shard_map.101 = (f32[14,2,128,128]{3,2,1,0:T(8,128)}, f32[14,2,128,128]{3,2,1,0:T(8,128)}) custom-call(bf16[8,2,128,128]{3,2,1,0:T(8,128)(2,1)S(1)} %collective-permute-done.10.refs_0_, f32[14,2,128,128]{3,2,1,0:T(8,128)} %get-tuple-element.53.refs_1_, f32[14,2,128,128]{3,2,1,0:T(8,128)} %get-tuple-element.54.refs_2_), custom_call_target="tpu_custom_call", output_to_operand_aliasing={{0}: (1, {}), {1}: (2, {})} | custom-call | flops 1024 | bytes 1024 | tf_op jit(solution)/shard_map/pallas_call | solution.py:563
  96.3 0.0 collective-permute-done.8.refs_0_
  96.3 4.9 %collective-permute-done.9.refs_1_ = bf16[6,2,128,128]{3,2,1,0:T(8,128)(2,1)S(1)} collective-permute-done((bf16[6,2,128,128]{3,2,1,0:T(8,128)(2,1)S(1)}, bf16[6,2,128,128]{3,2,1,0:T(8,128)(2,1)S(1)}, u32[]{:S(2)}, u32[]{:S(2)}) %collective-permute-start.9) | collective-permute-done | bytes 393248 | tf_op jit(solution)/shard_map/ppermute | solution.py:533
  101.2 1.3 %shard_map.102 = (f32[14,2,128,128]{3,2,1,0:T(8,128)}, f32[14,2,128,128]{3,2,1,0:T(8,128)}) custom-call(bf16[6,2,128,128]{3,2,1,0:T(8,128)(2,1)S(1)} %collective-permute-done.8.refs_0_, bf16[6,2,128,128]{3,2,1,0:T(8,128)(2,1)S(1)} %collective-permute-done.9.refs_1_, ...), custom_call_target="tpu_custom_call", output_to_operand_aliasing={{0}: (2, {}), {1}: (3, {})} | custom-call | flops 1024 | bytes 1024 | tf_op jit(solution)/shard_map/pallas_call | solution.py:563
  (1 shorter events, 0.0 us)
Async XLA Ops:
  0.6 6.9 %copy-start = (bf16[1,14,2,128,128]{4,3,2,1,0:T(8,128)(2,1)S(1)}, bf16[1,14,2,128,128]{4,3,2,1,0:T(8,128)(2,1)}, u32[]{:S(2)}) copy-start(bf16[1,14,2,128,128]{4,3,2,1,0:T(8,128)(2,1)} %param.7) | copy-start | bytes 2752516
  0.6 1.3 %copy-start.1 = (bf16[1,2,128,2048]{3,2,1,0:T(8,128)(2,1)S(1)}, bf16[1,2,128,2048]{3,2,1,0:T(8,128)(2,1)}, u32[]{:S(2)}) copy-start(bf16[1,2,128,2048]{3,2,1,0:T(8,128)(2,1)} %param.6) | copy-start | bytes 3145732
  2.0 17.1 %collective-permute-start.2 = (bf16[1,128,2048]{2,1,0:T(8,128)(2,1)S(1)}, bf16[1,128,2048]{2,1,0:T(8,128)(2,1)S(1)}, u32[]{:S(2)}, u32[]{:S(2)}) collective-permute-start(bf16[1,128,2048]{2,1,0:T(8,128)(2,1)S(1)} %get-tuple-element.34), channel_id=1, source_target_pairs={{0,1},{1,0},{2,3},{3,2},{4,5},{5,4},{6,7},{7,6},{8,9},{9,8},{10,11... | collective-permute-start | bytes 1572872 | tf_op jit(solution)/shard_map/ppermute | solution.py:443
  4.1 20.3 %collective-permute-start.1 = (bf16[1,96,2048]{2,1,0:T(8,128)(2,1)S(1)}, bf16[1,96,2048]{2,1,0:T(8,128)(2,1)S(1)}, u32[]{:S(2)}, u32[]{:S(2)}) collective-permute-start(bf16[1,96,2048]{2,1,0:T(8,128)(2,1)S(1)} %get-tuple-element.33), channel_id=1, source_target_pairs={{0,1},{1,0},{2,3},{3,2},{4,5},{5,4},{6,7},{7,6},{8,9},{9,8},{10,11... | collective-permute-start | bytes 1179656 | tf_op jit(solution)/shard_map/ppermute | solution.py:443
  4.2 22.8 %collective-permute-start = (bf16[1,32,2048]{2,1,0:T(8,128)(2,1)S(1)}, bf16[1,32,2048]{2,1,0:T(8,128)(2,1)S(1)}, u32[]{:S(2)}, u32[]{:S(2)}) collective-permute-start(bf16[1,32,2048]{2,1,0:T(8,128)(2,1)S(1)} %get-tuple-element.31), channel_id=1, source_target_pairs={{0,1},{1,0},{2,3},{3,2},{4,5},{5,4},{6,7},{7,6},{8,9},{9,8},{10,11... | collective-permute-start | bytes 393224 | tf_op jit(solution)/shard_map/ppermute | solution.py:443
  5.6 0.8 copy-start.6
  7.5 1.2 %copy-start.2 = (bf16[1,2,128,2048]{3,2,1,0:T(8,128)(2,1)S(1)}, bf16[1,2,128,2048]{3,2,1,0:T(8,128)(2,1)}, u32[]{:S(2)}) copy-start(bf16[1,2,128,2048]{3,2,1,0:T(8,128)(2,1)} %param.6) | copy-start | bytes 3145732
  8.7 1.2 %copy-start.4 = (bf16[1,14,2,128,128]{4,3,2,1,0:T(8,128)(2,1)S(1)}, bf16[1,14,2,128,128]{4,3,2,1,0:T(8,128)(2,1)}, u32[]{:S(2)}) copy-start(bf16[1,14,2,128,128]{4,3,2,1,0:T(8,128)(2,1)} %param.8) | copy-start | bytes 2752516
  24.4 2.9 %collective-permute-start.3 = (f32[8,128]{1,0:T(8,128)S(1)}, f32[8,128]{1,0:T(8,128)S(1)}, u32[]{:S(2)}, u32[]{:S(2)}) collective-permute-start(f32[8,128]{1,0:T(8,128)S(1)} %get-tuple-element.38.mine_ref), channel_id=1, source_target_pairs={{0,1},{1,0},{2,3},{3,2},{4,5},{5,4},{6,7},{7,6},{8,9},{9,8},{10,11... | collective-permute-start | bytes 12296 | tf_op jit(solution)/shard_map/ppermute | solution.py:443
  24.5 2.8 %copy-start.3 = (bf16[1,2,128,2048]{3,2,1,0:T(8,128)(2,1)S(1)}, bf16[1,2,128,2048]{3,2,1,0:T(8,128)(2,1)}, u32[]{:S(2)}) copy-start(bf16[1,2,128,2048]{3,2,1,0:T(8,128)(2,1)} %param.6) | copy-start | bytes 3145732
  28.9 15.6 %collective-permute-start.6 = (bf16[1,128,2048]{2,1,0:T(8,128)(2,1)S(1)}, bf16[1,128,2048]{2,1,0:T(8,128)(2,1)S(1)}, u32[]{:S(2)}, u32[]{:S(2)}) collective-permute-start(bf16[1,128,2048]{2,1,0:T(8,128)(2,1)S(1)} %get-tuple-element.40.refs_0_), channel_id=1, source_target_pairs={{0,1},{1,0},{2,3},{3,2},{4,5},{5,4},{6,7},{7,6},{8,9},{9,8},{10,11... | collective-permute-start | bytes 1572872 | tf_op jit(solution)/shard_map/ppermute | solution.py:443
  35.0 17.6 %collective-permute-start.5 = (bf16[1,96,2048]{2,1,0:T(8,128)(2,1)S(1)}, bf16[1,96,2048]{2,1,0:T(8,128)(2,1)S(1)}, u32[]{:S(2)}, u32[]{:S(2)}) collective-permute-start(bf16[1,96,2048]{2,1,0:T(8,128)(2,1)S(1)} %get-tuple-element.42), channel_id=1, source_target_pairs={{0,1},{1,0},{2,3},{3,2},{4,5},{5,4},{6,7},{7,6},{8,9},{9,8},{10,11... | collective-permute-start | bytes 1179656 | tf_op jit(solution)/shard_map/ppermute | solution.py:443
  35.6 19.8 %collective-permute-start.4 = (bf16[1,32,2048]{2,1,0:T(8,128)(2,1)S(1)}, bf16[1,32,2048]{2,1,0:T(8,128)(2,1)S(1)}, u32[]{:S(2)}, u32[]{:S(2)}) collective-permute-start(bf16[1,32,2048]{2,1,0:T(8,128)(2,1)S(1)} %get-tuple-element.41), channel_id=1, source_target_pairs={{0,1},{1,0},{2,3},{3,2},{4,5},{5,4},{6,7},{7,6},{8,9},{9,8},{10,11... | collective-permute-start | bytes 393224 | tf_op jit(solution)/shard_map/ppermute | solution.py:443
  36.5 8.0 %copy-start.7 = (s32[1,2]{1,0:T(1,128)S(1)}, s32[1,2]{1,0:T(1,128)}, u32[]{:S(2)}) copy-start(s32[1,2]{1,0:T(1,128)} %param.11) | copy-start | bytes 28
  58.4 5.7 %collective-permute-start.7 = (f32[16,128]{1,0:T(8,128)S(1)}, f32[16,128]{1,0:T(8,128)S(1)}, u32[]{:S(2)}, u32[]{:S(2)}) collective-permute-start(f32[16,128]{1,0:T(8,128)S(1)} %get-tuple-element.48.my_sums_ref), channel_id=1, source_target_pairs={{0,1},{1,0},{2,3},{3,2},{4,5},{5,4},{6,7},{7,6},{8,9},{9,8},{10,11... | collective-permute-start | bytes 24584 | tf_op jit(solution)/shard_map/ppermute | solution.py:443
  64.1 13.5 %copy-start.5 = (bf16[1,14,2,128,128]{4,3,2,1,0:T(8,128)(2,1)S(1)}, bf16[1,14,2,128,128]{4,3,2,1,0:T(8,128)(2,1)}, u32[]{:S(2)}) copy-start(bf16[1,14,2,128,128]{4,3,2,1,0:T(8,128)(2,1)} %param.8) | copy-start | bytes 2752516
  69.4 24.7 %collective-permute-start.11 = (bf16[8,2,128,128]{3,2,1,0:T(8,128)(2,1)S(1)}, bf16[8,2,128,128]{3,2,1,0:T(8,128)(2,1)S(1)}, u32[]{:S(2)}, u32[]{:S(2)}) collective-permute-start(bf16[8,2,128,128]{3,2,1,0:T(8,128)(2,1)S(1)} %get-tuple-element.52), channel_id=1, source_target_pairs={{0,2},{2,4},{4,6},{6,8},{8,10},{10,12},{12,14},{14,16},{16,18},{18... | collective-permute-start | bytes 1572872 | tf_op jit(solution)/shard_map/ppermute | solution.py:533
  81.3 13.9 %collective-permute-start.10 = (bf16[8,2,128,128]{3,2,1,0:T(8,128)(2,1)S(1)}, bf16[8,2,128,128]{3,2,1,0:T(8,128)(2,1)S(1)}, u32[]{:S(2)}, u32[]{:S(2)}) collective-permute-start(bf16[8,2,128,128]{3,2,1,0:T(8,128)(2,1)S(1)} %shard_map.99), channel_id=1, source_target_pairs={{2,0},{4,2},{6,4},{8,6},{10,8},{12,10},{14,12},{16,14},{18,16},{20... | collective-permute-start | bytes 1572872 | tf_op jit(solution)/shard_map/ppermute | solution.py:533
  85.8 10.5 %collective-permute-start.8 = (bf16[6,2,128,128]{3,2,1,0:T(8,128)(2,1)S(1)}, bf16[6,2,128,128]{3,2,1,0:T(8,128)(2,1)S(1)}, u32[]{:S(2)}, u32[]{:S(2)}) collective-permute-start(bf16[6,2,128,128]{3,2,1,0:T(8,128)(2,1)S(1)} %shard_map.97), channel_id=1, source_target_pairs={{0,2},{2,4},{4,6},{6,8},{8,10},{10,12},{12,14},{14,16},{16,18},{18... | collective-permute-start | bytes 1179656 | tf_op jit(solution)/shard_map/ppermute | solution.py:533
  92.1 9.1 %collective-permute-start.9 = (bf16[6,2,128,128]{3,2,1,0:T(8,128)(2,1)S(1)}, bf16[6,2,128,128]{3,2,1,0:T(8,128)(2,1)S(1)}, u32[]{:S(2)}, u32[]{:S(2)}) collective-permute-start(bf16[6,2,128,128]{3,2,1,0:T(8,128)(2,1)S(1)} %shard_map.98), channel_id=1, source_target_pairs={{2,0},{4,2},{6,4},{8,6},{10,8},{12,10},{14,12},{16,14},{18,16},{20... | collective-permute-start | bytes 1179656 | tf_op jit(solution)/shard_map/ppermute | solution.py:533

commit v3 on v2

--- a/solution.py
+++ b/solution.py
@@ -170,16 +170,18 @@
     return jnp.where(den > 0, num / jnp.where(den > 0, den, 1.0), 0.0)
 
 
-def cut(x_ref, *out_refs):
-    for (b, begin, end), out_ref in zip(pieces_of(*x_ref.shape[:2]), out_refs):
+def cut(first, x_ref, *out_refs):
+    for (b, begin, end), out_ref in zip(pieces_of(*x_ref.shape[:2])[first:], out_refs):
         out_ref[0] = x_ref[b, begin:end]
 
 
 def first_local(
-    rel_ref, kron_ref, x_ref, left_ref, right_ref,
-    right_t_ref, image_ref, sums_ref,
-    turned_ref, mixed_ref, *lists,
-):
+    rel_ref, ops_ref, x_ref, left_ref, right_ref,
+    kron_ref, right_t_ref, image_ref, sums_ref,
+    turned_ref, mixed_ref, *scratch,
+):
+    lists, spread_ref = scratch[:-1], scratch[-1]
+    make_kron(ops_ref, kron_ref, spread_ref)
     chan, dests = left_ref.shape[:2]
 
     def turn(n, carry):
@@ -202,35 +204,25 @@
     put_sums(sums_ref, totals)
 
 
-def local_sources(
-    rel_ref, kron_ref, x_ref, left_ref, right_t_ref,
+def more_remote(
+    block, rel_ref, kron_ref, other_ref, left_ref, right_t_ref, before_ref,
     acc_ref,
     turned_ref, mixed_ref, *lists,
 ):
-    acc_ref[...] = jnp.zeros_like(acc_ref)
-    steps = list_pairs(rel_ref, 0, left_ref.shape[1], *lists)
-    add_pairs(steps, lists, kron_ref, x_ref, left_ref, right_t_ref, acc_ref, turned_ref, mixed_ref)
+    low = left_ref.shape[1] + block
+    steps = list_pairs(rel_ref, low, low + 1, *lists)
+    add_pairs(steps, lists, kron_ref, other_ref, left_ref, right_t_ref, acc_ref, turned_ref, mixed_ref)
 
 
 def first_remote(
     rel_ref, kron_ref, other_ref, left_ref, right_t_ref, before_ref, local_sums_ref,
-    acc_ref, sums_ref,
-    turned_ref, mixed_ref, *lists,
-):
-    dests = left_ref.shape[1]
+    acc_ref, sums_ref, *scratch,
+):
     sums_ref[...] = local_sums_ref[...]
-    steps = list_pairs(rel_ref, dests, dests + 1, *lists)
-    add_pairs(steps, lists, kron_ref, other_ref, left_ref, right_t_ref, acc_ref, turned_ref, mixed_ref)
-
-
-def more_remote(
-    rel_ref, kron_ref, other_ref, left_ref, right_t_ref, before_ref,
-    acc_ref,
-    turned_ref, mixed_ref, *lists,
-):
-    dests = left_ref.shape[1]
-    steps = list_pairs(rel_ref, dests + 1, 2 * dests, *lists)
-    add_pairs(steps, lists, kron_ref, other_ref, left_ref, right_t_ref, acc_ref, turned_ref, mixed_ref)
+    more_remote(
+        left_ref.shape[1] - 1, rel_ref, kron_ref, other_ref, left_ref, right_t_ref, before_ref,
+        acc_ref, *scratch,
+    )
 
 
 def first_finish(
@@ -270,15 +262,15 @@
         tail_ref[0] = all_ref[dest, begin:rows]
 
 
-def second_remote(
-    rel_ref, rank_ref, kron_ref, other_ref, left_ref, right_t_ref, before_ref, x_ref, image_ref,
-    guess_ref,
+def second_local(
+    rel_ref, rank_ref, kron_ref, guess_ref, left_ref, right_t_ref, x_ref, image_ref,
     acc_ref, sums_ref,
     turned_ref, mixed_ref, *lists,
 ):
     dests, rows, _ = x_ref.shape
-    steps = list_pairs(rel_ref, dests, dests + 1, *lists)
-    add_pairs(steps, lists, kron_ref, other_ref, left_ref, right_t_ref, acc_ref, turned_ref, mixed_ref)
+    acc_ref[...] = jnp.zeros_like(acc_ref)
+    steps = list_pairs(rel_ref, 0, dests, *lists)
+    add_pairs(steps, lists, kron_ref, guess_ref, left_ref, right_t_ref, acc_ref, turned_ref, mixed_ref)
 
     def sums(b, r, start, carry):
         x = x_ref[b, r, :].astype(F32)
@@ -469,26 +461,29 @@
 
     places = pieces_of(dests, rows)
     kinds = tuple(shape((1, end - begin, width), BF16) for _, begin, end in places)
-    own = call(cut, [VMEM], kinds, [], x)
+    own = [
+        call(functools.partial(cut, 0), [VMEM], kinds[0], [], x),
+        *call(functools.partial(cut, 1), [VMEM], kinds[1:], [], x),
+    ]
     other = [trade(value) for value in own]
-    kron = call(
-        make_kron, [VMEM], shape((chan, phys * GROUP, phys * GROUP), BF16),
-        [pltpu.VMEM((chan * phys, phys * GROUP), F32)], ops,
-    )
-    right_t, image, mine = call(
+    kron, right_t, image, mine = call(
         first_local, [SMEM] + [VMEM] * 4,
-        (shape(right.shape, BF16), wave_f32, sums_kind), pair_scratch,
-        rel, kron, x, left, right,
+        (
+            shape((chan, phys * GROUP, phys * GROUP), BF16), shape(right.shape, BF16), wave_f32,
+            sums_kind,
+        ),
+        pair_scratch + [pltpu.VMEM((chan * phys, phys * GROUP), F32)],
+        rel, ops, x, left, right,
+    )
+    image = call(
+        functools.partial(more_remote, 0), [SMEM] + [VMEM] * 5, wave_f32, pair_scratch,
+        rel, kron, other[0], left, right_t, image, aliases={5: 0},
     )
     image, mine = call(
         first_remote, [SMEM] + [VMEM] * 6, (wave_f32, sums_kind), pair_scratch,
-        rel, kron, other[0], left, right_t, image, mine, aliases={5: 0},
+        rel, kron, other[1], left, right_t, image, mine, aliases={5: 0},
     )
     theirs = trade(mine)
-    image = call(
-        more_remote, [SMEM] + [VMEM] * 5, wave_f32, pair_scratch,
-        rel, kron, other[1], left, right_t, image, aliases={5: 0},
-    )
     image, first_guess = call(
         functools.partial(first_finish, 0), [SMEM] + [VMEM] * 8,
         (wave_f32, kinds[0]), pair_scratch,
@@ -500,16 +495,16 @@
         rel, kron, other[2], left, right_t, image, x, mine, theirs, first_guess, aliases={5: 0},
     )
     other = [trade(first_guess), trade(head), trade(tail)]
+    acc, early_sums = call(
+        second_local, [SMEM] * 2 + [VMEM] * 6, (wave_f32, sums_kind), pair_scratch,
+        rel, ranks[0], kron, guess, left, right_t, x, image,
+    )
     acc = call(
-        local_sources, [SMEM] + [VMEM] * 4, wave_f32, pair_scratch,
-        rel, kron, guess, left, right_t,
-    )
-    acc, early_sums = call(
-        second_remote, [SMEM] * 2 + [VMEM] * 8, (wave_f32, sums_kind), pair_scratch,
-        rel, ranks[0], kron, other[0], left, right_t, acc, x, image, guess, aliases={6: 0},
+        functools.partial(more_remote, 0), [SMEM] + [VMEM] * 5, wave_f32, pair_scratch,
+        rel, kron, other[0], left, right_t, acc, aliases={5: 0},
     )
     acc = call(
-        more_remote, [SMEM] + [VMEM] * 5, wave_f32, pair_scratch,
+        functools.partial(more_remote, 1), [SMEM] + [VMEM] * 5, wave_f32, pair_scratch,
         rel, kron, other[1], left, right_t, acc, aliases={5: 0},
     )
     kept, my_sums = call(

time: 103 us -> 106 us (1.029)
  the two profiles are of different devices: /device:TPU:1 before, /device:TPU:21 now
where the time goes in v3:
time: 106 us
  Pallas kernels  64.6 us (61%)
  starting transfers between devices  26.1 us (25%)
  waiting for transfers between devices  10.4 us (10%)
  local copies, waits for them, and re-layouts  3.41 us (3%)
    pallas_call x14, Pallas kernels, call(): pl.pallas_call(body, in_specs=specs, out_specs=jax.tree.map(lambda _: VME...  55.8 us
    ppermute x4, starting transfers between devices, sent(): lax.ppermute(value, 'seg', [(s, s + steps) for s in range(begin, end)])  19.2 us
    ppermute x8, starting transfers between devices, trade(): return lax.ppermute(value, 'blk', swap)  6.89 us
    ppermute x4, waiting for transfers between devices, sent(): lax.ppermute(value, 'seg', [(s, s + steps) for s in range(begin, end)])  5.81 us
    pallas_call x1, Pallas kernels, shards(): pl.pallas_call(functools.partial(normalize_and_left, 0, early, env_scale,...  5.29 us
    ppermute x8, waiting for transfers between devices, trade(): return lax.ppermute(value, 'blk', swap)  4.55 us
    pallas_call x3, Pallas kernels, widened(): pl.pallas_call(functools.partial(widen, places), in_specs=[VMEM] * count...  3.49 us
    unnamed x16, local copies, waits for them, and re-layouts  3.31 us
  transfers between devices with their start and end apart: 12, of which 4 were waited for; matrix products, arithmetic and copies ran while one was open for 0% of the time, Pallas kernels for 49%

profile of v3, /device:TPU:21, one launch (start us, length us, event | category | flops | bytes accessed | tf_op | source)
XLA Modules:
  0.0 105.6 jit_solution(3606018124322404282)
XLA Ops:
  0.6 0.0 copy-start
  0.6 0.0 copy-start.1
  0.7 1.3 %copy-done.1 = bf16[1,2,128,2048]{3,2,1,0:T(8,128)(2,1)S(1)} copy-done((bf16[1,2,128,2048]{3,2,1,0:T(8,128)(2,1)S(1)}, bf16[1,2,128,2048]{3,2,1,0:T(8,128)(2,1)}, u32[]{:S(2)}) %copy-start.1) | copy-done | bytes 1048600
  1.9 0.0 copy-start.7
  1.9 0.0 copy-start.2
  2.0 1.3 %collective-permute-start.2 = (bf16[1,128,2048]{2,1,0:T(8,128)(2,1)S(1)}, bf16[1,128,2048]{2,1,0:T(8,128)(2,1)S(1)}, u32[]{:S(2)}, u32[]{:S(2)}) collective-permute-start(bf16[1,128,2048]{2,1,0:T(8,128)(2,1)S(1)} %shard_map.87), channel_id=1, source_target_pairs={{0,1},{1,0},{2,3},{3,2},{4,5},{5,4},{6,7},{7,6},{8,9},{9,8},{10,11... | collective-permute-start | bytes 1572872 | tf_op jit(solution)/shard_map/ppermute | solution.py:435
  3.3 0.8 shard_map.86
  4.1 0.3 collective-permute-start.1
  4.3 1.2 %collective-permute-start = (bf16[1,32,2048]{2,1,0:T(8,128)(2,1)}, bf16[1,32,2048]{2,1,0:T(8,128)(2,1)S(1)}, u32[]{:S(2)}, u32[]{:S(2)}) collective-permute-start(bf16[1,32,2048]{2,1,0:T(8,128)(2,1)} %get-tuple-element.32), channel_id=1, source_target_pairs={{0,1},{1,0},{2,3},{3,2},{4,5},{5,4},{6,7},{7,6},{8,9},{9,8},{10,11... | collective-permute-start | bytes 393224 | tf_op jit(solution)/shard_map/ppermute | solution.py:435
  5.6 0.0 copy-done.7
  5.6 0.1 copy.20
  5.7 0.0 copy-done
  5.7 0.0 copy-done.2
  5.7 0.0 copy-start.3
  5.7 1.2 %copy-done.3 = bf16[1,14,2,128,128]{4,3,2,1,0:T(8,128)(2,1)S(1)} copy-done((bf16[1,14,2,128,128]{4,3,2,1,0:T(8,128)(2,1)S(1)}, bf16[1,14,2,128,128]{4,3,2,1,0:T(8,128)(2,1)}, u32[]{:S(2)}) %copy-start.3) | copy-done | bytes 917528
  6.9 0.0 copy-start.5
  6.9 0.8 copy-done.5
  7.7 10.3 %shard_map.85 = (bf16[14,128,128]{2,1,0:T(8,128)(2,1)S(1)}, bf16[14,2,128,128]{3,2,1,0:T(8,128)(2,1)S(1)}, f32[2,128,2048]{2,1,0:T(8,128)S(1)}, f32[8,128]{1,0:T(8,128)S(1)}) custom-call(s32[14,2]{1,0:T(8,128)S(1)} %negate_select_fusion.rel_ref, bf16[14,16,16]{2,1,0:T(8,128)(2,1)S(1)} %bitcast.32, bf16[2,128,2048]{2,1,0:T(8,128)(2,1)S(1)} %bitcast.23, ...), custom_call_target="tpu_custom_call" | custom-call | flops 1024 | bytes 1024 | tf_op jit(solution)/shard_map/pallas_call | solution.py:451
  18.0 0.0 collective-permute-done.2.other_ref
  18.0 4.5 %shard_map.88.before_ref = f32[2,128,2048]{2,1,0:T(8,128)S(1)} custom-call(s32[14,2]{1,0:T(8,128)S(1)} %negate_select_fusion.rel_ref, bf16[14,128,128]{2,1,0:T(8,128)(2,1)S(1)} %get-tuple-element.31.kron_ref, bf16[1,128,2048]{2,1,0:T(8,128)(2,1)S(1)} %collective-permute-done.2.other_ref, ...), custom_call_target="tpu_custom_call", output_to_operand_aliasing={{}: (5, {})} | custom-call | flops 1024 | bytes 1024 | tf_op jit(solution)/shard_map/pallas_call | solution.py:451
  22.5 0.8 collective-permute-done.1.other_ref
  23.3 3.9 %shard_map.89 = (f32[2,128,2048]{2,1,0:T(8,128)S(1)}, f32[8,128]{1,0:T(8,128)S(1)}) custom-call(s32[14,2]{1,0:T(8,128)S(1)} %negate_select_fusion.rel_ref, bf16[14,128,128]{2,1,0:T(8,128)(2,1)S(1)} %get-tuple-element.31.kron_ref, bf16[1,96,2048]{2,1,0:T(8,128)(2,1)S(1)} %collective-permute-done.1.other_ref, ...), custom_call_target="tpu_custom_call", output_to_operand_aliasing={{0}: (5, {})} | custom-call | flops 1024 | bytes 1024 | tf_op jit(solution)/shard_map/pallas_call | solution.py:451
  27.2 1.3 %collective-permute-start.3 = (f32[8,128]{1,0:T(8,128)S(1)}, f32[8,128]{1,0:T(8,128)S(1)}, u32[]{:S(2)}, u32[]{:S(2)}) collective-permute-start(f32[8,128]{1,0:T(8,128)S(1)} %get-tuple-element.38.mine_ref), channel_id=1, source_target_pairs={{0,1},{1,0},{2,3},{3,2},{4,5},{5,4},{6,7},{7,6},{8,9},{9,8},{10,11... | collective-permute-start | bytes 12296 | tf_op jit(solution)/shard_map/ppermute | solution.py:435
  28.5 0.0 collective-permute-done.other_ref
  28.5 1.2 %collective-permute-done.3.theirs_ref = f32[8,128]{1,0:T(8,128)S(1)} collective-permute-done((f32[8,128]{1,0:T(8,128)S(1)}, f32[8,128]{1,0:T(8,128)S(1)}, u32[]{:S(2)}, u32[]{:S(2)}) %collective-permute-start.3) | collective-permute-done | bytes 4128 | tf_op jit(solution)/shard_map/ppermute | solution.py:435
  29.7 2.1 %shard_map.90 = (f32[2,128,2048]{2,1,0:T(8,128)S(1)}, bf16[1,128,2048]{2,1,0:T(8,128)(2,1)S(1)}) custom-call(s32[14,2]{1,0:T(8,128)S(1)} %negate_select_fusion.rel_ref, bf16[14,128,128]{2,1,0:T(8,128)(2,1)S(1)} %get-tuple-element.31.kron_ref, bf16[1,32,2048]{2,1,0:T(8,128)(2,1)S(1)} %collective-permute-done.other_ref, ...), custom_call_target="tpu_custom_call", output_to_operand_aliasing={{0}: (5, {})} | custom-call | flops 1024 | bytes 1024 | tf_op jit(solution)/shard_map/pallas_call | solution.py:451
  31.9 1.3 %collective-permute-start.6 = (bf16[1,128,2048]{2,1,0:T(8,128)(2,1)S(1)}, bf16[1,128,2048]{2,1,0:T(8,128)(2,1)S(1)}, u32[]{:S(2)}, u32[]{:S(2)}) collective-permute-start(bf16[1,128,2048]{2,1,0:T(8,128)(2,1)S(1)} %get-tuple-element.40.refs_0_), channel_id=1, source_target_pairs={{0,1},{1,0},{2,3},{3,2},{4,5},{5,4},{6,7},{7,6},{8,9},{9,8},{10,11... | collective-permute-start | bytes 1572872 | tf_op jit(solution)/shard_map/ppermute | solution.py:435
  33.2 0.0 copy-start.6
  33.2 2.2 %shard_map.91 = (f32[2,128,2048]{2,1,0:T(8,128)S(1)}, bf16[1,96,2048]{2,1,0:T(8,128)(2,1)S(1)}, bf16[1,32,2048]{2,1,0:T(8,128)(2,1)S(1)}, bf16[2,128,2048]{2,1,0:T(8,128)(2,1)S(1)}) custom-call(s32[14,2]{1,0:T(8,128)S(1)} %negate_select_fusion.rel_ref, bf16[14,128,128]{2,1,0:T(8,128)(2,1)S(1)} %get-tuple-element.31.kron_ref, ...), custom_call_target="tpu_custom_call", output_to_operand_aliasing={{0}: (5, {})} | custom-call | flops 1024 | bytes 1024 | tf_op jit(solution)/shard_map/pallas_call | solution.py:451
  35.4 0.3 collective-permute-start.5
  35.7 1.2 %collective-permute-start.4 = (bf16[1,32,2048]{2,1,0:T(8,128)(2,1)S(1)}, bf16[1,32,2048]{2,1,0:T(8,128)(2,1)S(1)}, u32[]{:S(2)}, u32[]{:S(2)}) collective-permute-start(bf16[1,32,2048]{2,1,0:T(8,128)(2,1)S(1)} %get-tuple-element.41), channel_id=1, source_target_pairs={{0,1},{1,0},{2,3},{3,2},{4,5},{5,4},{6,7},{7,6},{8,9},{9,8},{10,11... | collective-permute-start | bytes 393224 | tf_op jit(solution)/shard_map/ppermute | solution.py:435
  36.9 0.0 copy-done.6
  36.9 10.3 %shard_map.92 = (f32[2,128,2048]{2,1,0:T(8,128)S(1)}, f32[8,128]{1,0:T(8,128)S(1)}) custom-call(s32[14,2]{1,0:T(8,128)S(1)} %negate_select_fusion.rel_ref, s32[2]{0:T(128)S(1)} %bitcast.33, bf16[14,128,128]{2,1,0:T(8,128)(2,1)S(1)} %get-tuple-element.31.kron_ref, bf16[2,128,2048]{2,1,0:T(8,128)(2,1)S(1)} %get-tuple-element.43.guess_ref, ...), custom_call_target="tpu_custom_call" | custom-call | flops 1024 | bytes 1024 | tf_op jit(solution)/shard_map/pallas_call | solution.py:451
  47.2 0.0 collective-permute-done.6.other_ref
  47.2 4.6 %shard_map.93.before_ref = f32[2,128,2048]{2,1,0:T(8,128)S(1)} custom-call(s32[14,2]{1,0:T(8,128)S(1)} %negate_select_fusion.rel_ref, bf16[14,128,128]{2,1,0:T(8,128)(2,1)S(1)} %get-tuple-element.31.kron_ref, bf16[1,128,2048]{2,1,0:T(8,128)(2,1)S(1)} %collective-permute-done.6.other_ref, ...), custom_call_target="tpu_custom_call", output_to_operand_aliasing={{}: (5, {})} | custom-call | flops 1024 | bytes 1024 | tf_op jit(solution)/shard_map/pallas_call | solution.py:451
  51.9 0.0 collective-permute-done.5.other_ref
  51.9 4.0 %shard_map.94.before_ref = f32[2,128,2048]{2,1,0:T(8,128)S(1)} custom-call(s32[14,2]{1,0:T(8,128)S(1)} %negate_select_fusion.rel_ref, bf16[14,128,128]{2,1,0:T(8,128)(2,1)S(1)} %get-tuple-element.31.kron_ref, bf16[1,96,2048]{2,1,0:T(8,128)(2,1)S(1)} %collective-permute-done.5.other_ref, ...), custom_call_target="tpu_custom_call", output_to_operand_aliasing={{}: (5, {})} | custom-call | flops 1024 | bytes 1024 | tf_op jit(solution)/shard_map/pallas_call | solution.py:451
  55.8 0.0 collective-permute-done.4.other_ref
  55.9 4.1 %shard_map.95 = (f32[2,128,2048]{2,1,0:T(8,128)S(1)}, f32[16,128]{1,0:T(8,128)S(1)}) custom-call(s32[14,2]{1,0:T(8,128)S(1)} %negate_select_fusion.rel_ref, s32[2]{0:T(128)S(1)} %bitcast.34, bf16[14,128,128]{2,1,0:T(8,128)(2,1)S(1)} %get-tuple-element.31.kron_ref, ...), custom_call_target="tpu_custom_call", output_to_operand_aliasing={{0}: (6, {})} | custom-call | flops 1024 | bytes 1024 | tf_op jit(solution)/shard_map/pallas_call | solution.py:451
  59.9 0.1 collective-permute-start.7
  60.0 2.5 %collective-permute-done.7.their_sums_ref = f32[16,128]{1,0:T(8,128)S(1)} collective-permute-done((f32[16,128]{1,0:T(8,128)S(1)}, f32[16,128]{1,0:T(8,128)S(1)}, u32[]{:S(2)}, u32[]{:S(2)}) %collective-permute-start.7) | collective-permute-done | bytes 8224 | tf_op jit(solution)/shard_map/ppermute | solution.py:435
  62.5 0.0 copy-start.4
  62.5 5.3 %shard_map.96 = (bf16[2,128,2048]{2,1,0:T(8,128)(2,1)}, bf16[2,128,2048]{2,1,0:T(8,128)(2,1)S(1)}, bf16[2,128,2048]{2,1,0:T(8,128)(2,1)S(1)}, bf16[8,2,128,128]{3,2,1,0:T(8,128)(2,1)S(1)}) custom-call(s32[2]{0:T(128)S(1)} %bitcast.35, f32[2,128,2048]{2,1,0:T(8,128)S(1)} %get-tuple-element.47.kept_ref, bf16[2,128,2048]{2,1,0:T(8,128)(2,1)S(1)} %get-tuple-element.43.guess_ref, ...), custom_call_target="tpu_custom_call" | custom-call | flops 1024 | bytes 1024 | tf_op jit(solution)/shard_map/pallas_call | solution.py:539
  67.8 10.8 %collective-permute-start.11 = (bf16[8,2,128,128]{3,2,1,0:T(8,128)(2,1)S(1)}, bf16[8,2,128,128]{3,2,1,0:T(8,128)(2,1)S(1)}, u32[]{:S(2)}, u32[]{:S(2)}) collective-permute-start(bf16[8,2,128,128]{3,2,1,0:T(8,128)(2,1)S(1)} %get-tuple-element.52), channel_id=1, source_target_pairs={{0,2},{2,4},{4,6},{6,8},{8,10},{10,12},{12,14},{14,16},{16,18},{18... | collective-permute-start | bytes 1572872 | tf_op jit(solution)/shard_map/ppermute | solution.py:528
  78.7 0.0 copy-done.4
  78.7 3.7 %shard_map.99 = bf16[8,2,128,128]{3,2,1,0:T(8,128)(2,1)S(1)} custom-call(bf16[14,2,128,128]{3,2,1,0:T(8,128)(2,1)S(1)} %bitcast.30, bf16[2,128,2048]{2,1,0:T(8,128)(2,1)S(1)} %get-tuple-element.51.outer_ref.inner_ref, bf16[2,128,2048]{2,1,0:T(8,128)(2,1)S(1)} %get-tuple-element.50.inner_ref.outer_ref), custom_call_target="tpu_custom_call" | custom-call | flops 1024 | bytes 1024 | tf_op jit(solution)/shard_map/pallas_call | solution.py:451
  82.4 1.9 %collective-permute-start.10 = (bf16[8,2,128,128]{3,2,1,0:T(8,128)(2,1)S(1)}, bf16[8,2,128,128]{3,2,1,0:T(8,128)(2,1)S(1)}, u32[]{:S(2)}, u32[]{:S(2)}) collective-permute-start(bf16[8,2,128,128]{3,2,1,0:T(8,128)(2,1)S(1)} %shard_map.99), channel_id=1, source_target_pairs={{2,0},{4,2},{6,4},{8,6},{10,8},{12,10},{14,12},{16,14},{18,16},{20... | collective-permute-start | bytes 1572872 | tf_op jit(solution)/shard_map/ppermute | solution.py:528
  84.3 2.6 %shard_map.97 = bf16[6,2,128,128]{3,2,1,0:T(8,128)(2,1)S(1)} custom-call(bf16[14,2,128,128]{3,2,1,0:T(8,128)(2,1)S(1)} %bitcast.20, bf16[2,128,2048]{2,1,0:T(8,128)(2,1)S(1)} %get-tuple-element.50.inner_ref.outer_ref, bf16[2,128,2048]{2,1,0:T(8,128)(2,1)S(1)} %get-tuple-element.51.outer_ref.inner_ref), custom_call_target="tpu_custom_call" | custom-call | flops 1024 | bytes 1024 | tf_op jit(solution)/shard_map/pallas_call | solution.py:451
  86.9 4.5 %collective-permute-start.8 = (bf16[6,2,128,128]{3,2,1,0:T(8,128)(2,1)S(1)}, bf16[6,2,128,128]{3,2,1,0:T(8,128)(2,1)S(1)}, u32[]{:S(2)}, u32[]{:S(2)}) collective-permute-start(bf16[6,2,128,128]{3,2,1,0:T(8,128)(2,1)S(1)} %shard_map.97), channel_id=1, source_target_pairs={{0,2},{2,4},{4,6},{6,8},{8,10},{10,12},{12,14},{14,16},{16,18},{18... | collective-permute-start | bytes 1179656 | tf_op jit(solution)/shard_map/ppermute | solution.py:528
  91.4 2.7 %shard_map.98 = bf16[6,2,128,128]{3,2,1,0:T(8,128)(2,1)S(1)} custom-call(bf16[14,2,128,128]{3,2,1,0:T(8,128)(2,1)S(1)} %bitcast.31, bf16[2,128,2048]{2,1,0:T(8,128)(2,1)S(1)} %get-tuple-element.51.outer_ref.inner_ref, bf16[2,128,2048]{2,1,0:T(8,128)(2,1)S(1)} %get-tuple-element.50.inner_ref.outer_ref), custom_call_target="tpu_custom_call" | custom-call | flops 1024 | bytes 1024 | tf_op jit(solution)/shard_map/pallas_call | solution.py:451
  94.1 1.9 %collective-permute-start.9 = (bf16[6,2,128,128]{3,2,1,0:T(8,128)(2,1)S(1)}, bf16[6,2,128,128]{3,2,1,0:T(8,128)(2,1)S(1)}, u32[]{:S(2)}, u32[]{:S(2)}) collective-permute-start(bf16[6,2,128,128]{3,2,1,0:T(8,128)(2,1)S(1)} %shard_map.98), channel_id=1, source_target_pairs={{2,0},{4,2},{6,4},{8,6},{10,8},{12,10},{14,12},{16,14},{18,16},{20... | collective-permute-start | bytes 1179656 | tf_op jit(solution)/shard_map/ppermute | solution.py:528
  96.1 0.0 collective-permute-done.11.refs_0_
  96.1 1.1 %shard_map.100 = (f32[14,2,128,128]{3,2,1,0:T(8,128)}, f32[14,2,128,128]{3,2,1,0:T(8,128)}) custom-call(bf16[8,2,128,128]{3,2,1,0:T(8,128)(2,1)S(1)} %collective-permute-done.11.refs_0_), custom_call_target="tpu_custom_call" | custom-call | flops 1024 | bytes 1024 | tf_op jit(solution)/shard_map/pallas_call | solution.py:558
  97.2 0.0 collective-permute-done.10.refs_0_
  97.2 1.1 %shard_map.101 = (f32[14,2,128,128]{3,2,1,0:T(8,128)}, f32[14,2,128,128]{3,2,1,0:T(8,128)}) custom-call(bf16[8,2,128,128]{3,2,1,0:T(8,128)(2,1)S(1)} %collective-permute-done.10.refs_0_, f32[14,2,128,128]{3,2,1,0:T(8,128)} %get-tuple-element.53.refs_1_, f32[14,2,128,128]{3,2,1,0:T(8,128)} %get-tuple-element.54.refs_2_), custom_call_target="tpu_custom_call", output_to_operand_aliasing={{0}: (1, {}), {1}: (2, {})} | custom-call | flops 1024 | bytes 1024 | tf_op jit(solution)/shard_map/pallas_call | solution.py:558
  98.3 0.0 collective-permute-done.8.refs_0_
  98.3 5.8 %collective-permute-done.9.refs_1_ = bf16[6,2,128,128]{3,2,1,0:T(8,128)(2,1)S(1)} collective-permute-done((bf16[6,2,128,128]{3,2,1,0:T(8,128)(2,1)S(1)}, bf16[6,2,128,128]{3,2,1,0:T(8,128)(2,1)S(1)}, u32[]{:S(2)}, u32[]{:S(2)}) %collective-permute-start.9) | collective-permute-done | bytes 393248 | tf_op jit(solution)/shard_map/ppermute | solution.py:528
  104.1 1.3 %shard_map.102 = (f32[14,2,128,128]{3,2,1,0:T(8,128)}, f32[14,2,128,128]{3,2,1,0:T(8,128)}) custom-call(bf16[6,2,128,128]{3,2,1,0:T(8,128)(2,1)S(1)} %collective-permute-done.8.refs_0_, bf16[6,2,128,128]{3,2,1,0:T(8,128)(2,1)S(1)} %collective-permute-done.9.refs_1_, ...), custom_call_target="tpu_custom_call", output_to_operand_aliasing={{0}: (2, {}), {1}: (3, {})} | custom-call | flops 1024 | bytes 1024 | tf_op jit(solution)/shard_map/pallas_call | solution.py:558
  (3 shorter events, 0.1 us)
Async XLA Ops:
  0.6 5.0 %copy-start = (bf16[1,14,2,128,128]{4,3,2,1,0:T(8,128)(2,1)S(1)}, bf16[1,14,2,128,128]{4,3,2,1,0:T(8,128)(2,1)}, u32[]{:S(2)}) copy-start(bf16[1,14,2,128,128]{4,3,2,1,0:T(8,128)(2,1)} %param.7) | copy-start | bytes 2752516
  0.6 1.3 %copy-start.1 = (bf16[1,2,128,2048]{3,2,1,0:T(8,128)(2,1)S(1)}, bf16[1,2,128,2048]{3,2,1,0:T(8,128)(2,1)}, u32[]{:S(2)}) copy-start(bf16[1,2,128,2048]{3,2,1,0:T(8,128)(2,1)} %param.6) | copy-start | bytes 3145732
  1.9 3.6 %copy-start.7 = (s32[1,14,4]{1,2,0:T(4,128)S(1)}, s32[1,14,4]{1,2,0:T(4,128)}, u32[]{:S(2)}) copy-start(s32[1,14,4]{1,2,0:T(4,128)} %param.10) | copy-start | bytes 676
  1.9 3.7 %copy-start.2 = (bf16[1,2,128,2048]{3,2,1,0:T(8,128)(2,1)S(1)}, bf16[1,2,128,2048]{3,2,1,0:T(8,128)(2,1)}, u32[]{:S(2)}) copy-start(bf16[1,2,128,2048]{3,2,1,0:T(8,128)(2,1)} %param.6) | copy-start | bytes 3145732
  2.0 16.0 %collective-permute-start.2 = (bf16[1,128,2048]{2,1,0:T(8,128)(2,1)S(1)}, bf16[1,128,2048]{2,1,0:T(8,128)(2,1)S(1)}, u32[]{:S(2)}, u32[]{:S(2)}) collective-permute-start(bf16[1,128,2048]{2,1,0:T(8,128)(2,1)S(1)} %shard_map.87), channel_id=1, source_target_pairs={{0,1},{1,0},{2,3},{3,2},{4,5},{5,4},{6,7},{7,6},{8,9},{9,8},{10,11... | collective-permute-start | bytes 1572872 | tf_op jit(solution)/shard_map/ppermute | solution.py:435
  4.1 19.2 %collective-permute-start.1 = (bf16[1,96,2048]{2,1,0:T(8,128)(2,1)}, bf16[1,96,2048]{2,1,0:T(8,128)(2,1)S(1)}, u32[]{:S(2)}, u32[]{:S(2)}) collective-permute-start(bf16[1,96,2048]{2,1,0:T(8,128)(2,1)} %get-tuple-element.34), channel_id=1, source_target_pairs={{0,1},{1,0},{2,3},{3,2},{4,5},{5,4},{6,7},{7,6},{8,9},{9,8},{10,11... | collective-permute-start | bytes 1179656 | tf_op jit(solution)/shard_map/ppermute | solution.py:435
  4.3 24.1 %collective-permute-start = (bf16[1,32,2048]{2,1,0:T(8,128)(2,1)}, bf16[1,32,2048]{2,1,0:T(8,128)(2,1)S(1)}, u32[]{:S(2)}, u32[]{:S(2)}) collective-permute-start(bf16[1,32,2048]{2,1,0:T(8,128)(2,1)} %get-tuple-element.32), channel_id=1, source_target_pairs={{0,1},{1,0},{2,3},{3,2},{4,5},{5,4},{6,7},{7,6},{8,9},{9,8},{10,11... | collective-permute-start | bytes 393224 | tf_op jit(solution)/shard_map/ppermute | solution.py:435
  5.7 1.2 %copy-start.3 = (bf16[1,14,2,128,128]{4,3,2,1,0:T(8,128)(2,1)S(1)}, bf16[1,14,2,128,128]{4,3,2,1,0:T(8,128)(2,1)}, u32[]{:S(2)}) copy-start(bf16[1,14,2,128,128]{4,3,2,1,0:T(8,128)(2,1)} %param.8) | copy-start | bytes 2752516
  6.9 0.8 copy-start.5
  27.2 2.5 %collective-permute-start.3 = (f32[8,128]{1,0:T(8,128)S(1)}, f32[8,128]{1,0:T(8,128)S(1)}, u32[]{:S(2)}, u32[]{:S(2)}) collective-permute-start(f32[8,128]{1,0:T(8,128)S(1)} %get-tuple-element.38.mine_ref), channel_id=1, source_target_pairs={{0,1},{1,0},{2,3},{3,2},{4,5},{5,4},{6,7},{7,6},{8,9},{9,8},{10,11... | collective-permute-start | bytes 12296 | tf_op jit(solution)/shard_map/ppermute | solution.py:435
  31.9 15.3 %collective-permute-start.6 = (bf16[1,128,2048]{2,1,0:T(8,128)(2,1)S(1)}, bf16[1,128,2048]{2,1,0:T(8,128)(2,1)S(1)}, u32[]{:S(2)}, u32[]{:S(2)}) collective-permute-start(bf16[1,128,2048]{2,1,0:T(8,128)(2,1)S(1)} %get-tuple-element.40.refs_0_), channel_id=1, source_target_pairs={{0,1},{1,0},{2,3},{3,2},{4,5},{5,4},{6,7},{7,6},{8,9},{9,8},{10,11... | collective-permute-start | bytes 1572872 | tf_op jit(solution)/shard_map/ppermute | solution.py:435
  33.2 3.7 %copy-start.6 = (s32[1,2]{1,0:T(1,128)S(1)}, s32[1,2]{1,0:T(1,128)}, u32[]{:S(2)}) copy-start(s32[1,2]{1,0:T(1,128)} %param.11) | copy-start | bytes 28
  35.4 16.5 %collective-permute-start.5 = (bf16[1,96,2048]{2,1,0:T(8,128)(2,1)S(1)}, bf16[1,96,2048]{2,1,0:T(8,128)(2,1)S(1)}, u32[]{:S(2)}, u32[]{:S(2)}) collective-permute-start(bf16[1,96,2048]{2,1,0:T(8,128)(2,1)S(1)} %get-tuple-element.42), channel_id=1, source_target_pairs={{0,1},{1,0},{2,3},{3,2},{4,5},{5,4},{6,7},{7,6},{8,9},{9,8},{10,11... | collective-permute-start | bytes 1179656 | tf_op jit(solution)/shard_map/ppermute | solution.py:435
  35.7 20.2 %collective-permute-start.4 = (bf16[1,32,2048]{2,1,0:T(8,128)(2,1)S(1)}, bf16[1,32,2048]{2,1,0:T(8,128)(2,1)S(1)}, u32[]{:S(2)}, u32[]{:S(2)}) collective-permute-start(bf16[1,32,2048]{2,1,0:T(8,128)(2,1)S(1)} %get-tuple-element.41), channel_id=1, source_target_pairs={{0,1},{1,0},{2,3},{3,2},{4,5},{5,4},{6,7},{7,6},{8,9},{9,8},{10,11... | collective-permute-start | bytes 393224 | tf_op jit(solution)/shard_map/ppermute | solution.py:435
  59.9 2.6 %collective-permute-start.7 = (f32[16,128]{1,0:T(8,128)S(1)}, f32[16,128]{1,0:T(8,128)S(1)}, u32[]{:S(2)}, u32[]{:S(2)}) collective-permute-start(f32[16,128]{1,0:T(8,128)S(1)} %get-tuple-element.48.my_sums_ref), channel_id=1, source_target_pairs={{0,1},{1,0},{2,3},{3,2},{4,5},{5,4},{6,7},{7,6},{8,9},{9,8},{10,11... | collective-permute-start | bytes 24584 | tf_op jit(solution)/shard_map/ppermute | solution.py:435
  62.5 16.2 %copy-start.4 = (bf16[1,14,2,128,128]{4,3,2,1,0:T(8,128)(2,1)S(1)}, bf16[1,14,2,128,128]{4,3,2,1,0:T(8,128)(2,1)}, u32[]{:S(2)}) copy-start(bf16[1,14,2,128,128]{4,3,2,1,0:T(8,128)(2,1)} %param.8) | copy-start | bytes 2752516
  67.8 28.2 %collective-permute-start.11 = (bf16[8,2,128,128]{3,2,1,0:T(8,128)(2,1)S(1)}, bf16[8,2,128,128]{3,2,1,0:T(8,128)(2,1)S(1)}, u32[]{:S(2)}, u32[]{:S(2)}) collective-permute-start(bf16[8,2,128,128]{3,2,1,0:T(8,128)(2,1)S(1)} %get-tuple-element.52), channel_id=1, source_target_pairs={{0,2},{2,4},{4,6},{6,8},{8,10},{10,12},{12,14},{14,16},{16,18},{18... | collective-permute-start | bytes 1572872 | tf_op jit(solution)/shard_map/ppermute | solution.py:528
  82.4 14.8 %collective-permute-start.10 = (bf16[8,2,128,128]{3,2,1,0:T(8,128)(2,1)S(1)}, bf16[8,2,128,128]{3,2,1,0:T(8,128)(2,1)S(1)}, u32[]{:S(2)}, u32[]{:S(2)}) collective-permute-start(bf16[8,2,128,128]{3,2,1,0:T(8,128)(2,1)S(1)} %shard_map.99), channel_id=1, source_target_pairs={{2,0},{4,2},{6,4},{8,6},{10,8},{12,10},{14,12},{16,14},{18,16},{20... | collective-permute-start | bytes 1572872 | tf_op jit(solution)/shard_map/ppermute | solution.py:528
  86.9 11.4 %collective-permute-start.8 = (bf16[6,2,128,128]{3,2,1,0:T(8,128)(2,1)S(1)}, bf16[6,2,128,128]{3,2,1,0:T(8,128)(2,1)S(1)}, u32[]{:S(2)}, u32[]{:S(2)}) collective-permute-start(bf16[6,2,128,128]{3,2,1,0:T(8,128)(2,1)S(1)} %shard_map.97), channel_id=1, source_target_pairs={{0,2},{2,4},{4,6},{6,8},{8,10},{10,12},{12,14},{14,16},{16,18},{18... | collective-permute-start | bytes 1179656 | tf_op jit(solution)/shard_map/ppermute | solution.py:528
  94.1 10.0 %collective-permute-start.9 = (bf16[6,2,128,128]{3,2,1,0:T(8,128)(2,1)S(1)}, bf16[6,2,128,128]{3,2,1,0:T(8,128)(2,1)S(1)}, u32[]{:S(2)}, u32[]{:S(2)}) collective-permute-start(bf16[6,2,128,128]{3,2,1,0:T(8,128)(2,1)S(1)} %shard_map.98), channel_id=1, source_target_pairs={{2,0},{4,2},{6,4},{8,6},{10,8},{12,10},{14,12},{16,14},{18,16},{20... | collective-permute-start | bytes 1179656 | tf_op jit(solution)/shard_map/ppermute | solution.py:528

commit v4 on v3

--- a/solution.py
+++ b/solution.py
@@ -26,12 +26,6 @@
     return lax.dot_general(
         left, right, (((1,), (0,)), ((), ())), preferred_element_type=F32
     )
-
-
-def pieces_of(blocks, rows):
-    last = rows - rows // 4
-    whole = [(b, 0, rows) for b in range(blocks - 1)]
-    return whole + [(blocks - 1, 0, last), (blocks - 1, last, rows)]
 
 
 def make_kron(ops_ref, kron_ref, spread_ref):
@@ -170,18 +164,16 @@
     return jnp.where(den > 0, num / jnp.where(den > 0, den, 1.0), 0.0)
 
 
-def cut(first, x_ref, *out_refs):
-    for (b, begin, end), out_ref in zip(pieces_of(*x_ref.shape[:2])[first:], out_refs):
-        out_ref[0] = x_ref[b, begin:end]
+def cut(x_ref, *out_refs):
+    for b, out_ref in enumerate(out_refs):
+        out_ref[0] = x_ref[b]
 
 
 def first_local(
-    rel_ref, ops_ref, x_ref, left_ref, right_ref,
-    kron_ref, right_t_ref, image_ref, sums_ref,
-    turned_ref, mixed_ref, *scratch,
-):
-    lists, spread_ref = scratch[:-1], scratch[-1]
-    make_kron(ops_ref, kron_ref, spread_ref)
+    rel_ref, kron_ref, x_ref, left_ref, right_ref,
+    right_t_ref, image_ref, sums_ref,
+    turned_ref, mixed_ref, *lists,
+):
     chan, dests = left_ref.shape[:2]
 
     def turn(n, carry):
@@ -220,7 +212,7 @@
 ):
     sums_ref[...] = local_sums_ref[...]
     more_remote(
-        left_ref.shape[1] - 1, rel_ref, kron_ref, other_ref, left_ref, right_t_ref, before_ref,
+        0, rel_ref, kron_ref, other_ref, left_ref, right_t_ref, before_ref,
         acc_ref, *scratch,
     )
 
@@ -258,8 +250,9 @@
 
     row_loop(1, rows, update, 0, first=dest)
     if last:
-        head_ref[0] = all_ref[dest, 0:begin]
-        tail_ref[0] = all_ref[dest, begin:rows]
+        cut_row = head_ref.shape[1]
+        head_ref[0] = all_ref[dest, 0:cut_row]
+        tail_ref[0] = all_ref[dest, cut_row:rows]
 
 
 def second_local(
@@ -459,54 +452,48 @@
             input_output_aliases=aliases,
         )(*args)
 
-    places = pieces_of(dests, rows)
-    kinds = tuple(shape((1, end - begin, width), BF16) for _, begin, end in places)
-    own = [
-        call(functools.partial(cut, 0), [VMEM], kinds[0], [], x),
-        *call(functools.partial(cut, 1), [VMEM], kinds[1:], [], x),
-    ]
+    block = shape((1, rows, width), BF16)
+    own = call(cut, [VMEM], (block,) * dests, [], x)
     other = [trade(value) for value in own]
-    kron, right_t, image, mine = call(
+    kron = call(
+        make_kron, [VMEM], shape((chan, phys * GROUP, phys * GROUP), BF16),
+        [pltpu.VMEM((chan * phys, phys * GROUP), F32)], ops,
+    )
+    right_t, image, mine = call(
         first_local, [SMEM] + [VMEM] * 4,
-        (
-            shape((chan, phys * GROUP, phys * GROUP), BF16), shape(right.shape, BF16), wave_f32,
-            sums_kind,
-        ),
-        pair_scratch + [pltpu.VMEM((chan * phys, phys * GROUP), F32)],
-        rel, ops, x, left, right,
-    )
-    image = call(
-        functools.partial(more_remote, 0), [SMEM] + [VMEM] * 5, wave_f32, pair_scratch,
-        rel, kron, other[0], left, right_t, image, aliases={5: 0},
+        (shape(right.shape, BF16), wave_f32, sums_kind), pair_scratch,
+        rel, kron, x, left, right,
     )
     image, mine = call(
         first_remote, [SMEM] + [VMEM] * 6, (wave_f32, sums_kind), pair_scratch,
-        rel, kron, other[1], left, right_t, image, mine, aliases={5: 0},
+        rel, kron, other[0], left, right_t, image, mine, aliases={5: 0},
     )
     theirs = trade(mine)
     image, first_guess = call(
         functools.partial(first_finish, 0), [SMEM] + [VMEM] * 8,
-        (wave_f32, kinds[0]), pair_scratch,
-        rel, kron, other[2], left, right_t, image, x, mine, theirs, aliases={5: 0},
-    )
+        (wave_f32, block), pair_scratch,
+        rel, kron, other[1], left, right_t, image, x, mine, theirs, aliases={5: 0},
+    )
+    tail_rows = rows // 4
     image, head, tail, guess = call(
         functools.partial(first_finish, 1), [SMEM] + [VMEM] * 9,
-        (wave_f32, kinds[1], kinds[2], wave_b16), pair_scratch,
-        rel, kron, other[2], left, right_t, image, x, mine, theirs, first_guess, aliases={5: 0},
+        (
+            wave_f32, shape((1, rows - tail_rows, width), BF16), shape((1, tail_rows, width), BF16),
+            wave_b16,
+        ),
+        pair_scratch,
+        rel, kron, other[1], left, right_t, image, x, mine, theirs, first_guess, aliases={5: 0},
     )
     other = [trade(first_guess), trade(head), trade(tail)]
     acc, early_sums = call(
         second_local, [SMEM] * 2 + [VMEM] * 6, (wave_f32, sums_kind), pair_scratch,
         rel, ranks[0], kron, guess, left, right_t, x, image,
     )
-    acc = call(
-        functools.partial(more_remote, 0), [SMEM] + [VMEM] * 5, wave_f32, pair_scratch,
-        rel, kron, other[0], left, right_t, acc, aliases={5: 0},
-    )
-    acc = call(
-        functools.partial(more_remote, 1), [SMEM] + [VMEM] * 5, wave_f32, pair_scratch,
-        rel, kron, other[1], left, right_t, acc, aliases={5: 0},
-    )
+    for n in range(2):
+        acc = call(
+            functools.partial(more_remote, n), [SMEM] + [VMEM] * 5, wave_f32, pair_scratch,
+            rel, kron, other[n], left, right_t, acc, aliases={5: 0},
+        )
     kept, my_sums = call(
         second_finish, [SMEM] * 2 + [VMEM] * 10, (wave_f32, shape((16, LANES), F32)), pair_scratch,
         rel, ranks[0], kron, other[2], left, right_t, acc, x, guess, mine, theirs, early_sums,

time: 106 us -> 102 us (0.962)
  the two profiles are of different devices: /device:TPU:21 before, /device:TPU:1 now
where the time goes in v4:
time: 102 us; the launch traced here: 100 us
  Pallas kernels  59.6 us (58%)
  starting transfers between devices  22.6 us (22%)
  waiting for transfers between devices  11.8 us (12%)
  local copies, waits for them, and re-layouts  4.63 us (5%)
  between operations  1.05 us (1%)
    pallas_call x13, Pallas kernels, call(): pl.pallas_call(body, in_specs=specs, out_specs=jax.tree.map(lambda _: VME...  50.8 us
    ppermute x4, starting transfers between devices, sent(): lax.ppermute(value, 'seg', [(s, s + steps) for s in range(begin, end)])  16.1 us
    ppermute x7, waiting for transfers between devices, trade(): return lax.ppermute(value, 'blk', swap)  6.86 us
    ppermute x7, starting transfers between devices, trade(): return lax.ppermute(value, 'blk', swap)  6.45 us
    pallas_call x1, Pallas kernels, shards(): pl.pallas_call(functools.partial(normalize_and_left, 0, early, env_scale,...  5.29 us
    ppermute x4, waiting for transfers between devices, sent(): lax.ppermute(value, 'seg', [(s, s + steps) for s in range(begin, end)])  4.92 us
    unnamed x16, local copies, waits for them, and re-layouts  4.54 us
    pallas_call x3, Pallas kernels, widened(): pl.pallas_call(functools.partial(widen, places), in_specs=[VMEM] * count...  3.49 us
  transfers between devices with their start and end apart: 11, of which 5 were waited for; matrix products, arithmetic and copies ran while one was open for 1% of the time, Pallas kernels for 46%

profile of v4, /device:TPU:1, one launch (start us, length us, event | category | flops | bytes accessed | tf_op | source)
XLA Modules:
  0.0 100.4 jit_solution(5884763581284916775)
XLA Ops:
  0.6 0.0 copy-start
  0.6 0.0 copy-start.1
  0.7 1.3 %copy-done.1 = bf16[1,2,128,2048]{3,2,1,0:T(8,128)(2,1)S(1)} copy-done((bf16[1,2,128,2048]{3,2,1,0:T(8,128)(2,1)S(1)}, bf16[1,2,128,2048]{3,2,1,0:T(8,128)(2,1)}, u32[]{:S(2)}) %copy-start.1) | copy-done | bytes 1048600
  1.9 0.1 shard_map.86
  2.0 2.1 %collective-permute-start.1 = (bf16[1,128,2048]{2,1,0:T(8,128)(2,1)S(1)}, bf16[1,128,2048]{2,1,0:T(8,128)(2,1)S(1)}, u32[]{:S(2)}, u32[]{:S(2)}) collective-permute-start(bf16[1,128,2048]{2,1,0:T(8,128)(2,1)S(1)} %get-tuple-element.32), channel_id=1, source_target_pairs={{0,1},{1,0},{2,3},{3,2},{4,5},{5,4},{6,7},{7,6},{8,9},{9,8},{10,11... | collective-permute-start | bytes 1572872 | tf_op jit(solution)/shard_map/ppermute | solution.py:428
  4.1 0.1 collective-permute-start
  4.2 0.0 copy-start.6
  4.2 0.8 copy-done.6
  5.0 0.3 shard_map.85.kron_ref
  5.3 0.7 add_bitcast_fusion
  6.0 0.1 copy.19
  6.1 0.0 copy-done
  6.1 0.0 copy-start.2
  6.1 1.2 %copy-done.2 = bf16[1,2,128,2048]{3,2,1,0:T(8,128)(2,1)S(1)} copy-done((bf16[1,2,128,2048]{3,2,1,0:T(8,128)(2,1)S(1)}, bf16[1,2,128,2048]{3,2,1,0:T(8,128)(2,1)}, u32[]{:S(2)}) %copy-start.2) | copy-done | bytes 1048600
  7.3 0.0 copy-start.4
  7.3 1.2 %copy-done.4 = bf16[1,14,2,128,128]{4,3,2,1,0:T(8,128)(2,1)S(1)} copy-done((bf16[1,14,2,128,128]{4,3,2,1,0:T(8,128)(2,1)S(1)}, bf16[1,14,2,128,128]{4,3,2,1,0:T(8,128)(2,1)}, u32[]{:S(2)}) %copy-start.4) | copy-done | bytes 917528
  8.5 10.8 %shard_map.87 = (bf16[14,2,128,128]{3,2,1,0:T(8,128)(2,1)S(1)}, f32[2,128,2048]{2,1,0:T(8,128)S(1)}, f32[8,128]{1,0:T(8,128)S(1)}) custom-call(s32[14,2]{1,0:T(8,128)S(1)} %negate_select_fusion.rel_ref, bf16[14,128,128]{2,1,0:T(8,128)(2,1)S(1)} %shard_map.85.kron_ref, bf16[2,128,2048]{2,1,0:T(8,128)(2,1)S(1)} %bitcast.21, ...), custom_call_target="tpu_custom_call" | custom-call | flops 1024 | bytes 1024 | tf_op jit(solution)/shard_map/pallas_call | solution.py:444
  19.4 0.0 collective-permute-done.1.other_ref
  19.4 0.0 copy-start.3
  19.4 2.8 %shard_map.88 = (f32[2,128,2048]{2,1,0:T(8,128)S(1)}, f32[8,128]{1,0:T(8,128)S(1)}) custom-call(s32[14,2]{1,0:T(8,128)S(1)} %negate_select_fusion.rel_ref, bf16[14,128,128]{2,1,0:T(8,128)(2,1)S(1)} %shard_map.85.kron_ref, bf16[1,128,2048]{2,1,0:T(8,128)(2,1)S(1)} %collective-permute-done.1.other_ref, ...), custom_call_target="tpu_custom_call", output_to_operand_aliasing={{0}: (5, {})} | custom-call | flops 1024 | bytes 1024 | tf_op jit(solution)/shard_map/pallas_call | solution.py:444
  22.2 2.3 %collective-permute-start.2 = (f32[8,128]{1,0:T(8,128)S(1)}, f32[8,128]{1,0:T(8,128)S(1)}, u32[]{:S(2)}, u32[]{:S(2)}) collective-permute-start(f32[8,128]{1,0:T(8,128)S(1)} %get-tuple-element.36.mine_ref), channel_id=1, source_target_pairs={{0,1},{1,0},{2,3},{3,2},{4,5},{5,4},{6,7},{7,6},{8,9},{9,8},{10,11... | collective-permute-start | bytes 12296 | tf_op jit(solution)/shard_map/ppermute | solution.py:428
  24.4 2.6 %collective-permute-done.other_ref = bf16[1,128,2048]{2,1,0:T(8,128)(2,1)S(1)} collective-permute-done((bf16[1,128,2048]{2,1,0:T(8,128)(2,1)S(1)}, bf16[1,128,2048]{2,1,0:T(8,128)(2,1)S(1)}, u32[]{:S(2)}, u32[]{:S(2)}) %collective-permute-start) | collective-permute-done | bytes 524320 | tf_op jit(solution)/shard_map/ppermute | solution.py:428
  27.0 0.1 collective-permute-done.2.theirs_ref
  27.1 0.0 copy-done.3
  27.1 2.9 %shard_map.89 = (f32[2,128,2048]{2,1,0:T(8,128)S(1)}, bf16[1,128,2048]{2,1,0:T(8,128)(2,1)S(1)}) custom-call(s32[14,2]{1,0:T(8,128)S(1)} %negate_select_fusion.rel_ref, bf16[14,128,128]{2,1,0:T(8,128)(2,1)S(1)} %shard_map.85.kron_ref, bf16[1,128,2048]{2,1,0:T(8,128)(2,1)S(1)} %collective-permute-done.other_ref, ...), custom_call_target="tpu_custom_call", output_to_operand_aliasing={{0}: (5, {})} | custom-call | flops 1024 | bytes 1024 | tf_op jit(solution)/shard_map/pallas_call | solution.py:444
  30.0 0.4 collective-permute-start.5
  30.4 0.0 copy-start.7
  30.4 2.9 %shard_map.90 = (f32[2,128,2048]{2,1,0:T(8,128)S(1)}, bf16[1,96,2048]{2,1,0:T(8,128)(2,1)S(1)}, bf16[1,32,2048]{2,1,0:T(8,128)(2,1)S(1)}, bf16[2,128,2048]{2,1,0:T(8,128)(2,1)S(1)}) custom-call(s32[14,2]{1,0:T(8,128)S(1)} %negate_select_fusion.rel_ref, bf16[14,128,128]{2,1,0:T(8,128)(2,1)S(1)} %shard_map.85.kron_ref, ...), custom_call_target="tpu_custom_call", output_to_operand_aliasing={{0}: (5, {})} | custom-call | flops 1024 | bytes 1024 | tf_op jit(solution)/shard_map/pallas_call | solution.py:444
  33.3 1.2 %collective-permute-start.4 = (bf16[1,96,2048]{2,1,0:T(8,128)(2,1)S(1)}, bf16[1,96,2048]{2,1,0:T(8,128)(2,1)S(1)}, u32[]{:S(2)}, u32[]{:S(2)}) collective-permute-start(bf16[1,96,2048]{2,1,0:T(8,128)(2,1)S(1)} %get-tuple-element.40), channel_id=1, source_target_pairs={{0,1},{1,0},{2,3},{3,2},{4,5},{5,4},{6,7},{7,6},{8,9},{9,8},{10,11... | collective-permute-start | bytes 1179656 | tf_op jit(solution)/shard_map/ppermute | solution.py:428
  34.6 0.3 collective-permute-start.3
  34.9 0.0 copy-done.7
  34.9 11.1 %shard_map.91 = (f32[2,128,2048]{2,1,0:T(8,128)S(1)}, f32[8,128]{1,0:T(8,128)S(1)}) custom-call(s32[14,2]{1,0:T(8,128)S(1)} %negate_select_fusion.rel_ref, s32[2]{0:T(128)S(1)} %bitcast.31, bf16[14,128,128]{2,1,0:T(8,128)(2,1)S(1)} %shard_map.85.kron_ref, bf16[2,128,2048]{2,1,0:T(8,128)(2,1)S(1)} %get-tuple-element.41.guess_ref, ...), custom_call_target="tpu_custom_call" | custom-call | flops 1024 | bytes 1024 | tf_op jit(solution)/shard_map/pallas_call | solution.py:444
  46.0 0.0 collective-permute-done.5.other_ref
  46.0 3.0 %shard_map.92.before_ref = f32[2,128,2048]{2,1,0:T(8,128)S(1)} custom-call(s32[14,2]{1,0:T(8,128)S(1)} %negate_select_fusion.rel_ref, bf16[14,128,128]{2,1,0:T(8,128)(2,1)S(1)} %shard_map.85.kron_ref, bf16[1,128,2048]{2,1,0:T(8,128)(2,1)S(1)} %collective-permute-done.5.other_ref, ...), custom_call_target="tpu_custom_call", output_to_operand_aliasing={{}: (5, {})} | custom-call | flops 1024 | bytes 1024 | tf_op jit(solution)/shard_map/pallas_call | solution.py:444
  49.0 1.7 %collective-permute-done.4.other_ref = bf16[1,96,2048]{2,1,0:T(8,128)(2,1)S(1)} collective-permute-done((bf16[1,96,2048]{2,1,0:T(8,128)(2,1)S(1)}, bf16[1,96,2048]{2,1,0:T(8,128)(2,1)S(1)}, u32[]{:S(2)}, u32[]{:S(2)}) %collective-permute-start.4) | collective-permute-done | bytes 393248 | tf_op jit(solution)/shard_map/ppermute | solution.py:428
  50.7 3.9 %shard_map.93.before_ref = f32[2,128,2048]{2,1,0:T(8,128)S(1)} custom-call(s32[14,2]{1,0:T(8,128)S(1)} %negate_select_fusion.rel_ref, bf16[14,128,128]{2,1,0:T(8,128)(2,1)S(1)} %shard_map.85.kron_ref, bf16[1,96,2048]{2,1,0:T(8,128)(2,1)S(1)} %collective-permute-done.4.other_ref, ...), custom_call_target="tpu_custom_call", output_to_operand_aliasing={{}: (5, {})} | custom-call | flops 1024 | bytes 1024 | tf_op jit(solution)/shard_map/pallas_call | solution.py:444
  54.6 0.0 collective-permute-done.3.other_ref
  54.6 4.0 %shard_map.94 = (f32[2,128,2048]{2,1,0:T(8,128)S(1)}, f32[16,128]{1,0:T(8,128)S(1)}) custom-call(s32[14,2]{1,0:T(8,128)S(1)} %negate_select_fusion.rel_ref, s32[2]{0:T(128)S(1)} %bitcast.32, bf16[14,128,128]{2,1,0:T(8,128)(2,1)S(1)} %shard_map.85.kron_ref, ...), custom_call_target="tpu_custom_call", output_to_operand_aliasing={{0}: (6, {})} | custom-call | flops 1024 | bytes 1024 | tf_op jit(solution)/shard_map/pallas_call | solution.py:444
  58.7 0.1 collective-permute-start.6
  58.8 2.5 %collective-permute-done.6.their_sums_ref = f32[16,128]{1,0:T(8,128)S(1)} collective-permute-done((f32[16,128]{1,0:T(8,128)S(1)}, f32[16,128]{1,0:T(8,128)S(1)}, u32[]{:S(2)}, u32[]{:S(2)}) %collective-permute-start.6) | collective-permute-done | bytes 8224 | tf_op jit(solution)/shard_map/ppermute | solution.py:428
  61.3 0.0 copy-start.5
  61.3 5.3 %shard_map.95 = (bf16[2,128,2048]{2,1,0:T(8,128)(2,1)}, bf16[2,128,2048]{2,1,0:T(8,128)(2,1)S(1)}, bf16[2,128,2048]{2,1,0:T(8,128)(2,1)S(1)}, bf16[8,2,128,128]{3,2,1,0:T(8,128)(2,1)S(1)}) custom-call(s32[2]{0:T(128)S(1)} %bitcast.33, f32[2,128,2048]{2,1,0:T(8,128)S(1)} %get-tuple-element.45.kept_ref, bf16[2,128,2048]{2,1,0:T(8,128)(2,1)S(1)} %get-tuple-element.41.guess_ref, ...), custom_call_target="tpu_custom_call" | custom-call | flops 1024 | bytes 1024 | tf_op jit(solution)/shard_map/pallas_call | solution.py:526
  66.6 8.7 %collective-permute-start.10 = (bf16[8,2,128,128]{3,2,1,0:T(8,128)(2,1)S(1)}, bf16[8,2,128,128]{3,2,1,0:T(8,128)(2,1)S(1)}, u32[]{:S(2)}, u32[]{:S(2)}) collective-permute-start(bf16[8,2,128,128]{3,2,1,0:T(8,128)(2,1)S(1)} %get-tuple-element.50), channel_id=1, source_target_pairs={{0,2},{2,4},{4,6},{6,8},{8,10},{10,12},{12,14},{14,16},{16,18},{18... | collective-permute-start | bytes 1572872 | tf_op jit(solution)/shard_map/ppermute | solution.py:515
  75.2 0.0 copy-done.5
  75.2 3.7 %shard_map.98 = bf16[8,2,128,128]{3,2,1,0:T(8,128)(2,1)S(1)} custom-call(bf16[14,2,128,128]{3,2,1,0:T(8,128)(2,1)S(1)} %bitcast.28, bf16[2,128,2048]{2,1,0:T(8,128)(2,1)S(1)} %get-tuple-element.49.outer_ref.inner_ref, bf16[2,128,2048]{2,1,0:T(8,128)(2,1)S(1)} %get-tuple-element.48.inner_ref.outer_ref), custom_call_target="tpu_custom_call" | custom-call | flops 1024 | bytes 1024 | tf_op jit(solution)/shard_map/pallas_call | solution.py:444
  78.9 1.9 %collective-permute-start.9 = (bf16[8,2,128,128]{3,2,1,0:T(8,128)(2,1)S(1)}, bf16[8,2,128,128]{3,2,1,0:T(8,128)(2,1)S(1)}, u32[]{:S(2)}, u32[]{:S(2)}) collective-permute-start(bf16[8,2,128,128]{3,2,1,0:T(8,128)(2,1)S(1)} %shard_map.98), channel_id=1, source_target_pairs={{2,0},{4,2},{6,4},{8,6},{10,8},{12,10},{14,12},{16,14},{18,16},{20... | collective-permute-start | bytes 1572872 | tf_op jit(solution)/shard_map/ppermute | solution.py:515
  80.9 2.6 %shard_map.96 = bf16[6,2,128,128]{3,2,1,0:T(8,128)(2,1)S(1)} custom-call(bf16[14,2,128,128]{3,2,1,0:T(8,128)(2,1)S(1)} %bitcast.19, bf16[2,128,2048]{2,1,0:T(8,128)(2,1)S(1)} %get-tuple-element.48.inner_ref.outer_ref, bf16[2,128,2048]{2,1,0:T(8,128)(2,1)S(1)} %get-tuple-element.49.outer_ref.inner_ref), custom_call_target="tpu_custom_call" | custom-call | flops 1024 | bytes 1024 | tf_op jit(solution)/shard_map/pallas_call | solution.py:444
  83.5 3.6 %collective-permute-start.7 = (bf16[6,2,128,128]{3,2,1,0:T(8,128)(2,1)S(1)}, bf16[6,2,128,128]{3,2,1,0:T(8,128)(2,1)S(1)}, u32[]{:S(2)}, u32[]{:S(2)}) collective-permute-start(bf16[6,2,128,128]{3,2,1,0:T(8,128)(2,1)S(1)} %shard_map.96), channel_id=1, source_target_pairs={{0,2},{2,4},{4,6},{6,8},{8,10},{10,12},{12,14},{14,16},{16,18},{18... | collective-permute-start | bytes 1179656 | tf_op jit(solution)/shard_map/ppermute | solution.py:515
  87.1 2.7 %shard_map.97 = bf16[6,2,128,128]{3,2,1,0:T(8,128)(2,1)S(1)} custom-call(bf16[14,2,128,128]{3,2,1,0:T(8,128)(2,1)S(1)} %bitcast.29, bf16[2,128,2048]{2,1,0:T(8,128)(2,1)S(1)} %get-tuple-element.49.outer_ref.inner_ref, bf16[2,128,2048]{2,1,0:T(8,128)(2,1)S(1)} %get-tuple-element.48.inner_ref.outer_ref), custom_call_target="tpu_custom_call" | custom-call | flops 1024 | bytes 1024 | tf_op jit(solution)/shard_map/pallas_call | solution.py:444
  89.8 1.9 %collective-permute-start.8 = (bf16[6,2,128,128]{3,2,1,0:T(8,128)(2,1)S(1)}, bf16[6,2,128,128]{3,2,1,0:T(8,128)(2,1)S(1)}, u32[]{:S(2)}, u32[]{:S(2)}) collective-permute-start(bf16[6,2,128,128]{3,2,1,0:T(8,128)(2,1)S(1)} %shard_map.97), channel_id=1, source_target_pairs={{2,0},{4,2},{6,4},{8,6},{10,8},{12,10},{14,12},{16,14},{18,16},{20... | collective-permute-start | bytes 1179656 | tf_op jit(solution)/shard_map/ppermute | solution.py:515
  91.7 0.0 collective-permute-done.10.refs_0_
  91.8 1.1 %shard_map.99 = (f32[14,2,128,128]{3,2,1,0:T(8,128)}, f32[14,2,128,128]{3,2,1,0:T(8,128)}) custom-call(bf16[8,2,128,128]{3,2,1,0:T(8,128)(2,1)S(1)} %collective-permute-done.10.refs_0_), custom_call_target="tpu_custom_call" | custom-call | flops 1024 | bytes 1024 | tf_op jit(solution)/shard_map/pallas_call | solution.py:545
  92.9 0.0 collective-permute-done.9.refs_0_
  92.9 1.1 %shard_map.100 = (f32[14,2,128,128]{3,2,1,0:T(8,128)}, f32[14,2,128,128]{3,2,1,0:T(8,128)}) custom-call(bf16[8,2,128,128]{3,2,1,0:T(8,128)(2,1)S(1)} %collective-permute-done.9.refs_0_, f32[14,2,128,128]{3,2,1,0:T(8,128)} %get-tuple-element.51.refs_1_, f32[14,2,128,128]{3,2,1,0:T(8,128)} %get-tuple-element.52.refs_2_), custom_call_target="tpu_custom_call", output_to_operand_aliasing={{0}: (1, {}), {1}: (2, {})} | custom-call | flops 1024 | bytes 1024 | tf_op jit(solution)/shard_map/pallas_call | solution.py:545
  94.0 0.0 collective-permute-done.7.refs_0_
  94.0 4.9 %collective-permute-done.8.refs_1_ = bf16[6,2,128,128]{3,2,1,0:T(8,128)(2,1)S(1)} collective-permute-done((bf16[6,2,128,128]{3,2,1,0:T(8,128)(2,1)S(1)}, bf16[6,2,128,128]{3,2,1,0:T(8,128)(2,1)S(1)}, u32[]{:S(2)}, u32[]{:S(2)}) %collective-permute-start.8) | collective-permute-done | bytes 393248 | tf_op jit(solution)/shard_map/ppermute | solution.py:515
  98.9 1.3 %shard_map.101 = (f32[14,2,128,128]{3,2,1,0:T(8,128)}, f32[14,2,128,128]{3,2,1,0:T(8,128)}) custom-call(bf16[6,2,128,128]{3,2,1,0:T(8,128)(2,1)S(1)} %collective-permute-done.7.refs_0_, bf16[6,2,128,128]{3,2,1,0:T(8,128)(2,1)S(1)} %collective-permute-done.8.refs_1_, ...), custom_call_target="tpu_custom_call", output_to_operand_aliasing={{0}: (2, {}), {1}: (3, {})} | custom-call | flops 1024 | bytes 1024 | tf_op jit(solution)/shard_map/pallas_call | solution.py:545
  (1 shorter events, 0.0 us)
Async XLA Ops:
  0.6 5.5 %copy-start = (bf16[1,14,2,128,128]{4,3,2,1,0:T(8,128)(2,1)S(1)}, bf16[1,14,2,128,128]{4,3,2,1,0:T(8,128)(2,1)}, u32[]{:S(2)}) copy-start(bf16[1,14,2,128,128]{4,3,2,1,0:T(8,128)(2,1)} %param.7) | copy-start | bytes 2752516
  0.6 1.3 %copy-start.1 = (bf16[1,2,128,2048]{3,2,1,0:T(8,128)(2,1)S(1)}, bf16[1,2,128,2048]{3,2,1,0:T(8,128)(2,1)}, u32[]{:S(2)}) copy-start(bf16[1,2,128,2048]{3,2,1,0:T(8,128)(2,1)} %param.6) | copy-start | bytes 3145732
  2.0 17.3 %collective-permute-start.1 = (bf16[1,128,2048]{2,1,0:T(8,128)(2,1)S(1)}, bf16[1,128,2048]{2,1,0:T(8,128)(2,1)S(1)}, u32[]{:S(2)}, u32[]{:S(2)}) collective-permute-start(bf16[1,128,2048]{2,1,0:T(8,128)(2,1)S(1)} %get-tuple-element.32), channel_id=1, source_target_pairs={{0,1},{1,0},{2,3},{3,2},{4,5},{5,4},{6,7},{7,6},{8,9},{9,8},{10,11... | collective-permute-start | bytes 1572872 | tf_op jit(solution)/shard_map/ppermute | solution.py:428
  4.1 22.9 %collective-permute-start = (bf16[1,128,2048]{2,1,0:T(8,128)(2,1)S(1)}, bf16[1,128,2048]{2,1,0:T(8,128)(2,1)S(1)}, u32[]{:S(2)}, u32[]{:S(2)}) collective-permute-start(bf16[1,128,2048]{2,1,0:T(8,128)(2,1)S(1)} %get-tuple-element.30), channel_id=1, source_target_pairs={{0,1},{1,0},{2,3},{3,2},{4,5},{5,4},{6,7},{7,6},{8,9},{9,8},{10,11... | collective-permute-start | bytes 1572872 | tf_op jit(solution)/shard_map/ppermute | solution.py:428
  4.2 0.8 copy-start.6
  6.1 1.2 %copy-start.2 = (bf16[1,2,128,2048]{3,2,1,0:T(8,128)(2,1)S(1)}, bf16[1,2,128,2048]{3,2,1,0:T(8,128)(2,1)}, u32[]{:S(2)}) copy-start(bf16[1,2,128,2048]{3,2,1,0:T(8,128)(2,1)} %param.6) | copy-start | bytes 3145732
  7.3 1.2 %copy-start.4 = (bf16[1,14,2,128,128]{4,3,2,1,0:T(8,128)(2,1)S(1)}, bf16[1,14,2,128,128]{4,3,2,1,0:T(8,128)(2,1)}, u32[]{:S(2)}) copy-start(bf16[1,14,2,128,128]{4,3,2,1,0:T(8,128)(2,1)} %param.8) | copy-start | bytes 2752516
  19.4 7.7 %copy-start.3 = (bf16[1,2,128,2048]{3,2,1,0:T(8,128)(2,1)S(1)}, bf16[1,2,128,2048]{3,2,1,0:T(8,128)(2,1)}, u32[]{:S(2)}) copy-start(bf16[1,2,128,2048]{3,2,1,0:T(8,128)(2,1)} %param.6) | copy-start | bytes 3145732
  22.2 4.9 %collective-permute-start.2 = (f32[8,128]{1,0:T(8,128)S(1)}, f32[8,128]{1,0:T(8,128)S(1)}, u32[]{:S(2)}, u32[]{:S(2)}) collective-permute-start(f32[8,128]{1,0:T(8,128)S(1)} %get-tuple-element.36.mine_ref), channel_id=1, source_target_pairs={{0,1},{1,0},{2,3},{3,2},{4,5},{5,4},{6,7},{7,6},{8,9},{9,8},{10,11... | collective-permute-start | bytes 12296 | tf_op jit(solution)/shard_map/ppermute | solution.py:428
  30.0 16.0 %collective-permute-start.5 = (bf16[1,128,2048]{2,1,0:T(8,128)(2,1)S(1)}, bf16[1,128,2048]{2,1,0:T(8,128)(2,1)S(1)}, u32[]{:S(2)}, u32[]{:S(2)}) collective-permute-start(bf16[1,128,2048]{2,1,0:T(8,128)(2,1)S(1)} %get-tuple-element.38.refs_0_), channel_id=1, source_target_pairs={{0,1},{1,0},{2,3},{3,2},{4,5},{5,4},{6,7},{7,6},{8,9},{9,8},{10,11... | collective-permute-start | bytes 1572872 | tf_op jit(solution)/shard_map/ppermute | solution.py:428
  30.4 4.5 %copy-start.7 = (s32[1,2]{1,0:T(1,128)S(1)}, s32[1,2]{1,0:T(1,128)}, u32[]{:S(2)}) copy-start(s32[1,2]{1,0:T(1,128)} %param.11) | copy-start | bytes 28
  33.3 17.4 %collective-permute-start.4 = (bf16[1,96,2048]{2,1,0:T(8,128)(2,1)S(1)}, bf16[1,96,2048]{2,1,0:T(8,128)(2,1)S(1)}, u32[]{:S(2)}, u32[]{:S(2)}) collective-permute-start(bf16[1,96,2048]{2,1,0:T(8,128)(2,1)S(1)} %get-tuple-element.40), channel_id=1, source_target_pairs={{0,1},{1,0},{2,3},{3,2},{4,5},{5,4},{6,7},{7,6},{8,9},{9,8},{10,11... | collective-permute-start | bytes 1179656 | tf_op jit(solution)/shard_map/ppermute | solution.py:428
  34.6 20.1 %collective-permute-start.3 = (bf16[1,32,2048]{2,1,0:T(8,128)(2,1)S(1)}, bf16[1,32,2048]{2,1,0:T(8,128)(2,1)S(1)}, u32[]{:S(2)}, u32[]{:S(2)}) collective-permute-start(bf16[1,32,2048]{2,1,0:T(8,128)(2,1)S(1)} %get-tuple-element.39), channel_id=1, source_target_pairs={{0,1},{1,0},{2,3},{3,2},{4,5},{5,4},{6,7},{7,6},{8,9},{9,8},{10,11... | collective-permute-start | bytes 393224 | tf_op jit(solution)/shard_map/ppermute | solution.py:428
  58.7 2.6 %collective-permute-start.6 = (f32[16,128]{1,0:T(8,128)S(1)}, f32[16,128]{1,0:T(8,128)S(1)}, u32[]{:S(2)}, u32[]{:S(2)}) collective-permute-start(f32[16,128]{1,0:T(8,128)S(1)} %get-tuple-element.46.my_sums_ref), channel_id=1, source_target_pairs={{0,1},{1,0},{2,3},{3,2},{4,5},{5,4},{6,7},{7,6},{8,9},{9,8},{10,11... | collective-permute-start | bytes 24584 | tf_op jit(solution)/shard_map/ppermute | solution.py:428
  61.3 14.0 %copy-start.5 = (bf16[1,14,2,128,128]{4,3,2,1,0:T(8,128)(2,1)S(1)}, bf16[1,14,2,128,128]{4,3,2,1,0:T(8,128)(2,1)}, u32[]{:S(2)}) copy-start(bf16[1,14,2,128,128]{4,3,2,1,0:T(8,128)(2,1)} %param.8) | copy-start | bytes 2752516
  66.6 25.2 %collective-permute-start.10 = (bf16[8,2,128,128]{3,2,1,0:T(8,128)(2,1)S(1)}, bf16[8,2,128,128]{3,2,1,0:T(8,128)(2,1)S(1)}, u32[]{:S(2)}, u32[]{:S(2)}) collective-permute-start(bf16[8,2,128,128]{3,2,1,0:T(8,128)(2,1)S(1)} %get-tuple-element.50), channel_id=1, source_target_pairs={{0,2},{2,4},{4,6},{6,8},{8,10},{10,12},{12,14},{14,16},{16,18},{18... | collective-permute-start | bytes 1572872 | tf_op jit(solution)/shard_map/ppermute | solution.py:515
  78.9 13.9 %collective-permute-start.9 = (bf16[8,2,128,128]{3,2,1,0:T(8,128)(2,1)S(1)}, bf16[8,2,128,128]{3,2,1,0:T(8,128)(2,1)S(1)}, u32[]{:S(2)}, u32[]{:S(2)}) collective-permute-start(bf16[8,2,128,128]{3,2,1,0:T(8,128)(2,1)S(1)} %shard_map.98), channel_id=1, source_target_pairs={{2,0},{4,2},{6,4},{8,6},{10,8},{12,10},{14,12},{16,14},{18,16},{20... | collective-permute-start | bytes 1572872 | tf_op jit(solution)/shard_map/ppermute | solution.py:515
  83.5 10.5 %collective-permute-start.7 = (bf16[6,2,128,128]{3,2,1,0:T(8,128)(2,1)S(1)}, bf16[6,2,128,128]{3,2,1,0:T(8,128)(2,1)S(1)}, u32[]{:S(2)}, u32[]{:S(2)}) collective-permute-start(bf16[6,2,128,128]{3,2,1,0:T(8,128)(2,1)S(1)} %shard_map.96), channel_id=1, source_target_pairs={{0,2},{2,4},{4,6},{6,8},{8,10},{10,12},{12,14},{14,16},{16,18},{18... | collective-permute-start | bytes 1179656 | tf_op jit(solution)/shard_map/ppermute | solution.py:515
  89.8 9.1 %collective-permute-start.8 = (bf16[6,2,128,128]{3,2,1,0:T(8,128)(2,1)S(1)}, bf16[6,2,128,128]{3,2,1,0:T(8,128)(2,1)S(1)}, u32[]{:S(2)}, u32[]{:S(2)}) collective-permute-start(bf16[6,2,128,128]{3,2,1,0:T(8,128)(2,1)S(1)} %shard_map.97), channel_id=1, source_target_pairs={{2,0},{4,2},{6,4},{8,6},{10,8},{12,10},{14,12},{16,14},{18,16},{20... | collective-permute-start | bytes 1179656 | tf_op jit(solution)/shard_map/ppermute | solution.py:515

commit v5 on v1

--- a/solution.py
+++ b/solution.py
@@ -162,16 +162,40 @@
     return jnp.where(den > 0, num / jnp.where(den > 0, den, 1.0), 0.0)
 
 
-def cut(x_ref, *out_refs):
-    for b, out_ref in enumerate(out_refs):
-        out_ref[0] = x_ref[b]
+def choose_order(map_ref, rel_ref, arrived_ref, order_ref):
+    chan, dests = rel_ref.shape
+    for k in range(chan):
+        for b in range(dests):
+            rel_ref[k, b] = map_ref[k, b]
+
+    def uses(first, source):
+        total = jnp.int32(0)
+        for k in range(chan):
+            for b in range(first, first + dests):
+                total = total + jnp.where(map_ref[k, b] == source, 1, 0)
+        return total
+
+    swap_mine = uses(dests, 0) < uses(dests, 1)
+    swap_theirs = uses(0, dests) < uses(0, dests + 1)
+    order_ref[0] = jnp.where(swap_mine, 1, 0)
+    order_ref[1] = jnp.where(swap_mine, 0, 1)
+    for k in range(chan):
+        for b in range(dests):
+            source = rel_ref[k, b]
+            other = 2 * dests + 1 - source
+            arrived_ref[k, b] = jnp.where(swap_theirs & (source >= dests), other, source)
+
+
+def cut(b, x_ref, out_ref):
+    out_ref[0] = x_ref[b]
 
 
 def first_local(
-    rel_ref, kron_ref, x_ref, left_ref, right_ref,
-    right_t_ref, image_ref, sums_ref,
+    map_ref, kron_ref, x_ref, left_ref, right_ref,
+    right_t_ref, image_ref, sums_ref, rel_ref, arrived_ref, order_ref,
     turned_ref, mixed_ref, *lists,
 ):
+    choose_order(map_ref, rel_ref, arrived_ref, order_ref)
     chan, dests = left_ref.shape[:2]
 
     def turn(n, carry):
@@ -194,14 +218,14 @@
     put_sums(sums_ref, totals)
 
 
-def local_sources(
-    rel_ref, kron_ref, x_ref, left_ref, right_t_ref,
+def remote_sources(
+    rel_ref, kron_ref, other_ref, left_ref, right_t_ref, before_ref,
     acc_ref,
     turned_ref, mixed_ref, *lists,
 ):
-    acc_ref[...] = jnp.zeros_like(acc_ref)
-    steps = list_pairs(rel_ref, 0, left_ref.shape[1], *lists)
-    add_pairs(steps, lists, kron_ref, x_ref, left_ref, right_t_ref, acc_ref, turned_ref, mixed_ref)
+    dests = left_ref.shape[1]
+    steps = list_pairs(rel_ref, dests, dests + 1, *lists)
+    add_pairs(steps, lists, kron_ref, other_ref, left_ref, right_t_ref, acc_ref, turned_ref, mixed_ref)
 
 
 def first_remote(
@@ -216,14 +240,15 @@
 
 
 def first_finish(
-    dest, rel_ref, kron_ref, other_ref, left_ref, right_t_ref, before_ref, x_ref, mine_ref,
-    theirs_ref, *refs,
-):
-    dests = left_ref.shape[1]
-    last = dest == dests - 1
+    turn, rel_ref, order_ref, kron_ref, other_ref, left_ref, right_t_ref, before_ref, x_ref,
+    mine_ref, theirs_ref, *refs,
+):
+    dests, rows = x_ref.shape[:2]
+    dest = order_ref[turn]
+    last = turn == dests - 1
     if last:
         earlier_ref, acc_ref, guess_ref, all_ref = refs[:4]
-        all_ref[0:dest] = earlier_ref[...]
+        all_ref[order_ref[0]] = earlier_ref[0]
     else:
         acc_ref, guess_ref = refs[:2]
     turned_ref, mixed_ref = refs[-6:-4]
@@ -241,18 +266,18 @@
             all_ref[b, r, :] = guess
         return carry
 
-    row_loop(1, x_ref.shape[1], update, 0, first=dest)
-
-
-def second_remote(
-    rel_ref, rank_ref, kron_ref, other_ref, left_ref, right_t_ref, before_ref, x_ref, image_ref,
-    guess_ref,
+    row_loop(1, rows, update, 0, first=dest)
+
+
+def second_local(
+    rel_ref, rank_ref, kron_ref, guess_ref, left_ref, right_t_ref, x_ref, image_ref,
     acc_ref, sums_ref,
     turned_ref, mixed_ref, *lists,
 ):
     dests, rows, _ = x_ref.shape
-    steps = list_pairs(rel_ref, dests, dests + 1, *lists)
-    add_pairs(steps, lists, kron_ref, other_ref, left_ref, right_t_ref, acc_ref, turned_ref, mixed_ref)
+    acc_ref[...] = jnp.zeros_like(acc_ref)
+    steps = list_pairs(rel_ref, 0, dests, *lists)
+    add_pairs(steps, lists, kron_ref, guess_ref, left_ref, right_t_ref, acc_ref, turned_ref, mixed_ref)
 
     def sums(b, r, start, carry):
         x = x_ref[b, r, :].astype(F32)
@@ -296,7 +321,7 @@
 
 def normalize(
     cells, rank_ref, kept_ref, guess_ref, x_ref, mine_ref, theirs_ref, my_sums_ref, their_sums_ref,
-    state_ref, turned_ref,
+    state_ref,
 ):
     both = my_sums_ref[...] + their_sums_ref[...]
     xv, xx, gv, xg, gg, gg_kept, xx_kept, xg_kept, kg, kx, kg_kept, kx_kept, kk_kept = (
@@ -331,54 +356,86 @@
                 + of_guess * guess_ref[b, :, cols].astype(F32)
                 + of_state * x_ref[b, :, cols].astype(F32)
             )
-            state = (kept * factor).astype(BF16)
-            state_ref[b, :, cols] = state
-            turned_ref[b, :, cols] = state.T
+            state_ref[b, :, cols] = (kept * factor).astype(BF16)
         return carry
 
     lax.fori_loop(0, blocks * per, one, 0)
 
 
+def env_middle(k, b, env_ref, inner_ref, mid_ref, place):
+    rows, width = inner_ref.shape[1:]
+    env = jnp.concatenate([env_ref[k, b], env_ref[k + 1, b]], axis=0)
+    mid = dot(env, inner_ref[b]).astype(BF16)
+    for p in range(width // LANES):
+        for i in range(2):
+            mid_ref[place, p * rows : (p + 1) * rows, i * LANES : (i + 1) * LANES] = mid[
+                i * rows : (i + 1) * rows, p * LANES : (p + 1) * LANES
+            ]
+
+
+def env_result(k, b, scale, outer_ref, mid_ref, place, out_ref):
+    out = (dot(outer_ref[b], mid_ref[place]) * scale).astype(BF16)
+    out_ref[k, b] = out[:, :LANES]
+    out_ref[k + 1, b] = out[:, LANES:]
+
+
 def environments(first, count, scale, env_ref, inner_ref, outer_ref, out_ref, mid_ref):
-    dests, rows, width = outer_ref.shape
-    phys = width // LANES
+    dests = outer_ref.shape[0]
     pairs = mid_ref.shape[0] // dests
 
     def step(n, carry):
         for j in range(pairs):
-            k = first + 2 * (n * pairs + j)
             for b in range(dests):
-                env = jnp.concatenate([env_ref[k, b], env_ref[k + 1, b]], axis=0)
-                mid = dot(env, inner_ref[b]).astype(BF16)
-                for p in range(phys):
-                    for i in range(2):
-                        mid_ref[
-                            j * dests + b, p * rows : (p + 1) * rows, i * LANES : (i + 1) * LANES
-                        ] = mid[i * rows : (i + 1) * rows, p * LANES : (p + 1) * LANES]
+                env_middle(first + 2 * (n * pairs + j), b, env_ref, inner_ref, mid_ref, j * dests + b)
         for j in range(pairs):
-            place = 2 * (n * pairs + j)
             for b in range(dests):
-                out = (dot(outer_ref[b], mid_ref[j * dests + b]) * scale).astype(BF16)
-                out_ref[place, b] = out[:, :LANES]
-                out_ref[place + 1, b] = out[:, LANES:]
+                env_result(2 * (n * pairs + j), b, scale, outer_ref, mid_ref, j * dests + b, out_ref)
         return carry
 
     lax.fori_loop(0, count // (2 * pairs), step, 0)
 
 
+def left_beside_turn(count, scale, env_ref, state_ref, turned_ref, out_ref, mid_ref):
+    dests, _, width = state_ref.shape
+    phys = width // LANES
+    rounds = count // 4
+    tiles = dests * phys // rounds
+
+    def before(n, carry):
+        for t in range(tiles):
+            tile = n * tiles + t
+            cols = pl.ds(pl.multiple_of(lax.rem(tile, phys) * LANES, LANES), LANES)
+            turned_ref[tile // phys, :, cols] = state_ref[tile // phys, :, cols].T
+        for j in range(2):
+            for b in range(dests):
+                place = (2 * n + j) * dests + b
+                env_middle(2 * (2 * n + j), b, env_ref, state_ref, mid_ref, place)
+        return carry
+
+    def after(n, carry):
+        for j in range(2):
+            for b in range(dests):
+                place = (2 * n + j) * dests + b
+                env_result(2 * (2 * n + j), b, scale, turned_ref, mid_ref, place, out_ref)
+        return carry
+
+    lax.fori_loop(0, rounds, before, 0)
+    lax.fori_loop(0, rounds, after, 0)
+
+
 def normalize_and_left(
-    first, count, scale, cells,
+    count, scale, cells,
     rank_ref, kept_ref, guess_ref, x_ref, mine_ref, theirs_ref, my_sums_ref, their_sums_ref, env_ref,
     new_ref, state_ref, turned_ref, out_ref,
     mid_ref, sem,
 ):
     normalize(
         cells, rank_ref, kept_ref, guess_ref, x_ref, mine_ref, theirs_ref, my_sums_ref,
-        their_sums_ref, state_ref, turned_ref,
+        their_sums_ref, state_ref,
     )
     copy = pltpu.make_async_copy(state_ref, new_ref, sem)
     copy.start()
-    environments(first, count, scale, env_ref, state_ref, turned_ref, out_ref, mid_ref)
+    left_beside_turn(count, scale, env_ref, state_ref, turned_ref, out_ref, mid_ref)
     copy.wait()
 
 
@@ -405,8 +462,10 @@
     total_blocks = groups * dests
     first_block = lax.axis_index("blk") * dests
     x, left, right, ops = state[0], left_env[0], right_env[0], site_ops[0]
-    local_map = lax.dynamic_slice_in_dim(sector_map[0], first_block, dests, 1)
-    rel = lax.rem(local_map - first_block + total_blocks, total_blocks)
+
+    twice = jnp.concatenate([sector_map[0]] * 2, axis=1)
+    turned_map = lax.dynamic_slice_in_dim(twice, first_block, total_blocks, 1)
+    turned_map = lax.rem(turned_map - first_block + total_blocks, total_blocks)
 
     swap = [(g, groups - 1 - g) for g in range(groups)]
 
@@ -426,11 +485,11 @@
         pltpu.VMEM((2 * rows, width), BF16),
     ] + lists
 
-    def call(body, specs, outs, scratch, *args, aliases={}):
+    def call(body, specs, outs, scratch, *args, aliases={}, out_specs=None):
         return pl.pallas_call(
             body,
             in_specs=specs,
-            out_specs=jax.tree.map(lambda _: VMEM, outs),
+            out_specs=out_specs or jax.tree.map(lambda _: VMEM, outs),
             out_shape=outs,
             scratch_shapes=scratch,
             compiler_params=PARAMS,
@@ -439,16 +498,20 @@
         )(*args)
 
     block = shape((1, rows, width), BF16)
-    own = call(cut, [VMEM], (block,) * dests, [], x)
+    own = [call(functools.partial(cut, b), [VMEM], block, [], x) for b in range(dests)]
     other = [trade(value) for value in own]
     kron = call(
         make_kron, [VMEM], shape((chan, phys * GROUP, phys * GROUP), BF16),
         [pltpu.VMEM((chan * phys, phys * GROUP), F32)], ops,
     )
-    right_t, image, mine = call(
+    rel_kind = shape((chan, dests), jnp.int32)
+    right_t, image, mine, rel, arrived, order = call(
         first_local, [SMEM] + [VMEM] * 4,
-        (shape(right.shape, BF16), wave_f32, sums_kind), pair_scratch,
-        rel, kron, x, left, right,
+        (
+            shape(right.shape, BF16), wave_f32, sums_kind, rel_kind, rel_kind,
+            shape((dests,), jnp.int32),
+        ),
+        pair_scratch, turned_map, kron, x, left, right, out_specs=(VMEM,) * 3 + (SMEM,) * 3,
     )
     image, mine = call(
         first_remote, [SMEM] + [VMEM] * 6, (wave_f32, sums_kind), pair_scratch,
@@ -456,27 +519,28 @@
     )
     theirs = trade(mine)
     image, first_guess = call(
-        functools.partial(first_finish, 0), [SMEM] + [VMEM] * 8,
+        functools.partial(first_finish, 0), [SMEM] * 2 + [VMEM] * 8,
         (wave_f32, block), pair_scratch,
-        rel, kron, other[1], left, right_t, image, x, mine, theirs, aliases={5: 0},
+        rel, order, kron, other[1], left, right_t, image, x, mine, theirs, aliases={6: 0},
     )
     image, last_guess, guess = call(
-        functools.partial(first_finish, 1), [SMEM] + [VMEM] * 9,
+        functools.partial(first_finish, 1), [SMEM] * 2 + [VMEM] * 9,
         (wave_f32, block, wave_b16), pair_scratch,
-        rel, kron, other[1], left, right_t, image, x, mine, theirs, first_guess, aliases={5: 0},
+        rel, order, kron, other[1], left, right_t, image, x, mine, theirs, first_guess,
+        aliases={6: 0},
     )
     other = [trade(first_guess), trade(last_guess)]
+    acc, early_sums = call(
+        second_local, [SMEM] * 2 + [VMEM] * 6, (wave_f32, sums_kind), pair_scratch,
+        arrived, ranks[0], kron, guess, left, right_t, x, image,
+    )
     acc = call(
-        local_sources, [SMEM] + [VMEM] * 4, wave_f32, pair_scratch,
-        rel, kron, guess, left, right_t,
-    )
-    acc, early_sums = call(
-        second_remote, [SMEM] * 2 + [VMEM] * 8, (wave_f32, sums_kind), pair_scratch,
-        rel, ranks[0], kron, other[0], left, right_t, acc, x, image, guess, aliases={6: 0},
+        remote_sources, [SMEM] + [VMEM] * 5, wave_f32, pair_scratch,
+        arrived, kron, other[0], left, right_t, acc, aliases={5: 0},
     )
     kept, my_sums = call(
         second_finish, [SMEM] * 2 + [VMEM] * 10, (wave_f32, shape((16, LANES), F32)), pair_scratch,
-        rel, ranks[0], kron, other[1], left, right_t, acc, x, guess, mine, theirs, early_sums,
+        arrived, ranks[0], kron, other[1], left, right_t, acc, x, guess, mine, theirs, early_sums,
         aliases={6: 0},
     )
     their_sums = trade(my_sums)
@@ -504,11 +568,11 @@
         )
 
     new_state, state_kept, turned, piece = pl.pallas_call(
-        functools.partial(normalize_and_left, 0, early, env_scale, cells),
+        functools.partial(normalize_and_left, early, env_scale, cells),
         in_specs=[SMEM] + [VMEM] * 8,
         out_specs=(HBM, VMEM, VMEM, VMEM),
         out_shape=(wave_b16, wave_b16, wave_b16, env_kind(early)),
-        scratch_shapes=mid(early) + [pltpu.SemaphoreType.DMA],
+        scratch_shapes=[pltpu.VMEM((early // 2 * dests, width, 2 * LANES), BF16)] + [pltpu.SemaphoreType.DMA],
         compiler_params=PARAMS,
         cost_estimate=COST,
     )(ranks[0], kept, guess, x, mine, theirs, my_sums, their_sums, left)

time: 101 us -> 101 us (level)
  the two profiles are of different devices: /device:TPU:1 before, /device:TPU:13 now
where the time goes in v5:
time: 101 us
  Pallas kernels  61.4 us (61%)
  starting transfers between devices  20.9 us (21%)
  waiting for transfers between devices  16 us (16%)
  local copies, waits for them, and re-layouts  1.42 us (1%)
  between operations  1.05 us (1%)
    pallas_call x13, Pallas kernels, call(): pl.pallas_call(body, in_specs=specs, out_specs=out_specs or jax.tree.map(...  52.2 us
    ppermute x4, starting transfers between devices, sent(): lax.ppermute(value, 'seg', [(s, s + steps) for s in range(begin, end)])  15.2 us
    ppermute x6, waiting for transfers between devices, trade(): return lax.ppermute(value, 'blk', swap)  10.2 us
    ppermute x4, waiting for transfers between devices, sent(): lax.ppermute(value, 'seg', [(s, s + steps) for s in range(begin, end)])  5.81 us
    ppermute x6, starting transfers between devices, trade(): return lax.ppermute(value, 'blk', swap)  5.71 us
    pallas_call x1, Pallas kernels, shards(): pl.pallas_call(functools.partial(normalize_and_left, early, env_scale, ce...  5.71 us
    pallas_call x3, Pallas kernels, widened(): pl.pallas_call(functools.partial(widen, places), in_specs=[VMEM] * count...  3.49 us
  transfers between devices with their start and end apart: 10, of which 6 were waited for; matrix products, arithmetic and copies ran while one was open for 0% of the time, Pallas kernels for 45%

profile of v5, /device:TPU:13, one launch (start us, length us, event | category | flops | bytes accessed | tf_op | source)
XLA Modules:
  0.0 100.9 jit_solution(3061338094895355713)
XLA Ops:
  0.6 0.0 copy-start
  0.6 0.0 copy-start.1
  0.7 1.3 %copy-done.1 = bf16[1,2,128,2048]{3,2,1,0:T(8,128)(2,1)S(1)} copy-done((bf16[1,2,128,2048]{3,2,1,0:T(8,128)(2,1)S(1)}, bf16[1,2,128,2048]{3,2,1,0:T(8,128)(2,1)}, u32[]{:S(2)}) %copy-start.1) | copy-done | bytes 1048600
  1.9 0.0 copy-start.4
  1.9 0.0 copy-start.6
  2.0 0.0 copy-start.2
  2.0 0.0 copy-start.3
  2.0 0.8 shard_map.88
  2.8 1.2 %collective-permute-start.1 = (bf16[1,128,2048]{2,1,0:T(8,128)(2,1)}, bf16[1,128,2048]{2,1,0:T(8,128)(2,1)}, u32[]{:S(2)}, u32[]{:S(2)}) collective-permute-start(bf16[1,128,2048]{2,1,0:T(8,128)(2,1)} %shard_map.88), channel_id=1, source_target_pairs={{0,1},{1,0},{2,3},{3,2},{4,5},{5,4},{6,7},{7,6},{8,9},{9,8},{10,11... | collective-permute-start | bytes 1572872 | tf_op jit(solution)/shard_map/ppermute | solution.py:473
  4.0 0.8 shard_map.87
  4.8 0.3 collective-permute-start
  5.1 0.0 copy-done.4
  5.1 0.3 shard_map.85.kron_ref
  5.4 0.0 copy-done.6
  5.4 0.1 copy.18
  5.5 0.1 negate_select_fusion.map_ref
  5.6 0.0 copy-done
  5.6 0.0 copy-done.2
  5.6 0.0 copy-done.3
  5.6 10.1 %shard_map.86 = (bf16[14,2,128,128]{3,2,1,0:T(8,128)(2,1)S(1)}, f32[2,128,2048]{2,1,0:T(8,128)S(1)}, f32[8,128]{1,0:T(8,128)S(1)}, s32[14,2]{1,0:T(8,128)S(1)}, s32[14,2]{1,0:T(8,128)S(1)}, /*index=5*/s32[2]{0:T(128)S(1)}) custom-call(s32[14,4]{1,0:T(8,128)S(1)} %negate_select_fusion.map_ref, bf16[14,128,128]{2,1,0:T(8,128)(2,1)S(1)} %shard_map.85.kron_ref, ...), custom_call_target="tpu_custom_call" | custom-call | flops 1024 | bytes 1024 | tf_op jit(solution)/shard_map/pallas_call | solution.py:489
  15.7 0.2 collective-permute-done.1.other_ref
  15.9 4.8 %shard_map.89 = (f32[2,128,2048]{2,1,0:T(8,128)S(1)}, f32[8,128]{1,0:T(8,128)S(1)}) custom-call(s32[14,2]{1,0:T(8,128)S(1)} %get-tuple-element.31.rel_ref, bf16[14,128,128]{2,1,0:T(8,128)(2,1)S(1)} %shard_map.85.kron_ref, bf16[1,128,2048]{2,1,0:T(8,128)(2,1)} %collective-permute-done.1.other_ref, ...), custom_call_target="tpu_custom_call", output_to_operand_aliasing={{0}: (5, {})} | custom-call | flops 1024 | bytes 1024 | tf_op jit(solution)/shard_map/pallas_call | solution.py:489
  20.7 1.1 %collective-permute-start.2 = (f32[8,128]{1,0:T(8,128)S(1)}, f32[8,128]{1,0:T(8,128)S(1)}, u32[]{:S(2)}, u32[]{:S(2)}) collective-permute-start(f32[8,128]{1,0:T(8,128)S(1)} %get-tuple-element.37.mine_ref), channel_id=1, source_target_pairs={{0,1},{1,0},{2,3},{3,2},{4,5},{5,4},{6,7},{7,6},{8,9},{9,8},{10,11... | collective-permute-start | bytes 12296 | tf_op jit(solution)/shard_map/ppermute | solution.py:473
  21.8 5.3 %collective-permute-done.other_ref = bf16[1,128,2048]{2,1,0:T(8,128)(2,1)} collective-permute-done((bf16[1,128,2048]{2,1,0:T(8,128)(2,1)}, bf16[1,128,2048]{2,1,0:T(8,128)(2,1)}, u32[]{:S(2)}, u32[]{:S(2)}) %collective-permute-start) | collective-permute-done | bytes 524320 | tf_op jit(solution)/shard_map/ppermute | solution.py:473
  27.1 0.1 collective-permute-done.2.theirs_ref
  27.2 2.4 %shard_map.90 = (f32[2,128,2048]{2,1,0:T(8,128)S(1)}, bf16[1,128,2048]{2,1,0:T(8,128)(2,1)S(1)}) custom-call(s32[14,2]{1,0:T(8,128)S(1)} %get-tuple-element.31.rel_ref, s32[2]{0:T(128)S(1)} %get-tuple-element.32.order_ref, bf16[14,128,128]{2,1,0:T(8,128)(2,1)S(1)} %shard_map.85.kron_ref, ...), custom_call_target="tpu_custom_call", output_to_operand_aliasing={{0}: (6, {})} | custom-call | flops 1024 | bytes 1024 | tf_op jit(solution)/shard_map/pallas_call | solution.py:489
  29.7 2.1 %collective-permute-start.4 = (bf16[1,128,2048]{2,1,0:T(8,128)(2,1)S(1)}, bf16[1,128,2048]{2,1,0:T(8,128)(2,1)S(1)}, u32[]{:S(2)}, u32[]{:S(2)}) collective-permute-start(bf16[1,128,2048]{2,1,0:T(8,128)(2,1)S(1)} %get-tuple-element.39.refs_0_), channel_id=1, source_target_pairs={{0,1},{1,0},{2,3},{3,2},{4,5},{5,4},{6,7},{7,6},{8,9},{9,8},{10,11... | collective-permute-start | bytes 1572872 | tf_op jit(solution)/shard_map/ppermute | solution.py:473
  31.8 0.0 copy-start.5
  31.8 4.1 %shard_map.91 = (f32[2,128,2048]{2,1,0:T(8,128)S(1)}, bf16[1,128,2048]{2,1,0:T(8,128)(2,1)S(1)}, bf16[2,128,2048]{2,1,0:T(8,128)(2,1)S(1)}) custom-call(s32[14,2]{1,0:T(8,128)S(1)} %get-tuple-element.31.rel_ref, s32[2]{0:T(128)S(1)} %get-tuple-element.32.order_ref, bf16[14,128,128]{2,1,0:T(8,128)(2,1)S(1)} %shard_map.85.kron_ref, ...), custom_call_target="tpu_custom_call", output_to_operand_aliasing={{0}: (6, {})} | custom-call | flops 1024 | bytes 1024 | tf_op jit(solution)/shard_map/pallas_call | solution.py:489
  36.0 0.1 collective-permute-start.3
  36.0 0.0 copy-done.5
  36.0 9.5 %shard_map.92 = (f32[2,128,2048]{2,1,0:T(8,128)S(1)}, f32[8,128]{1,0:T(8,128)S(1)}) custom-call(s32[14,2]{1,0:T(8,128)S(1)} %get-tuple-element.30.rel_ref, s32[2]{0:T(128)S(1)} %bitcast.30, bf16[14,128,128]{2,1,0:T(8,128)(2,1)S(1)} %shard_map.85.kron_ref, bf16[2,128,2048]{2,1,0:T(8,128)(2,1)S(1)} %get-tuple-element.41.guess_ref, ...), custom_call_target="tpu_custom_call" | custom-call | flops 1024 | bytes 1024 | tf_op jit(solution)/shard_map/pallas_call | solution.py:489
  45.5 0.0 collective-permute-done.4.other_ref
  45.5 4.7 %shard_map.93.before_ref = f32[2,128,2048]{2,1,0:T(8,128)S(1)} custom-call(s32[14,2]{1,0:T(8,128)S(1)} %get-tuple-element.30.rel_ref, bf16[14,128,128]{2,1,0:T(8,128)(2,1)S(1)} %shard_map.85.kron_ref, bf16[1,128,2048]{2,1,0:T(8,128)(2,1)S(1)} %collective-permute-done.4.other_ref, ...), custom_call_target="tpu_custom_call", output_to_operand_aliasing={{}: (5, {})} | custom-call | flops 1024 | bytes 1024 | tf_op jit(solution)/shard_map/pallas_call | solution.py:489
  50.2 3.0 %collective-permute-done.3.other_ref = bf16[1,128,2048]{2,1,0:T(8,128)(2,1)S(1)} collective-permute-done((bf16[1,128,2048]{2,1,0:T(8,128)(2,1)S(1)}, bf16[1,128,2048]{2,1,0:T(8,128)(2,1)S(1)}, u32[]{:S(2)}, u32[]{:S(2)}) %collective-permute-start.3) | collective-permute-done | bytes 524320 | tf_op jit(solution)/shard_map/ppermute | solution.py:473
  53.2 5.5 %shard_map.94 = (f32[2,128,2048]{2,1,0:T(8,128)S(1)}, f32[16,128]{1,0:T(8,128)S(1)}) custom-call(s32[14,2]{1,0:T(8,128)S(1)} %get-tuple-element.30.rel_ref, s32[2]{0:T(128)S(1)} %bitcast.31, bf16[14,128,128]{2,1,0:T(8,128)(2,1)S(1)} %shard_map.85.kron_ref, ...), custom_call_target="tpu_custom_call", output_to_operand_aliasing={{0}: (6, {})} | custom-call | flops 1024 | bytes 1024 | tf_op jit(solution)/shard_map/pallas_call | solution.py:489
  58.8 0.9 collective-permute-start.5
  59.7 1.6 %collective-permute-done.5.their_sums_ref = f32[16,128]{1,0:T(8,128)S(1)} collective-permute-done((f32[16,128]{1,0:T(8,128)S(1)}, f32[16,128]{1,0:T(8,128)S(1)}, u32[]{:S(2)}, u32[]{:S(2)}) %collective-permute-start.5) | collective-permute-done | bytes 8224 | tf_op jit(solution)/shard_map/ppermute | solution.py:473
  61.3 5.7 %shard_map.95 = (bf16[2,128,2048]{2,1,0:T(8,128)(2,1)}, bf16[2,128,2048]{2,1,0:T(8,128)(2,1)S(1)}, bf16[2,128,2048]{2,1,0:T(8,128)(2,1)S(1)}, bf16[8,2,128,128]{3,2,1,0:T(8,128)(2,1)S(1)}) custom-call(s32[2]{0:T(128)S(1)} %bitcast.32, f32[2,128,2048]{2,1,0:T(8,128)S(1)} %get-tuple-element.45.kept_ref, bf16[2,128,2048]{2,1,0:T(8,128)(2,1)S(1)} %get-tuple-element.41.guess_ref, ...), custom_call_target="tpu_custom_call" | custom-call | flops 1024 | bytes 1024 | tf_op jit(solution)/shard_map/pallas_call | solution.py:570
  67.0 6.8 %collective-permute-start.9 = (bf16[8,2,128,128]{3,2,1,0:T(8,128)(2,1)S(1)}, bf16[8,2,128,128]{3,2,1,0:T(8,128)(2,1)S(1)}, u32[]{:S(2)}, u32[]{:S(2)}) collective-permute-start(bf16[8,2,128,128]{3,2,1,0:T(8,128)(2,1)S(1)} %get-tuple-element.50), channel_id=1, source_target_pairs={{0,2},{2,4},{4,6},{6,8},{8,10},{10,12},{12,14},{14,16},{16,18},{18... | collective-permute-start | bytes 1572872 | tf_op jit(solution)/shard_map/ppermute | solution.py:559
  73.9 3.7 %shard_map.98 = bf16[8,2,128,128]{3,2,1,0:T(8,128)(2,1)S(1)} custom-call(bf16[14,2,128,128]{3,2,1,0:T(8,128)(2,1)S(1)} %bitcast.27, bf16[2,128,2048]{2,1,0:T(8,128)(2,1)S(1)} %get-tuple-element.49.outer_ref.inner_ref, bf16[2,128,2048]{2,1,0:T(8,128)(2,1)S(1)} %get-tuple-element.48.inner_ref.outer_ref), custom_call_target="tpu_custom_call" | custom-call | flops 1024 | bytes 1024 | tf_op jit(solution)/shard_map/pallas_call | solution.py:489
  77.6 1.9 %collective-permute-start.8 = (bf16[8,2,128,128]{3,2,1,0:T(8,128)(2,1)S(1)}, bf16[8,2,128,128]{3,2,1,0:T(8,128)(2,1)S(1)}, u32[]{:S(2)}, u32[]{:S(2)}) collective-permute-start(bf16[8,2,128,128]{3,2,1,0:T(8,128)(2,1)S(1)} %shard_map.98), channel_id=1, source_target_pairs={{2,0},{4,2},{6,4},{8,6},{10,8},{12,10},{14,12},{16,14},{18,16},{20... | collective-permute-start | bytes 1572872 | tf_op jit(solution)/shard_map/ppermute | solution.py:559
  79.5 2.7 %shard_map.96 = bf16[6,2,128,128]{3,2,1,0:T(8,128)(2,1)S(1)} custom-call(bf16[14,2,128,128]{3,2,1,0:T(8,128)(2,1)S(1)} %bitcast.17, bf16[2,128,2048]{2,1,0:T(8,128)(2,1)S(1)} %get-tuple-element.48.inner_ref.outer_ref, bf16[2,128,2048]{2,1,0:T(8,128)(2,1)S(1)} %get-tuple-element.49.outer_ref.inner_ref), custom_call_target="tpu_custom_call" | custom-call | flops 1024 | bytes 1024 | tf_op jit(solution)/shard_map/pallas_call | solution.py:489
  82.2 4.5 %collective-permute-start.6 = (bf16[6,2,128,128]{3,2,1,0:T(8,128)(2,1)S(1)}, bf16[6,2,128,128]{3,2,1,0:T(8,128)(2,1)S(1)}, u32[]{:S(2)}, u32[]{:S(2)}) collective-permute-start(bf16[6,2,128,128]{3,2,1,0:T(8,128)(2,1)S(1)} %shard_map.96), channel_id=1, source_target_pairs={{0,2},{2,4},{4,6},{6,8},{8,10},{10,12},{12,14},{14,16},{16,18},{18... | collective-permute-start | bytes 1179656 | tf_op jit(solution)/shard_map/ppermute | solution.py:559
  86.7 2.7 %shard_map.97 = bf16[6,2,128,128]{3,2,1,0:T(8,128)(2,1)S(1)} custom-call(bf16[14,2,128,128]{3,2,1,0:T(8,128)(2,1)S(1)} %bitcast.28, bf16[2,128,2048]{2,1,0:T(8,128)(2,1)S(1)} %get-tuple-element.49.outer_ref.inner_ref, bf16[2,128,2048]{2,1,0:T(8,128)(2,1)S(1)} %get-tuple-element.48.inner_ref.outer_ref), custom_call_target="tpu_custom_call" | custom-call | flops 1024 | bytes 1024 | tf_op jit(solution)/shard_map/pallas_call | solution.py:489
  89.4 1.9 %collective-permute-start.7 = (bf16[6,2,128,128]{3,2,1,0:T(8,128)(2,1)S(1)}, bf16[6,2,128,128]{3,2,1,0:T(8,128)(2,1)S(1)}, u32[]{:S(2)}, u32[]{:S(2)}) collective-permute-start(bf16[6,2,128,128]{3,2,1,0:T(8,128)(2,1)S(1)} %shard_map.97), channel_id=1, source_target_pairs={{2,0},{4,2},{6,4},{8,6},{10,8},{12,10},{14,12},{16,14},{18,16},{20... | collective-permute-start | bytes 1179656 | tf_op jit(solution)/shard_map/ppermute | solution.py:559
  91.4 0.0 collective-permute-done.9.refs_0_
  91.4 1.1 %shard_map.99 = (f32[14,2,128,128]{3,2,1,0:T(8,128)}, f32[14,2,128,128]{3,2,1,0:T(8,128)}) custom-call(bf16[8,2,128,128]{3,2,1,0:T(8,128)(2,1)S(1)} %collective-permute-done.9.refs_0_), custom_call_target="tpu_custom_call" | custom-call | flops 1024 | bytes 1024 | tf_op jit(solution)/shard_map/pallas_call | solution.py:589
  92.5 0.0 collective-permute-done.8.refs_0_
  92.5 1.1 %shard_map.100 = (f32[14,2,128,128]{3,2,1,0:T(8,128)}, f32[14,2,128,128]{3,2,1,0:T(8,128)}) custom-call(bf16[8,2,128,128]{3,2,1,0:T(8,128)(2,1)S(1)} %collective-permute-done.8.refs_0_, f32[14,2,128,128]{3,2,1,0:T(8,128)} %get-tuple-element.51.refs_1_, f32[14,2,128,128]{3,2,1,0:T(8,128)} %get-tuple-element.52.refs_2_), custom_call_target="tpu_custom_call", output_to_operand_aliasing={{0}: (1, {}), {1}: (2, {})} | custom-call | flops 1024 | bytes 1024 | tf_op jit(solution)/shard_map/pallas_call | solution.py:589
  93.6 0.0 collective-permute-done.6.refs_0_
  93.6 5.8 %collective-permute-done.7.refs_1_ = bf16[6,2,128,128]{3,2,1,0:T(8,128)(2,1)S(1)} collective-permute-done((bf16[6,2,128,128]{3,2,1,0:T(8,128)(2,1)S(1)}, bf16[6,2,128,128]{3,2,1,0:T(8,128)(2,1)S(1)}, u32[]{:S(2)}, u32[]{:S(2)}) %collective-permute-start.7) | collective-permute-done | bytes 393248 | tf_op jit(solution)/shard_map/ppermute | solution.py:559
  99.4 1.3 %shard_map.101 = (f32[14,2,128,128]{3,2,1,0:T(8,128)}, f32[14,2,128,128]{3,2,1,0:T(8,128)}) custom-call(bf16[6,2,128,128]{3,2,1,0:T(8,128)(2,1)S(1)} %collective-permute-done.6.refs_0_, bf16[6,2,128,128]{3,2,1,0:T(8,128)(2,1)S(1)} %collective-permute-done.7.refs_1_, ...), custom_call_target="tpu_custom_call", output_to_operand_aliasing={{0}: (2, {}), {1}: (3, {})} | custom-call | flops 1024 | bytes 1024 | tf_op jit(solution)/shard_map/pallas_call | solution.py:589
Async XLA Ops:
  0.6 4.9 %copy-start = (bf16[1,14,2,128,128]{4,3,2,1,0:T(8,128)(2,1)S(1)}, bf16[1,14,2,128,128]{4,3,2,1,0:T(8,128)(2,1)}, u32[]{:S(2)}) copy-start(bf16[1,14,2,128,128]{4,3,2,1,0:T(8,128)(2,1)} %param.7) | copy-start | bytes 2752516
  0.6 1.3 %copy-start.1 = (bf16[1,2,128,2048]{3,2,1,0:T(8,128)(2,1)S(1)}, bf16[1,2,128,2048]{3,2,1,0:T(8,128)(2,1)}, u32[]{:S(2)}) copy-start(bf16[1,2,128,2048]{3,2,1,0:T(8,128)(2,1)} %param.6) | copy-start | bytes 3145732
  1.9 3.1 %copy-start.4 = (bf16[1,14,16,16]{3,2,1,0:T(8,128)(2,1)S(1)}, bf16[1,14,16,16]{3,2,1,0:T(8,128)(2,1)}, u32[]{:S(2)}) copy-start(bf16[1,14,16,16]{3,2,1,0:T(8,128)(2,1)} %param.9) | copy-start | bytes 21508
  1.9 3.4 %copy-start.6 = (s32[1,14,4]{1,2,0:T(4,128)S(1)}, s32[1,14,4]{1,2,0:T(4,128)}, u32[]{:S(2)}) copy-start(s32[1,14,4]{1,2,0:T(4,128)} %param.10) | copy-start | bytes 676
  2.0 3.6 %copy-start.2 = (bf16[1,2,128,2048]{3,2,1,0:T(8,128)(2,1)S(1)}, bf16[1,2,128,2048]{3,2,1,0:T(8,128)(2,1)}, u32[]{:S(2)}) copy-start(bf16[1,2,128,2048]{3,2,1,0:T(8,128)(2,1)} %param.6) | copy-start | bytes 3145732
  2.0 3.6 %copy-start.3 = (bf16[1,14,2,128,128]{4,3,2,1,0:T(8,128)(2,1)S(1)}, bf16[1,14,2,128,128]{4,3,2,1,0:T(8,128)(2,1)}, u32[]{:S(2)}) copy-start(bf16[1,14,2,128,128]{4,3,2,1,0:T(8,128)(2,1)} %param.8) | copy-start | bytes 2752516
  2.8 13.1 %collective-permute-start.1 = (bf16[1,128,2048]{2,1,0:T(8,128)(2,1)}, bf16[1,128,2048]{2,1,0:T(8,128)(2,1)}, u32[]{:S(2)}, u32[]{:S(2)}) collective-permute-start(bf16[1,128,2048]{2,1,0:T(8,128)(2,1)} %shard_map.88), channel_id=1, source_target_pairs={{0,1},{1,0},{2,3},{3,2},{4,5},{5,4},{6,7},{7,6},{8,9},{9,8},{10,11... | collective-permute-start | bytes 1572872 | tf_op jit(solution)/shard_map/ppermute | solution.py:473
  4.8 22.3 %collective-permute-start = (bf16[1,128,2048]{2,1,0:T(8,128)(2,1)}, bf16[1,128,2048]{2,1,0:T(8,128)(2,1)}, u32[]{:S(2)}, u32[]{:S(2)}) collective-permute-start(bf16[1,128,2048]{2,1,0:T(8,128)(2,1)} %shard_map.87), channel_id=1, source_target_pairs={{0,1},{1,0},{2,3},{3,2},{4,5},{5,4},{6,7},{7,6},{8,9},{9,8},{10,11... | collective-permute-start | bytes 1572872 | tf_op jit(solution)/shard_map/ppermute | solution.py:473
  20.7 6.5 %collective-permute-start.2 = (f32[8,128]{1,0:T(8,128)S(1)}, f32[8,128]{1,0:T(8,128)S(1)}, u32[]{:S(2)}, u32[]{:S(2)}) collective-permute-start(f32[8,128]{1,0:T(8,128)S(1)} %get-tuple-element.37.mine_ref), channel_id=1, source_target_pairs={{0,1},{1,0},{2,3},{3,2},{4,5},{5,4},{6,7},{7,6},{8,9},{9,8},{10,11... | collective-permute-start | bytes 12296 | tf_op jit(solution)/shard_map/ppermute | solution.py:473
  29.7 15.9 %collective-permute-start.4 = (bf16[1,128,2048]{2,1,0:T(8,128)(2,1)S(1)}, bf16[1,128,2048]{2,1,0:T(8,128)(2,1)S(1)}, u32[]{:S(2)}, u32[]{:S(2)}) collective-permute-start(bf16[1,128,2048]{2,1,0:T(8,128)(2,1)S(1)} %get-tuple-element.39.refs_0_), channel_id=1, source_target_pairs={{0,1},{1,0},{2,3},{3,2},{4,5},{5,4},{6,7},{7,6},{8,9},{9,8},{10,11... | collective-permute-start | bytes 1572872 | tf_op jit(solution)/shard_map/ppermute | solution.py:473
  31.8 4.2 %copy-start.5 = (s32[1,2]{1,0:T(1,128)S(1)}, s32[1,2]{1,0:T(1,128)}, u32[]{:S(2)}) copy-start(s32[1,2]{1,0:T(1,128)} %param.11) | copy-start | bytes 28
  36.0 17.3 %collective-permute-start.3 = (bf16[1,128,2048]{2,1,0:T(8,128)(2,1)S(1)}, bf16[1,128,2048]{2,1,0:T(8,128)(2,1)S(1)}, u32[]{:S(2)}, u32[]{:S(2)}) collective-permute-start(bf16[1,128,2048]{2,1,0:T(8,128)(2,1)S(1)} %get-tuple-element.40), channel_id=1, source_target_pairs={{0,1},{1,0},{2,3},{3,2},{4,5},{5,4},{6,7},{7,6},{8,9},{9,8},{10,11... | collective-permute-start | bytes 1572872 | tf_op jit(solution)/shard_map/ppermute | solution.py:473
  58.8 2.6 %collective-permute-start.5 = (f32[16,128]{1,0:T(8,128)S(1)}, f32[16,128]{1,0:T(8,128)S(1)}, u32[]{:S(2)}, u32[]{:S(2)}) collective-permute-start(f32[16,128]{1,0:T(8,128)S(1)} %get-tuple-element.46.my_sums_ref), channel_id=1, source_target_pairs={{0,1},{1,0},{2,3},{3,2},{4,5},{5,4},{6,7},{7,6},{8,9},{9,8},{10,11... | collective-permute-start | bytes 24584 | tf_op jit(solution)/shard_map/ppermute | solution.py:473
  67.0 24.3 %collective-permute-start.9 = (bf16[8,2,128,128]{3,2,1,0:T(8,128)(2,1)S(1)}, bf16[8,2,128,128]{3,2,1,0:T(8,128)(2,1)S(1)}, u32[]{:S(2)}, u32[]{:S(2)}) collective-permute-start(bf16[8,2,128,128]{3,2,1,0:T(8,128)(2,1)S(1)} %get-tuple-element.50), channel_id=1, source_target_pairs={{0,2},{2,4},{4,6},{6,8},{8,10},{10,12},{12,14},{14,16},{16,18},{18... | collective-permute-start | bytes 1572872 | tf_op jit(solution)/shard_map/ppermute | solution.py:559
  77.6 14.9 %collective-permute-start.8 = (bf16[8,2,128,128]{3,2,1,0:T(8,128)(2,1)S(1)}, bf16[8,2,128,128]{3,2,1,0:T(8,128)(2,1)S(1)}, u32[]{:S(2)}, u32[]{:S(2)}) collective-permute-start(bf16[8,2,128,128]{3,2,1,0:T(8,128)(2,1)S(1)} %shard_map.98), channel_id=1, source_target_pairs={{2,0},{4,2},{6,4},{8,6},{10,8},{12,10},{14,12},{16,14},{18,16},{20... | collective-permute-start | bytes 1572872 | tf_op jit(solution)/shard_map/ppermute | solution.py:559
  82.2 11.4 %collective-permute-start.6 = (bf16[6,2,128,128]{3,2,1,0:T(8,128)(2,1)S(1)}, bf16[6,2,128,128]{3,2,1,0:T(8,128)(2,1)S(1)}, u32[]{:S(2)}, u32[]{:S(2)}) collective-permute-start(bf16[6,2,128,128]{3,2,1,0:T(8,128)(2,1)S(1)} %shard_map.96), channel_id=1, source_target_pairs={{0,2},{2,4},{4,6},{6,8},{8,10},{10,12},{12,14},{14,16},{16,18},{18... | collective-permute-start | bytes 1179656 | tf_op jit(solution)/shard_map/ppermute | solution.py:559
  89.4 10.0 %collective-permute-start.7 = (bf16[6,2,128,128]{3,2,1,0:T(8,128)(2,1)S(1)}, bf16[6,2,128,128]{3,2,1,0:T(8,128)(2,1)S(1)}, u32[]{:S(2)}, u32[]{:S(2)}) collective-permute-start(bf16[6,2,128,128]{3,2,1,0:T(8,128)(2,1)S(1)} %shard_map.97), channel_id=1, source_target_pairs={{2,0},{4,2},{6,4},{8,6},{10,8},{12,10},{14,12},{16,14},{18,16},{20... | collective-permute-start | bytes 1179656 | tf_op jit(solution)/shard_map/ppermute | solution.py:559

commit v6 on v5

--- a/solution.py
+++ b/solution.py
@@ -321,7 +321,7 @@
 
 def normalize(
     cells, rank_ref, kept_ref, guess_ref, x_ref, mine_ref, theirs_ref, my_sums_ref, their_sums_ref,
-    state_ref,
+    both_ref,
 ):
     both = my_sums_ref[...] + their_sums_ref[...]
     xv, xx, gv, xg, gg, gg_kept, xx_kept, xg_kept, kg, kx, kg_kept, kx_kept, kk_kept = (
@@ -356,103 +356,111 @@
                 + of_guess * guess_ref[b, :, cols].astype(F32)
                 + of_state * x_ref[b, :, cols].astype(F32)
             )
-            state_ref[b, :, cols] = (kept * factor).astype(BF16)
+            state = (kept * factor).astype(BF16)
+            both_ref[0, b, :, cols] = state
+            both_ref[1, b, :, cols] = state.T
         return carry
 
     lax.fori_loop(0, blocks * per, one, 0)
 
 
-def env_middle(k, b, env_ref, inner_ref, mid_ref, place):
-    rows, width = inner_ref.shape[1:]
-    env = jnp.concatenate([env_ref[k, b], env_ref[k + 1, b]], axis=0)
-    mid = dot(env, inner_ref[b]).astype(BF16)
-    for p in range(width // LANES):
-        for i in range(2):
-            mid_ref[place, p * rows : (p + 1) * rows, i * LANES : (i + 1) * LANES] = mid[
-                i * rows : (i + 1) * rows, p * LANES : (p + 1) * LANES
-            ]
-
-
-def env_result(k, b, scale, outer_ref, mid_ref, place, out_ref):
-    out = (dot(outer_ref[b], mid_ref[place]) * scale).astype(BF16)
-    out_ref[k, b] = out[:, :LANES]
-    out_ref[k + 1, b] = out[:, LANES:]
-
-
-def environments(first, count, scale, env_ref, inner_ref, outer_ref, out_ref, mid_ref):
-    dests = outer_ref.shape[0]
-    pairs = mid_ref.shape[0] // dests
-
-    def step(n, carry):
+def environments(
+    first, counts, scale, use_left, left_ref, right_ref, both_ref, out_ref, mid_ref
+):
+    _, dests, rows, width = both_ref.shape
+    phys = width // LANES
+    inner = jnp.where(use_left, 0, 1)
+
+    def step(begin, pairs):
         for j in range(pairs):
+            k = first + begin + 2 * j
             for b in range(dests):
-                env_middle(first + 2 * (n * pairs + j), b, env_ref, inner_ref, mid_ref, j * dests + b)
+                env = jnp.concatenate(
+                    [
+                        jnp.where(use_left, left_ref[k + i, b], right_ref[k + i, b])
+                        for i in range(2)
+                    ],
+                    axis=0,
+                )
+                mid = dot(env, both_ref[inner, b]).astype(BF16)
+                for p in range(phys):
+                    for i in range(2):
+                        mid_ref[
+                            j * dests + b, p * rows : (p + 1) * rows, i * LANES : (i + 1) * LANES
+                        ] = mid[i * rows : (i + 1) * rows, p * LANES : (p + 1) * LANES]
         for j in range(pairs):
+            k = begin + 2 * j
             for b in range(dests):
-                env_result(2 * (n * pairs + j), b, scale, outer_ref, mid_ref, j * dests + b, out_ref)
-        return carry
-
-    lax.fori_loop(0, count // (2 * pairs), step, 0)
-
-
-def left_beside_turn(count, scale, env_ref, state_ref, turned_ref, out_ref, mid_ref):
-    dests, _, width = state_ref.shape
-    phys = width // LANES
-    rounds = count // 4
-    tiles = dests * phys // rounds
-
-    def before(n, carry):
-        for t in range(tiles):
-            tile = n * tiles + t
-            cols = pl.ds(pl.multiple_of(lax.rem(tile, phys) * LANES, LANES), LANES)
-            turned_ref[tile // phys, :, cols] = state_ref[tile // phys, :, cols].T
-        for j in range(2):
-            for b in range(dests):
-                place = (2 * n + j) * dests + b
-                env_middle(2 * (2 * n + j), b, env_ref, state_ref, mid_ref, place)
-        return carry
-
-    def after(n, carry):
-        for j in range(2):
-            for b in range(dests):
-                place = (2 * n + j) * dests + b
-                env_result(2 * (2 * n + j), b, scale, turned_ref, mid_ref, place, out_ref)
-        return carry
-
-    lax.fori_loop(0, rounds, before, 0)
-    lax.fori_loop(0, rounds, after, 0)
-
-
-def normalize_and_left(
-    count, scale, cells,
-    rank_ref, kept_ref, guess_ref, x_ref, mine_ref, theirs_ref, my_sums_ref, their_sums_ref, env_ref,
-    new_ref, state_ref, turned_ref, out_ref,
+                out = (dot(both_ref[1 - inner, b], mid_ref[j * dests + b]) * scale).astype(BF16)
+                out_ref[k, b] = out[:, :LANES]
+                out_ref[k + 1, b] = out[:, LANES:]
+
+    begin = 0
+    for pairs, passes in counts:
+
+        def one(n, carry, begin=begin, pairs=pairs):
+            step(begin + 2 * pairs * n, pairs)
+            return carry
+
+        lax.fori_loop(0, passes, one, 0)
+        begin += 2 * pairs * passes
+
+
+def normalize_and_cross(
+    counts, scale, cells,
+    odd_ref, rank_ref, kept_ref, guess_ref, x_ref, mine_ref, theirs_ref, my_sums_ref,
+    their_sums_ref, left_ref, right_ref,
+    new_ref, both_ref, out_ref,
     mid_ref, sem,
 ):
     normalize(
         cells, rank_ref, kept_ref, guess_ref, x_ref, mine_ref, theirs_ref, my_sums_ref,
-        their_sums_ref, state_ref,
-    )
-    copy = pltpu.make_async_copy(state_ref, new_ref, sem)
+        their_sums_ref, both_ref,
+    )
+    copy = pltpu.make_async_copy(both_ref.at[0], new_ref, sem)
     copy.start()
-    left_beside_turn(count, scale, env_ref, state_ref, turned_ref, out_ref, mid_ref)
+    environments(
+        0, counts, scale, odd_ref[0] == 1, left_ref, right_ref, both_ref, out_ref, mid_ref
+    )
     copy.wait()
 
 
-def widen(places, *refs):
-    pieces, (outs, wides, sems) = refs[: len(places)], (refs[-5:-3], refs[-3:-1], refs[-1])
+def cross(first, counts, scale, odd_ref, left_ref, right_ref, both_ref, out_ref, mid_ref):
+    environments(
+        first, counts, scale, odd_ref[0] == 1, left_ref, right_ref, both_ref, out_ref, mid_ref
+    )
+
+
+def within(counts, scale, odd_ref, left_ref, right_ref, both_ref, *refs):
+    outs, all_ref, mid_ref = refs[:-2], refs[-2], refs[-1]
+    environments(
+        0, counts, scale, odd_ref[0] == 0, left_ref, right_ref, both_ref, all_ref, mid_ref
+    )
+    begin = 0
+    for out_ref in outs:
+        count = out_ref.shape[0]
+        out_ref[...] = all_ref[begin : begin + count]
+        begin += count
+
+
+def widen(begins, crossed, odd_ref, *refs):
+    pieces, (outs, wide_ref, sems) = refs[: len(begins)], (refs[-4:-2], refs[-2], refs[-1])
+    to_right = odd_ref[0] == (1 if crossed else 0)
     copies = []
-    for piece, (side, begin) in zip(pieces, places):
-        for n in range(0, piece.shape[0], 2):
-            span = pl.ds(begin + n, 2)
-            wides[side][begin + n : begin + n + 2] = piece[n : n + 2].astype(F32)
-            copy = pltpu.make_async_copy(
-                wides[side].at[span], outs[side].at[span], sems.at[len(copies)]
-            )
-            copy.start()
-            copies.append(copy)
-    for copy in copies:
-        copy.wait()
+    for piece, begin in zip(pieces, begins):
+        for n in range(piece.shape[0]):
+            place = begin + n
+            wide_ref[place] = piece[n].astype(F32)
+            pair = [
+                pltpu.make_async_copy(wide_ref.at[place], out.at[place], sems.at[place])
+                for out in outs
+            ]
+            pl.when(jnp.logical_not(to_right))(pair[0].start)
+            pl.when(to_right)(pair[1].start)
+            copies.append(pair)
+    for pair in copies:
+        pl.when(jnp.logical_not(to_right))(pair[0].wait)
+        pl.when(to_right)(pair[1].wait)
 
 
 def shards(state, left_env, right_env, site_ops, sector_map, ranks):
@@ -547,59 +555,54 @@
 
     env_scale = 1.0 / math.sqrt(phys * rows)
     cells = float(total_blocks * rows * width)
-    early, later = 8, 8
-
-    def mid(count):
-        pairs = next(n for n in (2, 3, 1) if count % (2 * n) == 0)
+    early = 8
+    count = lax.axis_size("seg")
+    odd = jnp.full((1,), lax.rem(lax.axis_index("seg"), 2), jnp.int32)
+
+    def swapped(value, low):
+        pairs = [(s, s + 1) for s in range(low, count - 1, 2)]
+        return lax.ppermute(value, "seg", pairs + [(t, s) for s, t in pairs])
+
+    def env_kind(number):
+        return shape((number,) + left.shape[1:], BF16)
+
+    def mid(pairs):
         return [pltpu.VMEM((pairs * dests, width, 2 * LANES), BF16)]
 
-    def sent(value, steps):
-        count = lax.axis_size("seg")
-        begin, end = max(0, -steps), min(count, count - steps)
-        return lax.ppermute(value, "seg", [(s, s + steps) for s in range(begin, end)])
-
-    def env_kind(count):
-        return shape((count,) + left.shape[1:], BF16)
-
-    def env_call(begin, count, env, inner, outer):
+    new_state, both, piece = call(
+        functools.partial(normalize_and_cross, ((2, 2),), env_scale, cells),
+        [SMEM] * 2 + [VMEM] * 9, (wave_b16, shape((2,) + wave, BF16), env_kind(early)),
+        mid(2) + [pltpu.SemaphoreType.DMA],
+        odd, ranks[0], kept, guess, x, mine, theirs, my_sums, their_sums, left, right,
+        out_specs=(HBM, VMEM, VMEM),
+    )
+    rest = call(
+        functools.partial(cross, early, ((3, 1),), env_scale),
+        [SMEM] + [VMEM] * 3, env_kind(chan - early), mid(3), odd, left, right, both,
+    )
+    sizes = (5, 5, 4)
+    inside = call(
+        functools.partial(within, ((2, 3), (1, 1)), env_scale),
+        [SMEM] + [VMEM] * 3, tuple(env_kind(size) for size in sizes),
+        [pltpu.VMEM(left.shape, BF16)] + mid(2), odd, left, right, both,
+    )
+    piece, rest = swapped(piece, 1), swapped(rest, 1)
+    inside = [swapped(value, 0) for value in inside]
+    env_f32 = shape(left.shape, F32)
+
+    def widened(begins, crossed, values, filled):
+        number = 1 + len(values)
         return call(
-            functools.partial(environments, begin, count, env_scale),
-            [VMEM] * 3, env_kind(count), mid(count), env, inner, outer,
+            functools.partial(widen, begins, crossed),
+            [SMEM] + [VMEM] * len(values) + [HBM] * len(filled), (env_f32, env_f32),
+            [pltpu.VMEM(left.shape, F32), pltpu.SemaphoreType.DMA((chan,))],
+            odd, *values, *filled,
+            aliases={number + n: n for n in range(len(filled))}, out_specs=(HBM, HBM),
         )
 
-    new_state, state_kept, turned, piece = pl.pallas_call(
-        functools.partial(normalize_and_left, early, env_scale, cells),
-        in_specs=[SMEM] + [VMEM] * 8,
-        out_specs=(HBM, VMEM, VMEM, VMEM),
-        out_shape=(wave_b16, wave_b16, wave_b16, env_kind(early)),
-        scratch_shapes=[pltpu.VMEM((early // 2 * dests, width, 2 * LANES), BF16)] + [pltpu.SemaphoreType.DMA],
-        compiler_params=PARAMS,
-        cost_estimate=COST,
-    )(ranks[0], kept, guess, x, mine, theirs, my_sums, their_sums, left)
-    pieces = [
-        sent(piece, 1),
-        sent(env_call(0, later, right, turned, state_kept), -1),
-        sent(env_call(early, chan - early, left, state_kept, turned), 1),
-        sent(env_call(later, chan - later, right, turned, state_kept), -1),
-    ]
-    env_f32 = shape(left.shape, F32)
-
-    def widened(places, values, filled):
-        count = len(values)
-        return pl.pallas_call(
-            functools.partial(widen, places),
-            in_specs=[VMEM] * count + [HBM] * len(filled),
-            out_specs=(HBM, HBM),
-            out_shape=(env_f32, env_f32),
-            input_output_aliases={count + n: n for n in range(len(filled))},
-            scratch_shapes=[pltpu.VMEM(left.shape, F32)] * 2 + [pltpu.SemaphoreType.DMA((chan,))],
-            compiler_params=PARAMS,
-            cost_estimate=COST,
-        )(*values, *filled)
-
-    filled = widened(((0, 0),), pieces[:1], ())
-    filled = widened(((1, 0),), pieces[1:2], filled)
-    received_left, received_right = widened(((0, early), (1, later)), pieces[2:], filled)
+    filled = widened((0,), True, [piece], ())
+    filled = widened((0, sizes[0], sizes[0] + sizes[1]), False, inside, filled)
+    received_left, received_right = widened((early,), True, [rest], filled)
     return (new_state[None], received_left[None], received_right[None])
 
 

time: 101 us -> 101 us (level)
  the two profiles are of different devices: /device:TPU:13 before, /device:TPU:1 now
where the time goes in v6:
time: 101 us; the launch traced here: 100 us
  Pallas kernels  59.1 us (59%)
  waiting for transfers between devices  18.8 us (19%)
  starting transfers between devices  15.6 us (15%)
  local copies, waits for them, and re-layouts  5.59 us (6%)
  between operations  1.04 us (1%)
    pallas_call x16, Pallas kernels, call(): pl.pallas_call(body, in_specs=specs, out_specs=out_specs or jax.tree.map(...  59.1 us
    ppermute x6, waiting for transfers between devices, trade(): return lax.ppermute(value, 'blk', swap)  12.9 us
    ppermute x5, starting transfers between devices, swapped(): return lax.ppermute(value, 'seg', pairs + [(t, s) for s, t in pairs])  8.83 us
    ppermute x6, starting transfers between devices, trade(): return lax.ppermute(value, 'blk', swap)  6.72 us
    ppermute x5, waiting for transfers between devices, swapped(): return lax.ppermute(value, 'seg', pairs + [(t, s) for s, t in pairs])  5.92 us
    unnamed x22, local copies, waits for them, and re-layouts  5.5 us
  transfers between devices with their start and end apart: 11, of which 7 were waited for; matrix products, arithmetic and copies ran while one was open for 0% of the time, Pallas kernels for 44%

profile of v6, /device:TPU:1, one launch (start us, length us, event | category | flops | bytes accessed | tf_op | source)
XLA Modules:
  0.0 100.2 jit_solution(12714848108101810942)
XLA Ops:
  0.6 0.0 copy-start
  0.6 0.0 copy-start.1
  0.7 1.3 %copy-done.1 = bf16[1,2,128,2048]{3,2,1,0:T(8,128)(2,1)S(1)} copy-done((bf16[1,2,128,2048]{3,2,1,0:T(8,128)(2,1)S(1)}, bf16[1,2,128,2048]{3,2,1,0:T(8,128)(2,1)}, u32[]{:S(2)}) %copy-start.1) | copy-done | bytes 1048600
  1.9 0.0 copy-start.8
  1.9 0.0 copy-start.10
  2.0 0.0 copy-start.2
  2.0 0.0 copy-start.5
  2.0 0.8 shard_map.88
  2.8 2.0 %collective-permute-start.1 = (bf16[1,128,2048]{2,1,0:T(8,128)(2,1)}, bf16[1,128,2048]{2,1,0:T(8,128)(2,1)}, u32[]{:S(2)}, u32[]{:S(2)}) collective-permute-start(bf16[1,128,2048]{2,1,0:T(8,128)(2,1)} %shard_map.88), channel_id=1, source_target_pairs={{0,1},{1,0},{2,3},{3,2},{4,5},{5,4},{6,7},{7,6},{8,9},{9,8},{10,11... | collective-permute-start | bytes 1572872 | tf_op jit(solution)/shard_map/ppermute | solution.py:481
  4.8 0.8 shard_map.87
  5.7 0.0 collective-permute-start
  5.7 0.0 copy-done.8
  5.7 0.3 shard_map.85.kron_ref
  5.9 0.0 copy-done.10
  6.0 0.1 copy.18
  6.0 0.1 negate_select_fusion.map_ref
  6.1 0.0 copy-done
  6.2 0.0 copy-done.2
  6.2 0.0 copy-done.5
  6.2 10.1 %shard_map.86 = (bf16[14,2,128,128]{3,2,1,0:T(8,128)(2,1)S(1)}, f32[2,128,2048]{2,1,0:T(8,128)S(1)}, f32[8,128]{1,0:T(8,128)S(1)}, s32[14,2]{1,0:T(8,128)S(1)}, s32[14,2]{1,0:T(8,128)S(1)}, /*index=5*/s32[2]{0:T(128)S(1)}) custom-call(s32[14,4]{1,0:T(8,128)S(1)} %negate_select_fusion.map_ref, bf16[14,128,128]{2,1,0:T(8,128)(2,1)S(1)} %shard_map.85.kron_ref, ...), custom_call_target="tpu_custom_call" | custom-call | flops 1024 | bytes 1024 | tf_op jit(solution)/shard_map/pallas_call | solution.py:497
  16.3 0.5 collective-permute-done.1.other_ref
  16.8 4.8 %shard_map.89 = (f32[2,128,2048]{2,1,0:T(8,128)S(1)}, f32[8,128]{1,0:T(8,128)S(1)}) custom-call(s32[14,2]{1,0:T(8,128)S(1)} %get-tuple-element.33.rel_ref, bf16[14,128,128]{2,1,0:T(8,128)(2,1)S(1)} %shard_map.85.kron_ref, bf16[1,128,2048]{2,1,0:T(8,128)(2,1)} %collective-permute-done.1.other_ref, ...), custom_call_target="tpu_custom_call", output_to_operand_aliasing={{0}: (5, {})} | custom-call | flops 1024 | bytes 1024 | tf_op jit(solution)/shard_map/pallas_call | solution.py:497
  21.6 1.1 %collective-permute-start.2 = (f32[8,128]{1,0:T(8,128)S(1)}, f32[8,128]{1,0:T(8,128)S(1)}, u32[]{:S(2)}, u32[]{:S(2)}) collective-permute-start(f32[8,128]{1,0:T(8,128)S(1)} %get-tuple-element.39.mine_ref), channel_id=1, source_target_pairs={{0,1},{1,0},{2,3},{3,2},{4,5},{5,4},{6,7},{7,6},{8,9},{9,8},{10,11... | collective-permute-start | bytes 12296 | tf_op jit(solution)/shard_map/ppermute | solution.py:481
  22.7 5.3 %collective-permute-done.other_ref = bf16[1,128,2048]{2,1,0:T(8,128)(2,1)} collective-permute-done((bf16[1,128,2048]{2,1,0:T(8,128)(2,1)}, bf16[1,128,2048]{2,1,0:T(8,128)(2,1)}, u32[]{:S(2)}, u32[]{:S(2)}) %collective-permute-start) | collective-permute-done | bytes 524320 | tf_op jit(solution)/shard_map/ppermute | solution.py:481
  28.0 0.1 collective-permute-done.2.theirs_ref
  28.1 3.3 %shard_map.90 = (f32[2,128,2048]{2,1,0:T(8,128)S(1)}, bf16[1,128,2048]{2,1,0:T(8,128)(2,1)S(1)}) custom-call(s32[14,2]{1,0:T(8,128)S(1)} %get-tuple-element.33.rel_ref, s32[2]{0:T(128)S(1)} %get-tuple-element.34.order_ref, bf16[14,128,128]{2,1,0:T(8,128)(2,1)S(1)} %shard_map.85.kron_ref, ...), custom_call_target="tpu_custom_call", output_to_operand_aliasing={{0}: (6, {})} | custom-call | flops 1024 | bytes 1024 | tf_op jit(solution)/shard_map/pallas_call | solution.py:497
  31.4 2.1 %collective-permute-start.4 = (bf16[1,128,2048]{2,1,0:T(8,128)(2,1)S(1)}, bf16[1,128,2048]{2,1,0:T(8,128)(2,1)S(1)}, u32[]{:S(2)}, u32[]{:S(2)}) collective-permute-start(bf16[1,128,2048]{2,1,0:T(8,128)(2,1)S(1)} %get-tuple-element.41.refs_0_), channel_id=1, source_target_pairs={{0,1},{1,0},{2,3},{3,2},{4,5},{5,4},{6,7},{7,6},{8,9},{9,8},{10,11... | collective-permute-start | bytes 1572872 | tf_op jit(solution)/shard_map/ppermute | solution.py:481
  33.5 0.0 copy-start.9
  33.5 2.5 %shard_map.91 = (f32[2,128,2048]{2,1,0:T(8,128)S(1)}, bf16[1,128,2048]{2,1,0:T(8,128)(2,1)S(1)}, bf16[2,128,2048]{2,1,0:T(8,128)(2,1)S(1)}) custom-call(s32[14,2]{1,0:T(8,128)S(1)} %get-tuple-element.33.rel_ref, s32[2]{0:T(128)S(1)} %get-tuple-element.34.order_ref, bf16[14,128,128]{2,1,0:T(8,128)(2,1)S(1)} %shard_map.85.kron_ref, ...), custom_call_target="tpu_custom_call", output_to_operand_aliasing={{0}: (6, {})} | custom-call | flops 1024 | bytes 1024 | tf_op jit(solution)/shard_map/pallas_call | solution.py:497
  36.0 0.0 copy-start.6
  36.0 0.1 collective-permute-start.3
  36.0 0.0 copy-done.9
  36.1 9.4 %shard_map.92 = (f32[2,128,2048]{2,1,0:T(8,128)S(1)}, f32[8,128]{1,0:T(8,128)S(1)}) custom-call(s32[14,2]{1,0:T(8,128)S(1)} %get-tuple-element.32.rel_ref, s32[2]{0:T(128)S(1)} %bitcast.33, bf16[14,128,128]{2,1,0:T(8,128)(2,1)S(1)} %shard_map.85.kron_ref, bf16[2,128,2048]{2,1,0:T(8,128)(2,1)S(1)} %get-tuple-element.43.guess_ref, ...), custom_call_target="tpu_custom_call" | custom-call | flops 1024 | bytes 1024 | tf_op jit(solution)/shard_map/pallas_call | solution.py:497
  45.5 0.0 collective-permute-done.4.other_ref
  45.5 4.6 %shard_map.93.before_ref = f32[2,128,2048]{2,1,0:T(8,128)S(1)} custom-call(s32[14,2]{1,0:T(8,128)S(1)} %get-tuple-element.32.rel_ref, bf16[14,128,128]{2,1,0:T(8,128)(2,1)S(1)} %shard_map.85.kron_ref, bf16[1,128,2048]{2,1,0:T(8,128)(2,1)S(1)} %collective-permute-done.4.other_ref, ...), custom_call_target="tpu_custom_call", output_to_operand_aliasing={{}: (5, {})} | custom-call | flops 1024 | bytes 1024 | tf_op jit(solution)/shard_map/pallas_call | solution.py:497
  50.1 5.9 %collective-permute-done.3.other_ref = bf16[1,128,2048]{2,1,0:T(8,128)(2,1)S(1)} collective-permute-done((bf16[1,128,2048]{2,1,0:T(8,128)(2,1)S(1)}, bf16[1,128,2048]{2,1,0:T(8,128)(2,1)S(1)}, u32[]{:S(2)}, u32[]{:S(2)}) %collective-permute-start.3) | collective-permute-done | bytes 524320 | tf_op jit(solution)/shard_map/ppermute | solution.py:481
  56.1 0.0 copy-done.6
  56.1 4.6 %shard_map.94 = (f32[2,128,2048]{2,1,0:T(8,128)S(1)}, f32[16,128]{1,0:T(8,128)S(1)}) custom-call(s32[14,2]{1,0:T(8,128)S(1)} %get-tuple-element.32.rel_ref, s32[2]{0:T(128)S(1)} %bitcast.34, bf16[14,128,128]{2,1,0:T(8,128)(2,1)S(1)} %shard_map.85.kron_ref, ...), custom_call_target="tpu_custom_call", output_to_operand_aliasing={{0}: (6, {})} | custom-call | flops 1024 | bytes 1024 | tf_op jit(solution)/shard_map/pallas_call | solution.py:497
  60.7 0.0 copy-start.3
  60.7 1.4 %copy-done.3 = f32[2,128,2048]{2,1,0:T(8,128)} copy-done((f32[2,128,2048]{2,1,0:T(8,128)}, f32[2,128,2048]{2,1,0:T(8,128)S(1)}, u32[]{:S(2)}) %copy-start.3) | copy-done | bytes 2097176
  62.0 1.5 %collective-permute-start.5 = (f32[16,128]{1,0:T(8,128)S(1)}, f32[16,128]{1,0:T(8,128)S(1)}, u32[]{:S(2)}, u32[]{:S(2)}) collective-permute-start(f32[16,128]{1,0:T(8,128)S(1)} %get-tuple-element.48.my_sums_ref), channel_id=1, source_target_pairs={{0,1},{1,0},{2,3},{3,2},{4,5},{5,4},{6,7},{7,6},{8,9},{9,8},{10,11... | collective-permute-start | bytes 24584 | tf_op jit(solution)/shard_map/ppermute | solution.py:481
  63.5 1.0 %collective-permute-done.5.their_sums_ref = f32[16,128]{1,0:T(8,128)S(1)} collective-permute-done((f32[16,128]{1,0:T(8,128)S(1)}, f32[16,128]{1,0:T(8,128)S(1)}, u32[]{:S(2)}, u32[]{:S(2)}) %collective-permute-start.5) | collective-permute-done | bytes 8224 | tf_op jit(solution)/shard_map/ppermute | solution.py:481
  64.5 0.0 copy-start.4
  64.5 1.6 %copy-done.4 = f32[2,128,2048]{2,1,0:T(8,128)S(1)} copy-done((f32[2,128,2048]{2,1,0:T(8,128)S(1)}, f32[2,128,2048]{2,1,0:T(8,128)}, u32[]{:S(2)}) %copy-start.4) | copy-done | bytes 2097176
  66.1 0.0 copy-start.7
  66.1 1.2 %copy-done.7 = bf16[2,128,2048]{2,1,0:T(8,128)(2,1)S(1)} copy-done((bf16[2,128,2048]{2,1,0:T(8,128)(2,1)S(1)}, bf16[2,128,2048]{2,1,0:T(8,128)(2,1)}, u32[]{:S(2)}) %copy-start.7) | copy-done | bytes 1048600
  67.4 5.5 %shard_map.95 = (bf16[2,128,2048]{2,1,0:T(8,128)(2,1)}, bf16[2,2,128,2048]{3,2,1,0:T(8,128)(2,1)S(1)}, bf16[8,2,128,128]{3,2,1,0:T(8,128)(2,1)S(1)}) custom-call(s32[1]{0:T(128)} %bitcast.odd_ref, s32[2]{0:T(128)S(1)} %bitcast.35, f32[2,128,2048]{2,1,0:T(8,128)S(1)} %copy-done.4, bf16[2,128,2048]{2,1,0:T(8,128)(2,1)S(1)} %copy-done.7, ...), custom_call_target="tpu_custom_call" | custom-call | flops 1024 | bytes 1024 | tf_op jit(solution)/shard_map/pallas_call | solution.py:497
  72.8 6.3 %collective-permute-start.10 = (bf16[8,2,128,128]{3,2,1,0:T(8,128)(2,1)S(1)}, bf16[8,2,128,128]{3,2,1,0:T(8,128)(2,1)S(1)}, u32[]{:S(2)}, u32[]{:S(2)}) collective-permute-start(bf16[8,2,128,128]{3,2,1,0:T(8,128)(2,1)S(1)} %get-tuple-element.54), channel_id=1, source_target_pairs={{2,4},{6,8},{10,12},{14,16},{18,20},{22,24},{26,28},{4,2},{8,6},{1... | collective-permute-start | bytes 1572872 | tf_op jit(solution)/shard_map/ppermute | solution.py:564
  79.1 2.6 %shard_map.96 = bf16[6,2,128,128]{3,2,1,0:T(8,128)(2,1)S(1)} custom-call(s32[1]{0:T(128)} %bitcast.odd_ref, bf16[14,2,128,128]{3,2,1,0:T(8,128)(2,1)S(1)} %bitcast.18, bf16[14,2,128,128]{3,2,1,0:T(8,128)(2,1)S(1)} %bitcast.30, bf16[2,2,128,2048]{3,2,1,0:T(8,128)(2,1)S(1)} %get-tuple-element.50.both_ref), custom_call_target="tpu_custom_call" | custom-call | flops 1024 | bytes 1024 | tf_op jit(solution)/shard_map/pallas_call | solution.py:497
  81.7 1.9 %collective-permute-start.6 = (bf16[6,2,128,128]{3,2,1,0:T(8,128)(2,1)S(1)}, bf16[6,2,128,128]{3,2,1,0:T(8,128)(2,1)S(1)}, u32[]{:S(2)}, u32[]{:S(2)}) collective-permute-start(bf16[6,2,128,128]{3,2,1,0:T(8,128)(2,1)S(1)} %shard_map.96), channel_id=1, source_target_pairs={{2,4},{6,8},{10,12},{14,16},{18,20},{22,24},{26,28},{4,2},{8,6},{1... | collective-permute-start | bytes 1179656 | tf_op jit(solution)/shard_map/ppermute | solution.py:564
  83.6 6.3 %shard_map.97 = (bf16[5,2,128,128]{3,2,1,0:T(8,128)(2,1)S(1)}, bf16[5,2,128,128]{3,2,1,0:T(8,128)(2,1)S(1)}, bf16[4,2,128,128]{3,2,1,0:T(8,128)(2,1)S(1)}) custom-call(s32[1]{0:T(128)} %bitcast.odd_ref, bf16[14,2,128,128]{3,2,1,0:T(8,128)(2,1)S(1)} %bitcast.19, bf16[14,2,128,128]{3,2,1,0:T(8,128)(2,1)S(1)} %bitcast.31, ...), custom_call_target="tpu_custom_call" | custom-call | flops 1024 | bytes 1024 | tf_op jit(solution)/shard_map/pallas_call | solution.py:497
  90.0 0.1 collective-permute-start.7
  90.1 0.5 collective-permute-start.8
  90.6 0.1 collective-permute-start.9
  90.6 4.2 %collective-permute-done.10.refs_0_ = bf16[8,2,128,128]{3,2,1,0:T(8,128)(2,1)S(1)} collective-permute-done((bf16[8,2,128,128]{3,2,1,0:T(8,128)(2,1)S(1)}, bf16[8,2,128,128]{3,2,1,0:T(8,128)(2,1)S(1)}, u32[]{:S(2)}, u32[]{:S(2)}) %collective-permute-start.10) | collective-permute-done | bytes 524320 | tf_op jit(solution)/shard_map/ppermute | solution.py:564
  94.8 1.1 %shard_map.98 = (f32[14,2,128,128]{3,2,1,0:T(8,128)}, f32[14,2,128,128]{3,2,1,0:T(8,128)}) custom-call(s32[1]{0:T(128)} %bitcast.odd_ref, bf16[8,2,128,128]{3,2,1,0:T(8,128)(2,1)S(1)} %collective-permute-done.10.refs_0_), custom_call_target="tpu_custom_call" | custom-call | flops 1024 | bytes 1024 | tf_op jit(solution)/shard_map/pallas_call | solution.py:497
  95.9 0.0 collective-permute-done.9.refs_2_
  95.9 0.0 collective-permute-done.7.refs_0_
  95.9 0.0 collective-permute-done.8.refs_1_
  95.9 1.3 %shard_map.99 = (f32[14,2,128,128]{3,2,1,0:T(8,128)}, f32[14,2,128,128]{3,2,1,0:T(8,128)}) custom-call(s32[1]{0:T(128)} %bitcast.odd_ref, bf16[5,2,128,128]{3,2,1,0:T(8,128)(2,1)S(1)} %collective-permute-done.7.refs_0_, bf16[5,2,128,128]{3,2,1,0:T(8,128)(2,1)S(1)} %collective-permute-done.8.refs_1_, ...), custom_call_target="tpu_custom_call", output_to_operand_aliasing={{0}: (4, {}), {1}: (5, {})} | custom-call | flops 1024 | bytes 1024 | tf_op jit(solution)/shard_map/pallas_call | solution.py:497
  97.3 1.7 %collective-permute-done.6.refs_0_ = bf16[6,2,128,128]{3,2,1,0:T(8,128)(2,1)S(1)} collective-permute-done((bf16[6,2,128,128]{3,2,1,0:T(8,128)(2,1)S(1)}, bf16[6,2,128,128]{3,2,1,0:T(8,128)(2,1)S(1)}, u32[]{:S(2)}, u32[]{:S(2)}) %collective-permute-start.6) | collective-permute-done | bytes 393248 | tf_op jit(solution)/shard_map/ppermute | solution.py:564
  99.0 1.0 shard_map.100
Async XLA Ops:
  0.6 5.5 %copy-start = (bf16[1,14,2,128,128]{4,3,2,1,0:T(8,128)(2,1)S(1)}, bf16[1,14,2,128,128]{4,3,2,1,0:T(8,128)(2,1)}, u32[]{:S(2)}) copy-start(bf16[1,14,2,128,128]{4,3,2,1,0:T(8,128)(2,1)} %param.7) | copy-start | bytes 2752516
  0.6 1.3 %copy-start.1 = (bf16[1,2,128,2048]{3,2,1,0:T(8,128)(2,1)S(1)}, bf16[1,2,128,2048]{3,2,1,0:T(8,128)(2,1)}, u32[]{:S(2)}) copy-start(bf16[1,2,128,2048]{3,2,1,0:T(8,128)(2,1)} %param.6) | copy-start | bytes 3145732
  1.9 3.7 %copy-start.8 = (bf16[1,14,16,16]{3,2,1,0:T(8,128)(2,1)S(1)}, bf16[1,14,16,16]{3,2,1,0:T(8,128)(2,1)}, u32[]{:S(2)}) copy-start(bf16[1,14,16,16]{3,2,1,0:T(8,128)(2,1)} %param.9) | copy-start | bytes 21508
  1.9 4.0 %copy-start.10 = (s32[1,14,4]{1,2,0:T(4,128)S(1)}, s32[1,14,4]{1,2,0:T(4,128)}, u32[]{:S(2)}) copy-start(s32[1,14,4]{1,2,0:T(4,128)} %param.10) | copy-start | bytes 676
  2.0 4.2 %copy-start.2 = (bf16[1,2,128,2048]{3,2,1,0:T(8,128)(2,1)S(1)}, bf16[1,2,128,2048]{3,2,1,0:T(8,128)(2,1)}, u32[]{:S(2)}) copy-start(bf16[1,2,128,2048]{3,2,1,0:T(8,128)(2,1)} %param.6) | copy-start | bytes 3145732
  2.0 4.2 %copy-start.5 = (bf16[1,14,2,128,128]{4,3,2,1,0:T(8,128)(2,1)S(1)}, bf16[1,14,2,128,128]{4,3,2,1,0:T(8,128)(2,1)}, u32[]{:S(2)}) copy-start(bf16[1,14,2,128,128]{4,3,2,1,0:T(8,128)(2,1)} %param.8) | copy-start | bytes 2752516
  2.8 14.0 %collective-permute-start.1 = (bf16[1,128,2048]{2,1,0:T(8,128)(2,1)}, bf16[1,128,2048]{2,1,0:T(8,128)(2,1)}, u32[]{:S(2)}, u32[]{:S(2)}) collective-permute-start(bf16[1,128,2048]{2,1,0:T(8,128)(2,1)} %shard_map.88), channel_id=1, source_target_pairs={{0,1},{1,0},{2,3},{3,2},{4,5},{5,4},{6,7},{7,6},{8,9},{9,8},{10,11... | collective-permute-start | bytes 1572872 | tf_op jit(solution)/shard_map/ppermute | solution.py:481
  5.7 22.4 %collective-permute-start = (bf16[1,128,2048]{2,1,0:T(8,128)(2,1)}, bf16[1,128,2048]{2,1,0:T(8,128)(2,1)}, u32[]{:S(2)}, u32[]{:S(2)}) collective-permute-start(bf16[1,128,2048]{2,1,0:T(8,128)(2,1)} %shard_map.87), channel_id=1, source_target_pairs={{0,1},{1,0},{2,3},{3,2},{4,5},{5,4},{6,7},{7,6},{8,9},{9,8},{10,11... | collective-permute-start | bytes 1572872 | tf_op jit(solution)/shard_map/ppermute | solution.py:481
  21.6 6.5 %collective-permute-start.2 = (f32[8,128]{1,0:T(8,128)S(1)}, f32[8,128]{1,0:T(8,128)S(1)}, u32[]{:S(2)}, u32[]{:S(2)}) collective-permute-start(f32[8,128]{1,0:T(8,128)S(1)} %get-tuple-element.39.mine_ref), channel_id=1, source_target_pairs={{0,1},{1,0},{2,3},{3,2},{4,5},{5,4},{6,7},{7,6},{8,9},{9,8},{10,11... | collective-permute-start | bytes 12296 | tf_op jit(solution)/shard_map/ppermute | solution.py:481
  31.4 14.1 %collective-permute-start.4 = (bf16[1,128,2048]{2,1,0:T(8,128)(2,1)S(1)}, bf16[1,128,2048]{2,1,0:T(8,128)(2,1)S(1)}, u32[]{:S(2)}, u32[]{:S(2)}) collective-permute-start(bf16[1,128,2048]{2,1,0:T(8,128)(2,1)S(1)} %get-tuple-element.41.refs_0_), channel_id=1, source_target_pairs={{0,1},{1,0},{2,3},{3,2},{4,5},{5,4},{6,7},{7,6},{8,9},{9,8},{10,11... | collective-permute-start | bytes 1572872 | tf_op jit(solution)/shard_map/ppermute | solution.py:481
  33.5 2.6 %copy-start.9 = (s32[1,2]{1,0:T(1,128)S(1)}, s32[1,2]{1,0:T(1,128)}, u32[]{:S(2)}) copy-start(s32[1,2]{1,0:T(1,128)} %param.11) | copy-start | bytes 28
  36.0 20.1 %copy-start.6 = (bf16[2,128,2048]{2,1,0:T(8,128)(2,1)}, bf16[2,128,2048]{2,1,0:T(8,128)(2,1)S(1)}, u32[]{:S(2)}) copy-start(bf16[2,128,2048]{2,1,0:T(8,128)(2,1)S(1)} %get-tuple-element.43.guess_ref) | copy-start | bytes 3145732
  36.0 20.1 %collective-permute-start.3 = (bf16[1,128,2048]{2,1,0:T(8,128)(2,1)S(1)}, bf16[1,128,2048]{2,1,0:T(8,128)(2,1)S(1)}, u32[]{:S(2)}, u32[]{:S(2)}) collective-permute-start(bf16[1,128,2048]{2,1,0:T(8,128)(2,1)S(1)} %get-tuple-element.42), channel_id=1, source_target_pairs={{0,1},{1,0},{2,3},{3,2},{4,5},{5,4},{6,7},{7,6},{8,9},{9,8},{10,11... | collective-permute-start | bytes 1572872 | tf_op jit(solution)/shard_map/ppermute | solution.py:481
  60.7 1.4 %copy-start.3 = (f32[2,128,2048]{2,1,0:T(8,128)}, f32[2,128,2048]{2,1,0:T(8,128)S(1)}, u32[]{:S(2)}) copy-start(f32[2,128,2048]{2,1,0:T(8,128)S(1)} %get-tuple-element.47.kept_ref) | copy-start | bytes 6291460
  62.0 2.5 %collective-permute-start.5 = (f32[16,128]{1,0:T(8,128)S(1)}, f32[16,128]{1,0:T(8,128)S(1)}, u32[]{:S(2)}, u32[]{:S(2)}) collective-permute-start(f32[16,128]{1,0:T(8,128)S(1)} %get-tuple-element.48.my_sums_ref), channel_id=1, source_target_pairs={{0,1},{1,0},{2,3},{3,2},{4,5},{5,4},{6,7},{7,6},{8,9},{9,8},{10,11... | collective-permute-start | bytes 24584 | tf_op jit(solution)/shard_map/ppermute | solution.py:481
  64.5 1.6 %copy-start.4 = (f32[2,128,2048]{2,1,0:T(8,128)S(1)}, f32[2,128,2048]{2,1,0:T(8,128)}, u32[]{:S(2)}) copy-start(f32[2,128,2048]{2,1,0:T(8,128)} %copy-done.3) | copy-start | bytes 6291460
  66.1 1.2 %copy-start.7 = (bf16[2,128,2048]{2,1,0:T(8,128)(2,1)S(1)}, bf16[2,128,2048]{2,1,0:T(8,128)(2,1)}, u32[]{:S(2)}) copy-start(bf16[2,128,2048]{2,1,0:T(8,128)(2,1)} %copy-done.6) | copy-start | bytes 3145732
  72.8 22.0 %collective-permute-start.10 = (bf16[8,2,128,128]{3,2,1,0:T(8,128)(2,1)S(1)}, bf16[8,2,128,128]{3,2,1,0:T(8,128)(2,1)S(1)}, u32[]{:S(2)}, u32[]{:S(2)}) collective-permute-start(bf16[8,2,128,128]{3,2,1,0:T(8,128)(2,1)S(1)} %get-tuple-element.54), channel_id=1, source_target_pairs={{2,4},{6,8},{10,12},{14,16},{18,20},{22,24},{26,28},{4,2},{8,6},{1... | collective-permute-start | bytes 1572872 | tf_op jit(solution)/shard_map/ppermute | solution.py:564
  81.7 17.3 %collective-permute-start.6 = (bf16[6,2,128,128]{3,2,1,0:T(8,128)(2,1)S(1)}, bf16[6,2,128,128]{3,2,1,0:T(8,128)(2,1)S(1)}, u32[]{:S(2)}, u32[]{:S(2)}) collective-permute-start(bf16[6,2,128,128]{3,2,1,0:T(8,128)(2,1)S(1)} %shard_map.96), channel_id=1, source_target_pairs={{2,4},{6,8},{10,12},{14,16},{18,20},{22,24},{26,28},{4,2},{8,6},{1... | collective-permute-start | bytes 1179656 | tf_op jit(solution)/shard_map/ppermute | solution.py:564
  90.0 5.9 %collective-permute-start.7 = (bf16[5,2,128,128]{3,2,1,0:T(8,128)(2,1)S(1)}, bf16[5,2,128,128]{3,2,1,0:T(8,128)(2,1)S(1)}, u32[]{:S(2)}, u32[]{:S(2)}) collective-permute-start(bf16[5,2,128,128]{3,2,1,0:T(8,128)(2,1)S(1)} %get-tuple-element.51), channel_id=1, source_target_pairs={{0,2},{4,6},{8,10},{12,14},{16,18},{20,22},{24,26},{28,30},{2,0},{... | collective-permute-start | bytes 983048 | tf_op jit(solution)/shard_map/ppermute | solution.py:564
  90.1 5.9 %collective-permute-start.8 = (bf16[5,2,128,128]{3,2,1,0:T(8,128)(2,1)S(1)}, bf16[5,2,128,128]{3,2,1,0:T(8,128)(2,1)S(1)}, u32[]{:S(2)}, u32[]{:S(2)}) collective-permute-start(bf16[5,2,128,128]{3,2,1,0:T(8,128)(2,1)S(1)} %get-tuple-element.52), channel_id=1, source_target_pairs={{0,2},{4,6},{8,10},{12,14},{16,18},{20,22},{24,26},{28,30},{2,0},{... | collective-permute-start | bytes 983048 | tf_op jit(solution)/shard_map/ppermute | solution.py:564
  90.6 5.4 %collective-permute-start.9 = (bf16[4,2,128,128]{3,2,1,0:T(8,128)(2,1)S(1)}, bf16[4,2,128,128]{3,2,1,0:T(8,128)(2,1)S(1)}, u32[]{:S(2)}, u32[]{:S(2)}) collective-permute-start(bf16[4,2,128,128]{3,2,1,0:T(8,128)(2,1)S(1)} %get-tuple-element.53), channel_id=1, source_target_pairs={{0,2},{4,6},{8,10},{12,14},{16,18},{20,22},{24,26},{28,30},{2,0},{... | collective-permute-start | bytes 786440 | tf_op jit(solution)/shard_map/ppermute | solution.py:564

commit v7 on v6

--- a/solution.py
+++ b/solution.py
@@ -19,7 +19,7 @@
 HBM = pl.BlockSpec(memory_space=pltpu.HBM)
 SMEM = pl.BlockSpec(memory_space=pltpu.SMEM)
 COST = pl.CostEstimate(flops=1024, bytes_accessed=1024, transcendentals=0)
-PARAMS = pltpu.CompilerParams(vmem_limit_bytes=32 * 1024 * 1024)
+PARAMS = pltpu.CompilerParams(vmem_limit_bytes=20 * 1024 * 1024)
 
 
 def dot(left, right):

time: 101 us -> 101 us (level); the launches traced: 100 us -> 98.8 us
  waiting for transfers between devices: 18.8 us -> 12.9 us
  Pallas kernels: 59.1 us -> 62.5 us
    ppermute x6, waiting for transfers between devices: 12.9 us -> 7.25 us  [trade(): return lax.ppermute(value, 'blk', swap)]
    pallas_call x16, Pallas kernels: 59.1 us -> 62.5 us  [call(): pl.pallas_call(body, in_specs=specs, out_specs=out_specs or jax.tree.map(...]
    ppermute x6, starting transfers between devices: 6.72 us -> 8.97 us  [trade(): return lax.ppermute(value, 'blk', swap)]
    ppermute x5, starting transfers between devices: 8.83 us -> 7.68 us  [swapped(): return lax.ppermute(value, 'seg', pairs + [(t, s) for s, t in pairs])]
  transfers between devices with their start and end apart: 11 -> 11, of which waited for: 7 -> 6; matrix products, arithmetic and copies ran while one was open for 0% -> 0% of each run, Pallas kernels for 44% -> 50%
where the time goes in v7:
time: 101 us; the launch traced here: 98.8 us
  Pallas kernels  62.5 us (62%)
  starting transfers between devices  16.6 us (16%)
  waiting for transfers between devices  12.9 us (13%)
  local copies, waits for them, and re-layouts  5.59 us (6%)
  between operations  1.06 us (1%)
    pallas_call x16, Pallas kernels, call(): pl.pallas_call(body, in_specs=specs, out_specs=out_specs or jax.tree.map(...  62.5 us
    ppermute x6, starting transfers between devices, trade(): return lax.ppermute(value, 'blk', swap)  8.97 us
    ppermute x5, starting transfers between devices, swapped(): return lax.ppermute(value, 'seg', pairs + [(t, s) for s, t in pairs])  7.68 us
    ppermute x6, waiting for transfers between devices, trade(): return lax.ppermute(value, 'blk', swap)  7.25 us
    ppermute x5, waiting for transfers between devices, swapped(): return lax.ppermute(value, 'seg', pairs + [(t, s) for s, t in pairs])  5.69 us
    unnamed x22, local copies, waits for them, and re-layouts  5.5 us
  transfers between devices with their start and end apart: 11, of which 6 were waited for; matrix products, arithmetic and copies ran while one was open for 0% of the time, Pallas kernels for 50%

profile of v7, /device:TPU:1, one launch (start us, length us, event | category | flops | bytes accessed | tf_op | source)
XLA Modules:
  0.0 98.8 jit_solution(17412977008627873024)
XLA Ops:
  0.6 0.0 copy-start
  0.6 0.0 copy-start.1
  0.7 1.3 %copy-done.1 = bf16[1,2,128,2048]{3,2,1,0:T(8,128)(2,1)S(1)} copy-done((bf16[1,2,128,2048]{3,2,1,0:T(8,128)(2,1)S(1)}, bf16[1,2,128,2048]{3,2,1,0:T(8,128)(2,1)}, u32[]{:S(2)}) %copy-start.1) | copy-done | bytes 1048600
  1.9 0.0 copy-start.8
  1.9 0.0 copy-start.10
  2.0 0.0 copy-start.2
  2.0 0.0 copy-start.5
  2.0 0.8 shard_map.88
  2.8 2.0 %collective-permute-start.1 = (bf16[1,128,2048]{2,1,0:T(8,128)(2,1)}, bf16[1,128,2048]{2,1,0:T(8,128)(2,1)}, u32[]{:S(2)}, u32[]{:S(2)}) collective-permute-start(bf16[1,128,2048]{2,1,0:T(8,128)(2,1)} %shard_map.88), channel_id=1, source_target_pairs={{0,1},{1,0},{2,3},{3,2},{4,5},{5,4},{6,7},{7,6},{8,9},{9,8},{10,11... | collective-permute-start | bytes 1572872 | tf_op jit(solution)/shard_map/ppermute | solution.py:481
  4.8 0.8 shard_map.87
  5.7 0.0 collective-permute-start
  5.7 0.0 copy-done.8
  5.7 0.3 shard_map.85.kron_ref
  5.9 0.0 copy-done.10
  6.0 0.1 copy.18
  6.0 0.1 negate_select_fusion.map_ref
  6.1 0.0 copy-done
  6.2 0.0 copy-done.2
  6.2 0.0 copy-done.5
  6.2 12.7 %shard_map.86 = (bf16[14,2,128,128]{3,2,1,0:T(8,128)(2,1)S(1)}, f32[2,128,2048]{2,1,0:T(8,128)S(1)}, f32[8,128]{1,0:T(8,128)S(1)}, s32[14,2]{1,0:T(8,128)S(1)}, s32[14,2]{1,0:T(8,128)S(1)}, /*index=5*/s32[2]{0:T(128)S(1)}) custom-call(s32[14,4]{1,0:T(8,128)S(1)} %negate_select_fusion.map_ref, bf16[14,128,128]{2,1,0:T(8,128)(2,1)S(1)} %shard_map.85.kron_ref, ...), custom_call_target="tpu_custom_call" | custom-call | flops 1024 | bytes 1024 | tf_op jit(solution)/shard_map/pallas_call | solution.py:497
  18.8 0.0 collective-permute-done.1.other_ref
  18.9 4.8 %shard_map.89 = (f32[2,128,2048]{2,1,0:T(8,128)S(1)}, f32[8,128]{1,0:T(8,128)S(1)}) custom-call(s32[14,2]{1,0:T(8,128)S(1)} %get-tuple-element.33.rel_ref, bf16[14,128,128]{2,1,0:T(8,128)(2,1)S(1)} %shard_map.85.kron_ref, bf16[1,128,2048]{2,1,0:T(8,128)(2,1)} %collective-permute-done.1.other_ref, ...), custom_call_target="tpu_custom_call", output_to_operand_aliasing={{0}: (5, {})} | custom-call | flops 1024 | bytes 1024 | tf_op jit(solution)/shard_map/pallas_call | solution.py:497
  23.7 0.1 collective-permute-start.2
  23.8 4.3 %collective-permute-done.other_ref = bf16[1,128,2048]{2,1,0:T(8,128)(2,1)} collective-permute-done((bf16[1,128,2048]{2,1,0:T(8,128)(2,1)}, bf16[1,128,2048]{2,1,0:T(8,128)(2,1)}, u32[]{:S(2)}, u32[]{:S(2)}) %collective-permute-start) | collective-permute-done | bytes 524320 | tf_op jit(solution)/shard_map/ppermute | solution.py:481
  28.0 0.1 collective-permute-done.2.theirs_ref
  28.1 2.5 %shard_map.90 = (f32[2,128,2048]{2,1,0:T(8,128)S(1)}, bf16[1,128,2048]{2,1,0:T(8,128)(2,1)S(1)}) custom-call(s32[14,2]{1,0:T(8,128)S(1)} %get-tuple-element.33.rel_ref, s32[2]{0:T(128)S(1)} %get-tuple-element.34.order_ref, bf16[14,128,128]{2,1,0:T(8,128)(2,1)S(1)} %shard_map.85.kron_ref, ...), custom_call_target="tpu_custom_call", output_to_operand_aliasing={{0}: (6, {})} | custom-call | flops 1024 | bytes 1024 | tf_op jit(solution)/shard_map/pallas_call | solution.py:497
  30.6 2.1 %collective-permute-start.4 = (bf16[1,128,2048]{2,1,0:T(8,128)(2,1)S(1)}, bf16[1,128,2048]{2,1,0:T(8,128)(2,1)S(1)}, u32[]{:S(2)}, u32[]{:S(2)}) collective-permute-start(bf16[1,128,2048]{2,1,0:T(8,128)(2,1)S(1)} %get-tuple-element.41.refs_0_), channel_id=1, source_target_pairs={{0,1},{1,0},{2,3},{3,2},{4,5},{5,4},{6,7},{7,6},{8,9},{9,8},{10,11... | collective-permute-start | bytes 1572872 | tf_op jit(solution)/shard_map/ppermute | solution.py:481
  32.6 0.0 copy-start.9
  32.6 2.5 %shard_map.91 = (f32[2,128,2048]{2,1,0:T(8,128)S(1)}, bf16[1,128,2048]{2,1,0:T(8,128)(2,1)S(1)}, bf16[2,128,2048]{2,1,0:T(8,128)(2,1)S(1)}) custom-call(s32[14,2]{1,0:T(8,128)S(1)} %get-tuple-element.33.rel_ref, s32[2]{0:T(128)S(1)} %get-tuple-element.34.order_ref, bf16[14,128,128]{2,1,0:T(8,128)(2,1)S(1)} %shard_map.85.kron_ref, ...), custom_call_target="tpu_custom_call", output_to_operand_aliasing={{0}: (6, {})} | custom-call | flops 1024 | bytes 1024 | tf_op jit(solution)/shard_map/pallas_call | solution.py:497
  35.1 0.0 copy-start.6
  35.1 0.9 collective-permute-start.3
  36.0 0.0 copy-done.9
  36.0 11.9 %shard_map.92 = (f32[2,128,2048]{2,1,0:T(8,128)S(1)}, f32[8,128]{1,0:T(8,128)S(1)}) custom-call(s32[14,2]{1,0:T(8,128)S(1)} %get-tuple-element.32.rel_ref, s32[2]{0:T(128)S(1)} %bitcast.33, bf16[14,128,128]{2,1,0:T(8,128)(2,1)S(1)} %shard_map.85.kron_ref, bf16[2,128,2048]{2,1,0:T(8,128)(2,1)S(1)} %get-tuple-element.43.guess_ref, ...), custom_call_target="tpu_custom_call" | custom-call | flops 1024 | bytes 1024 | tf_op jit(solution)/shard_map/pallas_call | solution.py:497
  48.0 0.0 collective-permute-done.4.other_ref
  48.0 4.6 %shard_map.93.before_ref = f32[2,128,2048]{2,1,0:T(8,128)S(1)} custom-call(s32[14,2]{1,0:T(8,128)S(1)} %get-tuple-element.32.rel_ref, bf16[14,128,128]{2,1,0:T(8,128)(2,1)S(1)} %shard_map.85.kron_ref, bf16[1,128,2048]{2,1,0:T(8,128)(2,1)S(1)} %collective-permute-done.4.other_ref, ...), custom_call_target="tpu_custom_call", output_to_operand_aliasing={{}: (5, {})} | custom-call | flops 1024 | bytes 1024 | tf_op jit(solution)/shard_map/pallas_call | solution.py:497
  52.6 1.8 %collective-permute-done.3.other_ref = bf16[1,128,2048]{2,1,0:T(8,128)(2,1)S(1)} collective-permute-done((bf16[1,128,2048]{2,1,0:T(8,128)(2,1)S(1)}, bf16[1,128,2048]{2,1,0:T(8,128)(2,1)S(1)}, u32[]{:S(2)}, u32[]{:S(2)}) %collective-permute-start.3) | collective-permute-done | bytes 524320 | tf_op jit(solution)/shard_map/ppermute | solution.py:481
  54.5 0.0 copy-done.6
  54.5 3.8 %shard_map.94 = (f32[2,128,2048]{2,1,0:T(8,128)S(1)}, f32[16,128]{1,0:T(8,128)S(1)}) custom-call(s32[14,2]{1,0:T(8,128)S(1)} %get-tuple-element.32.rel_ref, s32[2]{0:T(128)S(1)} %bitcast.34, bf16[14,128,128]{2,1,0:T(8,128)(2,1)S(1)} %shard_map.85.kron_ref, ...), custom_call_target="tpu_custom_call", output_to_operand_aliasing={{0}: (6, {})} | custom-call | flops 1024 | bytes 1024 | tf_op jit(solution)/shard_map/pallas_call | solution.py:497
  58.3 0.0 copy-start.3
  58.3 1.4 %copy-done.3 = f32[2,128,2048]{2,1,0:T(8,128)} copy-done((f32[2,128,2048]{2,1,0:T(8,128)}, f32[2,128,2048]{2,1,0:T(8,128)S(1)}, u32[]{:S(2)}) %copy-start.3) | copy-done | bytes 2097176
  59.6 3.9 %collective-permute-start.5 = (f32[16,128]{1,0:T(8,128)S(1)}, f32[16,128]{1,0:T(8,128)S(1)}, u32[]{:S(2)}, u32[]{:S(2)}) collective-permute-start(f32[16,128]{1,0:T(8,128)S(1)} %get-tuple-element.48.my_sums_ref), channel_id=1, source_target_pairs={{0,1},{1,0},{2,3},{3,2},{4,5},{5,4},{6,7},{7,6},{8,9},{9,8},{10,11... | collective-permute-start | bytes 24584 | tf_op jit(solution)/shard_map/ppermute | solution.py:481
  63.5 1.0 %collective-permute-done.5.their_sums_ref = f32[16,128]{1,0:T(8,128)S(1)} collective-permute-done((f32[16,128]{1,0:T(8,128)S(1)}, f32[16,128]{1,0:T(8,128)S(1)}, u32[]{:S(2)}, u32[]{:S(2)}) %collective-permute-start.5) | collective-permute-done | bytes 8224 | tf_op jit(solution)/shard_map/ppermute | solution.py:481
  64.5 0.0 copy-start.4
  64.5 1.6 %copy-done.4 = f32[2,128,2048]{2,1,0:T(8,128)S(1)} copy-done((f32[2,128,2048]{2,1,0:T(8,128)S(1)}, f32[2,128,2048]{2,1,0:T(8,128)}, u32[]{:S(2)}) %copy-start.4) | copy-done | bytes 2097176
  66.1 0.0 copy-start.7
  66.1 1.2 %copy-done.7 = bf16[2,128,2048]{2,1,0:T(8,128)(2,1)S(1)} copy-done((bf16[2,128,2048]{2,1,0:T(8,128)(2,1)S(1)}, bf16[2,128,2048]{2,1,0:T(8,128)(2,1)}, u32[]{:S(2)}) %copy-start.7) | copy-done | bytes 1048600
  67.4 5.5 %shard_map.95 = (bf16[2,128,2048]{2,1,0:T(8,128)(2,1)}, bf16[2,2,128,2048]{3,2,1,0:T(8,128)(2,1)S(1)}, bf16[8,2,128,128]{3,2,1,0:T(8,128)(2,1)S(1)}) custom-call(s32[1]{0:T(128)} %bitcast.odd_ref, s32[2]{0:T(128)S(1)} %bitcast.35, f32[2,128,2048]{2,1,0:T(8,128)S(1)} %copy-done.4, bf16[2,128,2048]{2,1,0:T(8,128)(2,1)S(1)} %copy-done.7, ...), custom_call_target="tpu_custom_call" | custom-call | flops 1024 | bytes 1024 | tf_op jit(solution)/shard_map/pallas_call | solution.py:497
  72.8 5.1 %collective-permute-start.10 = (bf16[8,2,128,128]{3,2,1,0:T(8,128)(2,1)S(1)}, bf16[8,2,128,128]{3,2,1,0:T(8,128)(2,1)S(1)}, u32[]{:S(2)}, u32[]{:S(2)}) collective-permute-start(bf16[8,2,128,128]{3,2,1,0:T(8,128)(2,1)S(1)} %get-tuple-element.54), channel_id=1, source_target_pairs={{2,4},{6,8},{10,12},{14,16},{18,20},{22,24},{26,28},{4,2},{8,6},{1... | collective-permute-start | bytes 1572872 | tf_op jit(solution)/shard_map/ppermute | solution.py:564
  77.9 2.6 %shard_map.96 = bf16[6,2,128,128]{3,2,1,0:T(8,128)(2,1)S(1)} custom-call(s32[1]{0:T(128)} %bitcast.odd_ref, bf16[14,2,128,128]{3,2,1,0:T(8,128)(2,1)S(1)} %bitcast.18, bf16[14,2,128,128]{3,2,1,0:T(8,128)(2,1)S(1)} %bitcast.30, bf16[2,2,128,2048]{3,2,1,0:T(8,128)(2,1)S(1)} %get-tuple-element.50.both_ref), custom_call_target="tpu_custom_call" | custom-call | flops 1024 | bytes 1024 | tf_op jit(solution)/shard_map/pallas_call | solution.py:497
  80.6 1.9 %collective-permute-start.6 = (bf16[6,2,128,128]{3,2,1,0:T(8,128)(2,1)S(1)}, bf16[6,2,128,128]{3,2,1,0:T(8,128)(2,1)S(1)}, u32[]{:S(2)}, u32[]{:S(2)}) collective-permute-start(bf16[6,2,128,128]{3,2,1,0:T(8,128)(2,1)S(1)} %shard_map.96), channel_id=1, source_target_pairs={{2,4},{6,8},{10,12},{14,16},{18,20},{22,24},{26,28},{4,2},{8,6},{1... | collective-permute-start | bytes 1179656 | tf_op jit(solution)/shard_map/ppermute | solution.py:564
  82.5 6.3 %shard_map.97 = (bf16[5,2,128,128]{3,2,1,0:T(8,128)(2,1)S(1)}, bf16[5,2,128,128]{3,2,1,0:T(8,128)(2,1)S(1)}, bf16[4,2,128,128]{3,2,1,0:T(8,128)(2,1)S(1)}) custom-call(s32[1]{0:T(128)} %bitcast.odd_ref, bf16[14,2,128,128]{3,2,1,0:T(8,128)(2,1)S(1)} %bitcast.19, bf16[14,2,128,128]{3,2,1,0:T(8,128)(2,1)S(1)} %bitcast.31, ...), custom_call_target="tpu_custom_call" | custom-call | flops 1024 | bytes 1024 | tf_op jit(solution)/shard_map/pallas_call | solution.py:497
  88.8 0.1 collective-permute-start.7
  88.9 0.5 collective-permute-start.8
  89.4 0.1 collective-permute-start.9
  89.5 3.9 %collective-permute-done.10.refs_0_ = bf16[8,2,128,128]{3,2,1,0:T(8,128)(2,1)S(1)} collective-permute-done((bf16[8,2,128,128]{3,2,1,0:T(8,128)(2,1)S(1)}, bf16[8,2,128,128]{3,2,1,0:T(8,128)(2,1)S(1)}, u32[]{:S(2)}, u32[]{:S(2)}) %collective-permute-start.10) | collective-permute-done | bytes 524320 | tf_op jit(solution)/shard_map/ppermute | solution.py:564
  93.4 1.1 %shard_map.98 = (f32[14,2,128,128]{3,2,1,0:T(8,128)}, f32[14,2,128,128]{3,2,1,0:T(8,128)}) custom-call(s32[1]{0:T(128)} %bitcast.odd_ref, bf16[8,2,128,128]{3,2,1,0:T(8,128)(2,1)S(1)} %collective-permute-done.10.refs_0_), custom_call_target="tpu_custom_call" | custom-call | flops 1024 | bytes 1024 | tf_op jit(solution)/shard_map/pallas_call | solution.py:497
  94.5 0.0 collective-permute-done.9.refs_2_
  94.5 0.0 collective-permute-done.7.refs_0_
  94.5 0.0 collective-permute-done.8.refs_1_
  94.6 1.3 %shard_map.99 = (f32[14,2,128,128]{3,2,1,0:T(8,128)}, f32[14,2,128,128]{3,2,1,0:T(8,128)}) custom-call(s32[1]{0:T(128)} %bitcast.odd_ref, bf16[5,2,128,128]{3,2,1,0:T(8,128)(2,1)S(1)} %collective-permute-done.7.refs_0_, bf16[5,2,128,128]{3,2,1,0:T(8,128)(2,1)S(1)} %collective-permute-done.8.refs_1_, ...), custom_call_target="tpu_custom_call", output_to_operand_aliasing={{0}: (4, {}), {1}: (5, {})} | custom-call | flops 1024 | bytes 1024 | tf_op jit(solution)/shard_map/pallas_call | solution.py:497
  95.9 1.7 %collective-permute-done.6.refs_0_ = bf16[6,2,128,128]{3,2,1,0:T(8,128)(2,1)S(1)} collective-permute-done((bf16[6,2,128,128]{3,2,1,0:T(8,128)(2,1)S(1)}, bf16[6,2,128,128]{3,2,1,0:T(8,128)(2,1)S(1)}, u32[]{:S(2)}, u32[]{:S(2)}) %collective-permute-start.6) | collective-permute-done | bytes 393248 | tf_op jit(solution)/shard_map/ppermute | solution.py:564
  97.6 1.0 %shard_map.100 = (f32[14,2,128,128]{3,2,1,0:T(8,128)}, f32[14,2,128,128]{3,2,1,0:T(8,128)}) custom-call(s32[1]{0:T(128)} %bitcast.odd_ref, bf16[6,2,128,128]{3,2,1,0:T(8,128)(2,1)S(1)} %collective-permute-done.6.refs_0_, f32[14,2,128,128]{3,2,1,0:T(8,128)} %get-tuple-element.57.refs_1_, ...), custom_call_target="tpu_custom_call", output_to_operand_aliasing={{0}: (2, {}), {1}: (3, {})} | custom-call | flops 1024 | bytes 1024 | tf_op jit(solution)/shard_map/pallas_call | solution.py:497
Async XLA Ops:
  0.6 5.5 %copy-start = (bf16[1,14,2,128,128]{4,3,2,1,0:T(8,128)(2,1)S(1)}, bf16[1,14,2,128,128]{4,3,2,1,0:T(8,128)(2,1)}, u32[]{:S(2)}) copy-start(bf16[1,14,2,128,128]{4,3,2,1,0:T(8,128)(2,1)} %param.7) | copy-start | bytes 2752516
  0.6 1.3 %copy-start.1 = (bf16[1,2,128,2048]{3,2,1,0:T(8,128)(2,1)S(1)}, bf16[1,2,128,2048]{3,2,1,0:T(8,128)(2,1)}, u32[]{:S(2)}) copy-start(bf16[1,2,128,2048]{3,2,1,0:T(8,128)(2,1)} %param.6) | copy-start | bytes 3145732
  1.9 3.7 %copy-start.8 = (bf16[1,14,16,16]{3,2,1,0:T(8,128)(2,1)S(1)}, bf16[1,14,16,16]{3,2,1,0:T(8,128)(2,1)}, u32[]{:S(2)}) copy-start(bf16[1,14,16,16]{3,2,1,0:T(8,128)(2,1)} %param.9) | copy-start | bytes 21508
  1.9 4.0 %copy-start.10 = (s32[1,14,4]{1,2,0:T(4,128)S(1)}, s32[1,14,4]{1,2,0:T(4,128)}, u32[]{:S(2)}) copy-start(s32[1,14,4]{1,2,0:T(4,128)} %param.10) | copy-start | bytes 676
  2.0 4.2 %copy-start.2 = (bf16[1,2,128,2048]{3,2,1,0:T(8,128)(2,1)S(1)}, bf16[1,2,128,2048]{3,2,1,0:T(8,128)(2,1)}, u32[]{:S(2)}) copy-start(bf16[1,2,128,2048]{3,2,1,0:T(8,128)(2,1)} %param.6) | copy-start | bytes 3145732
  2.0 4.2 %copy-start.5 = (bf16[1,14,2,128,128]{4,3,2,1,0:T(8,128)(2,1)S(1)}, bf16[1,14,2,128,128]{4,3,2,1,0:T(8,128)(2,1)}, u32[]{:S(2)}) copy-start(bf16[1,14,2,128,128]{4,3,2,1,0:T(8,128)(2,1)} %param.8) | copy-start | bytes 2752516
  2.8 16.1 %collective-permute-start.1 = (bf16[1,128,2048]{2,1,0:T(8,128)(2,1)}, bf16[1,128,2048]{2,1,0:T(8,128)(2,1)}, u32[]{:S(2)}, u32[]{:S(2)}) collective-permute-start(bf16[1,128,2048]{2,1,0:T(8,128)(2,1)} %shard_map.88), channel_id=1, source_target_pairs={{0,1},{1,0},{2,3},{3,2},{4,5},{5,4},{6,7},{7,6},{8,9},{9,8},{10,11... | collective-permute-start | bytes 1572872 | tf_op jit(solution)/shard_map/ppermute | solution.py:481
  5.7 22.4 %collective-permute-start = (bf16[1,128,2048]{2,1,0:T(8,128)(2,1)}, bf16[1,128,2048]{2,1,0:T(8,128)(2,1)}, u32[]{:S(2)}, u32[]{:S(2)}) collective-permute-start(bf16[1,128,2048]{2,1,0:T(8,128)(2,1)} %shard_map.87), channel_id=1, source_target_pairs={{0,1},{1,0},{2,3},{3,2},{4,5},{5,4},{6,7},{7,6},{8,9},{9,8},{10,11... | collective-permute-start | bytes 1572872 | tf_op jit(solution)/shard_map/ppermute | solution.py:481
  23.7 4.4 %collective-permute-start.2 = (f32[8,128]{1,0:T(8,128)S(1)}, f32[8,128]{1,0:T(8,128)S(1)}, u32[]{:S(2)}, u32[]{:S(2)}) collective-permute-start(f32[8,128]{1,0:T(8,128)S(1)} %get-tuple-element.39.mine_ref), channel_id=1, source_target_pairs={{0,1},{1,0},{2,3},{3,2},{4,5},{5,4},{6,7},{7,6},{8,9},{9,8},{10,11... | collective-permute-start | bytes 12296 | tf_op jit(solution)/shard_map/ppermute | solution.py:481
  30.6 17.4 %collective-permute-start.4 = (bf16[1,128,2048]{2,1,0:T(8,128)(2,1)S(1)}, bf16[1,128,2048]{2,1,0:T(8,128)(2,1)S(1)}, u32[]{:S(2)}, u32[]{:S(2)}) collective-permute-start(bf16[1,128,2048]{2,1,0:T(8,128)(2,1)S(1)} %get-tuple-element.41.refs_0_), channel_id=1, source_target_pairs={{0,1},{1,0},{2,3},{3,2},{4,5},{5,4},{6,7},{7,6},{8,9},{9,8},{10,11... | collective-permute-start | bytes 1572872 | tf_op jit(solution)/shard_map/ppermute | solution.py:481
  32.6 3.4 %copy-start.9 = (s32[1,2]{1,0:T(1,128)S(1)}, s32[1,2]{1,0:T(1,128)}, u32[]{:S(2)}) copy-start(s32[1,2]{1,0:T(1,128)} %param.11) | copy-start | bytes 28
  35.1 19.4 %copy-start.6 = (bf16[2,128,2048]{2,1,0:T(8,128)(2,1)}, bf16[2,128,2048]{2,1,0:T(8,128)(2,1)S(1)}, u32[]{:S(2)}) copy-start(bf16[2,128,2048]{2,1,0:T(8,128)(2,1)S(1)} %get-tuple-element.43.guess_ref) | copy-start | bytes 3145732
  35.1 19.3 %collective-permute-start.3 = (bf16[1,128,2048]{2,1,0:T(8,128)(2,1)S(1)}, bf16[1,128,2048]{2,1,0:T(8,128)(2,1)S(1)}, u32[]{:S(2)}, u32[]{:S(2)}) collective-permute-start(bf16[1,128,2048]{2,1,0:T(8,128)(2,1)S(1)} %get-tuple-element.42), channel_id=1, source_target_pairs={{0,1},{1,0},{2,3},{3,2},{4,5},{5,4},{6,7},{7,6},{8,9},{9,8},{10,11... | collective-permute-start | bytes 1572872 | tf_op jit(solution)/shard_map/ppermute | solution.py:481
  58.3 1.4 %copy-start.3 = (f32[2,128,2048]{2,1,0:T(8,128)}, f32[2,128,2048]{2,1,0:T(8,128)S(1)}, u32[]{:S(2)}) copy-start(f32[2,128,2048]{2,1,0:T(8,128)S(1)} %get-tuple-element.47.kept_ref) | copy-start | bytes 6291460
  59.6 4.9 %collective-permute-start.5 = (f32[16,128]{1,0:T(8,128)S(1)}, f32[16,128]{1,0:T(8,128)S(1)}, u32[]{:S(2)}, u32[]{:S(2)}) collective-permute-start(f32[16,128]{1,0:T(8,128)S(1)} %get-tuple-element.48.my_sums_ref), channel_id=1, source_target_pairs={{0,1},{1,0},{2,3},{3,2},{4,5},{5,4},{6,7},{7,6},{8,9},{9,8},{10,11... | collective-permute-start | bytes 24584 | tf_op jit(solution)/shard_map/ppermute | solution.py:481
  64.5 1.6 %copy-start.4 = (f32[2,128,2048]{2,1,0:T(8,128)S(1)}, f32[2,128,2048]{2,1,0:T(8,128)}, u32[]{:S(2)}) copy-start(f32[2,128,2048]{2,1,0:T(8,128)} %copy-done.3) | copy-start | bytes 6291460
  66.1 1.2 %copy-start.7 = (bf16[2,128,2048]{2,1,0:T(8,128)(2,1)S(1)}, bf16[2,128,2048]{2,1,0:T(8,128)(2,1)}, u32[]{:S(2)}) copy-start(bf16[2,128,2048]{2,1,0:T(8,128)(2,1)} %copy-done.6) | copy-start | bytes 3145732
  72.8 20.6 %collective-permute-start.10 = (bf16[8,2,128,128]{3,2,1,0:T(8,128)(2,1)S(1)}, bf16[8,2,128,128]{3,2,1,0:T(8,128)(2,1)S(1)}, u32[]{:S(2)}, u32[]{:S(2)}) collective-permute-start(bf16[8,2,128,128]{3,2,1,0:T(8,128)(2,1)S(1)} %get-tuple-element.54), channel_id=1, source_target_pairs={{2,4},{6,8},{10,12},{14,16},{18,20},{22,24},{26,28},{4,2},{8,6},{1... | collective-permute-start | bytes 1572872 | tf_op jit(solution)/shard_map/ppermute | solution.py:564
  80.6 17.1 %collective-permute-start.6 = (bf16[6,2,128,128]{3,2,1,0:T(8,128)(2,1)S(1)}, bf16[6,2,128,128]{3,2,1,0:T(8,128)(2,1)S(1)}, u32[]{:S(2)}, u32[]{:S(2)}) collective-permute-start(bf16[6,2,128,128]{3,2,1,0:T(8,128)(2,1)S(1)} %shard_map.96), channel_id=1, source_target_pairs={{2,4},{6,8},{10,12},{14,16},{18,20},{22,24},{26,28},{4,2},{8,6},{1... | collective-permute-start | bytes 1179656 | tf_op jit(solution)/shard_map/ppermute | solution.py:564
  88.8 5.7 %collective-permute-start.7 = (bf16[5,2,128,128]{3,2,1,0:T(8,128)(2,1)S(1)}, bf16[5,2,128,128]{3,2,1,0:T(8,128)(2,1)S(1)}, u32[]{:S(2)}, u32[]{:S(2)}) collective-permute-start(bf16[5,2,128,128]{3,2,1,0:T(8,128)(2,1)S(1)} %get-tuple-element.51), channel_id=1, source_target_pairs={{0,2},{4,6},{8,10},{12,14},{16,18},{20,22},{24,26},{28,30},{2,0},{... | collective-permute-start | bytes 983048 | tf_op jit(solution)/shard_map/ppermute | solution.py:564
  88.9 5.6 %collective-permute-start.8 = (bf16[5,2,128,128]{3,2,1,0:T(8,128)(2,1)S(1)}, bf16[5,2,128,128]{3,2,1,0:T(8,128)(2,1)S(1)}, u32[]{:S(2)}, u32[]{:S(2)}) collective-permute-start(bf16[5,2,128,128]{3,2,1,0:T(8,128)(2,1)S(1)} %get-tuple-element.52), channel_id=1, source_target_pairs={{0,2},{4,6},{8,10},{12,14},{16,18},{20,22},{24,26},{28,30},{2,0},{... | collective-permute-start | bytes 983048 | tf_op jit(solution)/shard_map/ppermute | solution.py:564
  89.4 5.1 %collective-permute-start.9 = (bf16[4,2,128,128]{3,2,1,0:T(8,128)(2,1)S(1)}, bf16[4,2,128,128]{3,2,1,0:T(8,128)(2,1)S(1)}, u32[]{:S(2)}, u32[]{:S(2)}) collective-permute-start(bf16[4,2,128,128]{3,2,1,0:T(8,128)(2,1)S(1)} %get-tuple-element.53), channel_id=1, source_target_pairs={{0,2},{4,6},{8,10},{12,14},{16,18},{20,22},{24,26},{28,30},{2,0},{... | collective-permute-start | bytes 786440 | tf_op jit(solution)/shard_map/ppermute | solution.py:564

commit v8 on v7

--- a/solution.py
+++ b/solution.py
@@ -191,8 +191,8 @@
 
 
 def first_local(
-    map_ref, kron_ref, x_ref, left_ref, right_ref,
-    right_t_ref, image_ref, sums_ref, rel_ref, arrived_ref, order_ref,
+    map_ref, odd_ref, kron_ref, x_ref, left_ref, right_ref,
+    right_t_ref, image_ref, sums_ref, crossing_ref, inside_ref, rel_ref, arrived_ref, order_ref,
     turned_ref, mixed_ref, *lists,
 ):
     choose_order(map_ref, rel_ref, arrived_ref, order_ref)
@@ -201,7 +201,10 @@
     def turn(n, carry):
         for k in range(2):
             for b in range(dests):
-                right_t_ref[2 * n + k, b] = right_ref[2 * n + k, b].T
+                one_left, one_right = left_ref[2 * n + k, b], right_ref[2 * n + k, b]
+                right_t_ref[2 * n + k, b] = one_right.T
+                crossing_ref[2 * n + k, b] = jnp.where(odd_ref[0] == 1, one_left, one_right)
+                inside_ref[2 * n + k, b] = jnp.where(odd_ref[0] == 1, one_right, one_left)
         return carry
 
     lax.fori_loop(0, chan // 2, turn, 0)
@@ -365,7 +368,7 @@
 
 
 def environments(
-    first, counts, scale, use_left, left_ref, right_ref, both_ref, out_ref, mid_ref
+    first, counts, scale, use_left, env_ref, both_ref, out_ref, mid_ref
 ):
     _, dests, rows, width = both_ref.shape
     phys = width // LANES
@@ -375,13 +378,7 @@
         for j in range(pairs):
             k = first + begin + 2 * j
             for b in range(dests):
-                env = jnp.concatenate(
-                    [
-                        jnp.where(use_left, left_ref[k + i, b], right_ref[k + i, b])
-                        for i in range(2)
-                    ],
-                    axis=0,
-                )
+                env = jnp.concatenate([env_ref[k, b], env_ref[k + 1, b]], axis=0)
                 mid = dot(env, both_ref[inner, b]).astype(BF16)
                 for p in range(phys):
                     for i in range(2):
@@ -409,7 +406,7 @@
 def normalize_and_cross(
     counts, scale, cells,
     odd_ref, rank_ref, kept_ref, guess_ref, x_ref, mine_ref, theirs_ref, my_sums_ref,
-    their_sums_ref, left_ref, right_ref,
+    their_sums_ref, env_ref,
     new_ref, both_ref, out_ref,
     mid_ref, sem,
 ):
@@ -419,23 +416,17 @@
     )
     copy = pltpu.make_async_copy(both_ref.at[0], new_ref, sem)
     copy.start()
-    environments(
-        0, counts, scale, odd_ref[0] == 1, left_ref, right_ref, both_ref, out_ref, mid_ref
-    )
+    environments(0, counts, scale, odd_ref[0] == 1, env_ref, both_ref, out_ref, mid_ref)
     copy.wait()
 
 
-def cross(first, counts, scale, odd_ref, left_ref, right_ref, both_ref, out_ref, mid_ref):
-    environments(
-        first, counts, scale, odd_ref[0] == 1, left_ref, right_ref, both_ref, out_ref, mid_ref
-    )
-
-
-def within(counts, scale, odd_ref, left_ref, right_ref, both_ref, *refs):
+def cross(first, counts, scale, odd_ref, env_ref, both_ref, out_ref, mid_ref):
+    environments(first, counts, scale, odd_ref[0] == 1, env_ref, both_ref, out_ref, mid_ref)
+
+
+def within(counts, scale, odd_ref, env_ref, both_ref, *refs):
     outs, all_ref, mid_ref = refs[:-2], refs[-2], refs[-1]
-    environments(
-        0, counts, scale, odd_ref[0] == 0, left_ref, right_ref, both_ref, all_ref, mid_ref
-    )
+    environments(0, counts, scale, odd_ref[0] == 0, env_ref, both_ref, all_ref, mid_ref)
     begin = 0
     for out_ref in outs:
         count = out_ref.shape[0]
@@ -513,13 +504,13 @@
         [pltpu.VMEM((chan * phys, phys * GROUP), F32)], ops,
     )
     rel_kind = shape((chan, dests), jnp.int32)
-    right_t, image, mine, rel, arrived, order = call(
-        first_local, [SMEM] + [VMEM] * 4,
-        (
-            shape(right.shape, BF16), wave_f32, sums_kind, rel_kind, rel_kind,
-            shape((dests,), jnp.int32),
-        ),
-        pair_scratch, turned_map, kron, x, left, right, out_specs=(VMEM,) * 3 + (SMEM,) * 3,
+    odd = jnp.full((1,), lax.rem(lax.axis_index("seg"), 2), jnp.int32)
+    envs = shape(right.shape, BF16)
+    right_t, image, mine, crossing, inner, rel, arrived, order = call(
+        first_local, [SMEM] * 2 + [VMEM] * 4,
+        (envs, wave_f32, sums_kind, envs, envs, rel_kind, rel_kind, shape((dests,), jnp.int32)),
+        pair_scratch, turned_map, odd, kron, x, left, right,
+        out_specs=(VMEM,) * 5 + (SMEM,) * 3,
     )
     image, mine = call(
         first_remote, [SMEM] + [VMEM] * 6, (wave_f32, sums_kind), pair_scratch,
@@ -557,7 +548,6 @@
     cells = float(total_blocks * rows * width)
     early = 8
     count = lax.axis_size("seg")
-    odd = jnp.full((1,), lax.rem(lax.axis_index("seg"), 2), jnp.int32)
 
     def swapped(value, low):
         pairs = [(s, s + 1) for s in range(low, count - 1, 2)]
@@ -571,20 +561,20 @@
 
     new_state, both, piece = call(
         functools.partial(normalize_and_cross, ((2, 2),), env_scale, cells),
-        [SMEM] * 2 + [VMEM] * 9, (wave_b16, shape((2,) + wave, BF16), env_kind(early)),
+        [SMEM] * 2 + [VMEM] * 8, (wave_b16, shape((2,) + wave, BF16), env_kind(early)),
         mid(2) + [pltpu.SemaphoreType.DMA],
-        odd, ranks[0], kept, guess, x, mine, theirs, my_sums, their_sums, left, right,
+        odd, ranks[0], kept, guess, x, mine, theirs, my_sums, their_sums, crossing,
         out_specs=(HBM, VMEM, VMEM),
     )
     rest = call(
         functools.partial(cross, early, ((3, 1),), env_scale),
-        [SMEM] + [VMEM] * 3, env_kind(chan - early), mid(3), odd, left, right, both,
+        [SMEM] + [VMEM] * 2, env_kind(chan - early), mid(3), odd, crossing, both,
     )
     sizes = (5, 5, 4)
     inside = call(
         functools.partial(within, ((2, 3), (1, 1)), env_scale),
-        [SMEM] + [VMEM] * 3, tuple(env_kind(size) for size in sizes),
-        [pltpu.VMEM(left.shape, BF16)] + mid(2), odd, left, right, both,
+        [SMEM] + [VMEM] * 2, tuple(env_kind(size) for size in sizes),
+        [pltpu.VMEM(left.shape, BF16)] + mid(2), odd, inner, both,
     )
     piece, rest = swapped(piece, 1), swapped(rest, 1)
     inside = [swapped(value, 0) for value in inside]

time: 101 us -> 95.9 us (0.950); the launches traced: 98.8 us -> 95.8 us
  waiting for transfers between devices: 12.9 us -> 16.5 us
  local copies, waits for them, and re-layouts: 5.59 us -> 2.51 us
  starting transfers between devices: 16.6 us -> 14.4 us
  Pallas kernels: 62.5 us -> 61.3 us
    ppermute x6, starting transfers between devices: 8.97 us -> 5.28 us  [trade(): return lax.ppermute(value, 'blk', swap)]
    unnamed x22 -> x14, local copies, waits for them, and re-layouts: 5.5 us -> 2.41 us
    ppermute x6, waiting for transfers between devices: 7.25 us -> 10.3 us  [trade(): return lax.ppermute(value, 'blk', swap)]
    ppermute x5, starting transfers between devices: 7.68 us -> 9.15 us  [swapped(): return lax.ppermute(value, 'seg', pairs + [(t, s) for s, t in pairs])]
    pallas_call x16, Pallas kernels: 62.5 us -> 61.3 us  [call(): pl.pallas_call(body, in_specs=specs, out_specs=out_specs or jax.tree.map(...]
  transfers between devices with their start and end apart: 11 -> 11, of which waited for: 6 -> 6; matrix products, arithmetic and copies ran while one was open for 0% -> 0% of each run, Pallas kernels for 50% -> 48%
where the time goes in v8:
time: 95.9 us; the launch traced here: 95.8 us
  Pallas kernels  61.3 us (64%)
  waiting for transfers between devices  16.5 us (17%)
  starting transfers between devices  14.4 us (15%)
  local copies, waits for them, and re-layouts  2.51 us (3%)
  between operations  1.05 us (1%)
    pallas_call x16, Pallas kernels, call(): pl.pallas_call(body, in_specs=specs, out_specs=out_specs or jax.tree.map(...  61.3 us
    ppermute x6, waiting for transfers between devices, trade(): return lax.ppermute(value, 'blk', swap)  10.3 us
    ppermute x5, starting transfers between devices, swapped(): return lax.ppermute(value, 'seg', pairs + [(t, s) for s, t in pairs])  9.15 us
    ppermute x5, waiting for transfers between devices, swapped(): return lax.ppermute(value, 'seg', pairs + [(t, s) for s, t in pairs])  6.14 us
    ppermute x6, starting transfers between devices, trade(): return lax.ppermute(value, 'blk', swap)  5.28 us
    unnamed x14, local copies, waits for them, and re-layouts  2.41 us
  transfers between devices with their start and end apart: 11, of which 6 were waited for; matrix products, arithmetic and copies ran while one was open for 0% of the time, Pallas kernels for 48%

profile of v8, /device:TPU:1, one launch (start us, length us, event | category | flops | bytes accessed | tf_op | source)
XLA Modules:
  0.0 95.8 jit_solution(5502103256868124798)
XLA Ops:
  0.6 0.0 copy-start
  0.6 1.2 %copy-done = bf16[1,2,128,2048]{3,2,1,0:T(8,128)(2,1)S(1)} copy-done((bf16[1,2,128,2048]{3,2,1,0:T(8,128)(2,1)S(1)}, bf16[1,2,128,2048]{3,2,1,0:T(8,128)(2,1)}, u32[]{:S(2)}) %copy-start) | copy-done | bytes 1048600
  1.9 0.0 copy-start.4
  1.9 0.0 copy-start.6
  1.9 0.0 copy-start.1
  1.9 0.0 copy-start.2
  1.9 0.8 shard_map.88
  2.7 2.0 %collective-permute-start.1 = (bf16[1,128,2048]{2,1,0:T(8,128)(2,1)}, bf16[1,128,2048]{2,1,0:T(8,128)(2,1)}, u32[]{:S(2)}, u32[]{:S(2)}) collective-permute-start(bf16[1,128,2048]{2,1,0:T(8,128)(2,1)} %shard_map.88), channel_id=1, source_target_pairs={{0,1},{1,0},{2,3},{3,2},{4,5},{5,4},{6,7},{7,6},{8,9},{9,8},{10,11... | collective-permute-start | bytes 1572872 | tf_op jit(solution)/shard_map/ppermute | solution.py:472
  4.8 0.1 collective-permute-start
  4.9 0.0 copy-done.4
  4.9 0.3 shard_map.85.kron_ref
  5.1 0.0 copy-done.6
  5.2 0.1 copy.18
  5.2 0.1 negate_select_fusion.map_ref
  5.3 0.0 copy-done.1
  5.4 0.0 copy-done.2
  5.4 0.0 copy-start.3
  5.4 1.2 %copy-done.3 = bf16[1,14,2,128,128]{4,3,2,1,0:T(8,128)(2,1)S(1)} copy-done((bf16[1,14,2,128,128]{4,3,2,1,0:T(8,128)(2,1)S(1)}, bf16[1,14,2,128,128]{4,3,2,1,0:T(8,128)(2,1)}, u32[]{:S(2)}) %copy-start.3) | copy-done | bytes 917528
  6.5 10.2 %shard_map.86 = (bf16[14,2,128,128]{3,2,1,0:T(8,128)(2,1)S(1)}, f32[2,128,2048]{2,1,0:T(8,128)S(1)}, f32[8,128]{1,0:T(8,128)S(1)}, bf16[14,2,128,128]{3,2,1,0:T(...) custom-call(s32[14,4]{1,0:T(8,128)S(1)} %negate_select_fusion.map_re, ...), custom_call_target="tpu_custom_call" | custom-call | flops 1024 | bytes 1024 | tf_op jit(solution)/shard_map/pallas_call | solution.py:488
  16.8 0.0 collective-permute-done.1.other_ref
  16.8 4.8 %shard_map.89 = (f32[2,128,2048]{2,1,0:T(8,128)S(1)}, f32[8,128]{1,0:T(8,128)S(1)}) custom-call(s32[14,2]{1,0:T(8,128)S(1)} %get-tuple-element.35.rel_ref, bf16[14,128,128]{2,1,0:T(8,128)(2,1)S(1)} %shard_map.85.kron_ref, bf16[1,128,2048]{2,1,0:T(8,128)(2,1)} %collective-permute-done.1.other_ref, ...), custom_call_target="tpu_custom_call", output_to_operand_aliasing={{0}: (5, {})} | custom-call | flops 1024 | bytes 1024 | tf_op jit(solution)/shard_map/pallas_call | solution.py:488
  21.6 1.5 %collective-permute-start.2 = (f32[8,128]{1,0:T(8,128)S(1)}, f32[8,128]{1,0:T(8,128)S(1)}, u32[]{:S(2)}, u32[]{:S(2)}) collective-permute-start(f32[8,128]{1,0:T(8,128)S(1)} %get-tuple-element.41.mine_ref), channel_id=1, source_target_pairs={{0,1},{1,0},{2,3},{3,2},{4,5},{5,4},{6,7},{7,6},{8,9},{9,8},{10,11... | collective-permute-start | bytes 12296 | tf_op jit(solution)/shard_map/ppermute | solution.py:472
  23.1 4.7 %collective-permute-done.other_ref = bf16[1,128,2048]{2,1,0:T(8,128)(2,1)S(1)} collective-permute-done((bf16[1,128,2048]{2,1,0:T(8,128)(2,1)S(1)}, bf16[1,128,2048]{2,1,0:T(8,128)(2,1)S(1)}, u32[]{:S(2)}, u32[]{:S(2)}) %collective-permute-start) | collective-permute-done | bytes 524320 | tf_op jit(solution)/shard_map/ppermute | solution.py:472
  27.8 0.1 collective-permute-done.2.theirs_ref
  27.9 2.9 %shard_map.90 = (f32[2,128,2048]{2,1,0:T(8,128)S(1)}, bf16[1,128,2048]{2,1,0:T(8,128)(2,1)S(1)}) custom-call(s32[14,2]{1,0:T(8,128)S(1)} %get-tuple-element.35.rel_ref, s32[2]{0:T(128)S(1)} %get-tuple-element.36.order_ref, bf16[14,128,128]{2,1,0:T(8,128)(2,1)S(1)} %shard_map.85.kron_ref, ...), custom_call_target="tpu_custom_call", output_to_operand_aliasing={{0}: (6, {})} | custom-call | flops 1024 | bytes 1024 | tf_op jit(solution)/shard_map/pallas_call | solution.py:488
  30.8 0.4 collective-permute-start.4
  31.2 0.0 copy-start.5
  31.2 3.8 %shard_map.91 = (f32[2,128,2048]{2,1,0:T(8,128)S(1)}, bf16[1,128,2048]{2,1,0:T(8,128)(2,1)S(1)}, bf16[2,128,2048]{2,1,0:T(8,128)(2,1)S(1)}) custom-call(s32[14,2]{1,0:T(8,128)S(1)} %get-tuple-element.35.rel_ref, s32[2]{0:T(128)S(1)} %get-tuple-element.36.order_ref, bf16[14,128,128]{2,1,0:T(8,128)(2,1)S(1)} %shard_map.85.kron_ref, ...), custom_call_target="tpu_custom_call", output_to_operand_aliasing={{0}: (6, {})} | custom-call | flops 1024 | bytes 1024 | tf_op jit(solution)/shard_map/pallas_call | solution.py:488
  35.0 1.2 %collective-permute-start.3 = (bf16[1,128,2048]{2,1,0:T(8,128)(2,1)S(1)}, bf16[1,128,2048]{2,1,0:T(8,128)(2,1)S(1)}, u32[]{:S(2)}, u32[]{:S(2)}) collective-permute-start(bf16[1,128,2048]{2,1,0:T(8,128)(2,1)S(1)} %get-tuple-element.44), channel_id=1, source_target_pairs={{0,1},{1,0},{2,3},{3,2},{4,5},{5,4},{6,7},{7,6},{8,9},{9,8},{10,11... | collective-permute-start | bytes 1572872 | tf_op jit(solution)/shard_map/ppermute | solution.py:472
  36.2 0.0 copy-done.5
  36.2 9.6 %shard_map.92 = (f32[2,128,2048]{2,1,0:T(8,128)S(1)}, f32[8,128]{1,0:T(8,128)S(1)}) custom-call(s32[14,2]{1,0:T(8,128)S(1)} %get-tuple-element.34.rel_ref, s32[2]{0:T(128)S(1)} %bitcast.27, bf16[14,128,128]{2,1,0:T(8,128)(2,1)S(1)} %shard_map.85.kron_ref, bf16[2,128,2048]{2,1,0:T(8,128)(2,1)S(1)} %get-tuple-element.45.guess_ref, ...), custom_call_target="tpu_custom_call" | custom-call | flops 1024 | bytes 1024 | tf_op jit(solution)/shard_map/pallas_call | solution.py:488
  45.8 0.0 collective-permute-done.4.other_ref
  45.8 5.5 %shard_map.93.before_ref = f32[2,128,2048]{2,1,0:T(8,128)S(1)} custom-call(s32[14,2]{1,0:T(8,128)S(1)} %get-tuple-element.34.rel_ref, bf16[14,128,128]{2,1,0:T(8,128)(2,1)S(1)} %shard_map.85.kron_ref, bf16[1,128,2048]{2,1,0:T(8,128)(2,1)S(1)} %collective-permute-done.4.other_ref, ...), custom_call_target="tpu_custom_call", output_to_operand_aliasing={{}: (5, {})} | custom-call | flops 1024 | bytes 1024 | tf_op jit(solution)/shard_map/pallas_call | solution.py:488
  51.3 3.0 %collective-permute-done.3.other_ref = bf16[1,128,2048]{2,1,0:T(8,128)(2,1)S(1)} collective-permute-done((bf16[1,128,2048]{2,1,0:T(8,128)(2,1)S(1)}, bf16[1,128,2048]{2,1,0:T(8,128)(2,1)S(1)}, u32[]{:S(2)}, u32[]{:S(2)}) %collective-permute-start.3) | collective-permute-done | bytes 524320 | tf_op jit(solution)/shard_map/ppermute | solution.py:472
  54.3 5.5 %shard_map.94 = (f32[2,128,2048]{2,1,0:T(8,128)S(1)}, f32[16,128]{1,0:T(8,128)S(1)}) custom-call(s32[14,2]{1,0:T(8,128)S(1)} %get-tuple-element.34.rel_ref, s32[2]{0:T(128)S(1)} %bitcast.28, bf16[14,128,128]{2,1,0:T(8,128)(2,1)S(1)} %shard_map.85.kron_ref, ...), custom_call_target="tpu_custom_call", output_to_operand_aliasing={{0}: (6, {})} | custom-call | flops 1024 | bytes 1024 | tf_op jit(solution)/shard_map/pallas_call | solution.py:488
  59.9 0.1 collective-permute-start.5
  60.0 2.5 %collective-permute-done.5.their_sums_ref = f32[16,128]{1,0:T(8,128)S(1)} collective-permute-done((f32[16,128]{1,0:T(8,128)S(1)}, f32[16,128]{1,0:T(8,128)S(1)}, u32[]{:S(2)}, u32[]{:S(2)}) %collective-permute-start.5) | collective-permute-done | bytes 8224 | tf_op jit(solution)/shard_map/ppermute | solution.py:472
  62.4 5.5 %shard_map.95 = (bf16[2,128,2048]{2,1,0:T(8,128)(2,1)}, bf16[2,2,128,2048]{3,2,1,0:T(8,128)(2,1)S(1)}, bf16[8,2,128,128]{3,2,1,0:T(8,128)(2,1)S(1)}) custom-call(s32[1]{0:T(128)} %bitcast.odd_ref, s32[2]{0:T(128)S(1)} %bitcast.29, f32[2,128,2048]{2,1,0:T(8,128)S(1)} %get-tuple-element.49.kept_ref, bf16[2,128,2048]{2,1,0:T(8,128)(2,1)S(1)} %get-tuple-element.45.guess_ref, ...), custom_call_target="tpu_custom_call" | custom-call | flops 1024 | bytes 1024 | tf_op jit(solution)/shard_map/pallas_call | solution.py:488
  67.9 6.6 %collective-permute-start.10 = (bf16[8,2,128,128]{3,2,1,0:T(8,128)(2,1)S(1)}, bf16[8,2,128,128]{3,2,1,0:T(8,128)(2,1)S(1)}, u32[]{:S(2)}, u32[]{:S(2)}) collective-permute-start(bf16[8,2,128,128]{3,2,1,0:T(8,128)(2,1)S(1)} %get-tuple-element.58), channel_id=1, source_target_pairs={{2,4},{6,8},{10,12},{14,16},{18,20},{22,24},{26,28},{4,2},{8,6},{1... | collective-permute-start | bytes 1572872 | tf_op jit(solution)/shard_map/ppermute | solution.py:554
  74.5 2.6 %shard_map.96 = bf16[6,2,128,128]{3,2,1,0:T(8,128)(2,1)S(1)} custom-call(s32[1]{0:T(128)} %bitcast.odd_ref, bf16[14,2,128,128]{3,2,1,0:T(8,128)(2,1)S(1)} %get-tuple-element.51.env_ref, bf16[2,2,128,2048]{3,2,1,0:T(8,128)(2,1)S(1)} %get-tuple-element.53.both_ref), custom_call_target="tpu_custom_call" | custom-call | flops 1024 | bytes 1024 | tf_op jit(solution)/shard_map/pallas_call | solution.py:488
  77.1 1.9 %collective-permute-start.6 = (bf16[6,2,128,128]{3,2,1,0:T(8,128)(2,1)S(1)}, bf16[6,2,128,128]{3,2,1,0:T(8,128)(2,1)S(1)}, u32[]{:S(2)}, u32[]{:S(2)}) collective-permute-start(bf16[6,2,128,128]{3,2,1,0:T(8,128)(2,1)S(1)} %shard_map.96), channel_id=1, source_target_pairs={{2,4},{6,8},{10,12},{14,16},{18,20},{22,24},{26,28},{4,2},{8,6},{1... | collective-permute-start | bytes 1179656 | tf_op jit(solution)/shard_map/ppermute | solution.py:554
  79.0 6.3 %shard_map.97 = (bf16[5,2,128,128]{3,2,1,0:T(8,128)(2,1)S(1)}, bf16[5,2,128,128]{3,2,1,0:T(8,128)(2,1)S(1)}, bf16[4,2,128,128]{3,2,1,0:T(8,128)(2,1)S(1)}) custom-call(s32[1]{0:T(128)} %bitcast.odd_ref, bf16[14,2,128,128]{3,2,1,0:T(8,128)(2,1)S(1)} %get-tuple-element.54.env_ref, bf16[2,2,128,2048]{3,2,1,0:T(8,128)(2,1)S(1)} %get-tuple-element.53.both_ref), custom_call_target="tpu_custom_call" | custom-call | flops 1024 | bytes 1024 | tf_op jit(solution)/shard_map/pallas_call | solution.py:488
  85.4 0.1 collective-permute-start.7
  85.5 0.5 collective-permute-start.8
  86.0 0.1 collective-permute-start.9
  86.0 4.4 %collective-permute-done.10.refs_0_ = bf16[8,2,128,128]{3,2,1,0:T(8,128)(2,1)S(1)} collective-permute-done((bf16[8,2,128,128]{3,2,1,0:T(8,128)(2,1)S(1)}, bf16[8,2,128,128]{3,2,1,0:T(8,128)(2,1)S(1)}, u32[]{:S(2)}, u32[]{:S(2)}) %collective-permute-start.10) | collective-permute-done | bytes 524320 | tf_op jit(solution)/shard_map/ppermute | solution.py:554
  90.4 1.1 %shard_map.98 = (f32[14,2,128,128]{3,2,1,0:T(8,128)}, f32[14,2,128,128]{3,2,1,0:T(8,128)}) custom-call(s32[1]{0:T(128)} %bitcast.odd_ref, bf16[8,2,128,128]{3,2,1,0:T(8,128)(2,1)S(1)} %collective-permute-done.10.refs_0_), custom_call_target="tpu_custom_call" | custom-call | flops 1024 | bytes 1024 | tf_op jit(solution)/shard_map/pallas_call | solution.py:488
  91.5 0.0 collective-permute-done.9.refs_2_
  91.5 0.0 collective-permute-done.7.refs_0_
  91.6 0.0 collective-permute-done.8.refs_1_
  91.6 1.3 %shard_map.99 = (f32[14,2,128,128]{3,2,1,0:T(8,128)}, f32[14,2,128,128]{3,2,1,0:T(8,128)}) custom-call(s32[1]{0:T(128)} %bitcast.odd_ref, bf16[5,2,128,128]{3,2,1,0:T(8,128)(2,1)S(1)} %collective-permute-done.7.refs_0_, bf16[5,2,128,128]{3,2,1,0:T(8,128)(2,1)S(1)} %collective-permute-done.8.refs_1_, ...), custom_call_target="tpu_custom_call", output_to_operand_aliasing={{0}: (4, {}), {1}: (5, {})} | custom-call | flops 1024 | bytes 1024 | tf_op jit(solution)/shard_map/pallas_call | solution.py:488
  92.9 1.7 %collective-permute-done.6.refs_0_ = bf16[6,2,128,128]{3,2,1,0:T(8,128)(2,1)S(1)} collective-permute-done((bf16[6,2,128,128]{3,2,1,0:T(8,128)(2,1)S(1)}, bf16[6,2,128,128]{3,2,1,0:T(8,128)(2,1)S(1)}, u32[]{:S(2)}, u32[]{:S(2)}) %collective-permute-start.6) | collective-permute-done | bytes 393248 | tf_op jit(solution)/shard_map/ppermute | solution.py:554
  94.7 1.0 %shard_map.100 = (f32[14,2,128,128]{3,2,1,0:T(8,128)}, f32[14,2,128,128]{3,2,1,0:T(8,128)}) custom-call(s32[1]{0:T(128)} %bitcast.odd_ref, bf16[6,2,128,128]{3,2,1,0:T(8,128)(2,1)S(1)} %collective-permute-done.6.refs_0_, f32[14,2,128,128]{3,2,1,0:T(8,128)} %get-tuple-element.61.refs_1_, ...), custom_call_target="tpu_custom_call", output_to_operand_aliasing={{0}: (2, {}), {1}: (3, {})} | custom-call | flops 1024 | bytes 1024 | tf_op jit(solution)/shard_map/pallas_call | solution.py:488
  (1 shorter events, 0.0 us)
Async XLA Ops:
  0.6 1.2 %copy-start = (bf16[1,2,128,2048]{3,2,1,0:T(8,128)(2,1)S(1)}, bf16[1,2,128,2048]{3,2,1,0:T(8,128)(2,1)}, u32[]{:S(2)}) copy-start(bf16[1,2,128,2048]{3,2,1,0:T(8,128)(2,1)} %param.6) | copy-start | bytes 3145732
  1.9 3.0 %copy-start.4 = (bf16[1,14,16,16]{3,2,1,0:T(8,128)(2,1)S(1)}, bf16[1,14,16,16]{3,2,1,0:T(8,128)(2,1)}, u32[]{:S(2)}) copy-start(bf16[1,14,16,16]{3,2,1,0:T(8,128)(2,1)} %param.9) | copy-start | bytes 21508
  1.9 3.3 %copy-start.6 = (s32[1,14,4]{1,2,0:T(4,128)S(1)}, s32[1,14,4]{1,2,0:T(4,128)}, u32[]{:S(2)}) copy-start(s32[1,14,4]{1,2,0:T(4,128)} %param.10) | copy-start | bytes 676
  1.9 3.5 %copy-start.1 = (bf16[1,2,128,2048]{3,2,1,0:T(8,128)(2,1)S(1)}, bf16[1,2,128,2048]{3,2,1,0:T(8,128)(2,1)}, u32[]{:S(2)}) copy-start(bf16[1,2,128,2048]{3,2,1,0:T(8,128)(2,1)} %param.6) | copy-start | bytes 3145732
  1.9 3.5 %copy-start.2 = (bf16[1,14,2,128,128]{4,3,2,1,0:T(8,128)(2,1)S(1)}, bf16[1,14,2,128,128]{4,3,2,1,0:T(8,128)(2,1)}, u32[]{:S(2)}) copy-start(bf16[1,14,2,128,128]{4,3,2,1,0:T(8,128)(2,1)} %param.7) | copy-start | bytes 2752516
  2.7 14.1 %collective-permute-start.1 = (bf16[1,128,2048]{2,1,0:T(8,128)(2,1)}, bf16[1,128,2048]{2,1,0:T(8,128)(2,1)}, u32[]{:S(2)}, u32[]{:S(2)}) collective-permute-start(bf16[1,128,2048]{2,1,0:T(8,128)(2,1)} %shard_map.88), channel_id=1, source_target_pairs={{0,1},{1,0},{2,3},{3,2},{4,5},{5,4},{6,7},{7,6},{8,9},{9,8},{10,11... | collective-permute-start | bytes 1572872 | tf_op jit(solution)/shard_map/ppermute | solution.py:472
  4.8 23.1 %collective-permute-start = (bf16[1,128,2048]{2,1,0:T(8,128)(2,1)S(1)}, bf16[1,128,2048]{2,1,0:T(8,128)(2,1)S(1)}, u32[]{:S(2)}, u32[]{:S(2)}) collective-permute-start(bf16[1,128,2048]{2,1,0:T(8,128)(2,1)S(1)} %shard_map.87), channel_id=1, source_target_pairs={{0,1},{1,0},{2,3},{3,2},{4,5},{5,4},{6,7},{7,6},{8,9},{9,8},{10,11... | collective-permute-start | bytes 1572872 | tf_op jit(solution)/shard_map/ppermute | solution.py:472
  5.4 1.2 %copy-start.3 = (bf16[1,14,2,128,128]{4,3,2,1,0:T(8,128)(2,1)S(1)}, bf16[1,14,2,128,128]{4,3,2,1,0:T(8,128)(2,1)}, u32[]{:S(2)}) copy-start(bf16[1,14,2,128,128]{4,3,2,1,0:T(8,128)(2,1)} %param.8) | copy-start | bytes 2752516
  21.6 6.3 %collective-permute-start.2 = (f32[8,128]{1,0:T(8,128)S(1)}, f32[8,128]{1,0:T(8,128)S(1)}, u32[]{:S(2)}, u32[]{:S(2)}) collective-permute-start(f32[8,128]{1,0:T(8,128)S(1)} %get-tuple-element.41.mine_ref), channel_id=1, source_target_pairs={{0,1},{1,0},{2,3},{3,2},{4,5},{5,4},{6,7},{7,6},{8,9},{9,8},{10,11... | collective-permute-start | bytes 12296 | tf_op jit(solution)/shard_map/ppermute | solution.py:472
  30.8 14.9 %collective-permute-start.4 = (bf16[1,128,2048]{2,1,0:T(8,128)(2,1)S(1)}, bf16[1,128,2048]{2,1,0:T(8,128)(2,1)S(1)}, u32[]{:S(2)}, u32[]{:S(2)}) collective-permute-start(bf16[1,128,2048]{2,1,0:T(8,128)(2,1)S(1)} %get-tuple-element.43.refs_0_), channel_id=1, source_target_pairs={{0,1},{1,0},{2,3},{3,2},{4,5},{5,4},{6,7},{7,6},{8,9},{9,8},{10,11... | collective-permute-start | bytes 1572872 | tf_op jit(solution)/shard_map/ppermute | solution.py:472
  31.2 5.0 %copy-start.5 = (s32[1,2]{1,0:T(1,128)S(1)}, s32[1,2]{1,0:T(1,128)}, u32[]{:S(2)}) copy-start(s32[1,2]{1,0:T(1,128)} %param.11) | copy-start | bytes 28
  35.0 19.3 %collective-permute-start.3 = (bf16[1,128,2048]{2,1,0:T(8,128)(2,1)S(1)}, bf16[1,128,2048]{2,1,0:T(8,128)(2,1)S(1)}, u32[]{:S(2)}, u32[]{:S(2)}) collective-permute-start(bf16[1,128,2048]{2,1,0:T(8,128)(2,1)S(1)} %get-tuple-element.44), channel_id=1, source_target_pairs={{0,1},{1,0},{2,3},{3,2},{4,5},{5,4},{6,7},{7,6},{8,9},{9,8},{10,11... | collective-permute-start | bytes 1572872 | tf_op jit(solution)/shard_map/ppermute | solution.py:472
  59.9 2.6 %collective-permute-start.5 = (f32[16,128]{1,0:T(8,128)S(1)}, f32[16,128]{1,0:T(8,128)S(1)}, u32[]{:S(2)}, u32[]{:S(2)}) collective-permute-start(f32[16,128]{1,0:T(8,128)S(1)} %get-tuple-element.50.my_sums_ref), channel_id=1, source_target_pairs={{0,1},{1,0},{2,3},{3,2},{4,5},{5,4},{6,7},{7,6},{8,9},{9,8},{10,11... | collective-permute-start | bytes 24584 | tf_op jit(solution)/shard_map/ppermute | solution.py:472
  67.9 22.5 %collective-permute-start.10 = (bf16[8,2,128,128]{3,2,1,0:T(8,128)(2,1)S(1)}, bf16[8,2,128,128]{3,2,1,0:T(8,128)(2,1)S(1)}, u32[]{:S(2)}, u32[]{:S(2)}) collective-permute-start(bf16[8,2,128,128]{3,2,1,0:T(8,128)(2,1)S(1)} %get-tuple-element.58), channel_id=1, source_target_pairs={{2,4},{6,8},{10,12},{14,16},{18,20},{22,24},{26,28},{4,2},{8,6},{1... | collective-permute-start | bytes 1572872 | tf_op jit(solution)/shard_map/ppermute | solution.py:554
  77.1 17.5 %collective-permute-start.6 = (bf16[6,2,128,128]{3,2,1,0:T(8,128)(2,1)S(1)}, bf16[6,2,128,128]{3,2,1,0:T(8,128)(2,1)S(1)}, u32[]{:S(2)}, u32[]{:S(2)}) collective-permute-start(bf16[6,2,128,128]{3,2,1,0:T(8,128)(2,1)S(1)} %shard_map.96), channel_id=1, source_target_pairs={{2,4},{6,8},{10,12},{14,16},{18,20},{22,24},{26,28},{4,2},{8,6},{1... | collective-permute-start | bytes 1179656 | tf_op jit(solution)/shard_map/ppermute | solution.py:554
  85.4 6.2 %collective-permute-start.7 = (bf16[5,2,128,128]{3,2,1,0:T(8,128)(2,1)S(1)}, bf16[5,2,128,128]{3,2,1,0:T(8,128)(2,1)S(1)}, u32[]{:S(2)}, u32[]{:S(2)}) collective-permute-start(bf16[5,2,128,128]{3,2,1,0:T(8,128)(2,1)S(1)} %get-tuple-element.55), channel_id=1, source_target_pairs={{0,2},{4,6},{8,10},{12,14},{16,18},{20,22},{24,26},{28,30},{2,0},{... | collective-permute-start | bytes 983048 | tf_op jit(solution)/shard_map/ppermute | solution.py:554
  85.5 6.1 %collective-permute-start.8 = (bf16[5,2,128,128]{3,2,1,0:T(8,128)(2,1)S(1)}, bf16[5,2,128,128]{3,2,1,0:T(8,128)(2,1)S(1)}, u32[]{:S(2)}, u32[]{:S(2)}) collective-permute-start(bf16[5,2,128,128]{3,2,1,0:T(8,128)(2,1)S(1)} %get-tuple-element.56), channel_id=1, source_target_pairs={{0,2},{4,6},{8,10},{12,14},{16,18},{20,22},{24,26},{28,30},{2,0},{... | collective-permute-start | bytes 983048 | tf_op jit(solution)/shard_map/ppermute | solution.py:554
  86.0 5.6 %collective-permute-start.9 = (bf16[4,2,128,128]{3,2,1,0:T(8,128)(2,1)S(1)}, bf16[4,2,128,128]{3,2,1,0:T(8,128)(2,1)S(1)}, u32[]{:S(2)}, u32[]{:S(2)}) collective-permute-start(bf16[4,2,128,128]{3,2,1,0:T(8,128)(2,1)S(1)} %get-tuple-element.57), channel_id=1, source_target_pairs={{0,2},{4,6},{8,10},{12,14},{16,18},{20,22},{24,26},{28,30},{2,0},{... | collective-permute-start | bytes 786440 | tf_op jit(solution)/shard_map/ppermute | solution.py:554

commit v9 on v8

--- a/solution.py
+++ b/solution.py
@@ -69,7 +69,9 @@
     return place // 2
 
 
-def add_pairs(steps, lists, kron_ref, x_ref, left_ref, right_t_ref, acc_ref, turned_ref, mixed_ref):
+def add_pairs(
+    steps, lists, kron_ref, x_ref, left_ref, right_t_ref, acc_ref, turned_ref, mixed_ref, start=0
+):
     chan_list, src_list, live_list, dest_list = lists
     rows = x_ref.shape[1]
     phys = x_ref.shape[2] // LANES
@@ -110,9 +112,9 @@
     def act_left(s):
         dest = dest_list[2 * s]
         left = jnp.concatenate(
-            [left_ref[chan_list[2 * s], dest], left_ref[chan_list[2 * s + 1], dest]], axis=1
+            [left_ref[chan_list[2 * s + i], dest][:, start : start + rows] for i in range(2)], axis=1
         )
-        acc_ref[dest] += dot(left, mixed_ref[...])
+        acc_ref[dest] += dot(left, mixed_ref[0 : 2 * rows, :])
 
     def middle(s, carry):
         act_site(s)
@@ -222,12 +224,12 @@
 
 
 def remote_sources(
-    rel_ref, kron_ref, other_ref, left_ref, right_t_ref, before_ref,
+    block, rel_ref, kron_ref, other_ref, left_ref, right_t_ref, before_ref,
     acc_ref,
     turned_ref, mixed_ref, *lists,
 ):
     dests = left_ref.shape[1]
-    steps = list_pairs(rel_ref, dests, dests + 1, *lists)
+    steps = list_pairs(rel_ref, dests + block, dests + block + 1, *lists)
     add_pairs(steps, lists, kron_ref, other_ref, left_ref, right_t_ref, acc_ref, turned_ref, mixed_ref)
 
 
@@ -250,7 +252,7 @@
     dest = order_ref[turn]
     last = turn == dests - 1
     if last:
-        earlier_ref, acc_ref, guess_ref, all_ref = refs[:4]
+        earlier_ref, acc_ref, head_ref, tail_ref, all_ref = refs[:5]
         all_ref[order_ref[0]] = earlier_ref[0]
     else:
         acc_ref, guess_ref = refs[:2]
@@ -264,12 +266,17 @@
     def update(b, r, start, carry):
         x = x_ref[b, r, :].astype(F32)
         guess = (keep_state * x - STEP_SIZE * acc_ref[b, r, :]).astype(BF16)
-        guess_ref[0, r, :] = guess
         if last:
             all_ref[b, r, :] = guess
+        else:
+            guess_ref[0, r, :] = guess
         return carry
 
     row_loop(1, rows, update, 0, first=dest)
+    if last:
+        split = head_ref.shape[1]
+        head_ref[0] = all_ref[dest, 0:split]
+        tail_ref[0] = all_ref[dest, split:rows]
 
 
 def second_local(
@@ -302,7 +309,10 @@
 ):
     dests, rows, width = x_ref.shape
     steps = list_pairs(rel_ref, dests + 1, 2 * dests, *lists)
-    add_pairs(steps, lists, kron_ref, other_ref, left_ref, right_t_ref, kept_ref, turned_ref, mixed_ref)
+    add_pairs(
+        steps, lists, kron_ref, other_ref, left_ref, right_t_ref, kept_ref, turned_ref, mixed_ref,
+        rows - other_ref.shape[1],
+    )
     shift = common_shift(mine_ref, theirs_ref)
     keep_guess = jnp.tile(1.0 + STEP_SIZE * shift, (1, width // LANES))
 
@@ -522,24 +532,29 @@
         (wave_f32, block), pair_scratch,
         rel, order, kron, other[1], left, right_t, image, x, mine, theirs, aliases={6: 0},
     )
-    image, last_guess, guess = call(
+    split = rows - rows // 4
+    image, head, tail, guess = call(
         functools.partial(first_finish, 1), [SMEM] * 2 + [VMEM] * 9,
-        (wave_f32, block, wave_b16), pair_scratch,
+        (
+            wave_f32, shape((1, split, width), BF16), shape((1, rows - split, width), BF16), wave_b16,
+        ),
+        pair_scratch,
         rel, order, kron, other[1], left, right_t, image, x, mine, theirs, first_guess,
         aliases={6: 0},
     )
-    other = [trade(first_guess), trade(last_guess)]
+    other = [trade(first_guess), trade(head), trade(tail)]
     acc, early_sums = call(
         second_local, [SMEM] * 2 + [VMEM] * 6, (wave_f32, sums_kind), pair_scratch,
         arrived, ranks[0], kron, guess, left, right_t, x, image,
     )
-    acc = call(
-        remote_sources, [SMEM] + [VMEM] * 5, wave_f32, pair_scratch,
-        arrived, kron, other[0], left, right_t, acc, aliases={5: 0},
-    )
+    for n in range(2):
+        acc = call(
+            functools.partial(remote_sources, n), [SMEM] + [VMEM] * 5, wave_f32, pair_scratch,
+            arrived, kron, other[n], left, right_t, acc, aliases={5: 0},
+        )
     kept, my_sums = call(
         second_finish, [SMEM] * 2 + [VMEM] * 10, (wave_f32, shape((16, LANES), F32)), pair_scratch,
-        arrived, ranks[0], kron, other[1], left, right_t, acc, x, guess, mine, theirs, early_sums,
+        arrived, ranks[0], kron, other[2], left, right_t, acc, x, guess, mine, theirs, early_sums,
         aliases={6: 0},
     )
     their_sums = trade(my_sums)

time: 95.9 us -> 96.7 us (level)
  waiting for transfers between devices: 16.5 us -> 12.6 us
  Pallas kernels: 61.3 us -> 63.8 us
  starting transfers between devices: 14.4 us -> 16.1 us
    ppermute x6 -> x7, waiting for transfers between devices: 10.3 us -> 6.41 us  [trade(): return lax.ppermute(value, 'blk', swap)]
    pallas_call x16 -> x17, Pallas kernels: 61.3 us -> 63.8 us  [call(): pl.pallas_call(body, in_specs=specs, out_specs=out_specs or jax.tree.map(...]
    ppermute x6 -> x7, starting transfers between devices: 5.28 us -> 7.33 us  [trade(): return lax.ppermute(value, 'blk', swap)]
  transfers between devices with their start and end apart: 11 -> 12, of which waited for: 6 -> 5; matrix products, arithmetic and copies ran while one was open for 0% -> 0% of each run, Pallas kernels for 48% -> 52%
where the time goes in v9:
time: 96.7 us; the launch traced here: 96 us
  Pallas kernels  63.8 us (66%)
  starting transfers between devices  16.1 us (17%)
  waiting for transfers between devices  12.6 us (13%)
  local copies, waits for them, and re-layouts  2.51 us (3%)
  between operations  1.07 us (1%)
    pallas_call x17, Pallas kernels, call(): pl.pallas_call(body, in_specs=specs, out_specs=out_specs or jax.tree.map(...  63.8 us
    ppermute x5, starting transfers between devices, swapped(): return lax.ppermute(value, 'seg', pairs + [(t, s) for s, t in pairs])  8.72 us
    ppermute x7, starting transfers between devices, trade(): return lax.ppermute(value, 'blk', swap)  7.33 us
    ppermute x7, waiting for transfers between devices, trade(): return lax.ppermute(value, 'blk', swap)  6.41 us
    ppermute x5, waiting for transfers between devices, swapped(): return lax.ppermute(value, 'seg', pairs + [(t, s) for s, t in pairs])  6.14 us
    unnamed x14, local copies, waits for them, and re-layouts  2.41 us
  transfers between devices with their start and end apart: 12, of which 5 were waited for; matrix products, arithmetic and copies ran while one was open for 0% of the time, Pallas kernels for 52%

profile of v9, /device:TPU:1, one launch (start us, length us, event | category | flops | bytes accessed | tf_op | source)
XLA Modules:
  0.0 96.0 jit_solution(5006660329696904309)
XLA Ops:
  0.6 0.0 copy-start
  0.6 1.2 %copy-done = bf16[1,2,128,2048]{3,2,1,0:T(8,128)(2,1)S(1)} copy-done((bf16[1,2,128,2048]{3,2,1,0:T(8,128)(2,1)S(1)}, bf16[1,2,128,2048]{3,2,1,0:T(8,128)(2,1)}, u32[]{:S(2)}) %copy-start) | copy-done | bytes 1048600
  1.9 0.0 copy-start.4
  1.9 0.0 copy-start.6
  1.9 0.0 copy-start.1
  1.9 0.0 copy-start.2
  1.9 0.8 shard_map.88
  2.7 2.0 %collective-permute-start.1 = (bf16[1,128,2048]{2,1,0:T(8,128)(2,1)}, bf16[1,128,2048]{2,1,0:T(8,128)(2,1)}, u32[]{:S(2)}, u32[]{:S(2)}) collective-permute-start(bf16[1,128,2048]{2,1,0:T(8,128)(2,1)} %shard_map.88), channel_id=1, source_target_pairs={{0,1},{1,0},{2,3},{3,2},{4,5},{5,4},{6,7},{7,6},{8,9},{9,8},{10,11... | collective-permute-start | bytes 1572872 | tf_op jit(solution)/shard_map/ppermute | solution.py:482
  4.8 0.1 collective-permute-start
  4.9 0.0 copy-done.4
  4.9 0.3 shard_map.85.kron_ref
  5.1 0.0 copy-done.6
  5.2 0.1 copy.19
  5.2 0.1 negate_select_fusion.map_ref
  5.3 0.0 copy-done.1
  5.4 0.0 copy-done.2
  5.4 0.0 copy-start.3
  5.4 1.2 %copy-done.3 = bf16[1,14,2,128,128]{4,3,2,1,0:T(8,128)(2,1)S(1)} copy-done((bf16[1,14,2,128,128]{4,3,2,1,0:T(8,128)(2,1)S(1)}, bf16[1,14,2,128,128]{4,3,2,1,0:T(8,128)(2,1)}, u32[]{:S(2)}) %copy-start.3) | copy-done | bytes 917528
  6.5 10.2 %shard_map.86 = (bf16[14,2,128,128]{3,2,1,0:T(8,128)(2,1)S(1)}, f32[2,128,2048]{2,1,0:T(8,128)S(1)}, f32[8,128]{1,0:T(8,128)S(1)}, bf16[14,2,128,128]{3,2,1,0:T(...) custom-call(s32[14,4]{1,0:T(8,128)S(1)} %negate_select_fusion.map_re, ...), custom_call_target="tpu_custom_call" | custom-call | flops 1024 | bytes 1024 | tf_op jit(solution)/shard_map/pallas_call | solution.py:498
  16.8 0.0 collective-permute-done.1.other_ref
  16.8 5.7 %shard_map.89 = (f32[2,128,2048]{2,1,0:T(8,128)S(1)}, f32[8,128]{1,0:T(8,128)S(1)}) custom-call(s32[14,2]{1,0:T(8,128)S(1)} %get-tuple-element.36.rel_ref, bf16[14,128,128]{2,1,0:T(8,128)(2,1)S(1)} %shard_map.85.kron_ref, bf16[1,128,2048]{2,1,0:T(8,128)(2,1)} %collective-permute-done.1.other_ref, ...), custom_call_target="tpu_custom_call", output_to_operand_aliasing={{0}: (5, {})} | custom-call | flops 1024 | bytes 1024 | tf_op jit(solution)/shard_map/pallas_call | solution.py:498
  22.4 1.5 %collective-permute-start.2 = (f32[8,128]{1,0:T(8,128)S(1)}, f32[8,128]{1,0:T(8,128)S(1)}, u32[]{:S(2)}, u32[]{:S(2)}) collective-permute-start(f32[8,128]{1,0:T(8,128)S(1)} %get-tuple-element.42.mine_ref), channel_id=1, source_target_pairs={{0,1},{1,0},{2,3},{3,2},{4,5},{5,4},{6,7},{7,6},{8,9},{9,8},{10,11... | collective-permute-start | bytes 12296 | tf_op jit(solution)/shard_map/ppermute | solution.py:482
  24.0 3.9 %collective-permute-done.other_ref = bf16[1,128,2048]{2,1,0:T(8,128)(2,1)S(1)} collective-permute-done((bf16[1,128,2048]{2,1,0:T(8,128)(2,1)S(1)}, bf16[1,128,2048]{2,1,0:T(8,128)(2,1)S(1)}, u32[]{:S(2)}, u32[]{:S(2)}) %collective-permute-start) | collective-permute-done | bytes 524320 | tf_op jit(solution)/shard_map/ppermute | solution.py:482
  27.8 0.1 collective-permute-done.2.theirs_ref
  27.9 2.1 %shard_map.90 = (f32[2,128,2048]{2,1,0:T(8,128)S(1)}, bf16[1,128,2048]{2,1,0:T(8,128)(2,1)S(1)}) custom-call(s32[14,2]{1,0:T(8,128)S(1)} %get-tuple-element.36.rel_ref, s32[2]{0:T(128)S(1)} %get-tuple-element.37.order_ref, bf16[14,128,128]{2,1,0:T(8,128)(2,1)S(1)} %shard_map.85.kron_ref, ...), custom_call_target="tpu_custom_call", output_to_operand_aliasing={{0}: (6, {})} | custom-call | flops 1024 | bytes 1024 | tf_op jit(solution)/shard_map/pallas_call | solution.py:498
  30.0 2.1 %collective-permute-start.5 = (bf16[1,128,2048]{2,1,0:T(8,128)(2,1)S(1)}, bf16[1,128,2048]{2,1,0:T(8,128)(2,1)S(1)}, u32[]{:S(2)}, u32[]{:S(2)}) collective-permute-start(bf16[1,128,2048]{2,1,0:T(8,128)(2,1)S(1)} %get-tuple-element.44.refs_0_), channel_id=1, source_target_pairs={{0,1},{1,0},{2,3},{3,2},{4,5},{5,4},{6,7},{7,6},{8,9},{9,8},{10,11... | collective-permute-start | bytes 1572872 | tf_op jit(solution)/shard_map/ppermute | solution.py:482
  32.1 0.0 copy-start.5
  32.1 3.8 %shard_map.91 = (f32[2,128,2048]{2,1,0:T(8,128)S(1)}, bf16[1,96,2048]{2,1,0:T(8,128)(2,1)S(1)}, bf16[1,32,2048]{2,1,0:T(8,128)(2,1)S(1)}, bf16[2,128,2048]{2,1,0:T(8,128)(2,1)S(1)}) custom-call(s32[14,2]{1,0:T(8,128)S(1)} %get-tuple-element.36.rel_ref, s32[2]{0:T(128)S(1)} %get-tuple-element.37.order_ref, ...), custom_call_target="tpu_custom_call", output_to_operand_aliasing={{0}: (6, {})} | custom-call | flops 1024 | bytes 1024 | tf_op jit(solution)/shard_map/pallas_call | solution.py:498
  35.9 0.1 collective-permute-start.4
  35.9 1.5 %collective-permute-start.3 = (bf16[1,32,2048]{2,1,0:T(8,128)(2,1)S(1)}, bf16[1,32,2048]{2,1,0:T(8,128)(2,1)S(1)}, u32[]{:S(2)}, u32[]{:S(2)}) collective-permute-start(bf16[1,32,2048]{2,1,0:T(8,128)(2,1)S(1)} %get-tuple-element.45), channel_id=1, source_target_pairs={{0,1},{1,0},{2,3},{3,2},{4,5},{5,4},{6,7},{7,6},{8,9},{9,8},{10,11... | collective-permute-start | bytes 393224 | tf_op jit(solution)/shard_map/ppermute | solution.py:482
  37.4 0.0 copy-done.5
  37.4 9.6 %shard_map.92 = (f32[2,128,2048]{2,1,0:T(8,128)S(1)}, f32[8,128]{1,0:T(8,128)S(1)}) custom-call(s32[14,2]{1,0:T(8,128)S(1)} %get-tuple-element.35.rel_ref, s32[2]{0:T(128)S(1)} %bitcast.28, bf16[14,128,128]{2,1,0:T(8,128)(2,1)S(1)} %shard_map.85.kron_ref, bf16[2,128,2048]{2,1,0:T(8,128)(2,1)S(1)} %get-tuple-element.47.guess_ref, ...), custom_call_target="tpu_custom_call" | custom-call | flops 1024 | bytes 1024 | tf_op jit(solution)/shard_map/pallas_call | solution.py:498
  47.0 0.0 collective-permute-done.5.other_ref
  47.0 5.5 %shard_map.93.before_ref = f32[2,128,2048]{2,1,0:T(8,128)S(1)} custom-call(s32[14,2]{1,0:T(8,128)S(1)} %get-tuple-element.35.rel_ref, bf16[14,128,128]{2,1,0:T(8,128)(2,1)S(1)} %shard_map.85.kron_ref, bf16[1,128,2048]{2,1,0:T(8,128)(2,1)S(1)} %collective-permute-done.5.other_ref, ...), custom_call_target="tpu_custom_call", output_to_operand_aliasing={{}: (5, {})} | custom-call | flops 1024 | bytes 1024 | tf_op jit(solution)/shard_map/pallas_call | solution.py:498
  52.5 0.0 collective-permute-done.4.other_ref
  52.5 3.9 %shard_map.94.before_ref = f32[2,128,2048]{2,1,0:T(8,128)S(1)} custom-call(s32[14,2]{1,0:T(8,128)S(1)} %get-tuple-element.35.rel_ref, bf16[14,128,128]{2,1,0:T(8,128)(2,1)S(1)} %shard_map.85.kron_ref, bf16[1,96,2048]{2,1,0:T(8,128)(2,1)S(1)} %collective-permute-done.4.other_ref, ...), custom_call_target="tpu_custom_call", output_to_operand_aliasing={{}: (5, {})} | custom-call | flops 1024 | bytes 1024 | tf_op jit(solution)/shard_map/pallas_call | solution.py:498
  56.4 0.0 collective-permute-done.3.other_ref
  56.4 4.1 %shard_map.95 = (f32[2,128,2048]{2,1,0:T(8,128)S(1)}, f32[16,128]{1,0:T(8,128)S(1)}) custom-call(s32[14,2]{1,0:T(8,128)S(1)} %get-tuple-element.35.rel_ref, s32[2]{0:T(128)S(1)} %bitcast.29, bf16[14,128,128]{2,1,0:T(8,128)(2,1)S(1)} %shard_map.85.kron_ref, ...), custom_call_target="tpu_custom_call", output_to_operand_aliasing={{0}: (6, {})} | custom-call | flops 1024 | bytes 1024 | tf_op jit(solution)/shard_map/pallas_call | solution.py:498
  60.5 0.1 collective-permute-start.6
  60.6 2.4 %collective-permute-done.6.their_sums_ref = f32[16,128]{1,0:T(8,128)S(1)} collective-permute-done((f32[16,128]{1,0:T(8,128)S(1)}, f32[16,128]{1,0:T(8,128)S(1)}, u32[]{:S(2)}, u32[]{:S(2)}) %collective-permute-start.6) | collective-permute-done | bytes 8224 | tf_op jit(solution)/shard_map/ppermute | solution.py:482
  63.1 5.5 %shard_map.96 = (bf16[2,128,2048]{2,1,0:T(8,128)(2,1)}, bf16[2,2,128,2048]{3,2,1,0:T(8,128)(2,1)S(1)}, bf16[8,2,128,128]{3,2,1,0:T(8,128)(2,1)S(1)}) custom-call(s32[1]{0:T(128)} %bitcast.odd_ref, s32[2]{0:T(128)S(1)} %bitcast.30, f32[2,128,2048]{2,1,0:T(8,128)S(1)} %get-tuple-element.51.kept_ref, bf16[2,128,2048]{2,1,0:T(8,128)(2,1)S(1)} %get-tuple-element.47.guess_ref, ...), custom_call_target="tpu_custom_call" | custom-call | flops 1024 | bytes 1024 | tf_op jit(solution)/shard_map/pallas_call | solution.py:498
  68.6 6.2 %collective-permute-start.11 = (bf16[8,2,128,128]{3,2,1,0:T(8,128)(2,1)S(1)}, bf16[8,2,128,128]{3,2,1,0:T(8,128)(2,1)S(1)}, u32[]{:S(2)}, u32[]{:S(2)}) collective-permute-start(bf16[8,2,128,128]{3,2,1,0:T(8,128)(2,1)S(1)} %get-tuple-element.60), channel_id=1, source_target_pairs={{2,4},{6,8},{10,12},{14,16},{18,20},{22,24},{26,28},{4,2},{8,6},{1... | collective-permute-start | bytes 1572872 | tf_op jit(solution)/shard_map/ppermute | solution.py:569
  74.7 2.6 %shard_map.97 = bf16[6,2,128,128]{3,2,1,0:T(8,128)(2,1)S(1)} custom-call(s32[1]{0:T(128)} %bitcast.odd_ref, bf16[14,2,128,128]{3,2,1,0:T(8,128)(2,1)S(1)} %get-tuple-element.53.env_ref, bf16[2,2,128,2048]{3,2,1,0:T(8,128)(2,1)S(1)} %get-tuple-element.55.both_ref), custom_call_target="tpu_custom_call" | custom-call | flops 1024 | bytes 1024 | tf_op jit(solution)/shard_map/pallas_call | solution.py:498
  77.3 1.9 %collective-permute-start.7 = (bf16[6,2,128,128]{3,2,1,0:T(8,128)(2,1)S(1)}, bf16[6,2,128,128]{3,2,1,0:T(8,128)(2,1)S(1)}, u32[]{:S(2)}, u32[]{:S(2)}) collective-permute-start(bf16[6,2,128,128]{3,2,1,0:T(8,128)(2,1)S(1)} %shard_map.97), channel_id=1, source_target_pairs={{2,4},{6,8},{10,12},{14,16},{18,20},{22,24},{26,28},{4,2},{8,6},{1... | collective-permute-start | bytes 1179656 | tf_op jit(solution)/shard_map/ppermute | solution.py:569
  79.3 6.3 %shard_map.98 = (bf16[5,2,128,128]{3,2,1,0:T(8,128)(2,1)S(1)}, bf16[5,2,128,128]{3,2,1,0:T(8,128)(2,1)S(1)}, bf16[4,2,128,128]{3,2,1,0:T(8,128)(2,1)S(1)}) custom-call(s32[1]{0:T(128)} %bitcast.odd_ref, bf16[14,2,128,128]{3,2,1,0:T(8,128)(2,1)S(1)} %get-tuple-element.56.env_ref, bf16[2,2,128,2048]{3,2,1,0:T(8,128)(2,1)S(1)} %get-tuple-element.55.both_ref), custom_call_target="tpu_custom_call" | custom-call | flops 1024 | bytes 1024 | tf_op jit(solution)/shard_map/pallas_call | solution.py:498
  85.6 0.1 collective-permute-start.8
  85.7 0.5 collective-permute-start.9
  86.2 0.1 collective-permute-start.10
  86.3 4.4 %collective-permute-done.11.refs_0_ = bf16[8,2,128,128]{3,2,1,0:T(8,128)(2,1)S(1)} collective-permute-done((bf16[8,2,128,128]{3,2,1,0:T(8,128)(2,1)S(1)}, bf16[8,2,128,128]{3,2,1,0:T(8,128)(2,1)S(1)}, u32[]{:S(2)}, u32[]{:S(2)}) %collective-permute-start.11) | collective-permute-done | bytes 524320 | tf_op jit(solution)/shard_map/ppermute | solution.py:569
  90.7 1.1 %shard_map.99 = (f32[14,2,128,128]{3,2,1,0:T(8,128)}, f32[14,2,128,128]{3,2,1,0:T(8,128)}) custom-call(s32[1]{0:T(128)} %bitcast.odd_ref, bf16[8,2,128,128]{3,2,1,0:T(8,128)(2,1)S(1)} %collective-permute-done.11.refs_0_), custom_call_target="tpu_custom_call" | custom-call | flops 1024 | bytes 1024 | tf_op jit(solution)/shard_map/pallas_call | solution.py:498
  91.7 0.0 collective-permute-done.10.refs_2_
  91.8 0.0 collective-permute-done.8.refs_0_
  91.8 0.0 collective-permute-done.9.refs_1_
  91.8 1.3 %shard_map.100 = (f32[14,2,128,128]{3,2,1,0:T(8,128)}, f32[14,2,128,128]{3,2,1,0:T(8,128)}) custom-call(s32[1]{0:T(128)} %bitcast.odd_ref, bf16[5,2,128,128]{3,2,1,0:T(8,128)(2,1)S(1)} %collective-permute-done.8.refs_0_, bf16[5,2,128,128]{3,2,1,0:T(8,128)(2,1)S(1)} %collective-permute-done.9.refs_1_, ...), custom_call_target="tpu_custom_call", output_to_operand_aliasing={{0}: (4, {}), {1}: (5, {})} | custom-call | flops 1024 | bytes 1024 | tf_op jit(solution)/shard_map/pallas_call | solution.py:498
  93.1 1.7 %collective-permute-done.7.refs_0_ = bf16[6,2,128,128]{3,2,1,0:T(8,128)(2,1)S(1)} collective-permute-done((bf16[6,2,128,128]{3,2,1,0:T(8,128)(2,1)S(1)}, bf16[6,2,128,128]{3,2,1,0:T(8,128)(2,1)S(1)}, u32[]{:S(2)}, u32[]{:S(2)}) %collective-permute-start.7) | collective-permute-done | bytes 393248 | tf_op jit(solution)/shard_map/ppermute | solution.py:569
  94.9 1.0 %shard_map.101 = (f32[14,2,128,128]{3,2,1,0:T(8,128)}, f32[14,2,128,128]{3,2,1,0:T(8,128)}) custom-call(s32[1]{0:T(128)} %bitcast.odd_ref, bf16[6,2,128,128]{3,2,1,0:T(8,128)(2,1)S(1)} %collective-permute-done.7.refs_0_, f32[14,2,128,128]{3,2,1,0:T(8,128)} %get-tuple-element.63.refs_1_, ...), custom_call_target="tpu_custom_call", output_to_operand_aliasing={{0}: (2, {}), {1}: (3, {})} | custom-call | flops 1024 | bytes 1024 | tf_op jit(solution)/shard_map/pallas_call | solution.py:498
  (1 shorter events, 0.0 us)
Async XLA Ops:
  0.6 1.2 %copy-start = (bf16[1,2,128,2048]{3,2,1,0:T(8,128)(2,1)S(1)}, bf16[1,2,128,2048]{3,2,1,0:T(8,128)(2,1)}, u32[]{:S(2)}) copy-start(bf16[1,2,128,2048]{3,2,1,0:T(8,128)(2,1)} %param.6) | copy-start | bytes 3145732
  1.9 3.0 %copy-start.4 = (bf16[1,14,16,16]{3,2,1,0:T(8,128)(2,1)S(1)}, bf16[1,14,16,16]{3,2,1,0:T(8,128)(2,1)}, u32[]{:S(2)}) copy-start(bf16[1,14,16,16]{3,2,1,0:T(8,128)(2,1)} %param.9) | copy-start | bytes 21508
  1.9 3.3 %copy-start.6 = (s32[1,14,4]{1,2,0:T(4,128)S(1)}, s32[1,14,4]{1,2,0:T(4,128)}, u32[]{:S(2)}) copy-start(s32[1,14,4]{1,2,0:T(4,128)} %param.10) | copy-start | bytes 676
  1.9 3.5 %copy-start.1 = (bf16[1,2,128,2048]{3,2,1,0:T(8,128)(2,1)S(1)}, bf16[1,2,128,2048]{3,2,1,0:T(8,128)(2,1)}, u32[]{:S(2)}) copy-start(bf16[1,2,128,2048]{3,2,1,0:T(8,128)(2,1)} %param.6) | copy-start | bytes 3145732
  1.9 3.5 %copy-start.2 = (bf16[1,14,2,128,128]{4,3,2,1,0:T(8,128)(2,1)S(1)}, bf16[1,14,2,128,128]{4,3,2,1,0:T(8,128)(2,1)}, u32[]{:S(2)}) copy-start(bf16[1,14,2,128,128]{4,3,2,1,0:T(8,128)(2,1)} %param.7) | copy-start | bytes 2752516
  2.7 14.1 %collective-permute-start.1 = (bf16[1,128,2048]{2,1,0:T(8,128)(2,1)}, bf16[1,128,2048]{2,1,0:T(8,128)(2,1)}, u32[]{:S(2)}, u32[]{:S(2)}) collective-permute-start(bf16[1,128,2048]{2,1,0:T(8,128)(2,1)} %shard_map.88), channel_id=1, source_target_pairs={{0,1},{1,0},{2,3},{3,2},{4,5},{5,4},{6,7},{7,6},{8,9},{9,8},{10,11... | collective-permute-start | bytes 1572872 | tf_op jit(solution)/shard_map/ppermute | solution.py:482
  4.8 23.1 %collective-permute-start = (bf16[1,128,2048]{2,1,0:T(8,128)(2,1)S(1)}, bf16[1,128,2048]{2,1,0:T(8,128)(2,1)S(1)}, u32[]{:S(2)}, u32[]{:S(2)}) collective-permute-start(bf16[1,128,2048]{2,1,0:T(8,128)(2,1)S(1)} %shard_map.87), channel_id=1, source_target_pairs={{0,1},{1,0},{2,3},{3,2},{4,5},{5,4},{6,7},{7,6},{8,9},{9,8},{10,11... | collective-permute-start | bytes 1572872 | tf_op jit(solution)/shard_map/ppermute | solution.py:482
  5.4 1.2 %copy-start.3 = (bf16[1,14,2,128,128]{4,3,2,1,0:T(8,128)(2,1)S(1)}, bf16[1,14,2,128,128]{4,3,2,1,0:T(8,128)(2,1)}, u32[]{:S(2)}) copy-start(bf16[1,14,2,128,128]{4,3,2,1,0:T(8,128)(2,1)} %param.8) | copy-start | bytes 2752516
  22.4 5.5 %collective-permute-start.2 = (f32[8,128]{1,0:T(8,128)S(1)}, f32[8,128]{1,0:T(8,128)S(1)}, u32[]{:S(2)}, u32[]{:S(2)}) collective-permute-start(f32[8,128]{1,0:T(8,128)S(1)} %get-tuple-element.42.mine_ref), channel_id=1, source_target_pairs={{0,1},{1,0},{2,3},{3,2},{4,5},{5,4},{6,7},{7,6},{8,9},{9,8},{10,11... | collective-permute-start | bytes 12296 | tf_op jit(solution)/shard_map/ppermute | solution.py:482
  30.0 17.0 %collective-permute-start.5 = (bf16[1,128,2048]{2,1,0:T(8,128)(2,1)S(1)}, bf16[1,128,2048]{2,1,0:T(8,128)(2,1)S(1)}, u32[]{:S(2)}, u32[]{:S(2)}) collective-permute-start(bf16[1,128,2048]{2,1,0:T(8,128)(2,1)S(1)} %get-tuple-element.44.refs_0_), channel_id=1, source_target_pairs={{0,1},{1,0},{2,3},{3,2},{4,5},{5,4},{6,7},{7,6},{8,9},{9,8},{10,11... | collective-permute-start | bytes 1572872 | tf_op jit(solution)/shard_map/ppermute | solution.py:482
  32.1 5.3 %copy-start.5 = (s32[1,2]{1,0:T(1,128)S(1)}, s32[1,2]{1,0:T(1,128)}, u32[]{:S(2)}) copy-start(s32[1,2]{1,0:T(1,128)} %param.11) | copy-start | bytes 28
  35.9 16.6 %collective-permute-start.4 = (bf16[1,96,2048]{2,1,0:T(8,128)(2,1)S(1)}, bf16[1,96,2048]{2,1,0:T(8,128)(2,1)S(1)}, u32[]{:S(2)}, u32[]{:S(2)}) collective-permute-start(bf16[1,96,2048]{2,1,0:T(8,128)(2,1)S(1)} %get-tuple-element.46), channel_id=1, source_target_pairs={{0,1},{1,0},{2,3},{3,2},{4,5},{5,4},{6,7},{7,6},{8,9},{9,8},{10,11... | collective-permute-start | bytes 1179656 | tf_op jit(solution)/shard_map/ppermute | solution.py:482
  35.9 20.5 %collective-permute-start.3 = (bf16[1,32,2048]{2,1,0:T(8,128)(2,1)S(1)}, bf16[1,32,2048]{2,1,0:T(8,128)(2,1)S(1)}, u32[]{:S(2)}, u32[]{:S(2)}) collective-permute-start(bf16[1,32,2048]{2,1,0:T(8,128)(2,1)S(1)} %get-tuple-element.45), channel_id=1, source_target_pairs={{0,1},{1,0},{2,3},{3,2},{4,5},{5,4},{6,7},{7,6},{8,9},{9,8},{10,11... | collective-permute-start | bytes 393224 | tf_op jit(solution)/shard_map/ppermute | solution.py:482
  60.5 2.6 %collective-permute-start.6 = (f32[16,128]{1,0:T(8,128)S(1)}, f32[16,128]{1,0:T(8,128)S(1)}, u32[]{:S(2)}, u32[]{:S(2)}) collective-permute-start(f32[16,128]{1,0:T(8,128)S(1)} %get-tuple-element.52.my_sums_ref), channel_id=1, source_target_pairs={{0,1},{1,0},{2,3},{3,2},{4,5},{5,4},{6,7},{7,6},{8,9},{9,8},{10,11... | collective-permute-start | bytes 24584 | tf_op jit(solution)/shard_map/ppermute | solution.py:482
  68.6 22.1 %collective-permute-start.11 = (bf16[8,2,128,128]{3,2,1,0:T(8,128)(2,1)S(1)}, bf16[8,2,128,128]{3,2,1,0:T(8,128)(2,1)S(1)}, u32[]{:S(2)}, u32[]{:S(2)}) collective-permute-start(bf16[8,2,128,128]{3,2,1,0:T(8,128)(2,1)S(1)} %get-tuple-element.60), channel_id=1, source_target_pairs={{2,4},{6,8},{10,12},{14,16},{18,20},{22,24},{26,28},{4,2},{8,6},{1... | collective-permute-start | bytes 1572872 | tf_op jit(solution)/shard_map/ppermute | solution.py:569
  77.3 17.5 %collective-permute-start.7 = (bf16[6,2,128,128]{3,2,1,0:T(8,128)(2,1)S(1)}, bf16[6,2,128,128]{3,2,1,0:T(8,128)(2,1)S(1)}, u32[]{:S(2)}, u32[]{:S(2)}) collective-permute-start(bf16[6,2,128,128]{3,2,1,0:T(8,128)(2,1)S(1)} %shard_map.97), channel_id=1, source_target_pairs={{2,4},{6,8},{10,12},{14,16},{18,20},{22,24},{26,28},{4,2},{8,6},{1... | collective-permute-start | bytes 1179656 | tf_op jit(solution)/shard_map/ppermute | solution.py:569
  85.6 6.2 %collective-permute-start.8 = (bf16[5,2,128,128]{3,2,1,0:T(8,128)(2,1)S(1)}, bf16[5,2,128,128]{3,2,1,0:T(8,128)(2,1)S(1)}, u32[]{:S(2)}, u32[]{:S(2)}) collective-permute-start(bf16[5,2,128,128]{3,2,1,0:T(8,128)(2,1)S(1)} %get-tuple-element.57), channel_id=1, source_target_pairs={{0,2},{4,6},{8,10},{12,14},{16,18},{20,22},{24,26},{28,30},{2,0},{... | collective-permute-start | bytes 983048 | tf_op jit(solution)/shard_map/ppermute | solution.py:569
  85.7 6.1 %collective-permute-start.9 = (bf16[5,2,128,128]{3,2,1,0:T(8,128)(2,1)S(1)}, bf16[5,2,128,128]{3,2,1,0:T(8,128)(2,1)S(1)}, u32[]{:S(2)}, u32[]{:S(2)}) collective-permute-start(bf16[5,2,128,128]{3,2,1,0:T(8,128)(2,1)S(1)} %get-tuple-element.58), channel_id=1, source_target_pairs={{0,2},{4,6},{8,10},{12,14},{16,18},{20,22},{24,26},{28,30},{2,0},{... | collective-permute-start | bytes 983048 | tf_op jit(solution)/shard_map/ppermute | solution.py:569
  86.2 5.6 %collective-permute-start.10 = (bf16[4,2,128,128]{3,2,1,0:T(8,128)(2,1)S(1)}, bf16[4,2,128,128]{3,2,1,0:T(8,128)(2,1)S(1)}, u32[]{:S(2)}, u32[]{:S(2)}) collective-permute-start(bf16[4,2,128,128]{3,2,1,0:T(8,128)(2,1)S(1)} %get-tuple-element.59), channel_id=1, source_target_pairs={{0,2},{4,6},{8,10},{12,14},{16,18},{20,22},{24,26},{28,30},{2,0},{... | collective-permute-start | bytes 786440 | tf_op jit(solution)/shard_map/ppermute | solution.py:569
